TPU v7x, 32 devices: a whole 2x2x4 slice. The times are simulated.
32 devices in a mesh: rows: 8 (over z, y), cols: 4 (over x, core).
Axes of the slice: x: 2, y: 2, z: 4, core: 2. Of those that a mesh axis runs over, the one named last changes fastest.
Arguments:
- coupling: float32 [256, 4, 2, 128, 128], P('rows', 'cols'), may hold values from 1.9 to 2120
- coupling_index: int32 [256, 4, 2], P('rows', 'cols'), may hold values from 0 to 7, as said below
- near_cost: float32 [256, 3, 128, 128], P('rows'), may hold values from 0 to 2
- near_index: int32 [256, 3], P('rows'), may hold values from 0 to 255, as said below
- source_weights: int32 [32768], P('rows'), may hold values from 1 to 98
- target_cost: float32 [4, 8, 3, 128, 128], P('cols', 'rows'), may hold values from 0 to 2
- target_index: int32 [4, 8, 3], P('cols'), may hold values from 0 to 7, as said below
- target_weights: int32 [4, 1024], P('cols', 'rows'), may hold values from 1 to 98
Outputs:
- cost_blocks: float32 [256, 4, 2, 128, 128], P('rows', 'cols')
- source_potential: float32 [32768], P('rows')
- target_potential: float32 [4, 1024], P('cols', 'rows')
Inputs may be any that keep to these rules, and one draw needn't show every extreme that they name: `coupling_index`: the 2 entries of one block row and group differ; every target block of every group is named by some block row. near_index[i, 0] = i; the 3 entries of a row differ and lie in the same aligned group of 4 block rows as i. target_index[c, j, 0] = j; the 3 entries of a row differ.
All inputs are finite; a program needn't handle non-finite values.
Results may differ from a plain program's by a relative error of at most 0.0003.
Values sent between devices are 32-bit elements; how exact they have to be, the bound alone decides.
No kernel may reach another device: no remote copies, remote signals or barrier semaphores. Data moves between devices by JAX's collectives and lax.ppermute only.
A program may use at most 256 MiB of HBM per device.

v0:
```python
import jax
import jax.numpy as jnp
from jax import lax
from jax.sharding import PartitionSpec as P

ITERS = 3


entropy = 0.01
very_low = -1e30
full_precision = lax.Precision.HIGHEST


def per_device(
    coupling,
    coupling_index,
    near_cost,
    near_index,
    source_weights,
    target_cost,
    target_index,
    target_weights,
):
    rows_here = coupling.shape[0]
    slot_count = coupling.shape[2]
    width = coupling.shape[3]
    near_count = near_cost.shape[1]
    group_blocks = target_index.shape[1]
    link_count = target_index.shape[2]
    target_here = target_cost.shape[1]
    row_devices = lax.axis_size("rows")
    col_devices = lax.axis_size("cols")
    first_row = lax.axis_index("rows") * rows_here
    source_count = rows_here * row_devices * width
    target_count = group_blocks * width * col_devices
    source_float = source_weights.astype(jnp.float32)
    source_total = lax.psum(jnp.sum(source_float), "rows")
    source_mass = (source_count * source_float / source_total).reshape(rows_here, width)
    group_cost, group_weights = (
        lax.all_gather(target_cost, "rows", axis=1, tiled=True),
        lax.all_gather(target_weights.astype(jnp.float32), "rows", axis=1, tiled=True),
    )
    target_total = lax.psum(jnp.sum(group_weights), "cols")
    target_mass = (target_count * group_weights[0] / target_total).reshape(group_blocks, width)
    group_cost = group_cost[0]
    links = target_index[0]
    scale_near = 1.0 / (near_count * width)
    scale_far = 1.0 / (slot_count * col_devices * width)
    local_near = near_index - first_row
    row_term = (
        jnp.einsum(
            "ikxy,iky->ix", near_cost * near_cost, source_mass[local_near], precision=full_precision
        )
        * scale_near
    )
    spread_terms = jnp.einsum(
        "jw,jmwz->jmz", target_mass, group_cost * group_cost, precision=full_precision
    )
    one_hot = (links[..., None] == jnp.arange(group_blocks)[None, None, :]).astype(jnp.float32)
    column_term = jnp.einsum("jmz,jmt->tz", spread_terms, one_hot, precision=full_precision) / (
        link_count * width
    )
    slots_here = coupling_index[:, 0, :]
    far_plan = coupling[local_near][:, :, 0]
    partial_blocks = jnp.einsum("ikxy,ikqyz->ikqxz", near_cost, far_plan, precision=full_precision)
    far_slots = slots_here[local_near]
    far_blocks = group_cost[far_slots]
    match = (links[far_slots][..., None] == slots_here[:, None, None, None, :]).astype(jnp.float32)
    through = jnp.einsum(
        "ikqxy,ikqmyz->ikqmxz", partial_blocks, far_blocks, precision=full_precision
    )
    product = jnp.einsum("ikqmxz,ikqml->ilxz", through, match, precision=full_precision)
    cost_blocks = (
        row_term[:, None, :, None]
        + column_term[slots_here][:, :, None, :]
        - 2.0 * scale_near * scale_far * product
    )
    log_source = jnp.log(source_mass)
    log_target = jnp.log(target_mass)
    selected = slots_here[..., None] == jnp.arange(group_blocks)[None, None, :]
    selected_float = selected.astype(jnp.float32)
    target_potential = jnp.zeros((group_blocks, width), jnp.float32)
    source_potential = jnp.zeros((rows_here, width), jnp.float32)
    for step in range(ITERS):
        scores = (target_potential[slots_here][:, :, None, :] - cost_blocks) / entropy
        row_peak = jnp.max(scores, axis=(1, 3))
        row_peak = lax.pmax(row_peak, "cols")
        row_part = jnp.sum(jnp.exp(scores - row_peak[:, None, :, None]), axis=(1, 3))
        row_total = lax.psum(row_part, "cols")
        source_potential = entropy * (log_source - (row_peak + jnp.log(row_total)))
        back_scores = (source_potential[:, None, :, None] - cost_blocks) / entropy
        slot_peak = jnp.max(back_scores, axis=2)
        column_peak = jnp.max(
            jnp.where(selected[..., None], slot_peak[:, :, None, :], very_low), axis=(0, 1)
        )
        column_peak = lax.pmax(column_peak, "rows")
        slot_total = jnp.sum(jnp.exp(back_scores - column_peak[slots_here][:, :, None, :]), axis=2)
        column_part = jnp.einsum(
            "iqt,iqz->tz", selected_float, slot_total, precision=full_precision
        )
        column_total = lax.psum(column_part, "rows")
        target_potential = entropy * (log_target - (column_peak + jnp.log(column_total)))
    own_target = lax.dynamic_slice_in_dim(
        target_potential, lax.axis_index("rows") * target_here, target_here, 0
    )
    return (cost_blocks[:, None], source_potential.reshape(rows_here * width), own_target)


def solution(mesh):
    placed = (
        P("rows", "cols", None, None, None),
        P("rows", "cols", None),
        P("rows", None, None, None),
        P("rows", None),
        P("rows"),
        P("cols", "rows", None, None, None),
        P("cols", None, None),
        P("cols", "rows"),
    )
    return jax.shard_map(
        per_device,
        mesh=mesh,
        in_specs=placed,
        out_specs=(P("rows", "cols", None, None, None), P("rows"), P("cols", "rows")),
        check_vma=False,
    )
```

profile of v0, /device:TPU:0, one launch (start us, length us, event | category | flops | bytes accessed | tf_op | source)
XLA Modules:
  0.0 788.6 jit_solution(12493696454763631099)
XLA Ops:
  11.4 23.7 %psum.56 = f32[]{:T(128)} all-reduce(f32[]{:T(128)} %convert_reduce_fusion), channel_id=1, replica_groups=mesh['rows'=8,'cols'=4] {'rows'}, use_global_device_ids=true, to_apply=%region_1.0 | all-reduce | flops 1 | bytes 8 | tf_op jit(solution)/shard_map/psum | solution.py:37
  35.8 16.3 %all_gather.6 = f32[1,1024]{1,0:T(1,128)S(1)} all-gather(f32[1,128]{1,0:T(1,128)S(1)} %convert_element_type.10), channel_id=1, replica_groups=mesh['rows'=8,'cols'=4] {'rows'}, dimensions={1}, use_global_device_ids=true | all-gather | bytes 4608 | tf_op jit(solution)/shard_map/all_gather | solution.py:41
  64.4 10.9 %gather_fusion.5 = f32[96,2,128,128]{3,2,1,0:T(8,128)} fusion(f32[32,2,128,128]{3,2,1,0:T(8,128)} %bitcast.101, s32[1024]{0:T(1024)S(1)} %pad_clamp_fusion.2), kind=kCustom, calls=%fused_computation.5 | custom fusion | bytes 25166208 | tf_op jit(solution)/shard_map/gather | solution.py:64
  77.3 8.9 %fusion.3 = f32[32,1,128,1]{2,1,3,0:T(1,128)S(1)} fusion(f32[32,3,128,1]{2,3,1,0:T(1,128)S(1)} %bitcast.107, f32[32,3,128,128]{3,2,1,0:T(8,128)} %param.10), kind=kOutput, calls=%fused_computation.16 | convolution fusion | flops 20447232 | bytes 6356992 | tf_op jit(solution)/shard_map/ikxy,iky->ix/dot_general | solution.py:51
  86.4 27.3 %fusion.1 = f32[32,3,2,128,128]{4,3,2,1,0:T(8,128)} fusion(f32[32,3,2,128,128]{4,3,2,1,0:T(8,128)} %bitcast.100, f32[32,3,128,128]{3,2,1,0:T(8,128)} %param.10), kind=kOutput, calls=%fused_computation.14 | convolution fusion | flops 4831838208 | bytes 31457280 | tf_op jit(solution)/shard_map/ikxy,ikqyz->ikqxz/dot_general | solution.py:65
  117.1 14.3 %gather_fusion.4 = f32[192,3,128,128]{3,2,1,0:T(8,128)} fusion(f32[8,3,128,128]{3,2,1,0:T(8,128)S(1)} %bitcast.97, s32[1024]{0:T(1024)S(1)} %pad_clamp_fusion), kind=kCustom, calls=%fused_computation.4 | custom fusion | bytes 75498240 | tf_op jit(solution)/shard_map/gather | solution.py:67
  131.3 69.6 %convolution_bitcast_fusion = f32[32,3,2,3,128,128]{4,5,3,2,1,0:T(8,128)} fusion(f32[32,3,2,3,128,128]{5,4,3,2,1,0:T(8,128)} %bitcast.99, f32[32,3,2,128,128]{4,3,2,1,0:T(8,128)} %fusion.1), kind=kOutput, calls=%fused_computation.12 | convolution fusion | flops 14495514624 | bytes 88080384 | tf_op jit(solution)/shard_map/ikqxy,ikqmyz->ikqmxz/dot_general | solution.py:69
  200.9 50.0 %copy.53 = f32[32,3,2,3,128,128]{5,3,2,1,4,0:T(4,128)} copy(f32[32,3,2,3,128,128]{4,5,3,2,1,0:T(8,128)} %convolution_bitcast_fusion) | data formatting | bytes 75497472 | tf_op jit(solution)/shard_map/ikqxy,ikqmyz->ikqmxz/transpose | solution.py:69
  250.9 99.5 %fusion.6 = (f32[32,128]{1,0:T(8,128)S(1)}, f32[32,2,128,128]{3,1,2,0:T(2,128)}) fusion(f32[32,2,128]{2,1,0:T(2,128)S(1)} %bitcast.110, f32[32,3,2,3,128,128]{5,3,2,1,4,0:T(4,128)} %copy.53, f32[32,2,128]{2,1,0:T(2,128)S(1)} %bitcast.124, f32[32,128]{1,0:T(8,128)S(1)} %broadcast_multiply_fusion, pred[32,3,2,3,2,1]{3,4,2,1,5,0:T(4,128)(4,1)S(1)} %fusion.15.clone.4), kind=kOutput, calls=%fused_computation.32 | convolution fusion | flops 232779776 | bytes 42042496 | tf_op jit(solution)/shard_map/ikqmxz,ikqml->ilxz/dot_general | solution.py:72
  350.4 10.7 %pmax.42 = f32[32,128]{1,0:T(8,128)S(1)} all-reduce(f32[32,128]{1,0:T(8,128)S(1)} %get-tuple-element.15), channel_id=1, replica_groups=mesh['rows'=8,'cols'=4] {'cols'}, use_global_device_ids=true, to_apply=%region_5.0 | all-reduce | flops 4096 | bytes 32768 | tf_op jit(solution)/shard_map/pmax | solution.py:87
  361.1 60.5 %exponential_reduce_fusion.5 = f32[32,128]{1,0:T(8,128)S(1)} fusion(f32[32,2,128,128]{3,1,2,0:T(2,128)} %get-tuple-element.16, f32[32,128]{1,0:T(8,128)S(1)} %pmax.42, f32[32,2,128]{2,1,0:T(2,128)S(1)} %bitcast.111), kind=kLoop, calls=%fused_computation.30 | loop fusion | flops 4190208 | bytes 4259840 | tf_op jit(solution)/shard_map/reduce_sum | solution.py:88
  421.7 10.1 %psum.58 = f32[32,128]{1,0:T(8,128)S(1)} all-reduce(f32[32,128]{1,0:T(8,128)S(1)} %exponential_reduce_fusion.5), channel_id=1, replica_groups=mesh['rows'=8,'cols'=4] {'cols'}, use_global_device_ids=true, to_apply=%region_7.0 | all-reduce | flops 4096 | bytes 32768 | tf_op jit(solution)/shard_map/psum | solution.py:89
  432.5 7.4 fusion.7
  440.1 19.1 %pmax.43 = f32[8,128]{1,0:T(8,128)S(1)} all-reduce(f32[8,128]{1,0:T(8,128)S(1)} %select_reduce_fusion.2), channel_id=1, replica_groups=mesh['rows'=8,'cols'=4] {'rows'}, use_global_device_ids=true, to_apply=%region_10.11 | all-reduce | flops 1024 | bytes 8192 | tf_op jit(solution)/shard_map/pmax | solution.py:96
  459.8 7.4 exponential_reduce_fusion.4
  467.4 17.5 %psum.59 = f32[8,128]{1,0:T(8,128)S(1)} all-reduce(f32[8,128]{1,0:T(8,128)S(1)} %convolution_bitcast_fusion.3), channel_id=1, replica_groups=mesh['rows'=8,'cols'=4] {'rows'}, use_global_device_ids=true, to_apply=%region_12.13 | all-reduce | flops 1024 | bytes 8192 | tf_op jit(solution)/shard_map/psum | solution.py:101
  485.6 11.3 %fusion.8 = f32[32,128]{1,0:T(8,128)S(1)} fusion(f32[32,2,128,128]{3,1,2,0:T(2,128)} %get-tuple-element.16, f32[32,2,128]{2,1,0:T(2,128)S(1)} %bitcast.103), kind=kLoop, calls=%fused_computation.34 | loop fusion | flops 3141632 | bytes 4243456 | tf_op jit(solution)/shard_map/reduce_max | solution.py:86
  496.9 10.1 %pmax.44 = f32[32,128]{1,0:T(8,128)S(1)} all-reduce(f32[32,128]{1,0:T(8,128)S(1)} %fusion.8), channel_id=1, replica_groups=mesh['rows'=8,'cols'=4] {'cols'}, use_global_device_ids=true, to_apply=%region_14.15 | all-reduce | flops 4096 | bytes 32768 | tf_op jit(solution)/shard_map/pmax | solution.py:87
  507.0 60.5 %exponential_reduce_fusion.3 = f32[32,128]{1,0:T(8,128)S(1)} fusion(f32[32,2,128,128]{3,1,2,0:T(2,128)} %get-tuple-element.16, f32[32,128]{1,0:T(8,128)S(1)} %pmax.44, f32[32,2,128]{2,1,0:T(2,128)S(1)} %bitcast.104), kind=kLoop, calls=%fused_computation.26 | loop fusion | flops 4190208 | bytes 4259840 | tf_op jit(solution)/shard_map/reduce_sum | solution.py:88
  567.6 10.3 %psum.60 = f32[32,128]{1,0:T(8,128)S(1)} all-reduce(f32[32,128]{1,0:T(8,128)S(1)} %exponential_reduce_fusion.3), channel_id=1, replica_groups=mesh['rows'=8,'cols'=4] {'cols'}, use_global_device_ids=true, to_apply=%region_16.17 | all-reduce | flops 4096 | bytes 32768 | tf_op jit(solution)/shard_map/psum | solution.py:89
  578.5 7.4 fusion.9
  586.1 19.1 %pmax.45 = f32[8,128]{1,0:T(8,128)S(1)} all-reduce(f32[8,128]{1,0:T(8,128)S(1)} %select_reduce_fusion.1), channel_id=1, replica_groups=mesh['rows'=8,'cols'=4] {'rows'}, use_global_device_ids=true, to_apply=%region_19.20 | all-reduce | flops 1024 | bytes 8192 | tf_op jit(solution)/shard_map/pmax | solution.py:96
  605.8 7.4 exponential_reduce_fusion.2
  613.4 17.1 %psum.61 = f32[8,128]{1,0:T(8,128)S(1)} all-reduce(f32[8,128]{1,0:T(8,128)S(1)} %convolution_bitcast_fusion.2), channel_id=1, replica_groups=mesh['rows'=8,'cols'=4] {'rows'}, use_global_device_ids=true, to_apply=%region_21.22 | all-reduce | flops 1024 | bytes 8192 | tf_op jit(solution)/shard_map/psum | solution.py:101
  631.2 11.3 %fusion.10 = f32[32,128]{1,0:T(8,128)S(1)} fusion(f32[32,2,128,128]{3,1,2,0:T(2,128)} %get-tuple-element.16, f32[32,2,128]{2,1,0:T(2,128)S(1)} %bitcast.105), kind=kLoop, calls=%fused_computation.36 | loop fusion | flops 3141632 | bytes 4243456 | tf_op jit(solution)/shard_map/reduce_max | solution.py:86
  642.5 10.3 %pmax.46 = f32[32,128]{1,0:T(8,128)S(1)} all-reduce(f32[32,128]{1,0:T(8,128)S(1)} %fusion.10), channel_id=1, replica_groups=mesh['rows'=8,'cols'=4] {'cols'}, use_global_device_ids=true, to_apply=%region_23.24 | all-reduce | flops 4096 | bytes 32768 | tf_op jit(solution)/shard_map/pmax | solution.py:87
  652.8 60.5 %exponential_reduce_fusion.1 = f32[32,128]{1,0:T(8,128)S(1)} fusion(f32[32,2,128,128]{3,1,2,0:T(2,128)} %get-tuple-element.16, f32[32,128]{1,0:T(8,128)S(1)} %pmax.46, f32[32,2,128]{2,1,0:T(2,128)S(1)} %bitcast.106), kind=kLoop, calls=%fused_computation.22 | loop fusion | flops 4190208 | bytes 4259840 | tf_op jit(solution)/shard_map/reduce_sum | solution.py:88
  713.4 10.1 %psum.62 = f32[32,128]{1,0:T(8,128)S(1)} all-reduce(f32[32,128]{1,0:T(8,128)S(1)} %exponential_reduce_fusion.1), channel_id=1, replica_groups=mesh['rows'=8,'cols'=4] {'cols'}, use_global_device_ids=true, to_apply=%region_25.26 | all-reduce | flops 4096 | bytes 32768 | tf_op jit(solution)/shard_map/psum | solution.py:89
  724.2 7.4 fusion.11
  731.7 19.1 %pmax.47 = f32[8,128]{1,0:T(8,128)S(1)} all-reduce(f32[8,128]{1,0:T(8,128)S(1)} %select_reduce_fusion), channel_id=1, replica_groups=mesh['rows'=8,'cols'=4] {'rows'}, use_global_device_ids=true, to_apply=%region_28.29 | all-reduce | flops 1024 | bytes 8192 | tf_op jit(solution)/shard_map/pmax | solution.py:96
  751.4 7.4 exponential_reduce_fusion
  759.1 17.1 %psum.63 = f32[8,128]{1,0:T(8,128)S(1)} all-reduce(f32[8,128]{1,0:T(8,128)S(1)} %convolution_bitcast_fusion.1), channel_id=1, replica_groups=mesh['rows'=8,'cols'=4] {'rows'}, use_global_device_ids=true, to_apply=%region_30.31 | all-reduce | flops 1024 | bytes 8192 | tf_op jit(solution)/shard_map/psum | solution.py:101
  (65 shorter events, 34.0 us)
Async XLA Ops:
  7.2 106.5 %all-gather.2.cloned.1.call-start = ((), (), s32[]{:S(2)}) async-start(), calls=%async_computation | async-start | bytes 1769472 | tf_op jit(solution)/shard_map/all_gather | solution.py:40
  113.7 3.4 copy-start
  350.4 81.4 %copy-start.1 = (s32[4096]{0:T(1024)S(1)}, s32[4096]{0:T(1024)}, u32[]{:S(2)}) copy-start(s32[4096]{0:T(1024)} %param.12) | copy-start | bytes 49156
  432.5 34.7 %copy-start.3 = (s32[32,1,2]{0,2,1:T(2,128)S(1)}, s32[32,1,2]{0,2,1:T(2,128)}, u32[]{:S(2)}) copy-start(s32[32,1,2]{0,2,1:T(2,128)} %param.9) | copy-start | bytes 772
  724.1 34.7 %copy-start.2 = (f32[32,128]{1,0:T(8,128)}, f32[32,128]{1,0:T(8,128)S(1)}, u32[]{:S(2)}) copy-start(f32[32,128]{1,0:T(8,128)S(1)} %subtract_multiply_fusion.6) | copy-start | bytes 49156
Sparse Core Ops, SparseCore 0:
  10.2 46.9 all-gather.1
where the time goes:
time: 797 us; the launch traced here: 789 us
  other arithmetic  258 us (32%)
  blocking collectives  217 us (27%)
  matrix products  209 us (26%)
  local copies, waits for them, and re-layouts  89.2 us (11%)
  between operations  14.5 us (2%)
    reduce_sum x3, other arithmetic, per_device(): jnp.sum(jnp.exp(scores - row_peak[:, None, :, None]), axis=(1, 3))  182 us
    dot_general x1, matrix products, per_device(): jnp.einsum('ikqmxz,ikqml->ilxz', through, match, precision=full_precision)  99.5 us
    dot_general x1, matrix products, per_device(): jnp.einsum('ikqxy,ikqmyz->ikqmxz', partial_blocks, far_blocks, precision=...  69.6 us
    pmax x3, blocking collectives, per_device(): column_peak = lax.pmax(column_peak, 'rows')  57.4 us
    psum x3, blocking collectives, per_device(): column_total = lax.psum(column_part, 'rows')  51.8 us
    transpose x1, local copies, waits for them, and re-layouts, per_device(): jnp.einsum('ikqxy,ikqmyz->ikqmxz', partial_blocks, far_blocks, precision=...  50 us
    pmax x3, blocking collectives, per_device(): row_peak = lax.pmax(row_peak, 'cols')  31.2 us
    psum x3, blocking collectives, per_device(): row_total = lax.psum(row_part, 'cols')  30.5 us
  transfers between devices with their start and end apart: 1, of which 0 were waited for; matrix products, arithmetic and copies ran while one was open for 8% of the time, Pallas kernels for 0%

commit v1 on v0

v1 whole, which is shorter than its diff:
```python
import functools
import math

import jax
import jax.numpy as jnp
from jax import lax
from jax.experimental import pallas as pl
from jax.experimental.pallas import tpu as pltpu
from jax.sharding import PartitionSpec as P

ITERS = 3
SUB = 4

entropy = 0.01
to_log2 = math.log2(math.e) / entropy
from_log2 = entropy * math.log(2.0)
very_low = -1e30
vmem_bytes = 40 * 1024 * 1024

SMEM = pl.BlockSpec(memory_space=pltpu.SMEM)


def whole(shape):
    return pl.BlockSpec(shape, lambda *_: (0,) * len(shape))


def split(x):
    high = x.astype(jnp.bfloat16)
    return high, (x - high.astype(jnp.float32)).astype(jnp.bfloat16)


def tree(parts, op):
    while len(parts) > 1:
        half = len(parts) // 2
        parts = [op(parts[s], parts[s + half]) for s in range(half)]
    return parts[0]


def log_sum(parts):
    peak = tree(parts, jnp.maximum)
    return peak + jnp.log2(tree([jnp.exp2(p - peak) for p in parts], jnp.add))


def send(x, axis, mask):
    size = lax.axis_size(axis)
    return lax.ppermute(x, axis, [(d, d ^ mask) for d in range(size)])


def exchange(x, axis):
    return [x] + [send(x, axis, s) for s in range(1, lax.axis_size(axis))]


def pack_kernel(source_ref, target_ref, out_ref):
    out_ref[...] = jnp.zeros_like(out_ref)
    for place, ref in enumerate((source_ref, target_ref)):
        total = jnp.sum(ref[...].astype(jnp.float32), axis=(0, 1), keepdims=True)
        out_ref[place : place + 1, :] = jnp.broadcast_to(total, (1, out_ref.shape[1]))
    out_ref[2 : 2 + target_ref.shape[0], :] = target_ref[...].astype(jnp.float32)


def near_kernel(near_index_ref, cost_ref, plan_ref, mass_ref, high_ref, low_ref, term_ref, plan_scr):
    g = pl.program_id(0)
    near_count = cost_ref.shape[1]
    width = cost_ref.shape[2]
    slots = plan_ref.shape[2]
    wide = slots * width
    for a in range(SUB):
        plan = jnp.concatenate([plan_ref[a, 0, q] for q in range(slots)], axis=1)
        high, low = split(plan)
        plan_scr[a, 0:width, :] = high
        plan_scr[a, width : 2 * width, :] = low
        plan_scr[a, 2 * width : 3 * width, :] = high
    lanes = lax.broadcasted_iota(jnp.int32, (width, SUB), 1)
    terms = jnp.zeros((width, SUB), jnp.float32)
    for i in range(SUB):
        acc = None
        for k in range(near_count):
            a = near_index_ref[k, g * SUB + i] & (SUB - 1)
            cost = cost_ref[i, k]
            high, low = split(cost)
            x = jnp.dot(
                jnp.concatenate([high, high, low], axis=1),
                plan_scr[a],
                preferred_element_type=jnp.float32,
            )
            x_high, x_low = split(x)
            high_ref[i, :, k * wide : (k + 1) * wide] = x_high
            low_ref[i, :, k * wide : (k + 1) * wide] = x_low
            weighted = cost * cost * mass_ref[pl.ds(g * SUB + a, 1), :].astype(jnp.float32)
            acc = weighted if acc is None else acc + weighted
        terms = jnp.where(lanes == i, jnp.sum(acc, axis=1, keepdims=True), terms)
    term_ref[0] = terms


def far_kernel(counts, row_axis, *refs):
    row_devices, target_here, source_count, target_count, group_blocks, link_count = counts
    near_index_ref, slot_ref, link_ref, high_ref, low_ref, term_ref, mass_ref = refs[:7]
    cost_parts = refs[7 : 7 + row_devices]
    packs = refs[7 + row_devices : 7 + 2 * row_devices]
    out_ref, peak_ref, log_source_ref, log_target_ref = refs[7 + 2 * row_devices : 11 + 2 * row_devices]
    far_high, far_low, table, column_scr, scale_scr, peak_scr, sum_scr = refs[11 + 2 * row_devices :]
    g = pl.program_id(0)
    steps = pl.num_programs(0)
    near_count = near_index_ref.shape[0]
    slots = slot_ref.shape[0]
    rows = high_ref.shape[0]
    width = high_ref.shape[1]
    zero_block = group_blocks * link_count

    @pl.when(g == 0)
    def _():
        me = lax.axis_index(row_axis)
        far_high[zero_block] = jnp.zeros((width, width), jnp.bfloat16)
        far_low[zero_block] = jnp.zeros((width, width), jnp.bfloat16)

        def clear(e, _):
            table[e] = zero_block
            return 0

        lax.fori_loop(0, group_blocks * group_blocks, clear, 0)

        def mark(j, _):
            for m in range(link_count):
                table[j * group_blocks + link_ref[m, 0, j]] = j * link_count + m
            return 0

        lax.fori_loop(0, group_blocks, mark, 0)
        total_source = tree([p[0:1, :] for p in packs], jnp.add)
        total_target = tree([p[1:2, :] for p in packs], jnp.add)
        log_source_ref[...] = jnp.log2(source_count * mass_ref[...].astype(jnp.float32) / total_source)
        scale_scr[...] = source_count / (total_source * (near_count * width))
        column_scr[...] = jnp.zeros_like(column_scr)
        for s in range(row_devices):
            for h in range(target_here):
                j = (me ^ s) * target_here + h
                mass = target_count * packs[s][2 + h : 3 + h, :] / total_target
                log_target_ref[pl.ds(j, 1), :] = jnp.log2(mass)
                tall = jnp.broadcast_to(mass, (width, width)).T
                for m in range(link_count):
                    block = cost_parts[s][0, h, m]
                    high, low = split(block)
                    far_high[j * link_count + m] = high
                    far_low[j * link_count + m] = low
                    spread = jnp.sum(tall * (block * block), axis=0, keepdims=True)
                    t = link_ref[m, 0, j]
                    column_scr[pl.ds(t, 1), :] += spread * (1.0 / (link_count * width))

    group_devices = target_count // (group_blocks * width)
    coef = 2.0 * (1.0 / (near_count * width)) * (1.0 / (slots * group_devices * width))
    lanes = lax.broadcasted_iota(jnp.int32, peak_scr.shape, 1)
    scale = scale_scr[0:1, 0:1]
    for i in range(rows):
        row = g * rows + i
        group = row - lax.rem(row, SUB)
        targets = [slot_ref[l, row] for l in range(slots)]
        far_rows = []
        for k in range(near_count):
            a = group + (near_index_ref[k, row] & (SUB - 1))
            for q in range(slots):
                j = slot_ref[q, a]
                far_rows.append([table[j * group_blocks + t] for t in targets])
        right_high = jnp.concatenate(
            [jnp.concatenate([far_high[e] for e in r], axis=1) for r in far_rows], axis=0
        )
        right_low = jnp.concatenate(
            [jnp.concatenate([far_low[e] for e in r], axis=1) for r in far_rows], axis=0
        )
        high = high_ref[i]
        product = jnp.dot(high, right_high, preferred_element_type=jnp.float32)
        product += jnp.dot(high, right_low, preferred_element_type=jnp.float32)
        product += jnp.dot(low_ref[i], right_high, preferred_element_type=jnp.float32)
        tall = term_ref[i // SUB, :, i % SUB : i % SUB + 1] * scale
        scores = []
        for l in range(slots):
            cost = tall + column_scr[pl.ds(targets[l], 1), :] - coef * product[:, l * width : (l + 1) * width]
            out_ref[i, 0, l] = cost
            scores.append(cost * -to_log2)
        row_pass(scores, row, lanes, peak_scr, sum_scr)

    @pl.when(g == steps - 1)
    def _():
        finish_rows(peak_ref, peak_scr, sum_scr)


def row_pass(scores, row, lanes, peak_scr, sum_scr):
    peak = jnp.max(functools.reduce(jnp.maximum, scores), axis=1, keepdims=True)
    total = functools.reduce(jnp.add, [jnp.exp2(s - peak) for s in scores])
    total = jnp.sum(total, axis=1, keepdims=True)
    peak_scr[...] = jnp.where(lanes == row, peak, peak_scr[...])
    sum_scr[...] = jnp.where(lanes == row, total, sum_scr[...])


def finish_rows(out_ref, peak_scr, sum_scr):
    rows = out_ref.shape[0]
    score = peak_scr[...] + jnp.log2(sum_scr[...])
    out_ref[...] = score.T[:rows, :]


def column_kernel(col_devices, *refs):
    cost_ref, select_ref, log_mass_ref = refs[:3]
    parts = refs[3 : 3 + col_devices]
    out_ref, potential_ref = refs[3 + col_devices : 5 + col_devices]
    potential_scr, peak_scr, sum_scr = refs[5 + col_devices :]
    g = pl.program_id(0)
    rows, _, slots, width, _ = cost_ref.shape

    @pl.when(g == 0)
    def _():
        scaled = log_mass_ref[...] - log_sum([p[...] for p in parts])
        potential_scr[...] = scaled
        potential_ref[...] = scaled * from_log2

    tall = potential_scr[pl.ds(pl.multiple_of(g * rows, rows), rows), :].T
    for i in range(rows):
        for l in range(slots):
            score = tall[:, i : i + 1] - cost_ref[i, 0, l] * to_log2
            peak = jnp.max(score, axis=0, keepdims=True)
            total = jnp.sum(jnp.exp2(score - peak), axis=0, keepdims=True)
            place = g * (rows * slots) + i * slots + l
            peak_scr[pl.ds(place, 1), :] = peak
            sum_scr[pl.ds(place, 1), :] = total

    @pl.when(g == pl.num_programs(0) - 1)
    def _():
        select = select_ref[...]
        peaks = peak_scr[...]
        sums = sum_scr[...]
        for t in range(out_ref.shape[0]):
            chosen = select == t
            peak = jnp.max(jnp.where(chosen, peaks, very_low), axis=0, keepdims=True)
            shifted = jnp.where(chosen, sums * jnp.exp2(jnp.minimum(peaks - peak, 0.0)), 0.0)
            total = jnp.sum(shifted, axis=0, keepdims=True)
            some = total > 0.0
            out_ref[t : t + 1, :] = jnp.where(
                some, peak + jnp.log2(jnp.where(some, total, 1.0)), very_low
            )


def row_kernel(row_devices, *refs):
    slot_ref, cost_ref, log_mass_ref = refs[:3]
    parts = refs[3 : 3 + row_devices]
    out_ref = refs[3 + row_devices]
    potential_scr, peak_scr, sum_scr = refs[4 + row_devices :]
    g = pl.program_id(0)
    rows, _, slots, _, _ = cost_ref.shape

    @pl.when(g == 0)
    def _():
        potential_scr[...] = log_mass_ref[...] - log_sum([p[...] for p in parts])

    lanes = lax.broadcasted_iota(jnp.int32, peak_scr.shape, 1)
    for i in range(rows):
        row = g * rows + i
        scores = [
            potential_scr[pl.ds(slot_ref[l, row], 1), :] - cost_ref[i, 0, l] * to_log2
            for l in range(slots)
        ]
        row_pass(scores, row, lanes, peak_scr, sum_scr)

    @pl.when(g == pl.num_programs(0) - 1)
    def _():
        finish_rows(out_ref, peak_scr, sum_scr)


def last_kernel(row_devices, target_here, row_axis, *refs):
    log_mass_ref = refs[0]
    parts = refs[1 : 1 + row_devices]
    out_ref, scr = refs[1 + row_devices :]
    scr[...] = (log_mass_ref[...] - log_sum([p[...] for p in parts])) * from_log2
    me = lax.axis_index(row_axis)
    for h in range(target_here):
        out_ref[h : h + 1, :] = scr[pl.ds(me * target_here + h, 1), :]


def per_device(
    coupling,
    coupling_index,
    near_cost,
    near_index,
    source_weights,
    target_cost,
    target_index,
    target_weights,
):
    rows_here = coupling.shape[0]
    slots = coupling.shape[2]
    width = coupling.shape[3]
    near_count = near_cost.shape[1]
    group_blocks = target_index.shape[1]
    link_count = target_index.shape[2]
    target_here = target_cost.shape[1]
    row_devices = lax.axis_size("rows")
    col_devices = lax.axis_size("cols")
    source_count = rows_here * row_devices * width
    target_count = group_blocks * width * col_devices
    f32 = jnp.float32
    params = pltpu.CompilerParams(vmem_limit_bytes=vmem_bytes)

    arrived = {0: target_cost}
    arrived[1] = send(target_cost, "rows", 1)
    for mask in range(2, row_devices, 2):
        arrived[mask] = send(target_cost, "rows", mask)
    for mask in range(2, row_devices, 2):
        arrived[mask + 1] = send(arrived[mask], "rows", 1)
    cost_parts = [arrived[s] for s in range(row_devices)]

    near_t = near_index.T
    slot_t = coupling_index[:, 0, :].T
    link_t = jnp.transpose(target_index, (2, 0, 1))
    mass = source_weights.reshape(rows_here, width)
    select = jnp.broadcast_to(
        coupling_index.reshape(rows_here * slots, 1), (rows_here * slots, width)
    )

    pack_rows = 8 * pl.cdiv(2 + target_here, 8)
    pack = pl.pallas_call(
        pack_kernel,
        out_shape=jax.ShapeDtypeStruct((pack_rows, width), f32),
        name="pack",
    )(mass, target_weights.reshape(target_here, width))
    target_sum = tree([p[1:2] for p in exchange(pack, "cols")], jnp.add)
    pack = jnp.concatenate([pack[0:1], target_sum, pack[2:]], axis=0)
    packs = exchange(pack, "rows")

    wide = near_count * slots * width
    groups = rows_here // SUB
    high, low, term = pl.pallas_call(
        near_kernel,
        grid=(groups,),
        in_specs=[
            SMEM,
            pl.BlockSpec((SUB, near_count, width, width), lambda g: (g, 0, 0, 0)),
            pl.BlockSpec((SUB, 1, slots, width, width), lambda g: (g, 0, 0, 0, 0)),
            whole((rows_here, width)),
        ],
        out_specs=[
            pl.BlockSpec((SUB, width, wide), lambda g: (g, 0, 0)),
            pl.BlockSpec((SUB, width, wide), lambda g: (g, 0, 0)),
            pl.BlockSpec((1, width, SUB), lambda g: (g, 0, 0)),
        ],
        out_shape=[
            jax.ShapeDtypeStruct((rows_here, width, wide), jnp.bfloat16),
            jax.ShapeDtypeStruct((rows_here, width, wide), jnp.bfloat16),
            jax.ShapeDtypeStruct((groups, width, SUB), f32),
        ],
        scratch_shapes=[pltpu.VMEM((SUB, 3 * width, slots * width), jnp.bfloat16)],
        compiler_params=params,
        cost_estimate=pl.CostEstimate(
            flops=6 * rows_here * wide * width * width,
            bytes_accessed=rows_here * width * (4 * near_count * width + 4 * slots * width + 4 * wide),
            transcendentals=0,
        ),
        name="near_product",
    )(near_t, near_cost, coupling, mass)

    step_rows = SUB
    steps = rows_here // step_rows
    cost_block = pl.BlockSpec((step_rows, 1, slots, width, width), lambda g: (g, 0, 0, 0, 0))
    cost_blocks, row_part, log_source, log_target = pl.pallas_call(
        functools.partial(
            far_kernel,
            (row_devices, target_here, source_count, target_count, group_blocks, link_count),
            "rows",
        ),
        grid=(steps,),
        in_specs=[
            SMEM,
            SMEM,
            SMEM,
            pl.BlockSpec((step_rows, width, wide), lambda g: (g, 0, 0)),
            pl.BlockSpec((step_rows, width, wide), lambda g: (g, 0, 0)),
            pl.BlockSpec((step_rows // SUB, width, SUB), lambda g: (g, 0, 0)),
            whole((rows_here, width)),
        ]
        + [whole(target_cost.shape)] * row_devices
        + [whole((pack_rows, width))] * row_devices,
        out_specs=[
            cost_block,
            whole((rows_here, width)),
            whole((rows_here, width)),
            whole((group_blocks, width)),
        ],
        out_shape=[
            jax.ShapeDtypeStruct(coupling.shape, f32),
            jax.ShapeDtypeStruct((rows_here, width), f32),
            jax.ShapeDtypeStruct((rows_here, width), f32),
            jax.ShapeDtypeStruct((group_blocks, width), f32),
        ],
        scratch_shapes=[
            pltpu.VMEM((group_blocks * link_count + 1, width, width), jnp.bfloat16),
            pltpu.VMEM((group_blocks * link_count + 1, width, width), jnp.bfloat16),
            pltpu.SMEM((group_blocks * group_blocks,), jnp.int32),
            pltpu.VMEM((group_blocks, width), f32),
            pltpu.VMEM((1, width), f32),
            pltpu.VMEM((width, width), f32),
            pltpu.VMEM((width, width), f32),
        ],
        compiler_params=params,
        name="far_product",
    )(near_t, slot_t, link_t, high, low, term, mass, *cost_parts, *packs)

    pass_rows = 8
    passes = rows_here // pass_rows
    pass_block = pl.BlockSpec((pass_rows, 1, slots, width, width), lambda g: (g, 0, 0, 0, 0))

    def column_step(row_parts):
        return pl.pallas_call(
            functools.partial(column_kernel, col_devices),
            grid=(passes,),
            in_specs=[pass_block, whole((rows_here * slots, width)), whole((rows_here, width))]
            + [whole((rows_here, width))] * col_devices,
            out_specs=[whole((group_blocks, width)), whole((rows_here, width))],
            out_shape=[
                jax.ShapeDtypeStruct((group_blocks, width), f32),
                jax.ShapeDtypeStruct((rows_here, width), f32),
            ],
            scratch_shapes=[
                pltpu.VMEM((rows_here, width), f32),
                pltpu.VMEM((rows_here * slots, width), f32),
                pltpu.VMEM((rows_here * slots, width), f32),
            ],
            compiler_params=params,
            name="column_pass",
        )(cost_blocks, select, log_source, *row_parts)

    def row_step(column_parts):
        return pl.pallas_call(
            functools.partial(row_kernel, row_devices),
            grid=(passes,),
            in_specs=[SMEM, pass_block, whole((group_blocks, width))]
            + [whole((group_blocks, width))] * row_devices,
            out_specs=whole((rows_here, width)),
            out_shape=jax.ShapeDtypeStruct((rows_here, width), f32),
            scratch_shapes=[
                pltpu.VMEM((group_blocks, width), f32),
                pltpu.VMEM((width, width), f32),
                pltpu.VMEM((width, width), f32),
            ],
            compiler_params=params,
            name="row_pass",
        )(slot_t, cost_blocks, log_target, *column_parts)

    for step in range(ITERS):
        column_part, source_potential = column_step(exchange(row_part, "cols"))
        column_parts = exchange(column_part, "rows")
        if step < ITERS - 1:
            row_part = row_step(column_parts)
    own_target = pl.pallas_call(
        functools.partial(last_kernel, row_devices, target_here, "rows"),
        out_shape=jax.ShapeDtypeStruct((target_here, width), f32),
        scratch_shapes=[pltpu.VMEM((group_blocks, width), f32)],
        name="last_potential",
    )(log_target, *column_parts)
    return (
        cost_blocks,
        source_potential.reshape(rows_here * width),
        own_target.reshape(1, target_here * width),
    )


def solution(mesh):
    placed = (
        P("rows", "cols", None, None, None),
        P("rows", "cols", None),
        P("rows", None, None, None),
        P("rows", None),
        P("rows"),
        P("cols", "rows", None, None, None),
        P("cols", None, None),
        P("cols", "rows"),
    )
    return jax.shard_map(
        per_device,
        mesh=mesh,
        in_specs=placed,
        out_specs=(P("rows", "cols", None, None, None), P("rows"), P("cols", "rows")),
        check_vma=False,
    )
```

time: 797 us -> 143 us (0.18)
  other arithmetic: 258 us -> 0.78 us
  blocking collectives: 217 us -> 0 us
  matrix products: 209 us -> 0 us
  local copies, waits for them, and re-layouts: 89.2 us -> 7.36 us
  starting transfers between devices: 0.04 us -> 65.3 us
  Pallas kernels: 0 us -> 39.3 us
  waiting for transfers between devices: 0.68 us -> 28.7 us
  between operations: 14.5 us -> 0.86 us
    dot_general x9 -> x0, matrix products: 209 us -> none  [the longest x1 99.5 us: per_device(): jnp.einsum('ikqmxz,ikqml->ilxz', through, match, precision=full_precision)]
    reduce_sum x8 -> x0, other arithmetic: 206 us -> none  [the longest x3 182 us: per_device(): jnp.sum(jnp.exp(scores - row_peak[:, None, :, None]), axis=(1, 3))]
    psum x8 -> x0, blocking collectives: 113 us -> none  [the longest x3 51.8 us: per_device(): column_total = lax.psum(column_part, 'rows')]
    pmax x6 -> x0, blocking collectives: 88.5 us -> none  [the longest x3 57.4 us: per_device(): column_peak = lax.pmax(column_peak, 'rows')]
    ppermute x0 -> x47, starting transfers between devices: none -> 65.3 us  [send(): return lax.ppermute(x, axis, [(d, d ^ mask) for d in range(size)])]
    transpose x1 -> x0, local copies, waits for them, and re-layouts: 50 us -> none  [per_device(): jnp.einsum('ikqxy,ikqmyz->ikqmxz', partial_blocks, far_blocks, precision=...]
    reduce_max x9 -> x0, other arithmetic: 45.4 us -> none  [the longest x3 22.8 us: per_device(): row_peak = jnp.max(scores, axis=(1, 3))]
    pallas_call x0 -> x9, Pallas kernels: none -> 39.3 us  [the longest x1 12.4 us: per_device(): pl.pallas_call(functools.partial(far_kernel, (row_devices, target_here, s...]
  transfers between devices with their start and end apart: 1 -> 47, of which waited for: 0 -> 16; matrix products, arithmetic and copies ran while one was open for 8% -> 1% of each run, Pallas kernels for 0% -> 7%
where the time goes in v1:
time: 143 us; the launch traced here: 142 us
  starting transfers between devices  65.3 us (46%)
  Pallas kernels  39.3 us (27%)
  waiting for transfers between devices  28.7 us (20%)
  local copies, waits for them, and re-layouts  7.36 us (5%)
    ppermute x47, starting transfers between devices, send(): return lax.ppermute(x, axis, [(d, d ^ mask) for d in range(size)])  65.3 us
    ppermute x47, waiting for transfers between devices, send(): return lax.ppermute(x, axis, [(d, d ^ mask) for d in range(size)])  28.7 us
    pallas_call x1, Pallas kernels, per_device(): pl.pallas_call(functools.partial(far_kernel, (row_devices, target_here, s...  12.4 us
    pallas_call x1, Pallas kernels, per_device(): pl.pallas_call(near_kernel, grid=(groups,), in_specs=[SMEM, pl.BlockSpec(...  10.4 us
    pallas_call x3, Pallas kernels, column_step(): pl.pallas_call(functools.partial(column_kernel, col_devices), grid=(passe...  7.91 us
    unnamed x35, local copies, waits for them, and re-layouts  6.49 us
    pallas_call x2, Pallas kernels, row_step(): pl.pallas_call(functools.partial(row_kernel, row_devices), grid=(passes,)...  5.84 us
  transfers between devices with their start and end apart: 47, of which 16 were waited for; matrix products, arithmetic and copies ran while one was open for 1% of the time, Pallas kernels for 7%

profile of v1, /device:TPU:0, one launch (start us, length us, event | category | flops | bytes accessed | tf_op | source)
XLA Modules:
  0.0 142.3 jit_solution(16472643450622148429)
XLA Ops:
  2.1 2.9 %collective-permute-start.7 = (f32[8,128]{1,0:T(8,128)}, f32[8,128]{1,0:T(8,128)S(1)}, u32[]{:S(2)}, u32[]{:S(2)}) collective-permute-start(f32[8,128]{1,0:T(8,128)} %pack.1), channel_id=1, source_target_pairs={{0,2},{1,3},{2,0},{3,1},{4,6},{5,7},{6,4},{7,5},{8,10},{9,11},{10,... | collective-permute-start | bytes 12296 | tf_op jit(solution)/shard_map/ppermute | solution.py:46
  5.2 2.1 %collective-permute-start.1 = (f32[1,1,3,128,128]{4,3,2,1,0:T(8,128)}, f32[1,1,3,128,128]{4,3,2,1,0:T(8,128)S(1)}, u32[]{:S(2)}, u32[]{:S(2)}) collective-permute-start(f32[1,1,3,128,128]{4,3,2,1,0:T(8,128)} %refs_7_.1), channel_id=1, source_target_pairs={{0,8},{4,12},{8,0},{12,4},{16,24},{20,28},{24,16},{28,20},{1,9},{5... | collective-permute-start | bytes 589832 | tf_op jit(solution)/shard_map/ppermute | solution.py:46
  7.3 2.6 %collective-permute-start.3 = (f32[1,1,3,128,128]{4,3,2,1,0:T(8,128)}, f32[1,1,3,128,128]{4,3,2,1,0:T(8,128)S(1)}, u32[]{:S(2)}, u32[]{:S(2)}) collective-permute-start(f32[1,1,3,128,128]{4,3,2,1,0:T(8,128)} %refs_7_.1), channel_id=1, source_target_pairs={{0,16},{4,20},{8,24},{12,28},{16,0},{20,4},{24,8},{28,12},{1,17},{... | collective-permute-start | bytes 589832 | tf_op jit(solution)/shard_map/ppermute | solution.py:46
  16.9 3.6 %collective-permute-done.11.refs_17_ = f32[8,128]{1,0:T(8,128)S(1)} collective-permute-done((f32[8,128]{1,0:T(8,128)S(1)}, f32[8,128]{1,0:T(8,128)S(1)}, u32[]{:S(2)}, u32[]{:S(2)}) %collective-permute-start.11) | collective-permute-done | bytes 4128 | tf_op jit(solution)/shard_map/ppermute | solution.py:46
  20.5 3.4 %collective-permute-start.13 = (f32[8,128]{1,0:T(8,128)S(1)}, f32[8,128]{1,0:T(8,128)S(1)}, u32[]{:S(2)}, u32[]{:S(2)}) collective-permute-start(f32[8,128]{1,0:T(8,128)S(1)} %pad_maximum_fusion.refs_15_), channel_id=1, source_target_pairs={{0,16},{4,20},{8,24},{12,28},{16,0},{20,4},{24,8},{28,12},{1,17},{... | collective-permute-start | bytes 12296 | tf_op jit(solution)/shard_map/ppermute | solution.py:46
  24.9 3.0 %collective-permute-done.13.refs_19_ = f32[8,128]{1,0:T(8,128)S(1)} collective-permute-done((f32[8,128]{1,0:T(8,128)S(1)}, f32[8,128]{1,0:T(8,128)S(1)}, u32[]{:S(2)}, u32[]{:S(2)}) %collective-permute-start.13) | collective-permute-done | bytes 4128 | tf_op jit(solution)/shard_map/ppermute | solution.py:46
  27.9 2.5 %collective-permute-start.15 = (f32[8,128]{1,0:T(8,128)S(1)}, f32[8,128]{1,0:T(8,128)S(1)}, u32[]{:S(2)}, u32[]{:S(2)}) collective-permute-start(f32[8,128]{1,0:T(8,128)S(1)} %pad_maximum_fusion.refs_15_), channel_id=1, source_target_pairs={{0,24},{4,28},{8,16},{12,20},{16,8},{20,12},{24,0},{28,4},{1,25},{... | collective-permute-start | bytes 12296 | tf_op jit(solution)/shard_map/ppermute | solution.py:46
  33.3 3.5 %collective-permute-start.16 = (f32[8,128]{1,0:T(8,128)S(1)}, f32[8,128]{1,0:T(8,128)S(1)}, u32[]{:S(2)}, u32[]{:S(2)}) collective-permute-start(f32[8,128]{1,0:T(8,128)S(1)} %pad_maximum_fusion.refs_15_), channel_id=1, source_target_pairs={{0,28},{4,24},{8,20},{12,16},{16,12},{20,8},{24,4},{28,0},{1,29},{... | collective-permute-start | bytes 12296 | tf_op jit(solution)/shard_map/ppermute | solution.py:46
  39.3 2.2 %copy-done.2 = f32[32,1,2,128,128]{4,3,2,1,0:T(8,128)S(1)} copy-done((f32[32,1,2,128,128]{4,3,2,1,0:T(8,128)S(1)}, f32[32,1,2,128,128]{4,3,2,1,0:T(8,128)}, u32[]{:S(2)}) %copy-start.2) | copy-done | bytes 4194328
  42.9 10.4 %near_product.1 = (bf16[32,128,768]{2,1,0:T(8,128)(2,1)S(1)}, bf16[32,128,768]{2,1,0:T(8,128)(2,1)}, f32[8,128,4]{2,1,0:T(8,128)S(1)}) custom-call(s32[3,32]{1,0:T(4,128)S(1)} %bitcast.15, f32[32,3,128,128]{3,2,1,0:T(8,128)} %cost_ref.1, f32[32,1,2,128,128]{4,3,2,1,0:T(8,128)S(1)} %copy-done.2, s32[32,128]{1,0:T(8,128)S(1)} %bitcast.10), custom_call_target="tpu_custom_call" | custom-call | flops 2415919104 | bytes 23068672 | tf_op jit(solution)/shard_map/near_product/pallas_call | solution.py:327
  53.4 12.4 %far_product.1 = (f32[32,1,2,128,128]{4,3,2,1,0:T(8,128)}, f32[32,128]{1,0:T(8,128)S(1)}, f32[32,128]{1,0:T(8,128)S(1)}, f32[8,128]{1,0:T(8,128)S(1)}) custom-call(s32[3,32]{1,0:T(4,128)S(1)} %bitcast.16, s32[2,32]{1,0:T(2,128)S(1)} %bitcast.12, s32[3,1,8]{2,1,0:T(1,128)S(1)} %bitcast.17, bf16[32,128,768]{2,1,0:T(8,128)(2,1)S(1)} %get-tuple-element.14.refs_3_, ...), custom_call_target="tpu_custom_call" | custom-call | tf_op jit(solution)/shard_map/far_product/pallas_call | solution.py:359
  70.6 2.2 %copy-done = f32[32,1,2,128,128]{4,3,2,1,0:T(8,128)S(1)} copy-done((f32[32,1,2,128,128]{4,3,2,1,0:T(8,128)S(1)}, f32[32,1,2,128,128]{4,3,2,1,0:T(8,128)}, u32[]{:S(2)}) %copy-start) | copy-done | bytes 4194328
  72.8 2.6 %column_pass.3 = (f32[8,128]{1,0:T(8,128)S(1)}, f32[32,128]{1,0:T(8,128)}) custom-call(f32[32,1,2,128,128]{4,3,2,1,0:T(8,128)S(1)} %copy-done, s32[64,128]{1,0:T(8,128)S(1)} %broadcast_in_dim.8.refs_1_, f32[32,128]{1,0:T(8,128)S(1)} %get-tuple-element.18.refs_2_, f32[32,128]{1,0:T(8,128)S(1)} %get-tuple-element.20.refs_3_, ...), custom_call_target="tpu_custom_call" | custom-call | tf_op jit(solution)/shard_map/column_pass/pallas_call | solution.py:407
  76.9 1.9 %collective-permute-start.22 = (f32[8,128]{1,0:T(8,128)S(1)}, f32[8,128]{1,0:T(8,128)S(1)}, u32[]{:S(2)}, u32[]{:S(2)}) collective-permute-start(f32[8,128]{1,0:T(8,128)S(1)} %get-tuple-element.21.refs_3_), channel_id=1, source_target_pairs={{0,12},{4,8},{8,4},{12,0},{16,28},{20,24},{24,20},{28,16},{1,13},{... | collective-permute-start | bytes 12296 | tf_op jit(solution)/shard_map/ppermute | solution.py:46
  78.9 3.9 %collective-permute-start.24 = (f32[8,128]{1,0:T(8,128)S(1)}, f32[8,128]{1,0:T(8,128)S(1)}, u32[]{:S(2)}, u32[]{:S(2)}) collective-permute-start(f32[8,128]{1,0:T(8,128)S(1)} %get-tuple-element.21.refs_3_), channel_id=1, source_target_pairs={{0,20},{4,16},{8,28},{12,24},{16,4},{20,0},{24,12},{28,8},{1,21},{... | collective-permute-start | bytes 12296 | tf_op jit(solution)/shard_map/ppermute | solution.py:46
  84.1 2.4 %collective-permute-start.26 = (f32[8,128]{1,0:T(8,128)S(1)}, f32[8,128]{1,0:T(8,128)S(1)}, u32[]{:S(2)}, u32[]{:S(2)}) collective-permute-start(f32[8,128]{1,0:T(8,128)S(1)} %get-tuple-element.21.refs_3_), channel_id=1, source_target_pairs={{0,28},{4,24},{8,20},{12,16},{16,12},{20,8},{24,4},{28,0},{1,29},{... | collective-permute-start | bytes 12296 | tf_op jit(solution)/shard_map/ppermute | solution.py:46
  88.2 2.2 %collective-permute-done.26.refs_10_ = f32[8,128]{1,0:T(8,128)S(1)} collective-permute-done((f32[8,128]{1,0:T(8,128)S(1)}, f32[8,128]{1,0:T(8,128)S(1)}, u32[]{:S(2)}, u32[]{:S(2)}) %collective-permute-start.26) | collective-permute-done | bytes 4128 | tf_op jit(solution)/shard_map/ppermute | solution.py:46
  90.4 2.9 %row_pass.2.refs_3_ = f32[32,128]{1,0:T(8,128)S(1)} custom-call(s32[2,32]{1,0:T(2,128)S(1)} %bitcast.13, f32[32,1,2,128,128]{4,3,2,1,0:T(8,128)S(1)} %copy-done.1, f32[8,128]{1,0:T(8,128)S(1)} %get-tuple-element.19.refs_2_.refs_0_, f32[8,128]{1,0:T(8,128)S(1)} %get-tuple-element.21.refs_3_, f32[8,128]{1,0:T(8,128)S(1)} %collective-permute-done.20.refs_4_, ...), custom_call_target="tpu_custom_call" | custom-call | tf_op jit(solution)/shard_map/row_pass/pallas_call | solution.py:427
  95.3 2.0 %collective-permute-done.28.refs_5_ = f32[32,128]{1,0:T(8,128)S(1)} collective-permute-done((f32[32,128]{1,0:T(8,128)S(1)}, f32[32,128]{1,0:T(8,128)S(1)}, u32[]{:S(2)}, u32[]{:S(2)}) %collective-permute-start.28) | collective-permute-done | bytes 16416 | tf_op jit(solution)/shard_map/ppermute | solution.py:46
  97.4 2.6 %column_pass.4 = (f32[8,128]{1,0:T(8,128)S(1)}, f32[32,128]{1,0:T(8,128)}) custom-call(f32[32,1,2,128,128]{4,3,2,1,0:T(8,128)S(1)} %copy-done.1, s32[64,128]{1,0:T(8,128)S(1)} %broadcast_in_dim.8.refs_1_, f32[32,128]{1,0:T(8,128)S(1)} %get-tuple-element.18.refs_2_, f32[32,128]{1,0:T(8,128)S(1)} %row_pass.2.refs_3_, ...), custom_call_target="tpu_custom_call" | custom-call | tf_op jit(solution)/shard_map/column_pass/pallas_call | solution.py:407
  100.5 3.1 %collective-permute-start.32 = (f32[8,128]{1,0:T(8,128)S(1)}, f32[8,128]{1,0:T(8,128)S(1)}, u32[]{:S(2)}, u32[]{:S(2)}) collective-permute-start(f32[8,128]{1,0:T(8,128)S(1)} %get-tuple-element.22.refs_3_), channel_id=1, source_target_pairs={{0,12},{4,8},{8,4},{12,0},{16,28},{20,24},{24,20},{28,16},{1,13},{... | collective-permute-start | bytes 12296 | tf_op jit(solution)/shard_map/ppermute | solution.py:46
  104.6 1.8 %collective-permute-start.34 = (f32[8,128]{1,0:T(8,128)S(1)}, f32[8,128]{1,0:T(8,128)S(1)}, u32[]{:S(2)}, u32[]{:S(2)}) collective-permute-start(f32[8,128]{1,0:T(8,128)S(1)} %get-tuple-element.22.refs_3_), channel_id=1, source_target_pairs={{0,20},{4,16},{8,28},{12,24},{16,4},{20,0},{24,12},{28,8},{1,21},{... | collective-permute-start | bytes 12296 | tf_op jit(solution)/shard_map/ppermute | solution.py:46
  106.3 2.6 %collective-permute-start.35 = (f32[8,128]{1,0:T(8,128)S(1)}, f32[8,128]{1,0:T(8,128)S(1)}, u32[]{:S(2)}, u32[]{:S(2)}) collective-permute-start(f32[8,128]{1,0:T(8,128)S(1)} %get-tuple-element.22.refs_3_), channel_id=1, source_target_pairs={{0,24},{4,28},{8,16},{12,20},{16,8},{20,12},{24,0},{28,4},{1,25},{... | collective-permute-start | bytes 12296 | tf_op jit(solution)/shard_map/ppermute | solution.py:46
  108.9 2.3 %collective-permute-start.36 = (f32[8,128]{1,0:T(8,128)S(1)}, f32[8,128]{1,0:T(8,128)S(1)}, u32[]{:S(2)}, u32[]{:S(2)}) collective-permute-start(f32[8,128]{1,0:T(8,128)S(1)} %get-tuple-element.22.refs_3_), channel_id=1, source_target_pairs={{0,28},{4,24},{8,20},{12,16},{16,12},{20,8},{24,4},{28,0},{1,29},{... | collective-permute-start | bytes 12296 | tf_op jit(solution)/shard_map/ppermute | solution.py:46
  111.7 3.5 %collective-permute-done.36.refs_10_ = f32[8,128]{1,0:T(8,128)S(1)} collective-permute-done((f32[8,128]{1,0:T(8,128)S(1)}, f32[8,128]{1,0:T(8,128)S(1)}, u32[]{:S(2)}, u32[]{:S(2)}) %collective-permute-start.36) | collective-permute-done | bytes 4128 | tf_op jit(solution)/shard_map/ppermute | solution.py:46
  115.2 2.9 %row_pass.3.refs_3_ = f32[32,128]{1,0:T(8,128)S(1)} custom-call(s32[2,32]{1,0:T(2,128)S(1)} %bitcast.14, f32[32,1,2,128,128]{4,3,2,1,0:T(8,128)S(1)} %copy-done.1, f32[8,128]{1,0:T(8,128)S(1)} %get-tuple-element.19.refs_2_.refs_0_, f32[8,128]{1,0:T(8,128)S(1)} %get-tuple-element.22.refs_3_, f32[8,128]{1,0:T(8,128)S(1)} %collective-permute-done.30.refs_4_, ...), custom_call_target="tpu_custom_call" | custom-call | tf_op jit(solution)/shard_map/row_pass/pallas_call | solution.py:427
  120.0 1.9 %collective-permute-done.38.refs_5_ = f32[32,128]{1,0:T(8,128)S(1)} collective-permute-done((f32[32,128]{1,0:T(8,128)S(1)}, f32[32,128]{1,0:T(8,128)S(1)}, u32[]{:S(2)}, u32[]{:S(2)}) %collective-permute-start.38) | collective-permute-done | bytes 16416 | tf_op jit(solution)/shard_map/ppermute | solution.py:46
  122.7 2.6 %column_pass.5 = (f32[8,128]{1,0:T(8,128)S(1)}, f32[32,128]{1,0:T(8,128)}) custom-call(f32[32,1,2,128,128]{4,3,2,1,0:T(8,128)S(1)} %copy-done.1, s32[64,128]{1,0:T(8,128)S(1)} %broadcast_in_dim.8.refs_1_, f32[32,128]{1,0:T(8,128)S(1)} %get-tuple-element.18.refs_2_, f32[32,128]{1,0:T(8,128)S(1)} %row_pass.3.refs_3_, ...), custom_call_target="tpu_custom_call" | custom-call | tf_op jit(solution)/shard_map/column_pass/pallas_call | solution.py:407
  126.9 1.9 %collective-permute-start.42 = (f32[8,128]{1,0:T(8,128)S(1)}, f32[8,128]{1,0:T(8,128)S(1)}, u32[]{:S(2)}, u32[]{:S(2)}) collective-permute-start(f32[8,128]{1,0:T(8,128)S(1)} %get-tuple-element.24.refs_1_), channel_id=1, source_target_pairs={{0,12},{4,8},{8,4},{12,0},{16,28},{20,24},{24,20},{28,16},{1,13},{... | collective-permute-start | bytes 12296 | tf_op jit(solution)/shard_map/ppermute | solution.py:46
  128.8 3.9 %collective-permute-start.44 = (f32[8,128]{1,0:T(8,128)S(1)}, f32[8,128]{1,0:T(8,128)S(1)}, u32[]{:S(2)}, u32[]{:S(2)}) collective-permute-start(f32[8,128]{1,0:T(8,128)S(1)} %get-tuple-element.24.refs_1_), channel_id=1, source_target_pairs={{0,20},{4,16},{8,28},{12,24},{16,4},{20,0},{24,12},{28,8},{1,21},{... | collective-permute-start | bytes 12296 | tf_op jit(solution)/shard_map/ppermute | solution.py:46
  134.1 2.4 %collective-permute-start.46 = (f32[8,128]{1,0:T(8,128)S(1)}, f32[8,128]{1,0:T(8,128)S(1)}, u32[]{:S(2)}, u32[]{:S(2)}) collective-permute-start(f32[8,128]{1,0:T(8,128)S(1)} %get-tuple-element.24.refs_1_), channel_id=1, source_target_pairs={{0,28},{4,24},{8,20},{12,16},{16,12},{20,8},{24,4},{28,0},{1,29},{... | collective-permute-start | bytes 12296 | tf_op jit(solution)/shard_map/ppermute | solution.py:46
  138.1 2.2 %collective-permute-done.46.refs_8_ = f32[8,128]{1,0:T(8,128)S(1)} collective-permute-done((f32[8,128]{1,0:T(8,128)S(1)}, f32[8,128]{1,0:T(8,128)S(1)}, u32[]{:S(2)}, u32[]{:S(2)}) %collective-permute-start.46) | collective-permute-done | bytes 4128 | tf_op jit(solution)/shard_map/ppermute | solution.py:46
  (111 shorter events, 38.7 us)
Async XLA Ops:
  2.1 8.4 %collective-permute-start.7 = (f32[8,128]{1,0:T(8,128)}, f32[8,128]{1,0:T(8,128)S(1)}, u32[]{:S(2)}, u32[]{:S(2)}) collective-permute-start(f32[8,128]{1,0:T(8,128)} %pack.1), channel_id=1, source_target_pairs={{0,2},{1,3},{2,0},{3,1},{4,6},{5,7},{6,4},{7,5},{8,10},{9,11},{10,... | collective-permute-start | bytes 12296 | tf_op jit(solution)/shard_map/ppermute | solution.py:46
  5.0 5.9 %collective-permute-start.8 = (f32[8,128]{1,0:T(8,128)}, f32[8,128]{1,0:T(8,128)S(1)}, u32[]{:S(2)}, u32[]{:S(2)}) collective-permute-start(f32[8,128]{1,0:T(8,128)} %pack.1), channel_id=1, source_target_pairs={{0,1},{1,0},{2,3},{3,2},{4,5},{5,4},{6,7},{7,6},{8,9},{9,8},{10,11... | collective-permute-start | bytes 12296 | tf_op jit(solution)/shard_map/ppermute | solution.py:46
  5.2 31.6 %collective-permute-start.1 = (f32[1,1,3,128,128]{4,3,2,1,0:T(8,128)}, f32[1,1,3,128,128]{4,3,2,1,0:T(8,128)S(1)}, u32[]{:S(2)}, u32[]{:S(2)}) collective-permute-start(f32[1,1,3,128,128]{4,3,2,1,0:T(8,128)} %refs_7_.1), channel_id=1, source_target_pairs={{0,8},{4,12},{8,0},{12,4},{16,24},{20,28},{24,16},{28,20},{1,9},{5... | collective-permute-start | bytes 589832 | tf_op jit(solution)/shard_map/ppermute | solution.py:46
  7.3 30.0 %collective-permute-start.3 = (f32[1,1,3,128,128]{4,3,2,1,0:T(8,128)}, f32[1,1,3,128,128]{4,3,2,1,0:T(8,128)S(1)}, u32[]{:S(2)}, u32[]{:S(2)}) collective-permute-start(f32[1,1,3,128,128]{4,3,2,1,0:T(8,128)} %refs_7_.1), channel_id=1, source_target_pairs={{0,16},{4,20},{8,24},{12,28},{16,0},{20,4},{24,8},{28,12},{1,17},{... | collective-permute-start | bytes 589832 | tf_op jit(solution)/shard_map/ppermute | solution.py:46
  10.5 28.3 %collective-permute-start.5 = (f32[1,1,3,128,128]{4,3,2,1,0:T(8,128)}, f32[1,1,3,128,128]{4,3,2,1,0:T(8,128)S(1)}, u32[]{:S(2)}, u32[]{:S(2)}) collective-permute-start(f32[1,1,3,128,128]{4,3,2,1,0:T(8,128)} %refs_7_.1), channel_id=1, source_target_pairs={{0,24},{4,28},{8,16},{12,20},{16,8},{20,12},{24,0},{28,4},{1,25},{... | collective-permute-start | bytes 589832 | tf_op jit(solution)/shard_map/ppermute | solution.py:46
  13.3 7.1 %collective-permute-start.11 = (f32[8,128]{1,0:T(8,128)S(1)}, f32[8,128]{1,0:T(8,128)S(1)}, u32[]{:S(2)}, u32[]{:S(2)}) collective-permute-start(f32[8,128]{1,0:T(8,128)S(1)} %pad_maximum_fusion.refs_15_), channel_id=1, source_target_pairs={{0,8},{4,12},{8,0},{12,4},{16,24},{20,28},{24,16},{28,20},{1,9},{5... | collective-permute-start | bytes 12296 | tf_op jit(solution)/shard_map/ppermute | solution.py:46
  15.4 8.5 %collective-permute-start.12 = (f32[8,128]{1,0:T(8,128)S(1)}, f32[8,128]{1,0:T(8,128)S(1)}, u32[]{:S(2)}, u32[]{:S(2)}) collective-permute-start(f32[8,128]{1,0:T(8,128)S(1)} %pad_maximum_fusion.refs_15_), channel_id=1, source_target_pairs={{0,12},{4,8},{8,4},{12,0},{16,28},{20,24},{24,20},{28,16},{1,13},{... | collective-permute-start | bytes 12296 | tf_op jit(solution)/shard_map/ppermute | solution.py:46
  20.5 7.4 %collective-permute-start.13 = (f32[8,128]{1,0:T(8,128)S(1)}, f32[8,128]{1,0:T(8,128)S(1)}, u32[]{:S(2)}, u32[]{:S(2)}) collective-permute-start(f32[8,128]{1,0:T(8,128)S(1)} %pad_maximum_fusion.refs_15_), channel_id=1, source_target_pairs={{0,16},{4,20},{8,24},{12,28},{16,0},{20,4},{24,8},{28,12},{1,17},{... | collective-permute-start | bytes 12296 | tf_op jit(solution)/shard_map/ppermute | solution.py:46
  23.9 6.5 %collective-permute-start.14 = (f32[8,128]{1,0:T(8,128)S(1)}, f32[8,128]{1,0:T(8,128)S(1)}, u32[]{:S(2)}, u32[]{:S(2)}) collective-permute-start(f32[8,128]{1,0:T(8,128)S(1)} %pad_maximum_fusion.refs_15_), channel_id=1, source_target_pairs={{0,20},{4,16},{8,28},{12,24},{16,4},{20,0},{24,12},{28,8},{1,21},{... | collective-permute-start | bytes 12296 | tf_op jit(solution)/shard_map/ppermute | solution.py:46
  30.4 22.9 %collective-permute-start = (f32[1,1,3,128,128]{4,3,2,1,0:T(8,128)}, f32[1,1,3,128,128]{4,3,2,1,0:T(8,128)S(1)}, u32[]{:S(2)}, u32[]{:S(2)}) collective-permute-start(f32[1,1,3,128,128]{4,3,2,1,0:T(8,128)} %refs_7_.1), channel_id=1, source_target_pairs={{0,4},{4,0},{8,12},{12,8},{16,20},{20,16},{24,28},{28,24},{1,5},{5... | collective-permute-start | bytes 589832 | tf_op jit(solution)/shard_map/ppermute | solution.py:46
  33.3 20.0 %collective-permute-start.16 = (f32[8,128]{1,0:T(8,128)S(1)}, f32[8,128]{1,0:T(8,128)S(1)}, u32[]{:S(2)}, u32[]{:S(2)}) collective-permute-start(f32[8,128]{1,0:T(8,128)S(1)} %pad_maximum_fusion.refs_15_), channel_id=1, source_target_pairs={{0,28},{4,24},{8,20},{12,16},{16,12},{20,8},{24,4},{28,0},{1,29},{... | collective-permute-start | bytes 12296 | tf_op jit(solution)/shard_map/ppermute | solution.py:46
  36.8 16.5 %collective-permute-start.2 = (f32[1,1,3,128,128]{4,3,2,1,0:T(8,128)S(1)}, f32[1,1,3,128,128]{4,3,2,1,0:T(8,128)S(1)}, u32[]{:S(2)}, u32[]{:S(2)}) collective-permute-start(f32[1,1,3,128,128]{4,3,2,1,0:T(8,128)S(1)} %collective-permute-done.1.refs_9_), channel_id=1, source_target_pairs={{0,4},{4,0},{8,12},{12,8},{16,20},{20,16},{24,28},{28,24},{1,5},{5... | collective-permute-start | bytes 589832 | tf_op jit(solution)/shard_map/ppermute | solution.py:46
  37.3 16.0 %collective-permute-start.4 = (f32[1,1,3,128,128]{4,3,2,1,0:T(8,128)S(1)}, f32[1,1,3,128,128]{4,3,2,1,0:T(8,128)S(1)}, u32[]{:S(2)}, u32[]{:S(2)}) collective-permute-start(f32[1,1,3,128,128]{4,3,2,1,0:T(8,128)S(1)} %collective-permute-done.3.refs_11_), channel_id=1, source_target_pairs={{0,4},{4,0},{8,12},{12,8},{16,20},{20,16},{24,28},{28,24},{1,5},{5... | collective-permute-start | bytes 589832 | tf_op jit(solution)/shard_map/ppermute | solution.py:46
  38.8 14.5 %collective-permute-start.6 = (f32[1,1,3,128,128]{4,3,2,1,0:T(8,128)S(1)}, f32[1,1,3,128,128]{4,3,2,1,0:T(8,128)S(1)}, u32[]{:S(2)}, u32[]{:S(2)}) collective-permute-start(f32[1,1,3,128,128]{4,3,2,1,0:T(8,128)S(1)} %collective-permute-done.5.refs_13_), channel_id=1, source_target_pairs={{0,4},{4,0},{8,12},{12,8},{16,20},{20,16},{24,28},{28,24},{1,5},{5... | collective-permute-start | bytes 589832 | tf_op jit(solution)/shard_map/ppermute | solution.py:46
  75.4 7.4 %collective-permute-start.20 = (f32[8,128]{1,0:T(8,128)S(1)}, f32[8,128]{1,0:T(8,128)S(1)}, u32[]{:S(2)}, u32[]{:S(2)}) collective-permute-start(f32[8,128]{1,0:T(8,128)S(1)} %get-tuple-element.21.refs_3_), channel_id=1, source_target_pairs={{0,4},{4,0},{8,12},{12,8},{16,20},{20,16},{24,28},{28,24},{1,5},{5... | collective-permute-start | bytes 12296 | tf_op jit(solution)/shard_map/ppermute | solution.py:46
  76.9 7.2 %collective-permute-start.21 = (f32[8,128]{1,0:T(8,128)S(1)}, f32[8,128]{1,0:T(8,128)S(1)}, u32[]{:S(2)}, u32[]{:S(2)}) collective-permute-start(f32[8,128]{1,0:T(8,128)S(1)} %get-tuple-element.21.refs_3_), channel_id=1, source_target_pairs={{0,8},{4,12},{8,0},{12,4},{16,24},{20,28},{24,16},{28,20},{1,9},{5... | collective-permute-start | bytes 12296 | tf_op jit(solution)/shard_map/ppermute | solution.py:46
  76.9 9.6 %collective-permute-start.22 = (f32[8,128]{1,0:T(8,128)S(1)}, f32[8,128]{1,0:T(8,128)S(1)}, u32[]{:S(2)}, u32[]{:S(2)}) collective-permute-start(f32[8,128]{1,0:T(8,128)S(1)} %get-tuple-element.21.refs_3_), channel_id=1, source_target_pairs={{0,12},{4,8},{8,4},{12,0},{16,28},{20,24},{24,20},{28,16},{1,13},{... | collective-permute-start | bytes 12296 | tf_op jit(solution)/shard_map/ppermute | solution.py:46
  78.9 7.7 %collective-permute-start.23 = (f32[8,128]{1,0:T(8,128)S(1)}, f32[8,128]{1,0:T(8,128)S(1)}, u32[]{:S(2)}, u32[]{:S(2)}) collective-permute-start(f32[8,128]{1,0:T(8,128)S(1)} %get-tuple-element.21.refs_3_), channel_id=1, source_target_pairs={{0,16},{4,20},{8,24},{12,28},{16,0},{20,4},{24,8},{28,12},{1,17},{... | collective-permute-start | bytes 12296 | tf_op jit(solution)/shard_map/ppermute | solution.py:46
  78.9 7.7 %collective-permute-start.24 = (f32[8,128]{1,0:T(8,128)S(1)}, f32[8,128]{1,0:T(8,128)S(1)}, u32[]{:S(2)}, u32[]{:S(2)}) collective-permute-start(f32[8,128]{1,0:T(8,128)S(1)} %get-tuple-element.21.refs_3_), channel_id=1, source_target_pairs={{0,20},{4,16},{8,28},{12,24},{16,4},{20,0},{24,12},{28,8},{1,21},{... | collective-permute-start | bytes 12296 | tf_op jit(solution)/shard_map/ppermute | solution.py:46
  84.1 6.3 %collective-permute-start.26 = (f32[8,128]{1,0:T(8,128)S(1)}, f32[8,128]{1,0:T(8,128)S(1)}, u32[]{:S(2)}, u32[]{:S(2)}) collective-permute-start(f32[8,128]{1,0:T(8,128)S(1)} %get-tuple-element.21.refs_3_), channel_id=1, source_target_pairs={{0,28},{4,24},{8,20},{12,16},{16,12},{20,8},{24,4},{28,0},{1,29},{... | collective-permute-start | bytes 12296 | tf_op jit(solution)/shard_map/ppermute | solution.py:46
  100.0 6.3 %collective-permute-start.30 = (f32[8,128]{1,0:T(8,128)S(1)}, f32[8,128]{1,0:T(8,128)S(1)}, u32[]{:S(2)}, u32[]{:S(2)}) collective-permute-start(f32[8,128]{1,0:T(8,128)S(1)} %get-tuple-element.22.refs_3_), channel_id=1, source_target_pairs={{0,4},{4,0},{8,12},{12,8},{16,20},{20,16},{24,28},{28,24},{1,5},{5... | collective-permute-start | bytes 12296 | tf_op jit(solution)/shard_map/ppermute | solution.py:46
  100.5 8.4 %collective-permute-start.31 = (f32[8,128]{1,0:T(8,128)S(1)}, f32[8,128]{1,0:T(8,128)S(1)}, u32[]{:S(2)}, u32[]{:S(2)}) collective-permute-start(f32[8,128]{1,0:T(8,128)S(1)} %get-tuple-element.22.refs_3_), channel_id=1, source_target_pairs={{0,8},{4,12},{8,0},{12,4},{16,24},{20,28},{24,16},{28,20},{1,9},{5... | collective-permute-start | bytes 12296 | tf_op jit(solution)/shard_map/ppermute | solution.py:46
  100.5 10.7 %collective-permute-start.32 = (f32[8,128]{1,0:T(8,128)S(1)}, f32[8,128]{1,0:T(8,128)S(1)}, u32[]{:S(2)}, u32[]{:S(2)}) collective-permute-start(f32[8,128]{1,0:T(8,128)S(1)} %get-tuple-element.22.refs_3_), channel_id=1, source_target_pairs={{0,12},{4,8},{8,4},{12,0},{16,28},{20,24},{24,20},{28,16},{1,13},{... | collective-permute-start | bytes 12296 | tf_op jit(solution)/shard_map/ppermute | solution.py:46
  103.5 7.7 %collective-permute-start.33 = (f32[8,128]{1,0:T(8,128)S(1)}, f32[8,128]{1,0:T(8,128)S(1)}, u32[]{:S(2)}, u32[]{:S(2)}) collective-permute-start(f32[8,128]{1,0:T(8,128)S(1)} %get-tuple-element.22.refs_3_), channel_id=1, source_target_pairs={{0,16},{4,20},{8,24},{12,28},{16,0},{20,4},{24,8},{28,12},{1,17},{... | collective-permute-start | bytes 12296 | tf_op jit(solution)/shard_map/ppermute | solution.py:46
  104.6 6.6 %collective-permute-start.34 = (f32[8,128]{1,0:T(8,128)S(1)}, f32[8,128]{1,0:T(8,128)S(1)}, u32[]{:S(2)}, u32[]{:S(2)}) collective-permute-start(f32[8,128]{1,0:T(8,128)S(1)} %get-tuple-element.22.refs_3_), channel_id=1, source_target_pairs={{0,20},{4,16},{8,28},{12,24},{16,4},{20,0},{24,12},{28,8},{1,21},{... | collective-permute-start | bytes 12296 | tf_op jit(solution)/shard_map/ppermute | solution.py:46
  108.9 6.3 %collective-permute-start.36 = (f32[8,128]{1,0:T(8,128)S(1)}, f32[8,128]{1,0:T(8,128)S(1)}, u32[]{:S(2)}, u32[]{:S(2)}) collective-permute-start(f32[8,128]{1,0:T(8,128)S(1)} %get-tuple-element.22.refs_3_), channel_id=1, source_target_pairs={{0,28},{4,24},{8,20},{12,16},{16,12},{20,8},{24,4},{28,0},{1,29},{... | collective-permute-start | bytes 12296 | tf_op jit(solution)/shard_map/ppermute | solution.py:46
  125.3 7.4 %collective-permute-start.40 = (f32[8,128]{1,0:T(8,128)S(1)}, f32[8,128]{1,0:T(8,128)S(1)}, u32[]{:S(2)}, u32[]{:S(2)}) collective-permute-start(f32[8,128]{1,0:T(8,128)S(1)} %get-tuple-element.24.refs_1_), channel_id=1, source_target_pairs={{0,4},{4,0},{8,12},{12,8},{16,20},{20,16},{24,28},{28,24},{1,5},{5... | collective-permute-start | bytes 12296 | tf_op jit(solution)/shard_map/ppermute | solution.py:46
  126.9 7.2 %collective-permute-start.41 = (f32[8,128]{1,0:T(8,128)S(1)}, f32[8,128]{1,0:T(8,128)S(1)}, u32[]{:S(2)}, u32[]{:S(2)}) collective-permute-start(f32[8,128]{1,0:T(8,128)S(1)} %get-tuple-element.24.refs_1_), channel_id=1, source_target_pairs={{0,8},{4,12},{8,0},{12,4},{16,24},{20,28},{24,16},{28,20},{1,9},{5... | collective-permute-start | bytes 12296 | tf_op jit(solution)/shard_map/ppermute | solution.py:46
  126.9 9.6 %collective-permute-start.42 = (f32[8,128]{1,0:T(8,128)S(1)}, f32[8,128]{1,0:T(8,128)S(1)}, u32[]{:S(2)}, u32[]{:S(2)}) collective-permute-start(f32[8,128]{1,0:T(8,128)S(1)} %get-tuple-element.24.refs_1_), channel_id=1, source_target_pairs={{0,12},{4,8},{8,4},{12,0},{16,28},{20,24},{24,20},{28,16},{1,13},{... | collective-permute-start | bytes 12296 | tf_op jit(solution)/shard_map/ppermute | solution.py:46
  128.8 7.7 %collective-permute-start.43 = (f32[8,128]{1,0:T(8,128)S(1)}, f32[8,128]{1,0:T(8,128)S(1)}, u32[]{:S(2)}, u32[]{:S(2)}) collective-permute-start(f32[8,128]{1,0:T(8,128)S(1)} %get-tuple-element.24.refs_1_), channel_id=1, source_target_pairs={{0,16},{4,20},{8,24},{12,28},{16,0},{20,4},{24,8},{28,12},{1,17},{... | collective-permute-start | bytes 12296 | tf_op jit(solution)/shard_map/ppermute | solution.py:46
  128.8 7.7 %collective-permute-start.44 = (f32[8,128]{1,0:T(8,128)S(1)}, f32[8,128]{1,0:T(8,128)S(1)}, u32[]{:S(2)}, u32[]{:S(2)}) collective-permute-start(f32[8,128]{1,0:T(8,128)S(1)} %get-tuple-element.24.refs_1_), channel_id=1, source_target_pairs={{0,20},{4,16},{8,28},{12,24},{16,4},{20,0},{24,12},{28,8},{1,21},{... | collective-permute-start | bytes 12296 | tf_op jit(solution)/shard_map/ppermute | solution.py:46
  134.1 6.3 %collective-permute-start.46 = (f32[8,128]{1,0:T(8,128)S(1)}, f32[8,128]{1,0:T(8,128)S(1)}, u32[]{:S(2)}, u32[]{:S(2)}) collective-permute-start(f32[8,128]{1,0:T(8,128)S(1)} %get-tuple-element.24.refs_1_), channel_id=1, source_target_pairs={{0,28},{4,24},{8,20},{12,16},{16,12},{20,8},{24,4},{28,0},{1,29},{... | collective-permute-start | bytes 12296 | tf_op jit(solution)/shard_map/ppermute | solution.py:46
  (32 other events, 290.4 us)

commit v2 on v1

--- a/solution.py
+++ b/solution.py
@@ -29,16 +29,20 @@
     return high, (x - high.astype(jnp.float32)).astype(jnp.bfloat16)
 
 
-def tree(parts, op):
-    while len(parts) > 1:
-        half = len(parts) // 2
-        parts = [op(parts[s], parts[s + half]) for s in range(half)]
-    return parts[0]
-
-
 def log_sum(parts):
-    peak = tree(parts, jnp.maximum)
-    return peak + jnp.log2(tree([jnp.exp2(p - peak) for p in parts], jnp.add))
+    peak = functools.reduce(jnp.maximum, parts)
+    return peak + jnp.log2(functools.reduce(jnp.add, [jnp.exp2(p - peak) for p in parts]))
+
+
+def parts_of(ref, devices):
+    rows = ref.shape[0] // devices
+    return [ref[d * rows : (d + 1) * rows, :] for d in range(devices)]
+
+
+def put_copies(ref, devices, value):
+    rows = value.shape[0]
+    for d in range(devices):
+        ref[d * rows : (d + 1) * rows, :] = value
 
 
 def send(x, axis, mask):
@@ -46,16 +50,18 @@
     return lax.ppermute(x, axis, [(d, d ^ mask) for d in range(size)])
 
 
-def exchange(x, axis):
-    return [x] + [send(x, axis, s) for s in range(1, lax.axis_size(axis))]
-
-
-def pack_kernel(source_ref, target_ref, out_ref):
+def exchange(copies, axis):
+    return lax.all_to_all(copies, axis, 0, 0, tiled=True)
+
+
+def pack_kernel(devices, source_ref, target_ref, out_ref):
+    rows = out_ref.shape[0] // devices
+    total = jnp.sum(source_ref[...].astype(jnp.float32), axis=(0, 1), keepdims=True)
+    target = target_ref[...].astype(jnp.float32)
     out_ref[...] = jnp.zeros_like(out_ref)
-    for place, ref in enumerate((source_ref, target_ref)):
-        total = jnp.sum(ref[...].astype(jnp.float32), axis=(0, 1), keepdims=True)
-        out_ref[place : place + 1, :] = jnp.broadcast_to(total, (1, out_ref.shape[1]))
-    out_ref[2 : 2 + target_ref.shape[0], :] = target_ref[...].astype(jnp.float32)
+    for d in range(devices):
+        out_ref[d * rows : d * rows + 1, :] = jnp.broadcast_to(total, (1, out_ref.shape[1]))
+        out_ref[d * rows + 1 : d * rows + 1 + target.shape[0], :] = target
 
 
 def near_kernel(near_index_ref, cost_ref, plan_ref, mass_ref, high_ref, low_ref, term_ref, plan_scr):
@@ -93,12 +99,11 @@
 
 
 def far_kernel(counts, row_axis, *refs):
-    row_devices, target_here, source_count, target_count, group_blocks, link_count = counts
+    row_devices, col_devices, target_here, source_count, target_count, group_blocks, link_count = counts
     near_index_ref, slot_ref, link_ref, high_ref, low_ref, term_ref, mass_ref = refs[:7]
     cost_parts = refs[7 : 7 + row_devices]
-    packs = refs[7 + row_devices : 7 + 2 * row_devices]
-    out_ref, peak_ref, log_source_ref, log_target_ref = refs[7 + 2 * row_devices : 11 + 2 * row_devices]
-    far_high, far_low, table, column_scr, scale_scr, peak_scr, sum_scr = refs[11 + 2 * row_devices :]
+    pack_ref, out_ref, peak_ref, log_source_ref, log_target_ref = refs[7 + row_devices : 12 + row_devices]
+    far_high, far_low, table, column_scr, scale_scr, peak_scr, sum_scr = refs[12 + row_devices :]
     g = pl.program_id(0)
     steps = pl.num_programs(0)
     near_count = near_index_ref.shape[0]
@@ -125,15 +130,29 @@
             return 0
 
         lax.fori_loop(0, group_blocks, mark, 0)
-        total_source = tree([p[0:1, :] for p in packs], jnp.add)
-        total_target = tree([p[1:2, :] for p in packs], jnp.add)
+        pack_rows = pack_ref.shape[0] // (row_devices * col_devices)
+        total_source = functools.reduce(
+            jnp.add,
+            [pack_ref[r * col_devices * pack_rows : r * col_devices * pack_rows + 1, :] for r in range(row_devices)],
+        )
+        targets = functools.reduce(
+            jnp.add,
+            [
+                pack_ref[d * pack_rows + 1 + h : d * pack_rows + 2 + h, :]
+                for d in range(row_devices * col_devices)
+                for h in range(target_here)
+            ],
+        )
+        total_target = jnp.sum(targets, axis=1, keepdims=True)
+        col = lax.axis_index("cols")
         log_source_ref[...] = jnp.log2(source_count * mass_ref[...].astype(jnp.float32) / total_source)
         scale_scr[...] = source_count / (total_source * (near_count * width))
         column_scr[...] = jnp.zeros_like(column_scr)
         for s in range(row_devices):
             for h in range(target_here):
                 j = (me ^ s) * target_here + h
-                mass = target_count * packs[s][2 + h : 3 + h, :] / total_target
+                place = ((me ^ s) * col_devices + col) * pack_rows + 1 + h
+                mass = target_count * pack_ref[pl.ds(place, 1), :] / total_target
                 log_target_ref[pl.ds(j, 1), :] = jnp.log2(mass)
                 tall = jnp.broadcast_to(mass, (width, width)).T
                 for m in range(link_count):
@@ -179,7 +198,7 @@
 
     @pl.when(g == steps - 1)
     def _():
-        finish_rows(peak_ref, peak_scr, sum_scr)
+        finish_rows(col_devices, peak_ref, peak_scr, sum_scr)
 
 
 def row_pass(scores, row, lanes, peak_scr, sum_scr):
@@ -190,23 +209,31 @@
     sum_scr[...] = jnp.where(lanes == row, total, sum_scr[...])
 
 
-def finish_rows(out_ref, peak_scr, sum_scr):
-    rows = out_ref.shape[0]
+def finish_rows(col_devices, out_ref, peak_scr, sum_scr):
+    rows = out_ref.shape[0] // col_devices
     score = peak_scr[...] + jnp.log2(sum_scr[...])
-    out_ref[...] = score.T[:rows, :]
-
-
-def column_kernel(col_devices, *refs):
-    cost_ref, select_ref, log_mass_ref = refs[:3]
-    parts = refs[3 : 3 + col_devices]
-    out_ref, potential_ref = refs[3 + col_devices : 5 + col_devices]
-    potential_scr, peak_scr, sum_scr = refs[5 + col_devices :]
+    put_copies(out_ref, col_devices, score.T[:rows, :])
+
+
+def column_kernel(
+    col_devices,
+    copies,
+    cost_ref,
+    select_ref,
+    log_mass_ref,
+    parts_ref,
+    out_ref,
+    potential_ref,
+    potential_scr,
+    peak_scr,
+    sum_scr,
+):
     g = pl.program_id(0)
     rows, _, slots, width, _ = cost_ref.shape
 
     @pl.when(g == 0)
     def _():
-        scaled = log_mass_ref[...] - log_sum([p[...] for p in parts])
+        scaled = log_mass_ref[...] - log_sum(parts_of(parts_ref, col_devices))
         potential_scr[...] = scaled
         potential_ref[...] = scaled * from_log2
 
@@ -225,7 +252,8 @@
         select = select_ref[...]
         peaks = peak_scr[...]
         sums = sum_scr[...]
-        for t in range(out_ref.shape[0]):
+        blocks = out_ref.shape[0] // copies
+        for t in range(blocks):
             chosen = select == t
             peak = jnp.max(jnp.where(chosen, peaks, very_low), axis=0, keepdims=True)
             shifted = jnp.where(chosen, sums * jnp.exp2(jnp.minimum(peaks - peak, 0.0)), 0.0)
@@ -234,19 +262,28 @@
             out_ref[t : t + 1, :] = jnp.where(
                 some, peak + jnp.log2(jnp.where(some, total, 1.0)), very_low
             )
-
-
-def row_kernel(row_devices, *refs):
-    slot_ref, cost_ref, log_mass_ref = refs[:3]
-    parts = refs[3 : 3 + row_devices]
-    out_ref = refs[3 + row_devices]
-    potential_scr, peak_scr, sum_scr = refs[4 + row_devices :]
+        if copies > 1:
+            put_copies(out_ref, copies, out_ref[0:blocks, :])
+
+
+def row_kernel(
+    row_devices,
+    col_devices,
+    slot_ref,
+    cost_ref,
+    log_mass_ref,
+    parts_ref,
+    out_ref,
+    potential_scr,
+    peak_scr,
+    sum_scr,
+):
     g = pl.program_id(0)
     rows, _, slots, _, _ = cost_ref.shape
 
     @pl.when(g == 0)
     def _():
-        potential_scr[...] = log_mass_ref[...] - log_sum([p[...] for p in parts])
+        potential_scr[...] = log_mass_ref[...] - log_sum(parts_of(parts_ref, row_devices))
 
     lanes = lax.broadcasted_iota(jnp.int32, peak_scr.shape, 1)
     for i in range(rows):
@@ -259,17 +296,14 @@
 
     @pl.when(g == pl.num_programs(0) - 1)
     def _():
-        finish_rows(out_ref, peak_scr, sum_scr)
-
-
-def last_kernel(row_devices, target_here, row_axis, *refs):
-    log_mass_ref = refs[0]
-    parts = refs[1 : 1 + row_devices]
-    out_ref, scr = refs[1 + row_devices :]
-    scr[...] = (log_mass_ref[...] - log_sum([p[...] for p in parts])) * from_log2
-    me = lax.axis_index(row_axis)
-    for h in range(target_here):
-        out_ref[h : h + 1, :] = scr[pl.ds(me * target_here + h, 1), :]
+        finish_rows(col_devices, out_ref, peak_scr, sum_scr)
+
+
+def last_kernel(row_devices, row_axis, log_mass_ref, parts_ref, out_ref):
+    here = out_ref.shape[0]
+    start = lax.axis_index(row_axis) * here
+    log_mass = log_mass_ref[pl.ds(start, here), :]
+    out_ref[...] = (log_mass - log_sum(parts_of(parts_ref, row_devices))) * from_log2
 
 
 def per_device(
@@ -312,15 +346,14 @@
         coupling_index.reshape(rows_here * slots, 1), (rows_here * slots, width)
     )
 
-    pack_rows = 8 * pl.cdiv(2 + target_here, 8)
+    pack_rows = 8 * pl.cdiv(1 + target_here, 8)
+    devices = row_devices * col_devices
     pack = pl.pallas_call(
-        pack_kernel,
-        out_shape=jax.ShapeDtypeStruct((pack_rows, width), f32),
+        functools.partial(pack_kernel, devices),
+        out_shape=jax.ShapeDtypeStruct((devices * pack_rows, width), f32),
         name="pack",
     )(mass, target_weights.reshape(target_here, width))
-    target_sum = tree([p[1:2] for p in exchange(pack, "cols")], jnp.add)
-    pack = jnp.concatenate([pack[0:1], target_sum, pack[2:]], axis=0)
-    packs = exchange(pack, "rows")
+    packs = exchange(pack, ("rows", "cols"))
 
     wide = near_count * slots * width
     groups = rows_here // SUB
@@ -359,7 +392,7 @@
     cost_blocks, row_part, log_source, log_target = pl.pallas_call(
         functools.partial(
             far_kernel,
-            (row_devices, target_here, source_count, target_count, group_blocks, link_count),
+            (row_devices, col_devices, target_here, source_count, target_count, group_blocks, link_count),
             "rows",
         ),
         grid=(steps,),
@@ -373,16 +406,16 @@
             whole((rows_here, width)),
         ]
         + [whole(target_cost.shape)] * row_devices
-        + [whole((pack_rows, width))] * row_devices,
+        + [whole(packs.shape)],
         out_specs=[
             cost_block,
-            whole((rows_here, width)),
+            whole((col_devices * rows_here, width)),
             whole((rows_here, width)),
             whole((group_blocks, width)),
         ],
         out_shape=[
             jax.ShapeDtypeStruct(coupling.shape, f32),
-            jax.ShapeDtypeStruct((rows_here, width), f32),
+            jax.ShapeDtypeStruct((col_devices * rows_here, width), f32),
             jax.ShapeDtypeStruct((rows_here, width), f32),
             jax.ShapeDtypeStruct((group_blocks, width), f32),
         ],
@@ -397,21 +430,25 @@
         ],
         compiler_params=params,
         name="far_product",
-    )(near_t, slot_t, link_t, high, low, term, mass, *cost_parts, *packs)
+    )(near_t, slot_t, link_t, high, low, term, mass, *cost_parts, packs)
 
     pass_rows = 8
     passes = rows_here // pass_rows
     pass_block = pl.BlockSpec((pass_rows, 1, slots, width, width), lambda g: (g, 0, 0, 0, 0))
 
-    def column_step(row_parts):
+    def column_step(row_parts, copies):
         return pl.pallas_call(
-            functools.partial(column_kernel, col_devices),
+            functools.partial(column_kernel, col_devices, copies),
             grid=(passes,),
-            in_specs=[pass_block, whole((rows_here * slots, width)), whole((rows_here, width))]
-            + [whole((rows_here, width))] * col_devices,
-            out_specs=[whole((group_blocks, width)), whole((rows_here, width))],
+            in_specs=[
+                pass_block,
+                whole((rows_here * slots, width)),
+                whole((rows_here, width)),
+                whole(row_parts.shape),
+            ],
+            out_specs=[whole((copies * group_blocks, width)), whole((rows_here, width))],
             out_shape=[
-                jax.ShapeDtypeStruct((group_blocks, width), f32),
+                jax.ShapeDtypeStruct((copies * group_blocks, width), f32),
                 jax.ShapeDtypeStruct((rows_here, width), f32),
             ],
             scratch_shapes=[
@@ -421,16 +458,15 @@
             ],
             compiler_params=params,
             name="column_pass",
-        )(cost_blocks, select, log_source, *row_parts)
+        )(cost_blocks, select, log_source, row_parts)
 
     def row_step(column_parts):
         return pl.pallas_call(
-            functools.partial(row_kernel, row_devices),
+            functools.partial(row_kernel, row_devices, col_devices),
             grid=(passes,),
-            in_specs=[SMEM, pass_block, whole((group_blocks, width))]
-            + [whole((group_blocks, width))] * row_devices,
-            out_specs=whole((rows_here, width)),
-            out_shape=jax.ShapeDtypeStruct((rows_here, width), f32),
+            in_specs=[SMEM, pass_block, whole((group_blocks, width)), whole(column_parts.shape)],
+            out_specs=whole((col_devices * rows_here, width)),
+            out_shape=jax.ShapeDtypeStruct((col_devices * rows_here, width), f32),
             scratch_shapes=[
                 pltpu.VMEM((group_blocks, width), f32),
                 pltpu.VMEM((width, width), f32),
@@ -438,19 +474,21 @@
             ],
             compiler_params=params,
             name="row_pass",
-        )(slot_t, cost_blocks, log_target, *column_parts)
+        )(slot_t, cost_blocks, log_target, column_parts)
 
     for step in range(ITERS):
-        column_part, source_potential = column_step(exchange(row_part, "cols"))
+        last = step == ITERS - 1
+        column_part, source_potential = column_step(
+            exchange(row_part, "cols"), 1 if last else row_devices
+        )
         column_parts = exchange(column_part, "rows")
-        if step < ITERS - 1:
+        if not last:
             row_part = row_step(column_parts)
     own_target = pl.pallas_call(
-        functools.partial(last_kernel, row_devices, target_here, "rows"),
+        functools.partial(last_kernel, row_devices, "rows"),
         out_shape=jax.ShapeDtypeStruct((target_here, width), f32),
-        scratch_shapes=[pltpu.VMEM((group_blocks, width), f32)],
         name="last_potential",
-    )(log_target, *column_parts)
+    )(log_target, column_parts)
     return (
         cost_blocks,
         source_potential.reshape(rows_here * width),

time: 143 us -> 126 us (0.88)
  starting transfers between devices: 65.3 us -> 19.1 us
  blocking collectives: 0 us -> 43.6 us
  waiting for transfers between devices: 28.7 us -> 10.5 us
  local copies, waits for them, and re-layouts: 7.36 us -> 11.5 us
    ppermute x47 -> x7, starting transfers between devices: 65.3 us -> 9.8 us  [send(): return lax.ppermute(x, axis, [(d, d ^ mask) for d in range(size)])]
    all_to_all x0 -> x5, blocking collectives: none -> 43.6 us  [exchange(): return lax.all_to_all(copies, axis, 0, 0, tiled=True)]
    ppermute x47 -> x7, waiting for transfers between devices: 28.7 us -> 6.56 us  [send(): return lax.ppermute(x, axis, [(d, d ^ mask) for d in range(size)])]
    all_to_all x0 -> x2, starting transfers between devices: none -> 9.35 us  [exchange(): return lax.all_to_all(copies, axis, 0, 0, tiled=True)]
    unnamed x35 -> x27, local copies, waits for them, and re-layouts: 6.49 us -> 11.3 us
    all_to_all x0 -> x2, waiting for transfers between devices: none -> 3.89 us  [exchange(): return lax.all_to_all(copies, axis, 0, 0, tiled=True)]
  transfers between devices with their start and end apart: 47 -> 9, of which waited for: 16 -> 2; matrix products, arithmetic and copies ran while one was open for 1% -> 0% of each run, Pallas kernels for 7% -> 9%
where the time goes in v2:
time: 126 us; the launch traced here: 125 us
  blocking collectives  43.6 us (35%)
  Pallas kernels  39.3 us (31%)
  starting transfers between devices  19.1 us (15%)
  local copies, waits for them, and re-layouts  11.5 us (9%)
  waiting for transfers between devices  10.5 us (8%)
    all_to_all x5, blocking collectives, exchange(): return lax.all_to_all(copies, axis, 0, 0, tiled=True)  43.6 us
    pallas_call x1, Pallas kernels, per_device(): pl.pallas_call(functools.partial(far_kernel, (row_devices, col_devices, t...  12.5 us
    unnamed x27, local copies, waits for them, and re-layouts  11.3 us
    pallas_call x1, Pallas kernels, per_device(): pl.pallas_call(near_kernel, grid=(groups,), in_specs=[SMEM, pl.BlockSpec(...  10.3 us
    ppermute x7, starting transfers between devices, send(): return lax.ppermute(x, axis, [(d, d ^ mask) for d in range(size)])  9.8 us
    all_to_all x2, starting transfers between devices, exchange(): return lax.all_to_all(copies, axis, 0, 0, tiled=True)  9.35 us
    pallas_call x3, Pallas kernels, column_step(): pl.pallas_call(functools.partial(column_kernel, col_devices, copies), gri...  7.92 us
    ppermute x7, waiting for transfers between devices, send(): return lax.ppermute(x, axis, [(d, d ^ mask) for d in range(size)])  6.56 us
  transfers between devices with their start and end apart: 9, of which 2 were waited for; matrix products, arithmetic and copies ran while one was open for 0% of the time, Pallas kernels for 9%

profile of v2, /device:TPU:0, one launch (start us, length us, event | category | flops | bytes accessed | tf_op | source)
XLA Modules:
  0.0 124.8 jit_solution(4081715618197895769)
XLA Ops:
  0.7 3.1 %collective-permute-start.1 = (f32[1,1,3,128,128]{4,3,2,1,0:T(8,128)}, f32[1,1,3,128,128]{4,3,2,1,0:T(8,128)S(1)}, u32[]{:S(2)}, u32[]{:S(2)}) collective-permute-start(f32[1,1,3,128,128]{4,3,2,1,0:T(8,128)} %refs_7_.1), channel_id=1, source_target_pairs={{0,8},{4,12},{8,0},{12,4},{16,24},{20,28},{24,16},{28,20},{1,9},{5... | collective-permute-start | bytes 589832 | tf_op jit(solution)/shard_map/ppermute | solution.py:50
  3.8 2.6 %collective-permute-start.3 = (f32[1,1,3,128,128]{4,3,2,1,0:T(8,128)}, f32[1,1,3,128,128]{4,3,2,1,0:T(8,128)S(1)}, u32[]{:S(2)}, u32[]{:S(2)}) collective-permute-start(f32[1,1,3,128,128]{4,3,2,1,0:T(8,128)} %refs_7_.1), channel_id=1, source_target_pairs={{0,16},{4,20},{8,24},{12,28},{16,0},{20,4},{24,8},{28,12},{1,17},{... | collective-permute-start | bytes 589832 | tf_op jit(solution)/shard_map/ppermute | solution.py:50
  6.4 1.5 %pack.1 = f32[256,128]{1,0:T(8,128)} custom-call(s32[32,128]{1,0:T(8,128)} %bitcast.31, s32[1,128]{1,0:T(1,128)} %target_ref.1), custom_call_target="tpu_custom_call" | custom-call | tf_op jit(solution)/shard_map/pack/pallas_call | solution.py:351
  7.9 6.1 %all-to-all-start = ((f32[32,8,128]{2,1,0:T(8,128)}), f32[32,8,128]{2,1,0:T(8,128)S(1)}, u32[]{:S(2)}, u32[]{:S(2)}) async-start(f32[32,8,128]{2,1,0:T(8,128)} %bitcast.45), calls=%async_computation | async-start | bytes 262144 | tf_op jit(solution)/shard_map/all_to_all | solution.py:54
  13.9 1.8 %collective-permute-start = (f32[1,1,3,128,128]{4,3,2,1,0:T(8,128)}, f32[1,1,3,128,128]{4,3,2,1,0:T(8,128)S(1)}, u32[]{:S(2)}, u32[]{:S(2)}) collective-permute-start(f32[1,1,3,128,128]{4,3,2,1,0:T(8,128)} %refs_7_.1), channel_id=1, source_target_pairs={{0,4},{4,0},{8,12},{12,8},{16,20},{20,16},{24,28},{28,24},{1,5},{5... | collective-permute-start | bytes 589832 | tf_op jit(solution)/shard_map/ppermute | solution.py:50
  15.8 0.3 collective-permute-start.2
  16.0 6.5 %collective-permute-done.3.refs_11_ = f32[1,1,3,128,128]{4,3,2,1,0:T(8,128)S(1)} collective-permute-done((f32[1,1,3,128,128]{4,3,2,1,0:T(8,128)}, f32[1,1,3,128,128]{4,3,2,1,0:T(8,128)S(1)}, u32[]{:S(2)}, u32[]{:S(2)}) %collective-permute-start.3) | collective-permute-done | bytes 196640 | tf_op jit(solution)/shard_map/ppermute | solution.py:50
  22.6 1.5 %collective-permute-start.4 = (f32[1,1,3,128,128]{4,3,2,1,0:T(8,128)S(1)}, f32[1,1,3,128,128]{4,3,2,1,0:T(8,128)S(1)}, u32[]{:S(2)}, u32[]{:S(2)}) collective-permute-start(f32[1,1,3,128,128]{4,3,2,1,0:T(8,128)S(1)} %collective-permute-done.3.refs_11_), channel_id=1, source_target_pairs={{0,4},{4,0},{8,12},{12,8},{16,20},{20,16},{24,28},{28,24},{1,5},{5... | collective-permute-start | bytes 589832 | tf_op jit(solution)/shard_map/ppermute | solution.py:50
  24.1 0.5 collective-permute-start.6
  24.6 2.2 %copy-done.4 = f32[32,1,2,128,128]{4,3,2,1,0:T(8,128)S(1)} copy-done((f32[32,1,2,128,128]{4,3,2,1,0:T(8,128)S(1)}, f32[32,1,2,128,128]{4,3,2,1,0:T(8,128)}, u32[]{:S(2)}) %copy-start.4) | copy-done | bytes 4194328
  26.8 0.7 copy-done.6
  27.5 0.7 copy-done.10
  28.2 10.3 %near_product.1 = (bf16[32,128,768]{2,1,0:T(8,128)(2,1)S(1)}, bf16[32,128,768]{2,1,0:T(8,128)(2,1)}, f32[8,128,4]{2,1,0:T(8,128)S(1)}) custom-call(s32[3,32]{1,0:T(4,128)S(1)} %bitcast.41, f32[32,3,128,128]{3,2,1,0:T(8,128)} %cost_ref.1, f32[32,1,2,128,128]{4,3,2,1,0:T(8,128)S(1)} %copy-done.4, s32[32,128]{1,0:T(8,128)S(1)} %bitcast.32), custom_call_target="tpu_custom_call" | custom-call | flops 2415919104 | bytes 23068672 | tf_op jit(solution)/shard_map/near_product/pallas_call | solution.py:360
  38.5 2.6 %copy-done.2 = bf16[32,128,768]{2,1,0:T(8,128)(2,1)} copy-done((bf16[32,128,768]{2,1,0:T(8,128)(2,1)}, bf16[32,128,768]{2,1,0:T(8,128)(2,1)S(1)}, u32[]{:S(2)}) %copy-start.2) | copy-done | bytes 6291480
  41.2 2.8 %copy-done.3 = bf16[32,128,768]{2,1,0:T(8,128)(2,1)S(1)} copy-done((bf16[32,128,768]{2,1,0:T(8,128)(2,1)S(1)}, bf16[32,128,768]{2,1,0:T(8,128)(2,1)}, u32[]{:S(2)}) %copy-start.3) | copy-done | bytes 6291480
  44.0 12.5 %far_product.1 = (f32[32,1,2,128,128]{4,3,2,1,0:T(8,128)}, f32[128,128]{1,0:T(8,128)}, f32[32,128]{1,0:T(8,128)S(1)}, f32[8,128]{1,0:T(8,128)S(1)}) custom-call(s32[3,32]{1,0:T(4,128)S(1)} %bitcast.42, s32[2,32]{1,0:T(2,128)S(1)} %bitcast.38, s32[3,1,8]{2,1,0:T(1,128)S(1)} %bitcast.44, bf16[32,128,768]{2,1,0:T(8,128)(2,1)S(1)} %copy-done.3, ...), custom_call_target="tpu_custom_call" | custom-call | tf_op jit(solution)/shard_map/far_product/pallas_call | solution.py:392
  56.5 3.3 %all-to-all-start.1 = ((f32[4,32,128]{2,1,0:T(8,128)}), f32[4,32,128]{2,1,0:T(8,128)S(1)}, u32[]{:S(2)}, u32[]{:S(2)}) async-start(f32[4,32,128]{2,1,0:T(8,128)} %bitcast.8), calls=%async_computation.1 | async-start | bytes 131072 | tf_op jit(solution)/shard_map/all_to_all | solution.py:54
  59.8 0.1 copy.13
  59.9 0.1 broadcast_in_dim.7
  60.0 3.9 %all-to-all-done.1 = f32[4,32,128]{2,1,0:T(8,128)S(1)} async-done(((f32[4,32,128]{2,1,0:T(8,128)}), f32[4,32,128]{2,1,0:T(8,128)S(1)}, u32[]{:S(2)}, u32[]{:S(2)}) %all-to-all-start.1) | async-done | bytes 65568 | tf_op jit(solution)/shard_map/all_to_all | solution.py:54
  64.0 2.2 %copy-done = f32[32,1,2,128,128]{4,3,2,1,0:T(8,128)S(1)} copy-done((f32[32,1,2,128,128]{4,3,2,1,0:T(8,128)S(1)}, f32[32,1,2,128,128]{4,3,2,1,0:T(8,128)}, u32[]{:S(2)}) %copy-start) | copy-done | bytes 4194328
  66.2 2.6 %column_pass.3 = (f32[64,128]{1,0:T(8,128)S(1)}, f32[32,128]{1,0:T(8,128)}) custom-call(f32[32,1,2,128,128]{4,3,2,1,0:T(8,128)S(1)} %copy-done, s32[64,128]{1,0:T(8,128)S(1)} %broadcast_in_dim.8.select_ref, f32[32,128]{1,0:T(8,128)S(1)} %get-tuple-element.18.log_mass_ref, f32[128,128]{1,0:T(8,128)S(1)} %bitcast.26), custom_call_target="tpu_custom_call" | custom-call | tf_op jit(solution)/shard_map/column_pass/pallas_call | solution.py:440
  68.8 12.3 %all_to_all.77 = f32[8,8,128]{2,1,0:T(8,128)S(1)} all-to-all(f32[8,8,128]{2,1,0:T(8,128)S(1)} %bitcast.36), channel_id=1, replica_groups=mesh['rows'=8,'cols'=4] {'rows'}, dimensions={0} | all-to-all | bytes 65536 | tf_op jit(solution)/shard_map/all_to_all | solution.py:54
  81.1 2.9 %row_pass.2 = f32[128,128]{1,0:T(8,128)S(1)} custom-call(s32[2,32]{1,0:T(2,128)S(1)} %bitcast.39, f32[32,1,2,128,128]{4,3,2,1,0:T(8,128)S(1)} %copy-done.1, f32[8,128]{1,0:T(8,128)S(1)} %get-tuple-element.19.log_mass_ref, f32[64,128]{1,0:T(8,128)S(1)} %bitcast.34), custom_call_target="tpu_custom_call" | custom-call | tf_op jit(solution)/shard_map/row_pass/pallas_call | solution.py:464
  84.0 6.5 %all_to_all.78 = f32[4,32,128]{2,1,0:T(8,128)S(1)} all-to-all(f32[4,32,128]{2,1,0:T(8,128)S(1)} %bitcast.29), channel_id=1, replica_groups=mesh['rows'=8,'cols'=4] {'cols'}, dimensions={0} | all-to-all | bytes 131072 | tf_op jit(solution)/shard_map/all_to_all | solution.py:54
  90.5 2.6 %column_pass.4 = (f32[64,128]{1,0:T(8,128)S(1)}, f32[32,128]{1,0:T(8,128)}) custom-call(f32[32,1,2,128,128]{4,3,2,1,0:T(8,128)S(1)} %copy-done.1, s32[64,128]{1,0:T(8,128)S(1)} %broadcast_in_dim.8.select_ref, f32[32,128]{1,0:T(8,128)S(1)} %get-tuple-element.18.log_mass_ref, f32[128,128]{1,0:T(8,128)S(1)} %bitcast.28), custom_call_target="tpu_custom_call" | custom-call | tf_op jit(solution)/shard_map/column_pass/pallas_call | solution.py:440
  93.1 9.0 %all_to_all.79 = f32[8,8,128]{2,1,0:T(8,128)S(1)} all-to-all(f32[8,8,128]{2,1,0:T(8,128)S(1)} %bitcast.37), channel_id=1, replica_groups=mesh['rows'=8,'cols'=4] {'rows'}, dimensions={0} | all-to-all | bytes 65536 | tf_op jit(solution)/shard_map/all_to_all | solution.py:54
  102.2 2.9 %row_pass.3 = f32[128,128]{1,0:T(8,128)S(1)} custom-call(s32[2,32]{1,0:T(2,128)S(1)} %bitcast.40, f32[32,1,2,128,128]{4,3,2,1,0:T(8,128)S(1)} %copy-done.1, f32[8,128]{1,0:T(8,128)S(1)} %get-tuple-element.19.log_mass_ref, f32[64,128]{1,0:T(8,128)S(1)} %bitcast.35), custom_call_target="tpu_custom_call" | custom-call | tf_op jit(solution)/shard_map/row_pass/pallas_call | solution.py:464
  105.1 6.5 %all_to_all.80 = f32[4,32,128]{2,1,0:T(8,128)S(1)} all-to-all(f32[4,32,128]{2,1,0:T(8,128)S(1)} %bitcast.30), channel_id=1, replica_groups=mesh['rows'=8,'cols'=4] {'cols'}, dimensions={0} | all-to-all | bytes 131072 | tf_op jit(solution)/shard_map/all_to_all | solution.py:54
  111.6 2.6 %column_pass.5 = (f32[8,128]{1,0:T(8,128)S(1)}, f32[32,128]{1,0:T(8,128)}) custom-call(f32[32,1,2,128,128]{4,3,2,1,0:T(8,128)S(1)} %copy-done.1, s32[64,128]{1,0:T(8,128)S(1)} %broadcast_in_dim.8.select_ref, f32[32,128]{1,0:T(8,128)S(1)} %get-tuple-element.18.log_mass_ref, f32[128,128]{1,0:T(8,128)S(1)} %bitcast.27), custom_call_target="tpu_custom_call" | custom-call | tf_op jit(solution)/shard_map/column_pass/pallas_call | solution.py:440
  114.2 9.3 %all_to_all.81 = f32[8,1,128]{2,1,0:T(1,128)} all-to-all(f32[8,1,128]{2,1,0:T(1,128)S(1)} %bitcast.43), channel_id=1, replica_groups=mesh['rows'=8,'cols'=4] {'rows'}, dimensions={0} | all-to-all | bytes 8192 | tf_op jit(solution)/shard_map/all_to_all | solution.py:54
  123.5 1.2 last_potential.1
  (29 shorter events, 0.1 us)
Async XLA Ops:
  0.6 40.6 %copy-start.5 = (f32[1,1,3,128,128]{4,3,2,1,0:T(8,128)S(1)}, f32[1,1,3,128,128]{4,3,2,1,0:T(8,128)}, u32[]{:S(2)}) copy-start(f32[1,1,3,128,128]{4,3,2,1,0:T(8,128)} %refs_7_.1) | copy-start | bytes 589828
  0.6 40.6 %copy-start.7 = (s32[4096]{0:T(1024)S(1)}, s32[4096]{0:T(1024)}, u32[]{:S(2)}) copy-start(s32[4096]{0:T(1024)} %param.12) | copy-start | bytes 49156
  0.7 40.5 %copy-start.11 = (s32[32,3]{0,1:T(4,128)S(1)}, s32[32,3]{0,1:T(4,128)}, u32[]{:S(2)}) copy-start(s32[32,3]{0,1:T(4,128)} %param.11) | copy-start | bytes 1156
  0.7 40.5 %copy-start.9 = (s32[32,1,2]{0,2,1:T(2,128)S(1)}, s32[32,1,2]{0,2,1:T(2,128)}, u32[]{:S(2)}) copy-start(s32[32,1,2]{0,2,1:T(2,128)} %param.9) | copy-start | bytes 772
  0.7 40.5 %copy-start.12 = (s32[1,8,3]{1,0,2:T(1,128)S(1)}, s32[1,8,3]{1,0,2:T(1,128)}, u32[]{:S(2)}) copy-start(s32[1,8,3]{1,0,2:T(1,128)} %param.14) | copy-start | bytes 292
  0.7 15.1 %collective-permute-start.1 = (f32[1,1,3,128,128]{4,3,2,1,0:T(8,128)}, f32[1,1,3,128,128]{4,3,2,1,0:T(8,128)S(1)}, u32[]{:S(2)}, u32[]{:S(2)}) collective-permute-start(f32[1,1,3,128,128]{4,3,2,1,0:T(8,128)} %refs_7_.1), channel_id=1, source_target_pairs={{0,8},{4,12},{8,0},{12,4},{16,24},{20,28},{24,16},{28,20},{1,9},{5... | collective-permute-start | bytes 589832 | tf_op jit(solution)/shard_map/ppermute | solution.py:50
  3.8 18.8 %collective-permute-start.3 = (f32[1,1,3,128,128]{4,3,2,1,0:T(8,128)}, f32[1,1,3,128,128]{4,3,2,1,0:T(8,128)S(1)}, u32[]{:S(2)}, u32[]{:S(2)}) collective-permute-start(f32[1,1,3,128,128]{4,3,2,1,0:T(8,128)} %refs_7_.1), channel_id=1, source_target_pairs={{0,16},{4,20},{8,24},{12,28},{16,0},{20,4},{24,8},{28,12},{1,17},{... | collective-permute-start | bytes 589832 | tf_op jit(solution)/shard_map/ppermute | solution.py:50
  6.4 17.7 %collective-permute-start.5 = (f32[1,1,3,128,128]{4,3,2,1,0:T(8,128)}, f32[1,1,3,128,128]{4,3,2,1,0:T(8,128)S(1)}, u32[]{:S(2)}, u32[]{:S(2)}) collective-permute-start(f32[1,1,3,128,128]{4,3,2,1,0:T(8,128)} %refs_7_.1), channel_id=1, source_target_pairs={{0,24},{4,28},{8,16},{12,20},{16,8},{20,12},{24,0},{28,4},{1,25},{... | collective-permute-start | bytes 589832 | tf_op jit(solution)/shard_map/ppermute | solution.py:50
  7.9 33.3 %all-to-all-start = ((f32[32,8,128]{2,1,0:T(8,128)}), f32[32,8,128]{2,1,0:T(8,128)S(1)}, u32[]{:S(2)}, u32[]{:S(2)}) async-start(f32[32,8,128]{2,1,0:T(8,128)} %bitcast.45), calls=%async_computation | async-start | bytes 262144 | tf_op jit(solution)/shard_map/all_to_all | solution.py:54
  13.9 27.2 %collective-permute-start = (f32[1,1,3,128,128]{4,3,2,1,0:T(8,128)}, f32[1,1,3,128,128]{4,3,2,1,0:T(8,128)S(1)}, u32[]{:S(2)}, u32[]{:S(2)}) collective-permute-start(f32[1,1,3,128,128]{4,3,2,1,0:T(8,128)} %refs_7_.1), channel_id=1, source_target_pairs={{0,4},{4,0},{8,12},{12,8},{16,20},{20,16},{24,28},{28,24},{1,5},{5... | collective-permute-start | bytes 589832 | tf_op jit(solution)/shard_map/ppermute | solution.py:50
  15.8 25.4 %collective-permute-start.2 = (f32[1,1,3,128,128]{4,3,2,1,0:T(8,128)S(1)}, f32[1,1,3,128,128]{4,3,2,1,0:T(8,128)S(1)}, u32[]{:S(2)}, u32[]{:S(2)}) collective-permute-start(f32[1,1,3,128,128]{4,3,2,1,0:T(8,128)S(1)} %collective-permute-done.1.refs_9_), channel_id=1, source_target_pairs={{0,4},{4,0},{8,12},{12,8},{16,20},{20,16},{24,28},{28,24},{1,5},{5... | collective-permute-start | bytes 589832 | tf_op jit(solution)/shard_map/ppermute | solution.py:50
  22.6 18.6 %collective-permute-start.4 = (f32[1,1,3,128,128]{4,3,2,1,0:T(8,128)S(1)}, f32[1,1,3,128,128]{4,3,2,1,0:T(8,128)S(1)}, u32[]{:S(2)}, u32[]{:S(2)}) collective-permute-start(f32[1,1,3,128,128]{4,3,2,1,0:T(8,128)S(1)} %collective-permute-done.3.refs_11_), channel_id=1, source_target_pairs={{0,4},{4,0},{8,12},{12,8},{16,20},{20,16},{24,28},{28,24},{1,5},{5... | collective-permute-start | bytes 589832 | tf_op jit(solution)/shard_map/ppermute | solution.py:50
  24.1 17.1 %collective-permute-start.6 = (f32[1,1,3,128,128]{4,3,2,1,0:T(8,128)S(1)}, f32[1,1,3,128,128]{4,3,2,1,0:T(8,128)S(1)}, u32[]{:S(2)}, u32[]{:S(2)}) collective-permute-start(f32[1,1,3,128,128]{4,3,2,1,0:T(8,128)S(1)} %collective-permute-done.5.refs_13_), channel_id=1, source_target_pairs={{0,4},{4,0},{8,12},{12,8},{16,20},{20,16},{24,28},{28,24},{1,5},{5... | collective-permute-start | bytes 589832 | tf_op jit(solution)/shard_map/ppermute | solution.py:50
  24.6 2.2 %copy-start.4 = (f32[32,1,2,128,128]{4,3,2,1,0:T(8,128)S(1)}, f32[32,1,2,128,128]{4,3,2,1,0:T(8,128)}, u32[]{:S(2)}) copy-start(f32[32,1,2,128,128]{4,3,2,1,0:T(8,128)} %plan_ref.1) | copy-start | bytes 12582916
  26.8 0.7 copy-start.6
  27.5 0.7 copy-start.10
  38.5 2.6 %copy-start.2 = (bf16[32,128,768]{2,1,0:T(8,128)(2,1)}, bf16[32,128,768]{2,1,0:T(8,128)(2,1)S(1)}, u32[]{:S(2)}) copy-start(bf16[32,128,768]{2,1,0:T(8,128)(2,1)S(1)} %get-tuple-element.14.refs_3_) | copy-start | bytes 18874372
  41.2 2.8 %copy-start.3 = (bf16[32,128,768]{2,1,0:T(8,128)(2,1)S(1)}, bf16[32,128,768]{2,1,0:T(8,128)(2,1)}, u32[]{:S(2)}) copy-start(bf16[32,128,768]{2,1,0:T(8,128)(2,1)} %copy-done.2) | copy-start | bytes 18874372
  56.5 45.7 %copy-start.8 = (f32[8,128]{1,0:T(8,128)}, f32[8,128]{1,0:T(8,128)S(1)}, u32[]{:S(2)}) copy-start(f32[8,128]{1,0:T(8,128)S(1)} %get-tuple-element.19.log_mass_ref) | copy-start | bytes 12292
  56.5 7.4 %all-to-all-start.1 = ((f32[4,32,128]{2,1,0:T(8,128)}), f32[4,32,128]{2,1,0:T(8,128)S(1)}, u32[]{:S(2)}, u32[]{:S(2)}) async-start(f32[4,32,128]{2,1,0:T(8,128)} %bitcast.8), calls=%async_computation.1 | async-start | bytes 131072 | tf_op jit(solution)/shard_map/all_to_all | solution.py:54
  64.0 2.2 %copy-start = (f32[32,1,2,128,128]{4,3,2,1,0:T(8,128)S(1)}, f32[32,1,2,128,128]{4,3,2,1,0:T(8,128)}, u32[]{:S(2)}) copy-start(f32[32,1,2,128,128]{4,3,2,1,0:T(8,128)} %get-tuple-element.11.cost_ref) | copy-start | bytes 12582916
  66.2 14.9 %copy-start.1 = (f32[32,1,2,128,128]{4,3,2,1,0:T(8,128)S(1)}, f32[32,1,2,128,128]{4,3,2,1,0:T(8,128)}, u32[]{:S(2)}) copy-start(f32[32,1,2,128,128]{4,3,2,1,0:T(8,128)} %get-tuple-element.11.cost_ref) | copy-start | bytes 12582916

commit v3 on v2

v3 whole, which is shorter than its diff:
```python
import functools
import math

import jax
import jax.numpy as jnp
from jax import lax
from jax.experimental import pallas as pl
from jax.experimental.pallas import tpu as pltpu
from jax.sharding import PartitionSpec as P

ITERS = 3
SUB = 4

entropy = 0.01
to_log2 = math.log2(math.e) / entropy
from_log2 = entropy * math.log(2.0)
very_low = -1e30
mib = 1024 * 1024

SMEM = pl.BlockSpec(memory_space=pltpu.SMEM)
VMEM = pl.BlockSpec(memory_space=pltpu.VMEM)
ANY = pl.BlockSpec(memory_space=pl.ANY)


def in_vmem(x):
    return pltpu.with_memory_space_constraint(x, pltpu.VMEM)


def whole(shape):
    return pl.BlockSpec(shape, lambda *_: (0,) * len(shape))


def split(x):
    high = x.astype(jnp.bfloat16)
    return high, (x - high.astype(jnp.float32)).astype(jnp.bfloat16)


def tree(parts, op):
    while len(parts) > 1:
        half = len(parts) // 2
        parts = [op(parts[s], parts[s + half]) for s in range(half)]
    return parts[0]


def log_sum(parts):
    peak = tree(parts, jnp.maximum)
    return peak + jnp.log2(tree([jnp.exp2(p - peak) for p in parts], jnp.add))


def parts_of(ref, devices):
    rows = ref.shape[0] // devices
    return [ref[d * rows : (d + 1) * rows, :] for d in range(devices)]


def put_copies(ref, devices, value):
    rows = value.shape[0]
    for d in range(devices):
        ref[d * rows : (d + 1) * rows, :] = value


def send(x, axis, mask):
    size = lax.axis_size(axis)
    return lax.ppermute(x, axis, [(d, d ^ mask) for d in range(size)])


def from_all(x, axis):
    return [x] + [send(x, axis, s) for s in range(1, lax.axis_size(axis))]


def exchange(copies, axis):
    return lax.all_to_all(copies, axis, 0, 0, tiled=True)


def pack_kernel(devices, source_ref, target_ref, out_ref):
    rows = out_ref.shape[0] // devices
    total = jnp.sum(source_ref[...].astype(jnp.float32), axis=(0, 1), keepdims=True)
    target = target_ref[...].astype(jnp.float32)
    out_ref[...] = jnp.zeros_like(out_ref)
    for d in range(devices):
        out_ref[d * rows : d * rows + 1, :] = jnp.broadcast_to(total, (1, out_ref.shape[1]))
        out_ref[d * rows + 1 : d * rows + 1 + target.shape[0], :] = target


def near_kernel(first, near_index_ref, cost_ref, plan_ref, mass_ref, *refs):
    x_ref, term_ref, plan_scr = refs[-3:]
    g = first + pl.program_id(0)
    near_count = cost_ref.shape[1]
    width = cost_ref.shape[2]
    slots = plan_ref.shape[2]
    wide = slots * width
    for a in range(SUB):
        plan = jnp.concatenate([plan_ref[a, 0, q] for q in range(slots)], axis=1)
        high, low = split(plan)
        plan_scr[a, 0:width, :] = high
        plan_scr[a, width : 2 * width, :] = low
        plan_scr[a, 2 * width : 3 * width, :] = high
    lanes = lax.broadcasted_iota(jnp.int32, (width, SUB), 1)
    terms = jnp.zeros((width, SUB), jnp.float32)
    for i in range(SUB):
        row = g * SUB + i
        acc = None
        for k in range(near_count):
            a = near_index_ref[k, row] & (SUB - 1)
            cost = cost_ref[i, k]
            high, low = split(cost)
            x = jnp.dot(
                jnp.concatenate([high, high, low], axis=1),
                plan_scr[a],
                preferred_element_type=jnp.float32,
            )
            x_high, x_low = split(x)
            x_ref[row, 0:width, k * wide : (k + 1) * wide] = x_high
            x_ref[row, width : 2 * width, k * wide : (k + 1) * wide] = x_low
            weighted = cost * cost * mass_ref[pl.ds(g * SUB + a, 1), :].astype(jnp.float32)
            acc = weighted if acc is None else acc + weighted
        terms = jnp.where(lanes == i, jnp.sum(acc, axis=1, keepdims=True), terms)
    term_ref[g] = terms


def relay_kernel(*refs):
    pass


def far_kernel(counts, row_axis, col_axis, *refs):
    row_devices, col_devices, target_here, source_count, target_count, group_blocks, link_count = counts
    near_index_ref, slot_ref, link_ref, x_ref, term_ref, mass_ref = refs[:6]
    cost_parts = refs[6 : 6 + row_devices]
    pack_ref, out_ref, work_ref, tall_ref, part_ref, log_source_ref, log_target_ref = refs[
        6 + row_devices : 13 + row_devices
    ]
    far_high, far_low, table, column_scr, scale_scr, peak_scr, sum_scr = refs[13 + row_devices :]
    g = pl.program_id(0)
    near_count = near_index_ref.shape[0]
    slots = slot_ref.shape[0]
    rows = out_ref.shape[0]
    width = out_ref.shape[3]
    zero_block = group_blocks * link_count

    @pl.when(g == 0)
    def _():
        me = lax.axis_index(row_axis)
        col = lax.axis_index(col_axis)
        far_high[zero_block] = jnp.zeros((width, width), jnp.bfloat16)
        far_low[zero_block] = jnp.zeros((width, width), jnp.bfloat16)

        def clear(e, _):
            table[e] = zero_block
            return 0

        lax.fori_loop(0, group_blocks * group_blocks, clear, 0)

        def mark(j, _):
            for m in range(link_count):
                table[j * group_blocks + link_ref[m, 0, j]] = j * link_count + m
            return 0

        lax.fori_loop(0, group_blocks, mark, 0)
        pack_rows = pack_ref.shape[0] // (row_devices * col_devices)
        total_source = functools.reduce(
            jnp.add,
            [pack_ref[r * col_devices * pack_rows : r * col_devices * pack_rows + 1, :] for r in range(row_devices)],
        )
        targets = functools.reduce(
            jnp.add,
            [
                pack_ref[d * pack_rows + 1 + h : d * pack_rows + 2 + h, :]
                for d in range(row_devices * col_devices)
                for h in range(target_here)
            ],
        )
        total_target = jnp.sum(targets, axis=1, keepdims=True)
        log_source_ref[...] = jnp.log2(source_count * mass_ref[...].astype(jnp.float32) / total_source)
        scale_scr[...] = source_count / (total_source * (near_count * width))
        column_scr[...] = jnp.zeros_like(column_scr)
        for s in range(row_devices):
            for h in range(target_here):
                j = (me ^ s) * target_here + h
                place = ((me ^ s) * col_devices + col) * pack_rows + 1 + h
                mass = target_count * pack_ref[pl.ds(place, 1), :] / total_target
                log_target_ref[pl.ds(j, 1), :] = jnp.log2(mass)
                tall = jnp.broadcast_to(mass, (width, width)).T
                for m in range(link_count):
                    block = cost_parts[s][0, h, m]
                    high, low = split(block)
                    far_high[j * link_count + m] = high
                    far_low[j * link_count + m] = low
                    spread = jnp.sum(tall * (block * block), axis=0, keepdims=True)
                    t = link_ref[m, 0, j]
                    column_scr[pl.ds(t, 1), :] += spread * (1.0 / (link_count * width))

    group_devices = target_count // (group_blocks * width)
    coef = 2.0 * (1.0 / (near_count * width)) * (1.0 / (slots * group_devices * width))
    scale = scale_scr[0:1, 0:1]
    for i in range(rows):
        row = g * rows + i
        group = row - lax.rem(row, SUB)
        targets = [slot_ref[l, row] for l in range(slots)]
        far_rows = []
        for k in range(near_count):
            a = group + (near_index_ref[k, row] & (SUB - 1))
            for q in range(slots):
                j = slot_ref[q, a]
                far_rows.append([table[j * group_blocks + t] for t in targets])
        right_high = jnp.concatenate(
            [jnp.concatenate([far_high[e] for e in r], axis=1) for r in far_rows], axis=0
        )
        right_low = jnp.concatenate(
            [jnp.concatenate([far_low[e] for e in r], axis=1) for r in far_rows], axis=0
        )
        both = jnp.dot(x_ref[row], right_high, preferred_element_type=jnp.float32)
        rest = jnp.dot(x_ref[row, 0:width, :], right_low, preferred_element_type=jnp.float32)
        product = both[0:width] + (both[width:] + rest)
        tall = term_ref[row // SUB, :, i % SUB : i % SUB + 1] * scale
        scores = []
        for l in range(slots):
            cost = tall + column_scr[pl.ds(targets[l], 1), :] - coef * product[:, l * width : (l + 1) * width]
            out_ref[i, 0, l] = cost
            scaled = cost * -to_log2
            work_ref[row, l] = scaled
            turned = scaled.T
            tall_ref[row, l] = turned
            scores.append(turned)
        row_pass(scores, row, peak_scr, sum_scr)

    @pl.when(g == pl.num_programs(0) - 1)
    def _():
        part_ref[...] = peak_scr[...] + jnp.log2(sum_scr[...])


def row_pass(scores, row, peak_scr, sum_scr):
    peak = jnp.max(functools.reduce(jnp.maximum, scores), axis=0, keepdims=True)
    total = functools.reduce(jnp.add, [jnp.exp2(s - peak) for s in scores])
    peak_scr[pl.ds(row, 1), :] = peak
    sum_scr[pl.ds(row, 1), :] = jnp.sum(total, axis=0, keepdims=True)


def column_kernel(col_devices, copies, work_ref, select_ref, log_mass_ref, *refs):
    parts = refs[:col_devices]
    out_ref, potential_ref, potential_scr, peak_scr, sum_scr = refs[col_devices:]
    rows, slots, width, _ = work_ref.shape
    together = math.gcd(rows, 8)
    scaled = log_mass_ref[...] - log_sum([p[...] for p in parts])
    potential_scr[...] = scaled
    potential_ref[...] = scaled * from_log2

    def some_rows(g, _):
        first = pl.multiple_of(g * together, together)
        tall = potential_scr[pl.ds(first, together), :].T
        for i in range(together):
            for l in range(slots):
                score = tall[:, i : i + 1] + work_ref[first + i, l]
                peak = jnp.max(score, axis=0, keepdims=True)
                total = jnp.sum(jnp.exp2(score - peak), axis=0, keepdims=True)
                place = (first + i) * slots + l
                peak_scr[pl.ds(place, 1), :] = peak
                sum_scr[pl.ds(place, 1), :] = total
        return 0

    lax.fori_loop(0, rows // together, some_rows, 0)
    select = select_ref[...]
    peaks = peak_scr[...]
    sums = sum_scr[...]
    blocks = out_ref.shape[0] // copies
    for t in range(blocks):
        chosen = select == t
        peak = jnp.max(jnp.where(chosen, peaks, very_low), axis=0, keepdims=True)
        shifted = jnp.where(chosen, sums * jnp.exp2(jnp.minimum(peaks - peak, 0.0)), 0.0)
        total = jnp.sum(shifted, axis=0, keepdims=True)
        some = total > 0.0
        out_ref[t : t + 1, :] = jnp.where(
            some, peak + jnp.log2(jnp.where(some, total, 1.0)), very_low
        )
    if copies > 1:
        put_copies(out_ref, copies, out_ref[0:blocks, :])


def row_kernel(
    row_devices, slot_ref, tall_ref, log_mass_ref, parts_ref, out_ref, wide_scr, peak_scr, sum_scr
):
    rows, slots, width, _ = tall_ref.shape
    together = math.gcd(rows, 8)
    potential = (log_mass_ref[...] - log_sum(parts_of(parts_ref, row_devices))).T
    for t in range(wide_scr.shape[0]):
        wide_scr[t] = jnp.broadcast_to(potential[:, t : t + 1], (width, width))

    def some_rows(g, _):
        for i in range(together):
            row = g * together + i
            scores = [wide_scr[slot_ref[l, row]] + tall_ref[row, l] for l in range(slots)]
            row_pass(scores, row, peak_scr, sum_scr)
        return 0

    lax.fori_loop(0, rows // together, some_rows, 0)
    out_ref[...] = peak_scr[...] + jnp.log2(sum_scr[...])


def last_kernel(row_devices, row_axis, log_mass_ref, parts_ref, out_ref):
    here = out_ref.shape[0]
    start = lax.axis_index(row_axis) * here
    log_mass = log_mass_ref[pl.ds(start, here), :]
    out_ref[...] = (log_mass - log_sum(parts_of(parts_ref, row_devices))) * from_log2


def per_device(
    coupling,
    coupling_index,
    near_cost,
    near_index,
    source_weights,
    target_cost,
    target_index,
    target_weights,
):
    rows_here = coupling.shape[0]
    slots = coupling.shape[2]
    width = coupling.shape[3]
    near_count = near_cost.shape[1]
    group_blocks = target_index.shape[1]
    link_count = target_index.shape[2]
    target_here = target_cost.shape[1]
    row_devices = lax.axis_size("rows")
    col_devices = lax.axis_size("cols")
    source_count = rows_here * row_devices * width
    target_count = group_blocks * width * col_devices
    f32 = jnp.float32
    arrived = {0: target_cost}
    late = [mask for mask in range(5, row_devices, 2)]
    for mask in range(1, row_devices):
        if mask not in late:
            arrived[mask] = send(target_cost, "rows", mask)

    near_t = near_index.T
    slot_t = coupling_index[:, 0, :].T
    link_t = jnp.transpose(target_index, (2, 0, 1))
    mass = source_weights.reshape(rows_here, width)
    select = jnp.broadcast_to(
        coupling_index.reshape(rows_here * slots, 1), (rows_here * slots, width)
    )

    pack_rows = 8 * pl.cdiv(1 + target_here, 8)
    devices = row_devices * col_devices
    pack = pl.pallas_call(
        functools.partial(pack_kernel, devices),
        out_shape=jax.ShapeDtypeStruct((devices * pack_rows, width), f32),
        name="pack",
    )(mass, target_weights.reshape(target_here, width))
    packs = exchange(pack, ("rows", "cols"))

    wide = near_count * slots * width
    groups = rows_here // SUB
    x_shape = pltpu.VMEM((rows_here, 2 * width, wide), jnp.bfloat16)
    term_shape = pltpu.VMEM((groups, width, SUB), f32)
    near_cost = pltpu.with_memory_space_constraint(near_cost, pltpu.HBM)
    coupling = pltpu.with_memory_space_constraint(coupling, pltpu.HBM)

    def near_product(first, count, *held):
        return pl.pallas_call(
            functools.partial(near_kernel, first),
            grid=(count,),
            in_specs=[
                SMEM,
                pl.BlockSpec((SUB, near_count, width, width), lambda g: (first + g, 0, 0, 0)),
                pl.BlockSpec((SUB, 1, slots, width, width), lambda g: (first + g, 0, 0, 0, 0)),
                whole((rows_here, width)),
            ]
            + [VMEM] * len(held),
            out_specs=[VMEM, VMEM],
            out_shape=[x_shape, term_shape],
            input_output_aliases={4: 0, 5: 1} if held else {},
            scratch_shapes=[pltpu.VMEM((SUB, 3 * width, slots * width), jnp.bfloat16)],
            compiler_params=pltpu.CompilerParams(vmem_limit_bytes=12 * mib),
            cost_estimate=pl.CostEstimate(
                flops=6 * count * SUB * wide * width * width,
                bytes_accessed=4 * count * SUB * width * (near_count + slots) * width,
                transcendentals=0,
            ),
            name="near_product",
        )(near_t, near_cost, coupling, mass, *map(in_vmem, held))

    held = near_product(0, (groups + 1) // 2)
    if late:
        sources = [mask - 1 for mask in late]
        passed = pl.pallas_call(
            relay_kernel,
            in_specs=[ANY] * (2 + len(sources)),
            out_specs=[ANY] * len(sources),
            out_shape=[jax.ShapeDtypeStruct(target_cost.shape, f32)] * len(sources),
            input_output_aliases={2 + e: e for e in range(len(sources))},
            name="relay",
        )(held[1], packs, *[arrived[mask] for mask in sources])
        for mask, block in zip(sources, passed):
            arrived[mask] = block
            arrived[mask + 1] = send(block, "rows", 1)
    cost_parts = [arrived[s] for s in range(row_devices)]
    x, term = near_product((groups + 1) // 2, groups // 2, *held)

    far_bytes = group_blocks * link_count * width * width * 4
    step_rows = SUB
    steps = rows_here // step_rows
    cost_block = pl.BlockSpec((step_rows, 1, slots, width, width), lambda g: (g, 0, 0, 0, 0))
    work_shape = pltpu.VMEM((rows_here, slots, width, width), f32)
    cost_blocks, work, tall, row_part, log_source, log_target = pl.pallas_call(
        functools.partial(
            far_kernel,
            (row_devices, col_devices, target_here, source_count, target_count, group_blocks, link_count),
            "rows",
            "cols",
        ),
        grid=(steps,),
        in_specs=[SMEM, SMEM, SMEM, VMEM, VMEM, whole((rows_here, width))]
        + [VMEM] * row_devices
        + [whole(packs.shape)],
        out_specs=[
            cost_block,
            VMEM,
            VMEM,
            whole((rows_here, width)),
            whole((rows_here, width)),
            whole((group_blocks, width)),
        ],
        out_shape=[
            jax.ShapeDtypeStruct(coupling.shape, f32),
            work_shape,
            work_shape,
            jax.ShapeDtypeStruct((rows_here, width), f32),
            jax.ShapeDtypeStruct((rows_here, width), f32),
            jax.ShapeDtypeStruct((group_blocks, width), f32),
        ],
        scratch_shapes=[
            pltpu.VMEM((group_blocks * link_count + 1, width, width), jnp.bfloat16),
            pltpu.VMEM((group_blocks * link_count + 1, width, width), jnp.bfloat16),
            pltpu.SMEM((group_blocks * group_blocks,), jnp.int32),
            pltpu.VMEM((group_blocks, width), f32),
            pltpu.VMEM((1, width), f32),
            pltpu.VMEM((rows_here, width), f32),
            pltpu.VMEM((rows_here, width), f32),
        ],
        compiler_params=pltpu.CompilerParams(vmem_limit_bytes=12 * mib + 2 * far_bytes),
        name="far_product",
    )(near_t, slot_t, link_t, in_vmem(x), in_vmem(term), mass, *cost_parts, packs)

    pass_params = pltpu.CompilerParams(vmem_limit_bytes=12 * mib)

    def column_step(row_parts, copies):
        return pl.pallas_call(
            functools.partial(column_kernel, col_devices, copies),
            in_specs=[VMEM] * (3 + col_devices),
            out_specs=[VMEM, VMEM],
            out_shape=[
                jax.ShapeDtypeStruct((copies * group_blocks, width), f32),
                jax.ShapeDtypeStruct((rows_here, width), f32),
            ],
            scratch_shapes=[
                pltpu.VMEM((rows_here, width), f32),
                pltpu.VMEM((rows_here * slots, width), f32),
                pltpu.VMEM((rows_here * slots, width), f32),
            ],
            compiler_params=pass_params,
            name="column_pass",
        )(in_vmem(work), select, log_source, *row_parts)

    def row_step(column_parts):
        return pl.pallas_call(
            functools.partial(row_kernel, row_devices),
            in_specs=[SMEM, VMEM, VMEM, VMEM],
            out_specs=VMEM,
            out_shape=jax.ShapeDtypeStruct((rows_here, width), f32),
            scratch_shapes=[
                pltpu.VMEM((group_blocks, width, width), f32),
                pltpu.VMEM((rows_here, width), f32),
                pltpu.VMEM((rows_here, width), f32),
            ],
            compiler_params=pass_params,
            name="row_pass",
        )(slot_t, in_vmem(tall), log_target, column_parts)

    for step in range(ITERS):
        last = step == ITERS - 1
        column_part, source_potential = column_step(
            from_all(row_part, "cols"), 1 if last else row_devices
        )
        column_parts = exchange(column_part, "rows")
        if not last:
            row_part = row_step(column_parts)
    own_target = pl.pallas_call(
        functools.partial(last_kernel, row_devices, "rows"),
        out_shape=jax.ShapeDtypeStruct((target_here, width), f32),
        name="last_potential",
    )(log_target, column_parts)
    return (
        cost_blocks,
        source_potential.reshape(rows_here * width),
        own_target.reshape(1, target_here * width),
    )


def solution(mesh):
    placed = (
        P("rows", "cols", None, None, None),
        P("rows", "cols", None),
        P("rows", None, None, None),
        P("rows", None),
        P("rows"),
        P("cols", "rows", None, None, None),
        P("cols", None, None),
        P("cols", "rows"),
    )
    return jax.shard_map(
        per_device,
        mesh=mesh,
        in_specs=placed,
        out_specs=(P("rows", "cols", None, None, None), P("rows"), P("cols", "rows")),
        check_vma=False,
    )
```

time: 126 us -> 129 us (1.024)
  local copies, waits for them, and re-layouts: 11.5 us -> 32.8 us
  blocking collectives: 43.6 us -> 31.4 us
  Pallas kernels: 39.3 us -> 33.3 us
  starting transfers between devices: 19.1 us -> 22.7 us
  waiting for transfers between devices: 10.5 us -> 7.64 us
    unnamed x27 -> x57, local copies, waits for them, and re-layouts: 11.3 us -> 32.6 us
    all_to_all x5 -> x3, blocking collectives: 43.6 us -> 31.4 us  [exchange(): return lax.all_to_all(copies, axis, 0, 0, tiled=True)]
    ppermute x7 -> x16, starting transfers between devices: 9.8 us -> 15.5 us  [send(): return lax.ppermute(x, axis, [(d, d ^ mask) for d in range(size)])]
    pallas_call x6 -> x8, Pallas kernels: 24.1 us -> 19.8 us  [the longest x2 10.1 us: near_product(): pl.pallas_call(functools.partial(near_kernel, first), grid=(count,), in_s...]
    all_to_all x2 -> x1, waiting for transfers between devices: 3.89 us -> 0.01 us  [exchange(): return lax.all_to_all(copies, axis, 0, 0, tiled=True)]
    all_to_all x2 -> x1, starting transfers between devices: 9.35 us -> 7.3 us  [exchange(): return lax.all_to_all(copies, axis, 0, 0, tiled=True)]
    pallas_call x1, Pallas kernels: 12.5 us -> 10.8 us  [per_device(): pl.pallas_call(functools.partial(far_kernel, (row_devices, col_devices, t...]
    ppermute x7 -> x16, waiting for transfers between devices: 6.56 us -> 7.64 us  [send(): return lax.ppermute(x, axis, [(d, d ^ mask) for d in range(size)])]
  transfers between devices with their start and end apart: 9 -> 17, of which waited for: 2 -> 7; matrix products, arithmetic and copies ran while one was open for 0% -> 0% of each run, Pallas kernels for 9% -> 8%
where the time goes in v3:
time: 129 us
  Pallas kernels  33.3 us (26%)
  local copies, waits for them, and re-layouts  32.8 us (25%)
  blocking collectives  31.4 us (24%)
  starting transfers between devices  22.7 us (18%)
  waiting for transfers between devices  7.64 us (6%)
    unnamed x57, local copies, waits for them, and re-layouts  32.6 us
    all_to_all x3, blocking collectives, exchange(): return lax.all_to_all(copies, axis, 0, 0, tiled=True)  31.4 us
    ppermute x16, starting transfers between devices, send(): return lax.ppermute(x, axis, [(d, d ^ mask) for d in range(size)])  15.5 us
    pallas_call x1, Pallas kernels, per_device(): pl.pallas_call(functools.partial(far_kernel, (row_devices, col_devices, t...  10.8 us
    pallas_call x2, Pallas kernels, near_product(): pl.pallas_call(functools.partial(near_kernel, first), grid=(count,), in_s...  10.1 us
    ppermute x16, waiting for transfers between devices, send(): return lax.ppermute(x, axis, [(d, d ^ mask) for d in range(size)])  7.64 us
    all_to_all x1, starting transfers between devices, exchange(): return lax.all_to_all(copies, axis, 0, 0, tiled=True)  7.3 us
    pallas_call x3, Pallas kernels, column_step(): pl.pallas_call(functools.partial(column_kernel, col_devices, copies), in_...  5.84 us
  transfers between devices with their start and end apart: 17, of which 7 were waited for; matrix products, arithmetic and copies ran while one was open for 0% of the time, Pallas kernels for 8%

profile of v3, /device:TPU:0, one launch (start us, length us, event | category | flops | bytes accessed | tf_op | source)
XLA Modules:
  0.0 128.7 jit_solution(3534822060903305546)
XLA Ops:
  0.6 1.5 %pack.1 = f32[256,128]{1,0:T(8,128)} custom-call(s32[32,128]{1,0:T(8,128)} %bitcast.21, s32[1,128]{1,0:T(1,128)} %target_ref.1), custom_call_target="tpu_custom_call" | custom-call | tf_op jit(solution)/shard_map/pack/pallas_call | solution.py:342
  2.1 7.3 %all-to-all-start = ((f32[32,8,128]{2,1,0:T(8,128)}), f32[32,8,128]{2,1,0:T(8,128)S(1)}, u32[]{:S(2)}, u32[]{:S(2)}) async-start(f32[32,8,128]{2,1,0:T(8,128)} %bitcast.37), calls=%async_computation | async-start | bytes 262144 | tf_op jit(solution)/shard_map/all_to_all | solution.py:71
  9.4 2.7 %collective-permute-start.3 = (f32[1,1,3,128,128]{4,3,2,1,0:T(8,128)}, f32[1,1,3,128,128]{4,3,2,1,0:T(8,128)S(1)}, u32[]{:S(2)}, u32[]{:S(2)}) collective-permute-start(f32[1,1,3,128,128]{4,3,2,1,0:T(8,128)} %refs_6_.1), channel_id=1, source_target_pairs={{0,16},{4,20},{8,24},{12,28},{16,0},{20,4},{24,8},{28,12},{1,17},{... | collective-permute-start | bytes 589832 | tf_op jit(solution)/shard_map/ppermute | solution.py:63
  12.2 1.5 %collective-permute-start.4 = (f32[1,1,3,128,128]{4,3,2,1,0:T(8,128)}, f32[1,1,3,128,128]{4,3,2,1,0:T(8,128)S(1)}, u32[]{:S(2)}, u32[]{:S(2)}) collective-permute-start(f32[1,1,3,128,128]{4,3,2,1,0:T(8,128)} %refs_6_.1), channel_id=1, source_target_pairs={{0,24},{4,28},{8,16},{12,20},{16,8},{20,12},{24,0},{28,4},{1,25},{... | collective-permute-start | bytes 589832 | tf_op jit(solution)/shard_map/ppermute | solution.py:63
  13.6 1.5 %collective-permute-start = (f32[1,1,3,128,128]{4,3,2,1,0:T(8,128)}, f32[1,1,3,128,128]{4,3,2,1,0:T(8,128)S(1)}, u32[]{:S(2)}, u32[]{:S(2)}) collective-permute-start(f32[1,1,3,128,128]{4,3,2,1,0:T(8,128)} %refs_6_.1), channel_id=1, source_target_pairs={{0,4},{4,0},{8,12},{12,8},{16,20},{20,16},{24,28},{28,24},{1,5},{5... | collective-permute-start | bytes 589832 | tf_op jit(solution)/shard_map/ppermute | solution.py:63
  15.2 1.9 %collective-permute-start.2 = (f32[1,1,3,128,128]{4,3,2,1,0:T(8,128)}, f32[1,1,3,128,128]{4,3,2,1,0:T(8,128)S(1)}, u32[]{:S(2)}, u32[]{:S(2)}) collective-permute-start(f32[1,1,3,128,128]{4,3,2,1,0:T(8,128)} %refs_6_.1), channel_id=1, source_target_pairs={{0,12},{4,8},{8,4},{12,0},{16,28},{20,24},{24,20},{28,16},{1,13},{... | collective-permute-start | bytes 589832 | tf_op jit(solution)/shard_map/ppermute | solution.py:63
  18.5 5.0 %near_product.2 = (bf16[32,256,768]{2,1,0:T(8,128)(2,1)S(1)}, f32[8,128,4]{2,1,0:T(8,128)S(1)}) custom-call(s32[3,32]{1,0:T(4,128)S(1)} %bitcast.29, f32[32,3,128,128]{3,2,1,0:T(8,128)} %cost_ref.3, f32[32,1,2,128,128]{4,3,2,1,0:T(8,128)} %plan_ref.3, s32[32,128]{1,0:T(8,128)S(1)} %bitcast.22), custom_call_target="tpu_custom_call" | custom-call | flops 1207959552 | bytes 5242880 | tf_op jit(solution)/shard_map/near_product/pallas_call | solution.py:357
  23.5 4.5 %copy-done = bf16[32,256,768]{2,1,0:T(8,128)(2,1)} copy-done((bf16[32,256,768]{2,1,0:T(8,128)(2,1)}, bf16[32,256,768]{2,1,0:T(8,128)(2,1)S(1)}, u32[]{:S(2)}) %copy-start) | copy-done | bytes 12582936
  30.0 1.5 %collective-permute-start.5 = (f32[1,1,3,128,128]{4,3,2,1,0:T(8,128)}, f32[1,1,3,128,128]{4,3,2,1,0:T(8,128)S(1)}, u32[]{:S(2)}, u32[]{:S(2)}) collective-permute-start(f32[1,1,3,128,128]{4,3,2,1,0:T(8,128)} %get-tuple-element.23.refs_10_), channel_id=1, source_target_pairs={{0,4},{4,0},{8,12},{12,8},{16,20},{20,16},{24,28},{28,24},{1,5},{5... | collective-permute-start | bytes 589832 | tf_op jit(solution)/shard_map/ppermute | solution.py:63
  32.0 4.6 %copy-done.1 = bf16[32,256,768]{2,1,0:T(8,128)(2,1)S(1)} copy-done((bf16[32,256,768]{2,1,0:T(8,128)(2,1)S(1)}, bf16[32,256,768]{2,1,0:T(8,128)(2,1)}, u32[]{:S(2)}) %copy-start.1) | copy-done | bytes 12582936
  37.7 5.1 %near_product.3 = (bf16[32,256,768]{2,1,0:T(8,128)(2,1)S(1)}, f32[8,128,4]{2,1,0:T(8,128)S(1)}) custom-call(s32[3,32]{1,0:T(4,128)S(1)} %bitcast.30, f32[32,3,128,128]{3,2,1,0:T(8,128)} %cost_ref.3, f32[32,1,2,128,128]{4,3,2,1,0:T(8,128)} %plan_ref.3, s32[32,128]{1,0:T(8,128)S(1)} %bitcast.23, ...), custom_call_target="tpu_custom_call", output_to_operand_aliasing={{0}: (4, {}), {1}: (5, {})} | custom-call | flops 1207959552 | bytes 5242880 | tf_op jit(solution)/shard_map/near_product/pallas_call | solution.py:357
  42.8 4.5 %copy-done.2 = bf16[32,256,768]{2,1,0:T(8,128)(2,1)} copy-done((bf16[32,256,768]{2,1,0:T(8,128)(2,1)}, bf16[32,256,768]{2,1,0:T(8,128)(2,1)S(1)}, u32[]{:S(2)}) %copy-start.2) | copy-done | bytes 12582936
  48.2 4.6 %copy-done.3 = bf16[32,256,768]{2,1,0:T(8,128)(2,1)S(1)} copy-done((bf16[32,256,768]{2,1,0:T(8,128)(2,1)S(1)}, bf16[32,256,768]{2,1,0:T(8,128)(2,1)}, u32[]{:S(2)}) %copy-start.3) | copy-done | bytes 12582936
  53.8 10.8 %far_product.1 = (f32[32,1,2,128,128]{4,3,2,1,0:T(8,128)}, f32[32,2,128,128]{3,2,1,0:T(8,128)S(1)}, f32[32,2,128,128]{3,2,1,0:T(8,128)S(1)}, f32[32,128]{1,0:T(8...) custom-call(s32[3,32]{1,0:T(4,128)S(1)} %bitcast.31, s32[2,32]{1,0:T(2,128)S(1)} %bitcast.32, ...), custom_call_target="tpu_custom_call" | custom-call | tf_op jit(solution)/shard_map/far_product/pallas_call | solution.py:402
  64.6 2.0 %copy-done.4 = f32[32,2,128,128]{3,2,1,0:T(8,128)} copy-done((f32[32,2,128,128]{3,2,1,0:T(8,128)}, f32[32,2,128,128]{3,2,1,0:T(8,128)S(1)}, u32[]{:S(2)}) %copy-start.4) | copy-done | bytes 4194328
  66.6 2.0 %copy-done.7 = f32[32,2,128,128]{3,2,1,0:T(8,128)} copy-done((f32[32,2,128,128]{3,2,1,0:T(8,128)}, f32[32,2,128,128]{3,2,1,0:T(8,128)S(1)}, u32[]{:S(2)}) %copy-start.7) | copy-done | bytes 4194328
  68.6 1.5 %collective-permute-start.8 = (f32[32,128]{1,0:T(8,128)S(1)}, f32[32,128]{1,0:T(8,128)S(1)}, u32[]{:S(2)}, u32[]{:S(2)}) collective-permute-start(f32[32,128]{1,0:T(8,128)S(1)} %get-tuple-element.30.refs_0_), channel_id=1, source_target_pairs={{0,2},{1,3},{2,0},{3,1},{4,6},{5,7},{6,4},{7,5},{8,10},{9,11},{10,... | collective-permute-start | bytes 49160 | tf_op jit(solution)/shard_map/ppermute | solution.py:63
  70.7 1.7 %collective-permute-done.8.refs_2_ = f32[32,128]{1,0:T(8,128)S(1)} collective-permute-done((f32[32,128]{1,0:T(8,128)S(1)}, f32[32,128]{1,0:T(8,128)S(1)}, u32[]{:S(2)}, u32[]{:S(2)}) %collective-permute-start.8) | collective-permute-done | bytes 16416 | tf_op jit(solution)/shard_map/ppermute | solution.py:63
  73.3 2.2 %copy-done.5 = f32[32,2,128,128]{3,2,1,0:T(8,128)S(1)} copy-done((f32[32,2,128,128]{3,2,1,0:T(8,128)S(1)}, f32[32,2,128,128]{3,2,1,0:T(8,128)}, u32[]{:S(2)}) %copy-start.5) | copy-done | bytes 4194328
  75.5 1.9 %column_pass.3 = (f32[64,128]{1,0:T(8,128)S(1)}, f32[32,128]{1,0:T(8,128)}) custom-call(f32[32,2,128,128]{3,2,1,0:T(8,128)S(1)} %copy-done.5, s32[64,128]{1,0:T(8,128)S(1)} %broadcast_in_dim.8.select_ref, f32[32,128]{1,0:T(8,128)S(1)} %get-tuple-element.27.log_mass_ref, f32[32,128]{1,0:T(8,128)S(1)} %get-tuple-element.30.refs_0_, ...), custom_call_target="tpu_custom_call" | custom-call | tf_op jit(solution)/shard_map/column_pass/pallas_call | solution.py:445
  77.5 12.9 %all_to_all.44 = f32[8,8,128]{2,1,0:T(8,128)S(1)} all-to-all(f32[8,8,128]{2,1,0:T(8,128)S(1)} %bitcast.27), channel_id=1, replica_groups=mesh['rows'=8,'cols'=4] {'rows'}, dimensions={0} | all-to-all | bytes 65536 | tf_op jit(solution)/shard_map/all_to_all | solution.py:71
  90.3 2.2 %copy-done.8 = f32[32,2,128,128]{3,2,1,0:T(8,128)S(1)} copy-done((f32[32,2,128,128]{3,2,1,0:T(8,128)S(1)}, f32[32,2,128,128]{3,2,1,0:T(8,128)}, u32[]{:S(2)}) %copy-start.8) | copy-done | bytes 4194328
  92.5 1.9 %row_pass.2.refs_0_ = f32[32,128]{1,0:T(8,128)S(1)} custom-call(s32[2,32]{1,0:T(2,128)S(1)} %bitcast.33, f32[32,2,128,128]{3,2,1,0:T(8,128)S(1)} %copy-done.8, f32[8,128]{1,0:T(8,128)S(1)} %get-tuple-element.29.log_mass_ref, f32[64,128]{1,0:T(8,128)S(1)} %bitcast.26), custom_call_target="tpu_custom_call" | custom-call | tf_op jit(solution)/shard_map/row_pass/pallas_call | solution.py:463
  96.4 2.0 %collective-permute-done.11.refs_2_ = f32[32,128]{1,0:T(8,128)S(1)} collective-permute-done((f32[32,128]{1,0:T(8,128)S(1)}, f32[32,128]{1,0:T(8,128)S(1)}, u32[]{:S(2)}, u32[]{:S(2)}) %collective-permute-start.11) | collective-permute-done | bytes 16416 | tf_op jit(solution)/shard_map/ppermute | solution.py:63
  98.5 1.9 %column_pass.4 = (f32[64,128]{1,0:T(8,128)S(1)}, f32[32,128]{1,0:T(8,128)}) custom-call(f32[32,2,128,128]{3,2,1,0:T(8,128)S(1)} %copy-done.6, s32[64,128]{1,0:T(8,128)S(1)} %broadcast_in_dim.8.select_ref, f32[32,128]{1,0:T(8,128)S(1)} %get-tuple-element.27.log_mass_ref, f32[32,128]{1,0:T(8,128)S(1)} %row_pass.2.refs_0_, ...), custom_call_target="tpu_custom_call" | custom-call | tf_op jit(solution)/shard_map/column_pass/pallas_call | solution.py:445
  100.5 9.0 %all_to_all.45 = f32[8,8,128]{2,1,0:T(8,128)S(1)} all-to-all(f32[8,8,128]{2,1,0:T(8,128)S(1)} %bitcast.28), channel_id=1, replica_groups=mesh['rows'=8,'cols'=4] {'rows'}, dimensions={0} | all-to-all | bytes 65536 | tf_op jit(solution)/shard_map/all_to_all | solution.py:71
  109.5 1.9 %row_pass.3.refs_0_ = f32[32,128]{1,0:T(8,128)S(1)} custom-call(s32[2,32]{1,0:T(2,128)S(1)} %bitcast.34, f32[32,2,128,128]{3,2,1,0:T(8,128)S(1)} %copy-done.9, f32[8,128]{1,0:T(8,128)S(1)} %get-tuple-element.29.log_mass_ref, f32[64,128]{1,0:T(8,128)S(1)} %bitcast.25), custom_call_target="tpu_custom_call" | custom-call | tf_op jit(solution)/shard_map/row_pass/pallas_call | solution.py:463
  111.5 1.3 %collective-permute-start.14 = (f32[32,128]{1,0:T(8,128)S(1)}, f32[32,128]{1,0:T(8,128)S(1)}, u32[]{:S(2)}, u32[]{:S(2)}) collective-permute-start(f32[32,128]{1,0:T(8,128)S(1)} %row_pass.3.refs_0_), channel_id=1, source_target_pairs={{0,2},{1,3},{2,0},{3,1},{4,6},{5,7},{6,4},{7,5},{8,10},{9,11},{10,... | collective-permute-start | bytes 49160 | tf_op jit(solution)/shard_map/ppermute | solution.py:63
  113.4 1.9 %collective-permute-done.14.refs_2_ = f32[32,128]{1,0:T(8,128)S(1)} collective-permute-done((f32[32,128]{1,0:T(8,128)S(1)}, f32[32,128]{1,0:T(8,128)S(1)}, u32[]{:S(2)}, u32[]{:S(2)}) %collective-permute-start.14) | collective-permute-done | bytes 16416 | tf_op jit(solution)/shard_map/ppermute | solution.py:63
  116.0 1.9 %column_pass.5 = (f32[8,128]{1,0:T(8,128)S(1)}, f32[32,128]{1,0:T(8,128)}) custom-call(f32[32,2,128,128]{3,2,1,0:T(8,128)S(1)} %copy-done.6, s32[64,128]{1,0:T(8,128)S(1)} %broadcast_in_dim.8.select_ref, f32[32,128]{1,0:T(8,128)S(1)} %get-tuple-element.27.log_mass_ref, f32[32,128]{1,0:T(8,128)S(1)} %row_pass.3.refs_0_, ...), custom_call_target="tpu_custom_call" | custom-call | tf_op jit(solution)/shard_map/column_pass/pallas_call | solution.py:445
  118.0 9.5 %all_to_all.46 = f32[8,1,128]{2,1,0:T(1,128)} all-to-all(f32[8,1,128]{2,1,0:T(1,128)S(1)} %bitcast.35), channel_id=1, replica_groups=mesh['rows'=8,'cols'=4] {'rows'}, dimensions={0} | all-to-all | bytes 8192 | tf_op jit(solution)/shard_map/all_to_all | solution.py:71
  127.5 1.2 last_potential.1
  (75 shorter events, 11.8 us)
Async XLA Ops:
  2.1 27.0 %all-to-all-start = ((f32[32,8,128]{2,1,0:T(8,128)}), f32[32,8,128]{2,1,0:T(8,128)S(1)}, u32[]{:S(2)}, u32[]{:S(2)}) async-start(f32[32,8,128]{2,1,0:T(8,128)} %bitcast.37), calls=%async_computation | async-start | bytes 262144 | tf_op jit(solution)/shard_map/all_to_all | solution.py:71
  9.4 19.7 %collective-permute-start.3 = (f32[1,1,3,128,128]{4,3,2,1,0:T(8,128)}, f32[1,1,3,128,128]{4,3,2,1,0:T(8,128)S(1)}, u32[]{:S(2)}, u32[]{:S(2)}) collective-permute-start(f32[1,1,3,128,128]{4,3,2,1,0:T(8,128)} %refs_6_.1), channel_id=1, source_target_pairs={{0,16},{4,20},{8,24},{12,28},{16,0},{20,4},{24,8},{28,12},{1,17},{... | collective-permute-start | bytes 589832 | tf_op jit(solution)/shard_map/ppermute | solution.py:63
  12.2 17.0 %collective-permute-start.4 = (f32[1,1,3,128,128]{4,3,2,1,0:T(8,128)}, f32[1,1,3,128,128]{4,3,2,1,0:T(8,128)S(1)}, u32[]{:S(2)}, u32[]{:S(2)}) collective-permute-start(f32[1,1,3,128,128]{4,3,2,1,0:T(8,128)} %refs_6_.1), channel_id=1, source_target_pairs={{0,24},{4,28},{8,16},{12,20},{16,8},{20,12},{24,0},{28,4},{1,25},{... | collective-permute-start | bytes 589832 | tf_op jit(solution)/shard_map/ppermute | solution.py:63
  13.6 34.5 %collective-permute-start = (f32[1,1,3,128,128]{4,3,2,1,0:T(8,128)}, f32[1,1,3,128,128]{4,3,2,1,0:T(8,128)S(1)}, u32[]{:S(2)}, u32[]{:S(2)}) collective-permute-start(f32[1,1,3,128,128]{4,3,2,1,0:T(8,128)} %refs_6_.1), channel_id=1, source_target_pairs={{0,4},{4,0},{8,12},{12,8},{16,20},{20,16},{24,28},{28,24},{1,5},{5... | collective-permute-start | bytes 589832 | tf_op jit(solution)/shard_map/ppermute | solution.py:63
  15.1 33.0 %collective-permute-start.1 = (f32[1,1,3,128,128]{4,3,2,1,0:T(8,128)}, f32[1,1,3,128,128]{4,3,2,1,0:T(8,128)S(1)}, u32[]{:S(2)}, u32[]{:S(2)}) collective-permute-start(f32[1,1,3,128,128]{4,3,2,1,0:T(8,128)} %refs_6_.1), channel_id=1, source_target_pairs={{0,8},{4,12},{8,0},{12,4},{16,24},{20,28},{24,16},{28,20},{1,9},{5... | collective-permute-start | bytes 589832 | tf_op jit(solution)/shard_map/ppermute | solution.py:63
  15.2 32.9 %collective-permute-start.2 = (f32[1,1,3,128,128]{4,3,2,1,0:T(8,128)}, f32[1,1,3,128,128]{4,3,2,1,0:T(8,128)S(1)}, u32[]{:S(2)}, u32[]{:S(2)}) collective-permute-start(f32[1,1,3,128,128]{4,3,2,1,0:T(8,128)} %refs_6_.1), channel_id=1, source_target_pairs={{0,12},{4,8},{8,4},{12,0},{16,28},{20,24},{24,20},{28,16},{1,13},{... | collective-permute-start | bytes 589832 | tf_op jit(solution)/shard_map/ppermute | solution.py:63
  18.5 13.5 %copy-start.21 = (s32[4096]{0:T(1024)S(1)}, s32[4096]{0:T(1024)}, u32[]{:S(2)}) copy-start(s32[4096]{0:T(1024)} %param.12) | copy-start | bytes 49156
  18.5 13.5 %copy-start.25 = (s32[32,3]{0,1:T(4,128)S(1)}, s32[32,3]{0,1:T(4,128)}, u32[]{:S(2)}) copy-start(s32[32,3]{0,1:T(4,128)} %param.11) | copy-start | bytes 1156
  23.5 4.6 %copy-start = (bf16[32,256,768]{2,1,0:T(8,128)(2,1)}, bf16[32,256,768]{2,1,0:T(8,128)(2,1)S(1)}, u32[]{:S(2)}) copy-start(bf16[32,256,768]{2,1,0:T(8,128)(2,1)S(1)} %get-tuple-element.19.refs_0_) | copy-start | bytes 37748740
  30.0 18.1 %collective-permute-start.5 = (f32[1,1,3,128,128]{4,3,2,1,0:T(8,128)}, f32[1,1,3,128,128]{4,3,2,1,0:T(8,128)S(1)}, u32[]{:S(2)}, u32[]{:S(2)}) collective-permute-start(f32[1,1,3,128,128]{4,3,2,1,0:T(8,128)} %get-tuple-element.23.refs_10_), channel_id=1, source_target_pairs={{0,4},{4,0},{8,12},{12,8},{16,20},{20,16},{24,28},{28,24},{1,5},{5... | collective-permute-start | bytes 589832 | tf_op jit(solution)/shard_map/ppermute | solution.py:63
  31.5 16.7 %collective-permute-start.6 = (f32[1,1,3,128,128]{4,3,2,1,0:T(8,128)}, f32[1,1,3,128,128]{4,3,2,1,0:T(8,128)S(1)}, u32[]{:S(2)}, u32[]{:S(2)}) collective-permute-start(f32[1,1,3,128,128]{4,3,2,1,0:T(8,128)} %get-tuple-element.24.refs_12_), channel_id=1, source_target_pairs={{0,4},{4,0},{8,12},{12,8},{16,20},{20,16},{24,28},{28,24},{1,5},{5... | collective-permute-start | bytes 589832 | tf_op jit(solution)/shard_map/ppermute | solution.py:63
  32.0 4.6 %copy-start.1 = (bf16[32,256,768]{2,1,0:T(8,128)(2,1)S(1)}, bf16[32,256,768]{2,1,0:T(8,128)(2,1)}, u32[]{:S(2)}) copy-start(bf16[32,256,768]{2,1,0:T(8,128)(2,1)} %copy-done) | copy-start | bytes 37748740
  37.7 10.5 %copy-start.15 = (f32[32,8,128]{2,1,0:T(8,128)S(1)}, f32[32,8,128]{2,1,0:T(8,128)}, u32[]{:S(2)}) copy-start(f32[32,8,128]{2,1,0:T(8,128)} %copy-done.14) | copy-start | bytes 393220
  37.7 10.5 %copy-start.17 = (f32[1,1,3,128,128]{4,3,2,1,0:T(8,128)S(1)}, f32[1,1,3,128,128]{4,3,2,1,0:T(8,128)}, u32[]{:S(2)}) copy-start(f32[1,1,3,128,128]{4,3,2,1,0:T(8,128)} %get-tuple-element.23.refs_10_) | copy-start | bytes 589828
  37.7 10.5 %copy-start.19 = (f32[1,1,3,128,128]{4,3,2,1,0:T(8,128)S(1)}, f32[1,1,3,128,128]{4,3,2,1,0:T(8,128)}, u32[]{:S(2)}) copy-start(f32[1,1,3,128,128]{4,3,2,1,0:T(8,128)} %get-tuple-element.24.refs_12_) | copy-start | bytes 589828
  37.7 10.5 %copy-start.22 = (f32[1,1,3,128,128]{4,3,2,1,0:T(8,128)S(1)}, f32[1,1,3,128,128]{4,3,2,1,0:T(8,128)}, u32[]{:S(2)}) copy-start(f32[1,1,3,128,128]{4,3,2,1,0:T(8,128)} %refs_6_.1) | copy-start | bytes 589828
  37.7 10.5 %copy-start.26 = (s32[32,1,2]{0,2,1:T(2,128)S(1)}, s32[32,1,2]{0,2,1:T(2,128)}, u32[]{:S(2)}) copy-start(s32[32,1,2]{0,2,1:T(2,128)} %param.9) | copy-start | bytes 772
  37.7 10.5 %copy-start.27 = (s32[1,8,3]{1,0,2:T(1,128)S(1)}, s32[1,8,3]{1,0,2:T(1,128)}, u32[]{:S(2)}) copy-start(s32[1,8,3]{1,0,2:T(1,128)} %param.14) | copy-start | bytes 292
  42.8 4.6 %copy-start.2 = (bf16[32,256,768]{2,1,0:T(8,128)(2,1)}, bf16[32,256,768]{2,1,0:T(8,128)(2,1)S(1)}, u32[]{:S(2)}) copy-start(bf16[32,256,768]{2,1,0:T(8,128)(2,1)S(1)} %get-tuple-element.21.refs_3_) | copy-start | bytes 37748740
  48.2 4.6 %copy-start.3 = (bf16[32,256,768]{2,1,0:T(8,128)(2,1)S(1)}, bf16[32,256,768]{2,1,0:T(8,128)(2,1)}, u32[]{:S(2)}) copy-start(bf16[32,256,768]{2,1,0:T(8,128)(2,1)} %copy-done.2) | copy-start | bytes 37748740
  68.6 40.9 %copy-start.23 = (f32[8,128]{1,0:T(8,128)}, f32[8,128]{1,0:T(8,128)S(1)}, u32[]{:S(2)}) copy-start(f32[8,128]{1,0:T(8,128)S(1)} %get-tuple-element.29.log_mass_ref) | copy-start | bytes 12292
  68.6 2.1 %collective-permute-start.7 = (f32[32,128]{1,0:T(8,128)S(1)}, f32[32,128]{1,0:T(8,128)S(1)}, u32[]{:S(2)}, u32[]{:S(2)}) collective-permute-start(f32[32,128]{1,0:T(8,128)S(1)} %get-tuple-element.30.refs_0_), channel_id=1, source_target_pairs={{0,1},{1,0},{2,3},{3,2},{4,5},{5,4},{6,7},{7,6},{8,9},{9,8},{10,11... | collective-permute-start | bytes 49160 | tf_op jit(solution)/shard_map/ppermute | solution.py:63
  68.6 3.7 %collective-permute-start.8 = (f32[32,128]{1,0:T(8,128)S(1)}, f32[32,128]{1,0:T(8,128)S(1)}, u32[]{:S(2)}, u32[]{:S(2)}) collective-permute-start(f32[32,128]{1,0:T(8,128)S(1)} %get-tuple-element.30.refs_0_), channel_id=1, source_target_pairs={{0,2},{1,3},{2,0},{3,1},{4,6},{5,7},{6,4},{7,5},{8,10},{9,11},{10,... | collective-permute-start | bytes 49160 | tf_op jit(solution)/shard_map/ppermute | solution.py:63
  70.1 3.2 %collective-permute-start.9 = (f32[32,128]{1,0:T(8,128)S(1)}, f32[32,128]{1,0:T(8,128)S(1)}, u32[]{:S(2)}, u32[]{:S(2)}) collective-permute-start(f32[32,128]{1,0:T(8,128)S(1)} %get-tuple-element.30.refs_0_), channel_id=1, source_target_pairs={{0,3},{1,2},{2,1},{3,0},{4,7},{5,6},{6,5},{7,4},{8,11},{9,10},{10,... | collective-permute-start | bytes 49160 | tf_op jit(solution)/shard_map/ppermute | solution.py:63
  75.5 23.0 %copy-start.6 = (f32[32,2,128,128]{3,2,1,0:T(8,128)S(1)}, f32[32,2,128,128]{3,2,1,0:T(8,128)}, u32[]{:S(2)}) copy-start(f32[32,2,128,128]{3,2,1,0:T(8,128)} %copy-done.4) | copy-start | bytes 12582916
  92.5 17.0 %copy-start.9 = (f32[32,2,128,128]{3,2,1,0:T(8,128)S(1)}, f32[32,2,128,128]{3,2,1,0:T(8,128)}, u32[]{:S(2)}) copy-start(f32[32,2,128,128]{3,2,1,0:T(8,128)} %copy-done.7) | copy-start | bytes 12582916
  94.5 1.9 %collective-permute-start.10 = (f32[32,128]{1,0:T(8,128)S(1)}, f32[32,128]{1,0:T(8,128)S(1)}, u32[]{:S(2)}, u32[]{:S(2)}) collective-permute-start(f32[32,128]{1,0:T(8,128)S(1)} %row_pass.2.refs_0_), channel_id=1, source_target_pairs={{0,1},{1,0},{2,3},{3,2},{4,5},{5,4},{6,7},{7,6},{8,9},{9,8},{10,11... | collective-permute-start | bytes 49160 | tf_op jit(solution)/shard_map/ppermute | solution.py:63
  94.5 3.8 %collective-permute-start.11 = (f32[32,128]{1,0:T(8,128)S(1)}, f32[32,128]{1,0:T(8,128)S(1)}, u32[]{:S(2)}, u32[]{:S(2)}) collective-permute-start(f32[32,128]{1,0:T(8,128)S(1)} %row_pass.2.refs_0_), channel_id=1, source_target_pairs={{0,2},{1,3},{2,0},{3,1},{4,6},{5,7},{6,4},{7,5},{8,10},{9,11},{10,... | collective-permute-start | bytes 49160 | tf_op jit(solution)/shard_map/ppermute | solution.py:63
  95.3 3.2 %collective-permute-start.12 = (f32[32,128]{1,0:T(8,128)S(1)}, f32[32,128]{1,0:T(8,128)S(1)}, u32[]{:S(2)}, u32[]{:S(2)}) collective-permute-start(f32[32,128]{1,0:T(8,128)S(1)} %row_pass.2.refs_0_), channel_id=1, source_target_pairs={{0,3},{1,2},{2,1},{3,0},{4,7},{5,6},{6,5},{7,4},{8,11},{9,10},{10,... | collective-permute-start | bytes 49160 | tf_op jit(solution)/shard_map/ppermute | solution.py:63
  111.5 1.9 %collective-permute-start.13 = (f32[32,128]{1,0:T(8,128)S(1)}, f32[32,128]{1,0:T(8,128)S(1)}, u32[]{:S(2)}, u32[]{:S(2)}) collective-permute-start(f32[32,128]{1,0:T(8,128)S(1)} %row_pass.3.refs_0_), channel_id=1, source_target_pairs={{0,1},{1,0},{2,3},{3,2},{4,5},{5,4},{6,7},{7,6},{8,9},{9,8},{10,11... | collective-permute-start | bytes 49160 | tf_op jit(solution)/shard_map/ppermute | solution.py:63
  111.5 3.8 %collective-permute-start.14 = (f32[32,128]{1,0:T(8,128)S(1)}, f32[32,128]{1,0:T(8,128)S(1)}, u32[]{:S(2)}, u32[]{:S(2)}) collective-permute-start(f32[32,128]{1,0:T(8,128)S(1)} %row_pass.3.refs_0_), channel_id=1, source_target_pairs={{0,2},{1,3},{2,0},{3,1},{4,6},{5,7},{6,4},{7,5},{8,10},{9,11},{10,... | collective-permute-start | bytes 49160 | tf_op jit(solution)/shard_map/ppermute | solution.py:63
  112.9 3.2 %collective-permute-start.15 = (f32[32,128]{1,0:T(8,128)S(1)}, f32[32,128]{1,0:T(8,128)S(1)}, u32[]{:S(2)}, u32[]{:S(2)}) collective-permute-start(f32[32,128]{1,0:T(8,128)S(1)} %row_pass.3.refs_0_), channel_id=1, source_target_pairs={{0,3},{1,2},{2,1},{3,0},{4,7},{5,6},{6,5},{7,4},{8,11},{9,10},{10,... | collective-permute-start | bytes 49160 | tf_op jit(solution)/shard_map/ppermute | solution.py:63
  (13 other events, 15.7 us)

commit v4 on v3

--- a/solution.py
+++ b/solution.py
@@ -22,8 +22,8 @@
 ANY = pl.BlockSpec(memory_space=pl.ANY)
 
 
-def in_vmem(x):
-    return pltpu.with_memory_space_constraint(x, pltpu.VMEM)
+def in_hbm(x):
+    return pltpu.with_memory_space_constraint(x, pltpu.HBM)
 
 
 def whole(shape):
@@ -71,7 +71,7 @@
     return lax.all_to_all(copies, axis, 0, 0, tiled=True)
 
 
-def pack_kernel(devices, source_ref, target_ref, out_ref):
+def pack_kernel(devices, after_ref, source_ref, target_ref, out_ref):
     rows = out_ref.shape[0] // devices
     total = jnp.sum(source_ref[...].astype(jnp.float32), axis=(0, 1), keepdims=True)
     target = target_ref[...].astype(jnp.float32)
@@ -109,12 +109,12 @@
                 preferred_element_type=jnp.float32,
             )
             x_high, x_low = split(x)
-            x_ref[row, 0:width, k * wide : (k + 1) * wide] = x_high
-            x_ref[row, width : 2 * width, k * wide : (k + 1) * wide] = x_low
+            x_ref[i, 0:width, k * wide : (k + 1) * wide] = x_high
+            x_ref[i, width : 2 * width, k * wide : (k + 1) * wide] = x_low
             weighted = cost * cost * mass_ref[pl.ds(g * SUB + a, 1), :].astype(jnp.float32)
             acc = weighted if acc is None else acc + weighted
         terms = jnp.where(lanes == i, jnp.sum(acc, axis=1, keepdims=True), terms)
-    term_ref[g] = terms
+    term_ref[0] = terms
 
 
 def relay_kernel(*refs):
@@ -125,10 +125,10 @@
     row_devices, col_devices, target_here, source_count, target_count, group_blocks, link_count = counts
     near_index_ref, slot_ref, link_ref, x_ref, term_ref, mass_ref = refs[:6]
     cost_parts = refs[6 : 6 + row_devices]
-    pack_ref, out_ref, work_ref, tall_ref, part_ref, log_source_ref, log_target_ref = refs[
-        6 + row_devices : 13 + row_devices
+    pack_ref, out_ref, tall_ref, part_ref, log_source_ref, log_target_ref = refs[
+        6 + row_devices : 12 + row_devices
     ]
-    far_high, far_low, table, column_scr, scale_scr, peak_scr, sum_scr = refs[13 + row_devices :]
+    far_high, far_low, table, column_scr, scale_scr, peak_scr, sum_scr = refs[12 + row_devices :]
     g = pl.program_id(0)
     near_count = near_index_ref.shape[0]
     slots = slot_ref.shape[0]
@@ -207,18 +207,16 @@
         right_low = jnp.concatenate(
             [jnp.concatenate([far_low[e] for e in r], axis=1) for r in far_rows], axis=0
         )
-        both = jnp.dot(x_ref[row], right_high, preferred_element_type=jnp.float32)
-        rest = jnp.dot(x_ref[row, 0:width, :], right_low, preferred_element_type=jnp.float32)
+        both = jnp.dot(x_ref[i], right_high, preferred_element_type=jnp.float32)
+        rest = jnp.dot(x_ref[i, 0:width, :], right_low, preferred_element_type=jnp.float32)
         product = both[0:width] + (both[width:] + rest)
-        tall = term_ref[row // SUB, :, i % SUB : i % SUB + 1] * scale
+        tall = term_ref[i // SUB, :, i % SUB : i % SUB + 1] * scale
         scores = []
         for l in range(slots):
             cost = tall + column_scr[pl.ds(targets[l], 1), :] - coef * product[:, l * width : (l + 1) * width]
             out_ref[i, 0, l] = cost
-            scaled = cost * -to_log2
-            work_ref[row, l] = scaled
-            turned = scaled.T
-            tall_ref[row, l] = turned
+            turned = (cost * -to_log2).T
+            tall_ref[i, l] = turned
             scores.append(turned)
         row_pass(scores, row, peak_scr, sum_scr)
 
@@ -234,64 +232,68 @@
     sum_scr[pl.ds(row, 1), :] = jnp.sum(total, axis=0, keepdims=True)
 
 
-def column_kernel(col_devices, copies, work_ref, select_ref, log_mass_ref, *refs):
+def column_kernel(col_devices, copies, cost_ref, select_ref, log_mass_ref, *refs):
     parts = refs[:col_devices]
     out_ref, potential_ref, potential_scr, peak_scr, sum_scr = refs[col_devices:]
-    rows, slots, width, _ = work_ref.shape
-    together = math.gcd(rows, 8)
-    scaled = log_mass_ref[...] - log_sum([p[...] for p in parts])
-    potential_scr[...] = scaled
-    potential_ref[...] = scaled * from_log2
-
-    def some_rows(g, _):
-        first = pl.multiple_of(g * together, together)
-        tall = potential_scr[pl.ds(first, together), :].T
-        for i in range(together):
-            for l in range(slots):
-                score = tall[:, i : i + 1] + work_ref[first + i, l]
-                peak = jnp.max(score, axis=0, keepdims=True)
-                total = jnp.sum(jnp.exp2(score - peak), axis=0, keepdims=True)
-                place = (first + i) * slots + l
-                peak_scr[pl.ds(place, 1), :] = peak
-                sum_scr[pl.ds(place, 1), :] = total
-        return 0
-
-    lax.fori_loop(0, rows // together, some_rows, 0)
-    select = select_ref[...]
-    peaks = peak_scr[...]
-    sums = sum_scr[...]
-    blocks = out_ref.shape[0] // copies
-    for t in range(blocks):
-        chosen = select == t
-        peak = jnp.max(jnp.where(chosen, peaks, very_low), axis=0, keepdims=True)
-        shifted = jnp.where(chosen, sums * jnp.exp2(jnp.minimum(peaks - peak, 0.0)), 0.0)
-        total = jnp.sum(shifted, axis=0, keepdims=True)
-        some = total > 0.0
-        out_ref[t : t + 1, :] = jnp.where(
-            some, peak + jnp.log2(jnp.where(some, total, 1.0)), very_low
-        )
-    if copies > 1:
-        put_copies(out_ref, copies, out_ref[0:blocks, :])
+    rows, _, slots, _, _ = cost_ref.shape
+    g = pl.program_id(0)
+
+    @pl.when(g == 0)
+    def _():
+        scaled = log_mass_ref[...] - log_sum([p[...] for p in parts])
+        potential_scr[...] = scaled
+        potential_ref[...] = scaled * from_log2
+
+    first = pl.multiple_of(g * rows, rows)
+    tall = potential_scr[pl.ds(first, rows), :].T
+    for i in range(rows):
+        for l in range(slots):
+            score = tall[:, i : i + 1] - cost_ref[i, 0, l] * to_log2
+            peak = jnp.max(score, axis=0, keepdims=True)
+            total = jnp.sum(jnp.exp2(score - peak), axis=0, keepdims=True)
+            place = (first + i) * slots + l
+            peak_scr[pl.ds(place, 1), :] = peak
+            sum_scr[pl.ds(place, 1), :] = total
+
+    @pl.when(g == pl.num_programs(0) - 1)
+    def _():
+        select = select_ref[...]
+        peaks = peak_scr[...]
+        sums = sum_scr[...]
+        blocks = out_ref.shape[0] // copies
+        for t in range(blocks):
+            chosen = select == t
+            peak = jnp.max(jnp.where(chosen, peaks, very_low), axis=0, keepdims=True)
+            shifted = jnp.where(chosen, sums * jnp.exp2(jnp.minimum(peaks - peak, 0.0)), 0.0)
+            total = jnp.sum(shifted, axis=0, keepdims=True)
+            some = total > 0.0
+            out_ref[t : t + 1, :] = jnp.where(
+                some, peak + jnp.log2(jnp.where(some, total, 1.0)), very_low
+            )
+        if copies > 1:
+            put_copies(out_ref, copies, out_ref[0:blocks, :])
 
 
 def row_kernel(
     row_devices, slot_ref, tall_ref, log_mass_ref, parts_ref, out_ref, wide_scr, peak_scr, sum_scr
 ):
     rows, slots, width, _ = tall_ref.shape
-    together = math.gcd(rows, 8)
-    potential = (log_mass_ref[...] - log_sum(parts_of(parts_ref, row_devices))).T
-    for t in range(wide_scr.shape[0]):
-        wide_scr[t] = jnp.broadcast_to(potential[:, t : t + 1], (width, width))
-
-    def some_rows(g, _):
-        for i in range(together):
-            row = g * together + i
-            scores = [wide_scr[slot_ref[l, row]] + tall_ref[row, l] for l in range(slots)]
-            row_pass(scores, row, peak_scr, sum_scr)
-        return 0
-
-    lax.fori_loop(0, rows // together, some_rows, 0)
-    out_ref[...] = peak_scr[...] + jnp.log2(sum_scr[...])
+    g = pl.program_id(0)
+
+    @pl.when(g == 0)
+    def _():
+        potential = (log_mass_ref[...] - log_sum(parts_of(parts_ref, row_devices))).T
+        for t in range(wide_scr.shape[0]):
+            wide_scr[t] = jnp.broadcast_to(potential[:, t : t + 1], (width, width))
+
+    for i in range(rows):
+        row = g * rows + i
+        scores = [wide_scr[slot_ref[l, row]] + tall_ref[i, l] for l in range(slots)]
+        row_pass(scores, row, peak_scr, sum_scr)
+
+    @pl.when(g == pl.num_programs(0) - 1)
+    def _():
+        out_ref[...] = peak_scr[...] + jnp.log2(sum_scr[...])
 
 
 def last_kernel(row_devices, row_axis, log_mass_ref, parts_ref, out_ref):
@@ -329,29 +331,20 @@
         if mask not in late:
             arrived[mask] = send(target_cost, "rows", mask)
 
-    near_t = near_index.T
-    slot_t = coupling_index[:, 0, :].T
-    link_t = jnp.transpose(target_index, (2, 0, 1))
-    mass = source_weights.reshape(rows_here, width)
+    near_t = in_hbm(near_index.T)
+    slot_t = in_hbm(coupling_index[:, 0, :].T)
+    link_t = in_hbm(jnp.transpose(target_index, (2, 0, 1)))
+    mass = in_hbm(source_weights.reshape(rows_here, width))
+    near_cost = in_hbm(near_cost)
+    coupling = in_hbm(coupling)
     select = jnp.broadcast_to(
         coupling_index.reshape(rows_here * slots, 1), (rows_here * slots, width)
     )
 
-    pack_rows = 8 * pl.cdiv(1 + target_here, 8)
-    devices = row_devices * col_devices
-    pack = pl.pallas_call(
-        functools.partial(pack_kernel, devices),
-        out_shape=jax.ShapeDtypeStruct((devices * pack_rows, width), f32),
-        name="pack",
-    )(mass, target_weights.reshape(target_here, width))
-    packs = exchange(pack, ("rows", "cols"))
-
     wide = near_count * slots * width
     groups = rows_here // SUB
-    x_shape = pltpu.VMEM((rows_here, 2 * width, wide), jnp.bfloat16)
-    term_shape = pltpu.VMEM((groups, width, SUB), f32)
-    near_cost = pltpu.with_memory_space_constraint(near_cost, pltpu.HBM)
-    coupling = pltpu.with_memory_space_constraint(coupling, pltpu.HBM)
+    x_shape = pltpu.HBM((rows_here, 2 * width, wide), jnp.bfloat16)
+    term_shape = pltpu.HBM((groups, width, SUB), f32)
 
     def near_product(first, count, *held):
         return pl.pallas_call(
@@ -363,31 +356,45 @@
                 pl.BlockSpec((SUB, 1, slots, width, width), lambda g: (first + g, 0, 0, 0, 0)),
                 whole((rows_here, width)),
             ]
-            + [VMEM] * len(held),
-            out_specs=[VMEM, VMEM],
+            + [ANY] * len(held),
+            out_specs=[
+                pl.BlockSpec((SUB, 2 * width, wide), lambda g: (first + g, 0, 0)),
+                pl.BlockSpec((1, width, SUB), lambda g: (first + g, 0, 0)),
+            ],
             out_shape=[x_shape, term_shape],
             input_output_aliases={4: 0, 5: 1} if held else {},
             scratch_shapes=[pltpu.VMEM((SUB, 3 * width, slots * width), jnp.bfloat16)],
-            compiler_params=pltpu.CompilerParams(vmem_limit_bytes=12 * mib),
+            compiler_params=pltpu.CompilerParams(vmem_limit_bytes=32 * mib),
             cost_estimate=pl.CostEstimate(
                 flops=6 * count * SUB * wide * width * width,
                 bytes_accessed=4 * count * SUB * width * (near_count + slots) * width,
                 transcendentals=0,
             ),
             name="near_product",
-        )(near_t, near_cost, coupling, mass, *map(in_vmem, held))
+        )(near_t, near_cost, coupling, mass, *map(in_hbm, held))
 
     held = near_product(0, (groups + 1) // 2)
+
+    pack_rows = 8 * pl.cdiv(1 + target_here, 8)
+    devices = row_devices * col_devices
+    pack = pl.pallas_call(
+        functools.partial(pack_kernel, devices),
+        in_specs=[ANY, VMEM, VMEM],
+        out_shape=jax.ShapeDtypeStruct((devices * pack_rows, width), f32),
+        name="pack",
+    )(in_hbm(held[1]), mass, in_hbm(target_weights.reshape(target_here, width)))
+    packs = exchange(pack, ("rows", "cols"))
+
     if late:
         sources = [mask - 1 for mask in late]
         passed = pl.pallas_call(
             relay_kernel,
-            in_specs=[ANY] * (2 + len(sources)),
+            in_specs=[ANY] * (1 + len(sources)),
             out_specs=[ANY] * len(sources),
             out_shape=[jax.ShapeDtypeStruct(target_cost.shape, f32)] * len(sources),
-            input_output_aliases={2 + e: e for e in range(len(sources))},
+            input_output_aliases={1 + e: e for e in range(len(sources))},
             name="relay",
-        )(held[1], packs, *[arrived[mask] for mask in sources])
+        )(packs, *[arrived[mask] for mask in sources])
         for mask, block in zip(sources, passed):
             arrived[mask] = block
             arrived[mask + 1] = send(block, "rows", 1)
@@ -398,8 +405,8 @@
     step_rows = SUB
     steps = rows_here // step_rows
     cost_block = pl.BlockSpec((step_rows, 1, slots, width, width), lambda g: (g, 0, 0, 0, 0))
-    work_shape = pltpu.VMEM((rows_here, slots, width, width), f32)
-    cost_blocks, work, tall, row_part, log_source, log_target = pl.pallas_call(
+    tall_block = pl.BlockSpec((step_rows, slots, width, width), lambda g: (g, 0, 0, 0))
+    cost_blocks, tall, row_part, log_source, log_target = pl.pallas_call(
         functools.partial(
             far_kernel,
             (row_devices, col_devices, target_here, source_count, target_count, group_blocks, link_count),
@@ -407,21 +414,26 @@
             "cols",
         ),
         grid=(steps,),
-        in_specs=[SMEM, SMEM, SMEM, VMEM, VMEM, whole((rows_here, width))]
+        in_specs=[
+            SMEM,
+            SMEM,
+            SMEM,
+            pl.BlockSpec((step_rows, 2 * width, wide), lambda g: (g, 0, 0)),
+            pl.BlockSpec((step_rows // SUB, width, SUB), lambda g: (g, 0, 0)),
+            whole((rows_here, width)),
+        ]
         + [VMEM] * row_devices
         + [whole(packs.shape)],
         out_specs=[
             cost_block,
-            VMEM,
-            VMEM,
+            tall_block,
             whole((rows_here, width)),
             whole((rows_here, width)),
             whole((group_blocks, width)),
         ],
         out_shape=[
-            jax.ShapeDtypeStruct(coupling.shape, f32),
-            work_shape,
-            work_shape,
+            pltpu.HBM(coupling.shape, f32),
+            pltpu.HBM((rows_here, slots, width, width), f32),
             jax.ShapeDtypeStruct((rows_here, width), f32),
             jax.ShapeDtypeStruct((rows_here, width), f32),
             jax.ShapeDtypeStruct((group_blocks, width), f32),
@@ -435,17 +447,24 @@
             pltpu.VMEM((rows_here, width), f32),
             pltpu.VMEM((rows_here, width), f32),
         ],
-        compiler_params=pltpu.CompilerParams(vmem_limit_bytes=12 * mib + 2 * far_bytes),
+        compiler_params=pltpu.CompilerParams(vmem_limit_bytes=20 * mib + 2 * far_bytes),
         name="far_product",
-    )(near_t, slot_t, link_t, in_vmem(x), in_vmem(term), mass, *cost_parts, packs)
-
-    pass_params = pltpu.CompilerParams(vmem_limit_bytes=12 * mib)
+    )(near_t, slot_t, link_t, in_hbm(x), in_hbm(term), mass, *cost_parts, packs)
+
+    pass_params = pltpu.CompilerParams(vmem_limit_bytes=32 * mib)
+    pass_rows = math.gcd(rows_here, 8)
+    passes = rows_here // pass_rows
 
     def column_step(row_parts, copies):
         return pl.pallas_call(
             functools.partial(column_kernel, col_devices, copies),
-            in_specs=[VMEM] * (3 + col_devices),
-            out_specs=[VMEM, VMEM],
+            grid=(passes,),
+            in_specs=[
+                pl.BlockSpec((pass_rows, 1, slots, width, width), lambda g: (g, 0, 0, 0, 0)),
+                whole((rows_here * slots, width)),
+            ]
+            + [whole((rows_here, width))] * (1 + col_devices),
+            out_specs=[whole((copies * group_blocks, width)), whole((rows_here, width))],
             out_shape=[
                 jax.ShapeDtypeStruct((copies * group_blocks, width), f32),
                 jax.ShapeDtypeStruct((rows_here, width), f32),
@@ -457,13 +476,19 @@
             ],
             compiler_params=pass_params,
             name="column_pass",
-        )(in_vmem(work), select, log_source, *row_parts)
+        )(in_hbm(cost_blocks), select, log_source, *row_parts)
 
     def row_step(column_parts):
         return pl.pallas_call(
             functools.partial(row_kernel, row_devices),
-            in_specs=[SMEM, VMEM, VMEM, VMEM],
-            out_specs=VMEM,
+            grid=(passes,),
+            in_specs=[
+                SMEM,
+                pl.BlockSpec((pass_rows, slots, width, width), lambda g: (g, 0, 0, 0)),
+                whole((group_blocks, width)),
+                whole(column_parts.shape),
+            ],
+            out_specs=whole((rows_here, width)),
             out_shape=jax.ShapeDtypeStruct((rows_here, width), f32),
             scratch_shapes=[
                 pltpu.VMEM((group_blocks, width, width), f32),
@@ -472,7 +497,7 @@
             ],
             compiler_params=pass_params,
             name="row_pass",
-        )(slot_t, in_vmem(tall), log_target, column_parts)
+        )(slot_t, in_hbm(tall), log_target, column_parts)
 
     for step in range(ITERS):
         last = step == ITERS - 1

time: 129 us -> 131 us (1.016)
  local copies, waits for them, and re-layouts: 32.8 us -> 1.05 us
  Pallas kernels: 33.3 us -> 52.6 us
  waiting for transfers between devices: 7.64 us -> 22.6 us
    unnamed x57 -> x19, local copies, waits for them, and re-layouts: 32.6 us -> 0.87 us
    ppermute x16, waiting for transfers between devices: 7.64 us -> 22.6 us  [send(): return lax.ppermute(x, axis, [(d, d ^ mask) for d in range(size)])]
    pallas_call x7, Pallas kernels: 11.2 us -> 23 us  [the longest x3 14 us: column_step(): pl.pallas_call(functools.partial(column_kernel, col_devices, copies), gri...]
    pallas_call x2, Pallas kernels: 10.1 us -> 14.1 us  [near_product(): pl.pallas_call(functools.partial(near_kernel, first), grid=(count,), in_s...]
    pallas_call x1, Pallas kernels: 10.8 us -> 14.3 us  [per_device(): pl.pallas_call(functools.partial(far_kernel, (row_devices, col_devices, t...]
  transfers between devices with their start and end apart: 17 -> 17, of which waited for: 7 -> 8; matrix products, arithmetic and copies ran while one was open for 0% -> 0% of each run, Pallas kernels for 8% -> 5%
where the time goes in v4:
time: 131 us; the launch traced here: 130 us
  Pallas kernels  52.6 us (40%)
  blocking collectives  30.4 us (23%)
  starting transfers between devices  22.8 us (17%)
  waiting for transfers between devices  22.6 us (17%)
    all_to_all x3, blocking collectives, exchange(): return lax.all_to_all(copies, axis, 0, 0, tiled=True)  30.4 us
    ppermute x16, waiting for transfers between devices, send(): return lax.ppermute(x, axis, [(d, d ^ mask) for d in range(size)])  22.6 us
    ppermute x16, starting transfers between devices, send(): return lax.ppermute(x, axis, [(d, d ^ mask) for d in range(size)])  15.5 us
    pallas_call x1, Pallas kernels, per_device(): pl.pallas_call(functools.partial(far_kernel, (row_devices, col_devices, t...  14.3 us
    pallas_call x2, Pallas kernels, near_product(): pl.pallas_call(functools.partial(near_kernel, first), grid=(count,), in_s...  14.1 us
    pallas_call x3, Pallas kernels, column_step(): pl.pallas_call(functools.partial(column_kernel, col_devices, copies), gri...  14 us
    pallas_call x2, Pallas kernels, row_step(): pl.pallas_call(functools.partial(row_kernel, row_devices), grid=(passes,)...  7.49 us
    all_to_all x1, starting transfers between devices, exchange(): return lax.all_to_all(copies, axis, 0, 0, tiled=True)  7.3 us
  transfers between devices with their start and end apart: 17, of which 8 were waited for; matrix products, arithmetic and copies ran while one was open for 0% of the time, Pallas kernels for 5%

profile of v4, /device:TPU:0, one launch (start us, length us, event | category | flops | bytes accessed | tf_op | source)
XLA Modules:
  0.0 130.1 jit_solution(14720587202527150591)
XLA Ops:
  0.6 7.0 %near_product.2 = (bf16[32,256,768]{2,1,0:T(8,128)(2,1)}, f32[8,128,4]{2,1,0:T(8,128)}) custom-call(s32[3,32]{1,0:T(4,128)} %bitcast.31, f32[32,3,128,128]{3,2,1,0:T(8,128)} %cost_ref.3, f32[32,1,2,128,128]{4,3,2,1,0:T(8,128)} %plan_ref.3, s32[32,128]{1,0:T(8,128)} %bitcast.27), custom_call_target="tpu_custom_call" | custom-call | flops 1207959552 | bytes 5242880 | tf_op jit(solution)/shard_map/near_product/pallas_call | solution.py:350
  7.7 1.5 %pack.1 = f32[256,128]{1,0:T(8,128)} custom-call(f32[8,128,4]{2,1,0:T(8,128)} %get-tuple-element.19.refs_1_.after_ref, s32[32,128]{1,0:T(8,128)} %bitcast.28, s32[1,128]{1,0:T(1,128)} %target_ref.1), custom_call_target="tpu_custom_call" | custom-call | tf_op jit(solution)/shard_map/pack/pallas_call | solution.py:380
  9.2 7.3 %all-to-all-start = ((f32[32,8,128]{2,1,0:T(8,128)}), f32[32,8,128]{2,1,0:T(8,128)S(1)}, u32[]{:S(2)}, u32[]{:S(2)}) async-start(f32[32,8,128]{2,1,0:T(8,128)} %bitcast.26), calls=%async_computation | async-start | bytes 262144 | tf_op jit(solution)/shard_map/all_to_all | solution.py:71
  16.5 2.7 %collective-permute-start.3 = (f32[1,1,3,128,128]{4,3,2,1,0:T(8,128)S(1)}, f32[1,1,3,128,128]{4,3,2,1,0:T(8,128)S(1)}, u32[]{:S(2)}, u32[]{:S(2)}) collective-permute-start(f32[1,1,3,128,128]{4,3,2,1,0:T(8,128)S(1)} %copy-done.6), channel_id=1, source_target_pairs={{0,16},{4,20},{8,24},{12,28},{16,0},{20,4},{24,8},{28,12},{1,17},{... | collective-permute-start | bytes 589832 | tf_op jit(solution)/shard_map/ppermute | solution.py:63
  19.2 1.5 %collective-permute-start.4 = (f32[1,1,3,128,128]{4,3,2,1,0:T(8,128)S(1)}, f32[1,1,3,128,128]{4,3,2,1,0:T(8,128)S(1)}, u32[]{:S(2)}, u32[]{:S(2)}) collective-permute-start(f32[1,1,3,128,128]{4,3,2,1,0:T(8,128)S(1)} %copy-done.6), channel_id=1, source_target_pairs={{0,24},{4,28},{8,16},{12,20},{16,8},{20,12},{24,0},{28,4},{1,25},{... | collective-permute-start | bytes 589832 | tf_op jit(solution)/shard_map/ppermute | solution.py:63
  20.7 1.5 %collective-permute-start = (f32[1,1,3,128,128]{4,3,2,1,0:T(8,128)S(1)}, f32[1,1,3,128,128]{4,3,2,1,0:T(8,128)S(1)}, u32[]{:S(2)}, u32[]{:S(2)}) collective-permute-start(f32[1,1,3,128,128]{4,3,2,1,0:T(8,128)S(1)} %copy-done.6), channel_id=1, source_target_pairs={{0,4},{4,0},{8,12},{12,8},{16,20},{20,16},{24,28},{28,24},{1,5},{5... | collective-permute-start | bytes 589832 | tf_op jit(solution)/shard_map/ppermute | solution.py:63
  22.2 1.9 %collective-permute-start.2 = (f32[1,1,3,128,128]{4,3,2,1,0:T(8,128)S(1)}, f32[1,1,3,128,128]{4,3,2,1,0:T(8,128)S(1)}, u32[]{:S(2)}, u32[]{:S(2)}) collective-permute-start(f32[1,1,3,128,128]{4,3,2,1,0:T(8,128)S(1)} %copy-done.6), channel_id=1, source_target_pairs={{0,12},{4,8},{8,4},{12,0},{16,28},{20,24},{24,20},{28,16},{1,13},{... | collective-permute-start | bytes 589832 | tf_op jit(solution)/shard_map/ppermute | solution.py:63
  24.2 12.0 %collective-permute-done.3.refs_1_ = f32[1,1,3,128,128]{4,3,2,1,0:T(8,128)S(1)} collective-permute-done((f32[1,1,3,128,128]{4,3,2,1,0:T(8,128)S(1)}, f32[1,1,3,128,128]{4,3,2,1,0:T(8,128)S(1)}, u32[]{:S(2)}, u32[]{:S(2)}) %collective-permute-start.3) | collective-permute-done | bytes 196640 | tf_op jit(solution)/shard_map/ppermute | solution.py:63
  36.2 0.7 copy-done.2
  37.0 1.5 %collective-permute-start.5 = (f32[1,1,3,128,128]{4,3,2,1,0:T(8,128)}, f32[1,1,3,128,128]{4,3,2,1,0:T(8,128)S(1)}, u32[]{:S(2)}, u32[]{:S(2)}) collective-permute-start(f32[1,1,3,128,128]{4,3,2,1,0:T(8,128)} %get-tuple-element.22.refs_10_), channel_id=1, source_target_pairs={{0,4},{4,0},{8,12},{12,8},{16,20},{20,16},{24,28},{28,24},{1,5},{5... | collective-permute-start | bytes 589832 | tf_op jit(solution)/shard_map/ppermute | solution.py:63
  38.5 0.6 collective-permute-start.6
  39.0 7.0 %near_product.3 = (bf16[32,256,768]{2,1,0:T(8,128)(2,1)}, f32[8,128,4]{2,1,0:T(8,128)}) custom-call(s32[3,32]{1,0:T(4,128)} %bitcast.32, f32[32,3,128,128]{3,2,1,0:T(8,128)} %cost_ref.3, f32[32,1,2,128,128]{4,3,2,1,0:T(8,128)} %plan_ref.3, s32[32,128]{1,0:T(8,128)} %bitcast.29, ...), custom_call_target="tpu_custom_call", output_to_operand_aliasing={{0}: (4, {}), {1}: (5, {})} | custom-call | flops 1207959552 | bytes 5242880 | tf_op jit(solution)/shard_map/near_product/pallas_call | solution.py:350
  46.1 3.1 %collective-permute-done.6.refs_13_ = f32[1,1,3,128,128]{4,3,2,1,0:T(8,128)S(1)} collective-permute-done((f32[1,1,3,128,128]{4,3,2,1,0:T(8,128)}, f32[1,1,3,128,128]{4,3,2,1,0:T(8,128)S(1)}, u32[]{:S(2)}, u32[]{:S(2)}) %collective-permute-start.6) | collective-permute-done | bytes 196640 | tf_op jit(solution)/shard_map/ppermute | solution.py:63
  49.2 14.3 %far_product.1 = (f32[32,1,2,128,128]{4,3,2,1,0:T(8,128)}, f32[32,2,128,128]{3,2,1,0:T(8,128)}, f32[32,128]{1,0:T(8,128)S(1)}, f32[32,128]{1,0:T(8,128)S(1)}, f32[8,128]{1,0:T(8,128)S(1)}) custom-call(s32[3,32]{1,0:T(4,128)} %bitcast.33, s32[2,32]{1,0:T(2,128)} %bitcast.35, s32[3,1,8]{2,1,0:T(1,128)} %bitcast.38, ...), custom_call_target="tpu_custom_call" | custom-call | tf_op jit(solution)/shard_map/far_product/pallas_call | solution.py:409
  63.6 1.6 %collective-permute-start.8 = (f32[32,128]{1,0:T(8,128)S(1)}, f32[32,128]{1,0:T(8,128)S(1)}, u32[]{:S(2)}, u32[]{:S(2)}) collective-permute-start(f32[32,128]{1,0:T(8,128)S(1)} %get-tuple-element.28.refs_0_), channel_id=1, source_target_pairs={{0,2},{1,3},{2,0},{3,1},{4,6},{5,7},{6,4},{7,5},{8,10},{9,11},{10,... | collective-permute-start | bytes 49160 | tf_op jit(solution)/shard_map/ppermute | solution.py:63
  65.6 1.7 %collective-permute-done.8.refs_2_ = f32[32,128]{1,0:T(8,128)S(1)} collective-permute-done((f32[32,128]{1,0:T(8,128)S(1)}, f32[32,128]{1,0:T(8,128)S(1)}, u32[]{:S(2)}, u32[]{:S(2)}) %collective-permute-start.8) | collective-permute-done | bytes 16416 | tf_op jit(solution)/shard_map/ppermute | solution.py:63
  67.4 1.0 collective-permute-done.9.refs_3_
  68.4 4.7 %column_pass.3 = (f32[64,128]{1,0:T(8,128)S(1)}, f32[32,128]{1,0:T(8,128)}) custom-call(f32[32,1,2,128,128]{4,3,2,1,0:T(8,128)} %get-tuple-element.15.cost_ref, s32[64,128]{1,0:T(8,128)S(1)} %broadcast_in_dim.8.select_ref, f32[32,128]{1,0:T(8,128)S(1)} %get-tuple-element.25.log_mass_ref, f32[32,128]{1,0:T(8,128)S(1)} %get-tuple-element.28.refs_0_, ...), custom_call_target="tpu_custom_call" | custom-call | tf_op jit(solution)/shard_map/column_pass/pallas_call | solution.py:459
  73.1 11.9 %all_to_all.44 = f32[8,8,128]{2,1,0:T(8,128)S(1)} all-to-all(f32[8,8,128]{2,1,0:T(8,128)S(1)} %bitcast.23), channel_id=1, replica_groups=mesh['rows'=8,'cols'=4] {'rows'}, dimensions={0} | all-to-all | bytes 65536 | tf_op jit(solution)/shard_map/all_to_all | solution.py:71
  84.9 3.7 %row_pass.2.refs_0_ = f32[32,128]{1,0:T(8,128)S(1)} custom-call(s32[2,32]{1,0:T(2,128)} %bitcast.36, f32[32,2,128,128]{3,2,1,0:T(8,128)} %get-tuple-element.26.tall_ref, f32[8,128]{1,0:T(8,128)S(1)} %get-tuple-element.27.log_mass_ref, f32[64,128]{1,0:T(8,128)S(1)} %bitcast.21), custom_call_target="tpu_custom_call" | custom-call | tf_op jit(solution)/shard_map/row_pass/pallas_call | solution.py:482
  88.7 0.8 collective-permute-start.11
  89.5 1.1 collective-permute-start.12
  90.6 1.9 %collective-permute-done.11.refs_2_ = f32[32,128]{1,0:T(8,128)S(1)} collective-permute-done((f32[32,128]{1,0:T(8,128)S(1)}, f32[32,128]{1,0:T(8,128)S(1)}, u32[]{:S(2)}, u32[]{:S(2)}) %collective-permute-start.11) | collective-permute-done | bytes 16416 | tf_op jit(solution)/shard_map/ppermute | solution.py:63
  92.7 4.7 %column_pass.4 = (f32[64,128]{1,0:T(8,128)S(1)}, f32[32,128]{1,0:T(8,128)}) custom-call(f32[32,1,2,128,128]{4,3,2,1,0:T(8,128)} %get-tuple-element.15.cost_ref, s32[64,128]{1,0:T(8,128)S(1)} %broadcast_in_dim.8.select_ref, f32[32,128]{1,0:T(8,128)S(1)} %get-tuple-element.25.log_mass_ref, f32[32,128]{1,0:T(8,128)S(1)} %row_pass.2.refs_0_, ...), custom_call_target="tpu_custom_call" | custom-call | tf_op jit(solution)/shard_map/column_pass/pallas_call | solution.py:459
  97.4 9.0 %all_to_all.45 = f32[8,8,128]{2,1,0:T(8,128)S(1)} all-to-all(f32[8,8,128]{2,1,0:T(8,128)S(1)} %bitcast.24), channel_id=1, replica_groups=mesh['rows'=8,'cols'=4] {'rows'}, dimensions={0} | all-to-all | bytes 65536 | tf_op jit(solution)/shard_map/all_to_all | solution.py:71
  106.4 3.7 %row_pass.3.refs_0_ = f32[32,128]{1,0:T(8,128)S(1)} custom-call(s32[2,32]{1,0:T(2,128)} %bitcast.37, f32[32,2,128,128]{3,2,1,0:T(8,128)} %get-tuple-element.26.tall_ref, f32[8,128]{1,0:T(8,128)S(1)} %get-tuple-element.27.log_mass_ref, f32[64,128]{1,0:T(8,128)S(1)} %bitcast.22), custom_call_target="tpu_custom_call" | custom-call | tf_op jit(solution)/shard_map/row_pass/pallas_call | solution.py:482
  110.3 1.3 %collective-permute-start.14 = (f32[32,128]{1,0:T(8,128)S(1)}, f32[32,128]{1,0:T(8,128)S(1)}, u32[]{:S(2)}, u32[]{:S(2)}) collective-permute-start(f32[32,128]{1,0:T(8,128)S(1)} %row_pass.3.refs_0_), channel_id=1, source_target_pairs={{0,2},{1,3},{2,0},{3,1},{4,6},{5,7},{6,4},{7,5},{8,10},{9,11},{10,... | collective-permute-start | bytes 49160 | tf_op jit(solution)/shard_map/ppermute | solution.py:63
  112.1 1.9 %collective-permute-done.14.refs_2_ = f32[32,128]{1,0:T(8,128)S(1)} collective-permute-done((f32[32,128]{1,0:T(8,128)S(1)}, f32[32,128]{1,0:T(8,128)S(1)}, u32[]{:S(2)}, u32[]{:S(2)}) %collective-permute-start.14) | collective-permute-done | bytes 16416 | tf_op jit(solution)/shard_map/ppermute | solution.py:63
  114.1 0.7 collective-permute-done.15.refs_3_
  114.8 4.7 %column_pass.5 = (f32[8,128]{1,0:T(8,128)S(1)}, f32[32,128]{1,0:T(8,128)}) custom-call(f32[32,1,2,128,128]{4,3,2,1,0:T(8,128)} %get-tuple-element.15.cost_ref, s32[64,128]{1,0:T(8,128)S(1)} %broadcast_in_dim.8.select_ref, f32[32,128]{1,0:T(8,128)S(1)} %get-tuple-element.25.log_mass_ref, f32[32,128]{1,0:T(8,128)S(1)} %row_pass.3.refs_0_, ...), custom_call_target="tpu_custom_call" | custom-call | tf_op jit(solution)/shard_map/column_pass/pallas_call | solution.py:459
  119.5 9.5 %all_to_all.46 = f32[8,1,128]{2,1,0:T(1,128)} all-to-all(f32[8,1,128]{2,1,0:T(1,128)S(1)} %bitcast.25), channel_id=1, replica_groups=mesh['rows'=8,'cols'=4] {'rows'}, dimensions={0} | all-to-all | bytes 8192 | tf_op jit(solution)/shard_map/all_to_all | solution.py:71
  128.9 1.2 last_potential.1
  (37 shorter events, 1.6 us)
Async XLA Ops:
  0.6 15.9 %copy-start.6 = (f32[1,1,3,128,128]{4,3,2,1,0:T(8,128)S(1)}, f32[1,1,3,128,128]{4,3,2,1,0:T(8,128)}, u32[]{:S(2)}) copy-start(f32[1,1,3,128,128]{4,3,2,1,0:T(8,128)} %refs_6_.1) | copy-start | bytes 589828
  9.2 27.0 %all-to-all-start = ((f32[32,8,128]{2,1,0:T(8,128)}), f32[32,8,128]{2,1,0:T(8,128)S(1)}, u32[]{:S(2)}, u32[]{:S(2)}) async-start(f32[32,8,128]{2,1,0:T(8,128)} %bitcast.26), calls=%async_computation | async-start | bytes 262144 | tf_op jit(solution)/shard_map/all_to_all | solution.py:71
  16.5 19.7 %collective-permute-start.3 = (f32[1,1,3,128,128]{4,3,2,1,0:T(8,128)S(1)}, f32[1,1,3,128,128]{4,3,2,1,0:T(8,128)S(1)}, u32[]{:S(2)}, u32[]{:S(2)}) collective-permute-start(f32[1,1,3,128,128]{4,3,2,1,0:T(8,128)S(1)} %copy-done.6), channel_id=1, source_target_pairs={{0,16},{4,20},{8,24},{12,28},{16,0},{20,4},{24,8},{28,12},{1,17},{... | collective-permute-start | bytes 589832 | tf_op jit(solution)/shard_map/ppermute | solution.py:63
  19.2 17.0 %collective-permute-start.4 = (f32[1,1,3,128,128]{4,3,2,1,0:T(8,128)S(1)}, f32[1,1,3,128,128]{4,3,2,1,0:T(8,128)S(1)}, u32[]{:S(2)}, u32[]{:S(2)}) collective-permute-start(f32[1,1,3,128,128]{4,3,2,1,0:T(8,128)S(1)} %copy-done.6), channel_id=1, source_target_pairs={{0,24},{4,28},{8,16},{12,20},{16,8},{20,12},{24,0},{28,4},{1,25},{... | collective-permute-start | bytes 589832 | tf_op jit(solution)/shard_map/ppermute | solution.py:63
  20.7 25.4 %collective-permute-start = (f32[1,1,3,128,128]{4,3,2,1,0:T(8,128)S(1)}, f32[1,1,3,128,128]{4,3,2,1,0:T(8,128)S(1)}, u32[]{:S(2)}, u32[]{:S(2)}) collective-permute-start(f32[1,1,3,128,128]{4,3,2,1,0:T(8,128)S(1)} %copy-done.6), channel_id=1, source_target_pairs={{0,4},{4,0},{8,12},{12,8},{16,20},{20,16},{24,28},{28,24},{1,5},{5... | collective-permute-start | bytes 589832 | tf_op jit(solution)/shard_map/ppermute | solution.py:63
  22.2 23.9 %collective-permute-start.1 = (f32[1,1,3,128,128]{4,3,2,1,0:T(8,128)S(1)}, f32[1,1,3,128,128]{4,3,2,1,0:T(8,128)S(1)}, u32[]{:S(2)}, u32[]{:S(2)}) collective-permute-start(f32[1,1,3,128,128]{4,3,2,1,0:T(8,128)S(1)} %copy-done.6), channel_id=1, source_target_pairs={{0,8},{4,12},{8,0},{12,4},{16,24},{20,28},{24,16},{28,20},{1,9},{5... | collective-permute-start | bytes 589832 | tf_op jit(solution)/shard_map/ppermute | solution.py:63
  22.2 23.8 %collective-permute-start.2 = (f32[1,1,3,128,128]{4,3,2,1,0:T(8,128)S(1)}, f32[1,1,3,128,128]{4,3,2,1,0:T(8,128)S(1)}, u32[]{:S(2)}, u32[]{:S(2)}) collective-permute-start(f32[1,1,3,128,128]{4,3,2,1,0:T(8,128)S(1)} %copy-done.6), channel_id=1, source_target_pairs={{0,12},{4,8},{8,4},{12,0},{16,28},{20,24},{24,20},{28,16},{1,13},{... | collective-permute-start | bytes 589832 | tf_op jit(solution)/shard_map/ppermute | solution.py:63
  36.2 0.7 copy-start.2
  36.2 0.7 copy-start.4
  36.2 0.8 copy-start
  37.0 9.1 %collective-permute-start.5 = (f32[1,1,3,128,128]{4,3,2,1,0:T(8,128)}, f32[1,1,3,128,128]{4,3,2,1,0:T(8,128)S(1)}, u32[]{:S(2)}, u32[]{:S(2)}) collective-permute-start(f32[1,1,3,128,128]{4,3,2,1,0:T(8,128)} %get-tuple-element.22.refs_10_), channel_id=1, source_target_pairs={{0,4},{4,0},{8,12},{12,8},{16,20},{20,16},{24,28},{28,24},{1,5},{5... | collective-permute-start | bytes 589832 | tf_op jit(solution)/shard_map/ppermute | solution.py:63
  38.5 10.7 %collective-permute-start.6 = (f32[1,1,3,128,128]{4,3,2,1,0:T(8,128)}, f32[1,1,3,128,128]{4,3,2,1,0:T(8,128)S(1)}, u32[]{:S(2)}, u32[]{:S(2)}) collective-permute-start(f32[1,1,3,128,128]{4,3,2,1,0:T(8,128)} %get-tuple-element.23.refs_12_), channel_id=1, source_target_pairs={{0,4},{4,0},{8,12},{12,8},{16,20},{20,16},{24,28},{28,24},{1,5},{5... | collective-permute-start | bytes 589832 | tf_op jit(solution)/shard_map/ppermute | solution.py:63
  39.0 10.1 %copy-start.1 = (f32[32,8,128]{2,1,0:T(8,128)S(1)}, f32[32,8,128]{2,1,0:T(8,128)}, u32[]{:S(2)}) copy-start(f32[32,8,128]{2,1,0:T(8,128)} %copy-done) | copy-start | bytes 393220
  39.0 10.1 %copy-start.3 = (f32[1,1,3,128,128]{4,3,2,1,0:T(8,128)S(1)}, f32[1,1,3,128,128]{4,3,2,1,0:T(8,128)}, u32[]{:S(2)}) copy-start(f32[1,1,3,128,128]{4,3,2,1,0:T(8,128)} %get-tuple-element.22.refs_10_) | copy-start | bytes 589828
  39.0 10.1 %copy-start.5 = (f32[1,1,3,128,128]{4,3,2,1,0:T(8,128)S(1)}, f32[1,1,3,128,128]{4,3,2,1,0:T(8,128)}, u32[]{:S(2)}) copy-start(f32[1,1,3,128,128]{4,3,2,1,0:T(8,128)} %get-tuple-element.23.refs_12_) | copy-start | bytes 589828
  49.2 16.2 %copy-start.8 = (s32[32,1,2]{0,2,1:T(2,128)S(1)}, s32[32,1,2]{0,2,1:T(2,128)}, u32[]{:S(2)}) copy-start(s32[32,1,2]{0,2,1:T(2,128)} %param.9) | copy-start | bytes 772
  63.5 42.9 %copy-start.7 = (f32[8,128]{1,0:T(8,128)}, f32[8,128]{1,0:T(8,128)S(1)}, u32[]{:S(2)}) copy-start(f32[8,128]{1,0:T(8,128)S(1)} %get-tuple-element.27.log_mass_ref) | copy-start | bytes 12292
  63.5 2.1 %collective-permute-start.7 = (f32[32,128]{1,0:T(8,128)S(1)}, f32[32,128]{1,0:T(8,128)S(1)}, u32[]{:S(2)}, u32[]{:S(2)}) collective-permute-start(f32[32,128]{1,0:T(8,128)S(1)} %get-tuple-element.28.refs_0_), channel_id=1, source_target_pairs={{0,1},{1,0},{2,3},{3,2},{4,5},{5,4},{6,7},{7,6},{8,9},{9,8},{10,11... | collective-permute-start | bytes 49160 | tf_op jit(solution)/shard_map/ppermute | solution.py:63
  63.6 3.8 %collective-permute-start.8 = (f32[32,128]{1,0:T(8,128)S(1)}, f32[32,128]{1,0:T(8,128)S(1)}, u32[]{:S(2)}, u32[]{:S(2)}) collective-permute-start(f32[32,128]{1,0:T(8,128)S(1)} %get-tuple-element.28.refs_0_), channel_id=1, source_target_pairs={{0,2},{1,3},{2,0},{3,1},{4,6},{5,7},{6,4},{7,5},{8,10},{9,11},{10,... | collective-permute-start | bytes 49160 | tf_op jit(solution)/shard_map/ppermute | solution.py:63
  65.1 3.2 %collective-permute-start.9 = (f32[32,128]{1,0:T(8,128)S(1)}, f32[32,128]{1,0:T(8,128)S(1)}, u32[]{:S(2)}, u32[]{:S(2)}) collective-permute-start(f32[32,128]{1,0:T(8,128)S(1)} %get-tuple-element.28.refs_0_), channel_id=1, source_target_pairs={{0,3},{1,2},{2,1},{3,0},{4,7},{5,6},{6,5},{7,4},{8,11},{9,10},{10,... | collective-permute-start | bytes 49160 | tf_op jit(solution)/shard_map/ppermute | solution.py:63
  88.7 1.9 %collective-permute-start.10 = (f32[32,128]{1,0:T(8,128)S(1)}, f32[32,128]{1,0:T(8,128)S(1)}, u32[]{:S(2)}, u32[]{:S(2)}) collective-permute-start(f32[32,128]{1,0:T(8,128)S(1)} %row_pass.2.refs_0_), channel_id=1, source_target_pairs={{0,1},{1,0},{2,3},{3,2},{4,5},{5,4},{6,7},{7,6},{8,9},{9,8},{10,11... | collective-permute-start | bytes 49160 | tf_op jit(solution)/shard_map/ppermute | solution.py:63
  88.7 3.8 %collective-permute-start.11 = (f32[32,128]{1,0:T(8,128)S(1)}, f32[32,128]{1,0:T(8,128)S(1)}, u32[]{:S(2)}, u32[]{:S(2)}) collective-permute-start(f32[32,128]{1,0:T(8,128)S(1)} %row_pass.2.refs_0_), channel_id=1, source_target_pairs={{0,2},{1,3},{2,0},{3,1},{4,6},{5,7},{6,4},{7,5},{8,10},{9,11},{10,... | collective-permute-start | bytes 49160 | tf_op jit(solution)/shard_map/ppermute | solution.py:63
  89.5 3.2 %collective-permute-start.12 = (f32[32,128]{1,0:T(8,128)S(1)}, f32[32,128]{1,0:T(8,128)S(1)}, u32[]{:S(2)}, u32[]{:S(2)}) collective-permute-start(f32[32,128]{1,0:T(8,128)S(1)} %row_pass.2.refs_0_), channel_id=1, source_target_pairs={{0,3},{1,2},{2,1},{3,0},{4,7},{5,6},{6,5},{7,4},{8,11},{9,10},{10,... | collective-permute-start | bytes 49160 | tf_op jit(solution)/shard_map/ppermute | solution.py:63
  110.2 1.9 %collective-permute-start.13 = (f32[32,128]{1,0:T(8,128)S(1)}, f32[32,128]{1,0:T(8,128)S(1)}, u32[]{:S(2)}, u32[]{:S(2)}) collective-permute-start(f32[32,128]{1,0:T(8,128)S(1)} %row_pass.3.refs_0_), channel_id=1, source_target_pairs={{0,1},{1,0},{2,3},{3,2},{4,5},{5,4},{6,7},{7,6},{8,9},{9,8},{10,11... | collective-permute-start | bytes 49160 | tf_op jit(solution)/shard_map/ppermute | solution.py:63
  110.3 3.8 %collective-permute-start.14 = (f32[32,128]{1,0:T(8,128)S(1)}, f32[32,128]{1,0:T(8,128)S(1)}, u32[]{:S(2)}, u32[]{:S(2)}) collective-permute-start(f32[32,128]{1,0:T(8,128)S(1)} %row_pass.3.refs_0_), channel_id=1, source_target_pairs={{0,2},{1,3},{2,0},{3,1},{4,6},{5,7},{6,4},{7,5},{8,10},{9,11},{10,... | collective-permute-start | bytes 49160 | tf_op jit(solution)/shard_map/ppermute | solution.py:63
  111.6 3.2 %collective-permute-start.15 = (f32[32,128]{1,0:T(8,128)S(1)}, f32[32,128]{1,0:T(8,128)S(1)}, u32[]{:S(2)}, u32[]{:S(2)}) collective-permute-start(f32[32,128]{1,0:T(8,128)S(1)} %row_pass.3.refs_0_), channel_id=1, source_target_pairs={{0,3},{1,2},{2,1},{3,0},{4,7},{5,6},{6,5},{7,4},{8,11},{9,10},{10,... | collective-permute-start | bytes 49160 | tf_op jit(solution)/shard_map/ppermute | solution.py:63

commit v5 on v3

--- a/solution.py
+++ b/solution.py
@@ -22,6 +22,10 @@
 ANY = pl.BlockSpec(memory_space=pl.ANY)
 
 
+def in_hbm(x):
+    return pltpu.with_memory_space_constraint(x, pltpu.HBM)
+
+
 def in_vmem(x):
     return pltpu.with_memory_space_constraint(x, pltpu.VMEM)
 
@@ -71,7 +75,7 @@
     return lax.all_to_all(copies, axis, 0, 0, tiled=True)
 
 
-def pack_kernel(devices, source_ref, target_ref, out_ref):
+def pack_kernel(devices, after_ref, source_ref, target_ref, out_ref):
     rows = out_ref.shape[0] // devices
     total = jnp.sum(source_ref[...].astype(jnp.float32), axis=(0, 1), keepdims=True)
     target = target_ref[...].astype(jnp.float32)
@@ -81,9 +85,8 @@
         out_ref[d * rows + 1 : d * rows + 1 + target.shape[0], :] = target
 
 
-def near_kernel(first, near_index_ref, cost_ref, plan_ref, mass_ref, *refs):
-    x_ref, term_ref, plan_scr = refs[-3:]
-    g = first + pl.program_id(0)
+def near_kernel(near_index_ref, cost_ref, plan_ref, mass_ref, x_ref, term_ref, plan_scr):
+    g = pl.program_id(0)
     near_count = cost_ref.shape[1]
     width = cost_ref.shape[2]
     slots = plan_ref.shape[2]
@@ -125,10 +128,10 @@
     row_devices, col_devices, target_here, source_count, target_count, group_blocks, link_count = counts
     near_index_ref, slot_ref, link_ref, x_ref, term_ref, mass_ref = refs[:6]
     cost_parts = refs[6 : 6 + row_devices]
-    pack_ref, out_ref, work_ref, tall_ref, part_ref, log_source_ref, log_target_ref = refs[
-        6 + row_devices : 13 + row_devices
+    pack_ref, out_ref, work_ref, tall_ref, part_ref, log_source_ref, log_target_ref, select_ref = refs[
+        6 + row_devices : 14 + row_devices
     ]
-    far_high, far_low, table, column_scr, scale_scr, peak_scr, sum_scr = refs[13 + row_devices :]
+    far_high, far_low, table, column_scr, scale_scr, peak_scr, sum_scr = refs[14 + row_devices :]
     g = pl.program_id(0)
     near_count = near_index_ref.shape[0]
     slots = slot_ref.shape[0]
@@ -215,6 +218,7 @@
         for l in range(slots):
             cost = tall + column_scr[pl.ds(targets[l], 1), :] - coef * product[:, l * width : (l + 1) * width]
             out_ref[i, 0, l] = cost
+            select_ref[pl.ds(row * slots + l, 1), :] = jnp.full((1, width), targets[l], jnp.int32)
             scaled = cost * -to_log2
             work_ref[row, l] = scaled
             turned = scaled.T
@@ -329,77 +333,71 @@
         if mask not in late:
             arrived[mask] = send(target_cost, "rows", mask)
 
-    near_t = near_index.T
-    slot_t = coupling_index[:, 0, :].T
-    link_t = jnp.transpose(target_index, (2, 0, 1))
-    mass = source_weights.reshape(rows_here, width)
-    select = jnp.broadcast_to(
-        coupling_index.reshape(rows_here * slots, 1), (rows_here * slots, width)
-    )
+    near_t = in_hbm(near_index.T)
+    slot_t = in_hbm(coupling_index[:, 0, :].T)
+    link_t = in_hbm(jnp.transpose(target_index, (2, 0, 1)))
+    mass = in_hbm(source_weights.reshape(rows_here, width))
+    small = pltpu.CompilerParams(vmem_limit_bytes=4 * mib)
+
+    wide = near_count * slots * width
+    groups = rows_here // SUB
+    x, term = pl.pallas_call(
+        near_kernel,
+        grid=(groups,),
+        in_specs=[
+            SMEM,
+            pl.BlockSpec((SUB, near_count, width, width), lambda g: (g, 0, 0, 0)),
+            pl.BlockSpec((SUB, 1, slots, width, width), lambda g: (g, 0, 0, 0, 0)),
+            whole((rows_here, width)),
+        ],
+        out_specs=[VMEM, VMEM],
+        out_shape=[
+            pltpu.VMEM((rows_here, 2 * width, wide), jnp.bfloat16),
+            pltpu.VMEM((groups, width, SUB), f32),
+        ],
+        scratch_shapes=[pltpu.VMEM((SUB, 3 * width, slots * width), jnp.bfloat16)],
+        compiler_params=pltpu.CompilerParams(vmem_limit_bytes=12 * mib),
+        cost_estimate=pl.CostEstimate(
+            flops=6 * rows_here * wide * width * width,
+            bytes_accessed=4 * rows_here * width * (near_count + slots) * width,
+            transcendentals=0,
+        ),
+        name="near_product",
+    )(near_t, in_hbm(near_cost), in_hbm(coupling), mass)
+
+    sources = [mask - 1 for mask in late] or [0]
+    passed = pl.pallas_call(
+        relay_kernel,
+        in_specs=[ANY] * (1 + len(sources)),
+        out_specs=[ANY] * len(sources),
+        out_shape=[jax.ShapeDtypeStruct(target_cost.shape, f32)] * len(sources),
+        input_output_aliases={1 + e: e for e in range(len(sources))},
+        compiler_params=small,
+        name="relay",
+    )(in_vmem(term), *[arrived[mask] for mask in sources])
+    for mask, block in zip(sources, passed):
+        arrived[mask] = block
+    for mask in late:
+        arrived[mask] = send(arrived[mask - 1], "rows", 1)
+    cost_parts = [arrived[s] for s in range(row_devices)]
 
     pack_rows = 8 * pl.cdiv(1 + target_here, 8)
     devices = row_devices * col_devices
     pack = pl.pallas_call(
         functools.partial(pack_kernel, devices),
+        in_specs=[ANY, VMEM, VMEM],
         out_shape=jax.ShapeDtypeStruct((devices * pack_rows, width), f32),
+        compiler_params=small,
         name="pack",
-    )(mass, target_weights.reshape(target_here, width))
+    )(passed[0], mass, in_hbm(target_weights.reshape(target_here, width)))
     packs = exchange(pack, ("rows", "cols"))
-
-    wide = near_count * slots * width
-    groups = rows_here // SUB
-    x_shape = pltpu.VMEM((rows_here, 2 * width, wide), jnp.bfloat16)
-    term_shape = pltpu.VMEM((groups, width, SUB), f32)
-    near_cost = pltpu.with_memory_space_constraint(near_cost, pltpu.HBM)
-    coupling = pltpu.with_memory_space_constraint(coupling, pltpu.HBM)
-
-    def near_product(first, count, *held):
-        return pl.pallas_call(
-            functools.partial(near_kernel, first),
-            grid=(count,),
-            in_specs=[
-                SMEM,
-                pl.BlockSpec((SUB, near_count, width, width), lambda g: (first + g, 0, 0, 0)),
-                pl.BlockSpec((SUB, 1, slots, width, width), lambda g: (first + g, 0, 0, 0, 0)),
-                whole((rows_here, width)),
-            ]
-            + [VMEM] * len(held),
-            out_specs=[VMEM, VMEM],
-            out_shape=[x_shape, term_shape],
-            input_output_aliases={4: 0, 5: 1} if held else {},
-            scratch_shapes=[pltpu.VMEM((SUB, 3 * width, slots * width), jnp.bfloat16)],
-            compiler_params=pltpu.CompilerParams(vmem_limit_bytes=12 * mib),
-            cost_estimate=pl.CostEstimate(
-                flops=6 * count * SUB * wide * width * width,
-                bytes_accessed=4 * count * SUB * width * (near_count + slots) * width,
-                transcendentals=0,
-            ),
-            name="near_product",
-        )(near_t, near_cost, coupling, mass, *map(in_vmem, held))
-
-    held = near_product(0, (groups + 1) // 2)
-    if late:
-        sources = [mask - 1 for mask in late]
-        passed = pl.pallas_call(
-            relay_kernel,
-            in_specs=[ANY] * (2 + len(sources)),
-            out_specs=[ANY] * len(sources),
-            out_shape=[jax.ShapeDtypeStruct(target_cost.shape, f32)] * len(sources),
-            input_output_aliases={2 + e: e for e in range(len(sources))},
-            name="relay",
-        )(held[1], packs, *[arrived[mask] for mask in sources])
-        for mask, block in zip(sources, passed):
-            arrived[mask] = block
-            arrived[mask + 1] = send(block, "rows", 1)
-    cost_parts = [arrived[s] for s in range(row_devices)]
-    x, term = near_product((groups + 1) // 2, groups // 2, *held)
 
     far_bytes = group_blocks * link_count * width * width * 4
     step_rows = SUB
     steps = rows_here // step_rows
     cost_block = pl.BlockSpec((step_rows, 1, slots, width, width), lambda g: (g, 0, 0, 0, 0))
     work_shape = pltpu.VMEM((rows_here, slots, width, width), f32)
-    cost_blocks, work, tall, row_part, log_source, log_target = pl.pallas_call(
+    cost_blocks, work, tall, row_part, log_source, log_target, select = pl.pallas_call(
         functools.partial(
             far_kernel,
             (row_devices, col_devices, target_here, source_count, target_count, group_blocks, link_count),
@@ -417,6 +415,7 @@
             whole((rows_here, width)),
             whole((rows_here, width)),
             whole((group_blocks, width)),
+            whole((rows_here * slots, width)),
         ],
         out_shape=[
             jax.ShapeDtypeStruct(coupling.shape, f32),
@@ -425,6 +424,7 @@
             jax.ShapeDtypeStruct((rows_here, width), f32),
             jax.ShapeDtypeStruct((rows_here, width), f32),
             jax.ShapeDtypeStruct((group_blocks, width), f32),
+            jax.ShapeDtypeStruct((rows_here * slots, width), jnp.int32),
         ],
         scratch_shapes=[
             pltpu.VMEM((group_blocks * link_count + 1, width, width), jnp.bfloat16),
@@ -485,6 +485,7 @@
     own_target = pl.pallas_call(
         functools.partial(last_kernel, row_devices, "rows"),
         out_shape=jax.ShapeDtypeStruct((target_here, width), f32),
+        compiler_params=small,
         name="last_potential",
     )(log_target, column_parts)
     return (

time: 129 us -> 119 us (0.922)
  local copies, waits for them, and re-layouts: 32.8 us -> 9.08 us
  waiting for transfers between devices: 7.64 us -> 23.2 us
  blocking collectives: 31.4 us -> 29.2 us
  starting transfers between devices: 22.7 us -> 24.4 us
  Pallas kernels: 33.3 us -> 31.7 us
    unnamed x57 -> x6, local copies, waits for them, and re-layouts: 32.6 us -> 9.08 us
    ppermute x16, waiting for transfers between devices: 7.64 us -> 23.2 us  [send(): return lax.ppermute(x, axis, [(d, d ^ mask) for d in range(size)])]
    all_to_all x3, blocking collectives: 31.4 us -> 29.2 us  [exchange(): return lax.all_to_all(copies, axis, 0, 0, tiled=True)]
    pallas_call x4 -> x3, Pallas kernels: 11.6 us -> 10.6 us  [the longest x1 9.14 us: per_device(): pl.pallas_call(near_kernel, grid=(groups,), in_specs=[SMEM, pl.BlockSpec(...]
  transfers between devices with their start and end apart: 17 -> 17, of which waited for: 7 -> 11; matrix products, arithmetic and copies ran while one was open for 0% -> 0% of each run, Pallas kernels for 8% -> 8%
where the time goes in v5:
time: 119 us; the launch traced here: 118 us
  Pallas kernels  31.7 us (27%)
  blocking collectives  29.2 us (25%)
  starting transfers between devices  24.4 us (21%)
  waiting for transfers between devices  23.2 us (19%)
  local copies, waits for them, and re-layouts  9.08 us (8%)
    all_to_all x3, blocking collectives, exchange(): return lax.all_to_all(copies, axis, 0, 0, tiled=True)  29.2 us
    ppermute x16, waiting for transfers between devices, send(): return lax.ppermute(x, axis, [(d, d ^ mask) for d in range(size)])  23.2 us
    ppermute x16, starting transfers between devices, send(): return lax.ppermute(x, axis, [(d, d ^ mask) for d in range(size)])  16.7 us
    pallas_call x1, Pallas kernels, per_device(): pl.pallas_call(functools.partial(far_kernel, (row_devices, col_devices, t...  10.6 us
    pallas_call x1, Pallas kernels, per_device(): pl.pallas_call(near_kernel, grid=(groups,), in_specs=[SMEM, pl.BlockSpec(...  9.14 us
    unnamed x6, local copies, waits for them, and re-layouts  9.08 us
    all_to_all x1, starting transfers between devices, exchange(): return lax.all_to_all(copies, axis, 0, 0, tiled=True)  7.63 us
    pallas_call x3, Pallas kernels, column_step(): pl.pallas_call(functools.partial(column_kernel, col_devices, copies), in_...  5.71 us
  transfers between devices with their start and end apart: 17, of which 11 were waited for; matrix products, arithmetic and copies ran while one was open for 0% of the time, Pallas kernels for 8%

profile of v5, /device:TPU:0, one launch (start us, length us, event | category | flops | bytes accessed | tf_op | source)
XLA Modules:
  0.0 118.2 jit_solution(15756736785325974222)
XLA Ops:
  0.6 4.1 %collective-permute-start.3 = (f32[1,1,3,128,128]{4,3,2,1,0:T(8,128)}, f32[1,1,3,128,128]{4,3,2,1,0:T(8,128)S(1)}, u32[]{:S(2)}, u32[]{:S(2)}) collective-permute-start(f32[1,1,3,128,128]{4,3,2,1,0:T(8,128)} %refs_6_.1), channel_id=1, source_target_pairs={{0,16},{4,20},{8,24},{12,28},{16,0},{20,4},{24,8},{28,12},{1,17},{... | collective-permute-start | bytes 589832 | tf_op jit(solution)/shard_map/ppermute | solution.py:67
  4.7 1.3 %collective-permute-start.4 = (f32[1,1,3,128,128]{4,3,2,1,0:T(8,128)}, f32[1,1,3,128,128]{4,3,2,1,0:T(8,128)S(1)}, u32[]{:S(2)}, u32[]{:S(2)}) collective-permute-start(f32[1,1,3,128,128]{4,3,2,1,0:T(8,128)} %refs_6_.1), channel_id=1, source_target_pairs={{0,24},{4,28},{8,16},{12,20},{16,8},{20,12},{24,0},{28,4},{1,25},{... | collective-permute-start | bytes 589832 | tf_op jit(solution)/shard_map/ppermute | solution.py:67
  6.1 9.1 %near_product.1 = (bf16[32,256,768]{2,1,0:T(8,128)(2,1)S(1)}, f32[8,128,4]{2,1,0:T(8,128)S(1)}) custom-call(s32[3,32]{1,0:T(4,128)} %bitcast.30, f32[32,3,128,128]{3,2,1,0:T(8,128)} %cost_ref.1, f32[32,1,2,128,128]{4,3,2,1,0:T(8,128)} %plan_ref.1, s32[32,128]{1,0:T(8,128)} %bitcast.24), custom_call_target="tpu_custom_call" | custom-call | flops 2415919104 | bytes 10485760 | tf_op jit(solution)/shard_map/near_product/pallas_call | solution.py:344
  15.2 4.5 %copy-done = bf16[32,256,768]{2,1,0:T(8,128)(2,1)} copy-done((bf16[32,256,768]{2,1,0:T(8,128)(2,1)}, bf16[32,256,768]{2,1,0:T(8,128)(2,1)S(1)}, u32[]{:S(2)}) %copy-start) | copy-done | bytes 12582936
  19.7 1.5 %pack.1 = f32[256,128]{1,0:T(8,128)} custom-call(f32[1,1,3,128,128]{4,3,2,1,0:T(8,128)S(1)} %get-tuple-element.20.after_ref.refs_10_, s32[32,128]{1,0:T(8,128)} %bitcast.25, s32[1,128]{1,0:T(1,128)} %target_ref.1), custom_call_target="tpu_custom_call" | custom-call | tf_op jit(solution)/shard_map/pack/pallas_call | solution.py:386
  21.2 7.6 %all-to-all-start = ((f32[32,8,128]{2,1,0:T(8,128)}), f32[32,8,128]{2,1,0:T(8,128)S(1)}, u32[]{:S(2)}, u32[]{:S(2)}) async-start(f32[32,8,128]{2,1,0:T(8,128)} %bitcast.5), calls=%async_computation | async-start | bytes 262144 | tf_op jit(solution)/shard_map/all_to_all | solution.py:75
  28.9 2.7 %collective-permute-start.2 = (f32[1,1,3,128,128]{4,3,2,1,0:T(8,128)S(1)}, f32[1,1,3,128,128]{4,3,2,1,0:T(8,128)S(1)}, u32[]{:S(2)}, u32[]{:S(2)}) collective-permute-start(f32[1,1,3,128,128]{4,3,2,1,0:T(8,128)S(1)} %copy-done.2), channel_id=1, source_target_pairs={{0,12},{4,8},{8,4},{12,0},{16,28},{20,24},{24,20},{28,16},{1,13},{... | collective-permute-start | bytes 589832 | tf_op jit(solution)/shard_map/ppermute | solution.py:67
  32.4 1.8 %collective-permute-start.6 = (f32[1,1,3,128,128]{4,3,2,1,0:T(8,128)S(1)}, f32[1,1,3,128,128]{4,3,2,1,0:T(8,128)S(1)}, u32[]{:S(2)}, u32[]{:S(2)}) collective-permute-start(f32[1,1,3,128,128]{4,3,2,1,0:T(8,128)S(1)} %get-tuple-element.21.refs_12_), channel_id=1, source_target_pairs={{0,4},{4,0},{8,12},{12,8},{16,20},{20,16},{24,28},{28,24},{1,5},{5... | collective-permute-start | bytes 589832 | tf_op jit(solution)/shard_map/ppermute | solution.py:67
  34.5 5.0 %collective-permute-done.2.refs_9_ = f32[1,1,3,128,128]{4,3,2,1,0:T(8,128)S(1)} collective-permute-done((f32[1,1,3,128,128]{4,3,2,1,0:T(8,128)S(1)}, f32[1,1,3,128,128]{4,3,2,1,0:T(8,128)S(1)}, u32[]{:S(2)}, u32[]{:S(2)}) %collective-permute-start.2) | collective-permute-done | bytes 196640 | tf_op jit(solution)/shard_map/ppermute | solution.py:67
  39.5 3.2 %collective-permute-done.1.refs_8_ = f32[1,1,3,128,128]{4,3,2,1,0:T(8,128)S(1)} collective-permute-done((f32[1,1,3,128,128]{4,3,2,1,0:T(8,128)S(1)}, f32[1,1,3,128,128]{4,3,2,1,0:T(8,128)S(1)}, u32[]{:S(2)}, u32[]{:S(2)}) %collective-permute-start.1) | collective-permute-done | bytes 196640 | tf_op jit(solution)/shard_map/ppermute | solution.py:67
  43.2 4.2 %collective-permute-done.6.refs_13_ = f32[1,1,3,128,128]{4,3,2,1,0:T(8,128)S(1)} collective-permute-done((f32[1,1,3,128,128]{4,3,2,1,0:T(8,128)S(1)}, f32[1,1,3,128,128]{4,3,2,1,0:T(8,128)S(1)}, u32[]{:S(2)}, u32[]{:S(2)}) %collective-permute-start.6) | collective-permute-done | bytes 196640 | tf_op jit(solution)/shard_map/ppermute | solution.py:67
  47.4 3.8 %collective-permute-done.5.refs_11_ = f32[1,1,3,128,128]{4,3,2,1,0:T(8,128)S(1)} collective-permute-done((f32[1,1,3,128,128]{4,3,2,1,0:T(8,128)S(1)}, f32[1,1,3,128,128]{4,3,2,1,0:T(8,128)S(1)}, u32[]{:S(2)}, u32[]{:S(2)}) %collective-permute-start.5) | collective-permute-done | bytes 196640 | tf_op jit(solution)/shard_map/ppermute | solution.py:67
  51.3 4.6 %copy-done.1 = bf16[32,256,768]{2,1,0:T(8,128)(2,1)S(1)} copy-done((bf16[32,256,768]{2,1,0:T(8,128)(2,1)S(1)}, bf16[32,256,768]{2,1,0:T(8,128)(2,1)}, u32[]{:S(2)}) %copy-start.1) | copy-done | bytes 12582936
  55.8 10.6 %far_product.1 = (f32[32,1,2,128,128]{4,3,2,1,0:T(8,128)}, f32[32,2,128,128]{3,2,1,0:T(8,128)S(1)}, f32[32,2,128,128]{3,2,1,0:T(8,128)S(1)}, f32[32,128]{1,0:T(8...) custom-call(s32[3,32]{1,0:T(4,128)} %bitcast.31, s32[2,32]{1,0:T(2,128)} %bitcast.27, ...), custom_call_target="tpu_custom_call" | custom-call | tf_op jit(solution)/shard_map/far_product/pallas_call | solution.py:400
  67.1 0.8 collective-permute-start.8
  68.3 1.4 %collective-permute-done.9.refs_3_ = f32[32,128]{1,0:T(8,128)S(1)} collective-permute-done((f32[32,128]{1,0:T(8,128)S(1)}, f32[32,128]{1,0:T(8,128)S(1)}, u32[]{:S(2)}, u32[]{:S(2)}) %collective-permute-start.9) | collective-permute-done | bytes 16416 | tf_op jit(solution)/shard_map/ppermute | solution.py:67
  69.7 1.1 collective-permute-done.8.refs_2_
  70.8 1.9 %column_pass.3 = (f32[64,128]{1,0:T(8,128)S(1)}, f32[32,128]{1,0:T(8,128)}) custom-call(f32[32,2,128,128]{3,2,1,0:T(8,128)S(1)} %get-tuple-element.23.work_ref, s32[64,128]{1,0:T(8,128)S(1)} %get-tuple-element.24.select_ref, f32[32,128]{1,0:T(8,128)S(1)} %get-tuple-element.25.log_mass_ref, f32[32,128]{1,0:T(8,128)S(1)} %get-tuple-element.28.refs_0_, ...), custom_call_target="tpu_custom_call" | custom-call | tf_op jit(solution)/shard_map/column_pass/pallas_call | solution.py:445
  72.7 11.3 %all_to_all.44 = f32[8,8,128]{2,1,0:T(8,128)S(1)} all-to-all(f32[8,8,128]{2,1,0:T(8,128)S(1)} %bitcast.20), channel_id=1, replica_groups=mesh['rows'=8,'cols'=4] {'rows'}, dimensions={0} | all-to-all | bytes 65536 | tf_op jit(solution)/shard_map/all_to_all | solution.py:75
  84.0 2.1 %row_pass.2.refs_0_ = f32[32,128]{1,0:T(8,128)S(1)} custom-call(s32[2,32]{1,0:T(2,128)} %bitcast.28, f32[32,2,128,128]{3,2,1,0:T(8,128)S(1)} %get-tuple-element.26.tall_ref, f32[8,128]{1,0:T(8,128)S(1)} %get-tuple-element.27.log_mass_ref, f32[64,128]{1,0:T(8,128)S(1)} %bitcast.19), custom_call_target="tpu_custom_call" | custom-call | tf_op jit(solution)/shard_map/row_pass/pallas_call | solution.py:463
  86.2 0.8 collective-permute-start.11
  87.0 1.1 collective-permute-start.10
  88.0 1.3 %collective-permute-done.12.refs_3_ = f32[32,128]{1,0:T(8,128)S(1)} collective-permute-done((f32[32,128]{1,0:T(8,128)S(1)}, f32[32,128]{1,0:T(8,128)S(1)}, u32[]{:S(2)}, u32[]{:S(2)}) %collective-permute-start.12) | collective-permute-done | bytes 16416 | tf_op jit(solution)/shard_map/ppermute | solution.py:67
  89.3 0.7 collective-permute-done.11.refs_2_
  90.0 1.9 %column_pass.4 = (f32[64,128]{1,0:T(8,128)S(1)}, f32[32,128]{1,0:T(8,128)}) custom-call(f32[32,2,128,128]{3,2,1,0:T(8,128)S(1)} %get-tuple-element.23.work_ref, s32[64,128]{1,0:T(8,128)S(1)} %get-tuple-element.24.select_ref, f32[32,128]{1,0:T(8,128)S(1)} %get-tuple-element.25.log_mass_ref, f32[32,128]{1,0:T(8,128)S(1)} %row_pass.2.refs_0_, ...), custom_call_target="tpu_custom_call" | custom-call | tf_op jit(solution)/shard_map/column_pass/pallas_call | solution.py:445
  91.9 9.0 %all_to_all.45 = f32[8,8,128]{2,1,0:T(8,128)S(1)} all-to-all(f32[8,8,128]{2,1,0:T(8,128)S(1)} %bitcast.21), channel_id=1, replica_groups=mesh['rows'=8,'cols'=4] {'rows'}, dimensions={0} | all-to-all | bytes 65536 | tf_op jit(solution)/shard_map/all_to_all | solution.py:75
  100.9 2.1 %row_pass.3.refs_0_ = f32[32,128]{1,0:T(8,128)S(1)} custom-call(s32[2,32]{1,0:T(2,128)} %bitcast.29, f32[32,2,128,128]{3,2,1,0:T(8,128)S(1)} %get-tuple-element.26.tall_ref, f32[8,128]{1,0:T(8,128)S(1)} %get-tuple-element.27.log_mass_ref, f32[64,128]{1,0:T(8,128)S(1)} %bitcast.18), custom_call_target="tpu_custom_call" | custom-call | tf_op jit(solution)/shard_map/row_pass/pallas_call | solution.py:463
  103.1 0.8 collective-permute-start.14
  103.9 1.1 collective-permute-start.13
  104.9 1.3 %collective-permute-done.15.refs_3_ = f32[32,128]{1,0:T(8,128)S(1)} collective-permute-done((f32[32,128]{1,0:T(8,128)S(1)}, f32[32,128]{1,0:T(8,128)S(1)}, u32[]{:S(2)}, u32[]{:S(2)}) %collective-permute-start.15) | collective-permute-done | bytes 16416 | tf_op jit(solution)/shard_map/ppermute | solution.py:67
  106.9 1.9 %column_pass.5 = (f32[8,128]{1,0:T(8,128)S(1)}, f32[32,128]{1,0:T(8,128)}) custom-call(f32[32,2,128,128]{3,2,1,0:T(8,128)S(1)} %get-tuple-element.23.work_ref, s32[64,128]{1,0:T(8,128)S(1)} %get-tuple-element.24.select_ref, f32[32,128]{1,0:T(8,128)S(1)} %get-tuple-element.25.log_mass_ref, f32[32,128]{1,0:T(8,128)S(1)} %row_pass.3.refs_0_, ...), custom_call_target="tpu_custom_call" | custom-call | tf_op jit(solution)/shard_map/column_pass/pallas_call | solution.py:445
  108.8 8.8 %all_to_all.46 = f32[8,1,128]{2,1,0:T(1,128)S(1)} all-to-all(f32[8,1,128]{2,1,0:T(1,128)S(1)} %bitcast.23), channel_id=1, replica_groups=mesh['rows'=8,'cols'=4] {'rows'}, dimensions={0} | all-to-all | bytes 8192 | tf_op jit(solution)/shard_map/all_to_all | solution.py:75
  (21 shorter events, 4.1 us)
Async XLA Ops:
  0.6 19.1 %collective-permute-start.3 = (f32[1,1,3,128,128]{4,3,2,1,0:T(8,128)}, f32[1,1,3,128,128]{4,3,2,1,0:T(8,128)S(1)}, u32[]{:S(2)}, u32[]{:S(2)}) collective-permute-start(f32[1,1,3,128,128]{4,3,2,1,0:T(8,128)} %refs_6_.1), channel_id=1, source_target_pairs={{0,16},{4,20},{8,24},{12,28},{16,0},{20,4},{24,8},{28,12},{1,17},{... | collective-permute-start | bytes 589832 | tf_op jit(solution)/shard_map/ppermute | solution.py:67
  4.7 15.0 %collective-permute-start.4 = (f32[1,1,3,128,128]{4,3,2,1,0:T(8,128)}, f32[1,1,3,128,128]{4,3,2,1,0:T(8,128)S(1)}, u32[]{:S(2)}, u32[]{:S(2)}) collective-permute-start(f32[1,1,3,128,128]{4,3,2,1,0:T(8,128)} %refs_6_.1), channel_id=1, source_target_pairs={{0,24},{4,28},{8,16},{12,20},{16,8},{20,12},{24,0},{28,4},{1,25},{... | collective-permute-start | bytes 589832 | tf_op jit(solution)/shard_map/ppermute | solution.py:67
  6.1 22.8 %copy-start.2 = (f32[1,1,3,128,128]{4,3,2,1,0:T(8,128)S(1)}, f32[1,1,3,128,128]{4,3,2,1,0:T(8,128)}, u32[]{:S(2)}) copy-start(f32[1,1,3,128,128]{4,3,2,1,0:T(8,128)} %refs_6_.1) | copy-start | bytes 589828
  15.2 4.5 %copy-start = (bf16[32,256,768]{2,1,0:T(8,128)(2,1)}, bf16[32,256,768]{2,1,0:T(8,128)(2,1)S(1)}, u32[]{:S(2)}) copy-start(bf16[32,256,768]{2,1,0:T(8,128)(2,1)S(1)} %get-tuple-element.18.refs_3_) | copy-start | bytes 37748740
  21.2 30.0 %all-to-all-start = ((f32[32,8,128]{2,1,0:T(8,128)}), f32[32,8,128]{2,1,0:T(8,128)S(1)}, u32[]{:S(2)}, u32[]{:S(2)}) async-start(f32[32,8,128]{2,1,0:T(8,128)} %bitcast.5), calls=%async_computation | async-start | bytes 262144 | tf_op jit(solution)/shard_map/all_to_all | solution.py:75
  28.9 10.6 %collective-permute-start.2 = (f32[1,1,3,128,128]{4,3,2,1,0:T(8,128)S(1)}, f32[1,1,3,128,128]{4,3,2,1,0:T(8,128)S(1)}, u32[]{:S(2)}, u32[]{:S(2)}) collective-permute-start(f32[1,1,3,128,128]{4,3,2,1,0:T(8,128)S(1)} %copy-done.2), channel_id=1, source_target_pairs={{0,12},{4,8},{8,4},{12,0},{16,28},{20,24},{24,20},{28,16},{1,13},{... | collective-permute-start | bytes 589832 | tf_op jit(solution)/shard_map/ppermute | solution.py:67
  31.6 11.0 %collective-permute-start.1 = (f32[1,1,3,128,128]{4,3,2,1,0:T(8,128)S(1)}, f32[1,1,3,128,128]{4,3,2,1,0:T(8,128)S(1)}, u32[]{:S(2)}, u32[]{:S(2)}) collective-permute-start(f32[1,1,3,128,128]{4,3,2,1,0:T(8,128)S(1)} %copy-done.2), channel_id=1, source_target_pairs={{0,8},{4,12},{8,0},{12,4},{16,24},{20,28},{24,16},{28,20},{1,9},{5... | collective-permute-start | bytes 589832 | tf_op jit(solution)/shard_map/ppermute | solution.py:67
  32.2 11.0 %collective-permute-start = (f32[1,1,3,128,128]{4,3,2,1,0:T(8,128)S(1)}, f32[1,1,3,128,128]{4,3,2,1,0:T(8,128)S(1)}, u32[]{:S(2)}, u32[]{:S(2)}) collective-permute-start(f32[1,1,3,128,128]{4,3,2,1,0:T(8,128)S(1)} %copy-done.2), channel_id=1, source_target_pairs={{0,4},{4,0},{8,12},{12,8},{16,20},{20,16},{24,28},{28,24},{1,5},{5... | collective-permute-start | bytes 589832 | tf_op jit(solution)/shard_map/ppermute | solution.py:67
  32.4 15.0 %collective-permute-start.6 = (f32[1,1,3,128,128]{4,3,2,1,0:T(8,128)S(1)}, f32[1,1,3,128,128]{4,3,2,1,0:T(8,128)S(1)}, u32[]{:S(2)}, u32[]{:S(2)}) collective-permute-start(f32[1,1,3,128,128]{4,3,2,1,0:T(8,128)S(1)} %get-tuple-element.21.refs_12_), channel_id=1, source_target_pairs={{0,4},{4,0},{8,12},{12,8},{16,20},{20,16},{24,28},{28,24},{1,5},{5... | collective-permute-start | bytes 589832 | tf_op jit(solution)/shard_map/ppermute | solution.py:67
  34.2 17.0 %collective-permute-start.5 = (f32[1,1,3,128,128]{4,3,2,1,0:T(8,128)S(1)}, f32[1,1,3,128,128]{4,3,2,1,0:T(8,128)S(1)}, u32[]{:S(2)}, u32[]{:S(2)}) collective-permute-start(f32[1,1,3,128,128]{4,3,2,1,0:T(8,128)S(1)} %get-tuple-element.20.after_ref.refs_10_), channel_id=1, source_target_pairs={{0,4},{4,0},{8,12},{12,8},{16,20},{20,16},{24,28},{28,24},{1,5},{5... | collective-permute-start | bytes 589832 | tf_op jit(solution)/shard_map/ppermute | solution.py:67
  51.3 4.6 %copy-start.1 = (bf16[32,256,768]{2,1,0:T(8,128)(2,1)S(1)}, bf16[32,256,768]{2,1,0:T(8,128)(2,1)}, u32[]{:S(2)}) copy-start(bf16[32,256,768]{2,1,0:T(8,128)(2,1)} %copy-done) | copy-start | bytes 37748740
  66.5 3.2 %collective-permute-start.9 = (f32[32,128]{1,0:T(8,128)S(1)}, f32[32,128]{1,0:T(8,128)S(1)}, u32[]{:S(2)}, u32[]{:S(2)}) collective-permute-start(f32[32,128]{1,0:T(8,128)S(1)} %get-tuple-element.28.refs_0_), channel_id=1, source_target_pairs={{0,3},{1,2},{2,1},{3,0},{4,7},{5,6},{6,5},{7,4},{8,11},{9,10},{10,... | collective-permute-start | bytes 49160 | tf_op jit(solution)/shard_map/ppermute | solution.py:67
  67.1 3.8 %collective-permute-start.8 = (f32[32,128]{1,0:T(8,128)S(1)}, f32[32,128]{1,0:T(8,128)S(1)}, u32[]{:S(2)}, u32[]{:S(2)}) collective-permute-start(f32[32,128]{1,0:T(8,128)S(1)} %get-tuple-element.28.refs_0_), channel_id=1, source_target_pairs={{0,2},{1,3},{2,0},{3,1},{4,6},{5,7},{6,4},{7,5},{8,10},{9,11},{10,... | collective-permute-start | bytes 49160 | tf_op jit(solution)/shard_map/ppermute | solution.py:67
  67.8 3.0 %collective-permute-start.7 = (f32[32,128]{1,0:T(8,128)S(1)}, f32[32,128]{1,0:T(8,128)S(1)}, u32[]{:S(2)}, u32[]{:S(2)}) collective-permute-start(f32[32,128]{1,0:T(8,128)S(1)} %get-tuple-element.28.refs_0_), channel_id=1, source_target_pairs={{0,1},{1,0},{2,3},{3,2},{4,5},{5,4},{6,7},{7,6},{8,9},{9,8},{10,11... | collective-permute-start | bytes 49160 | tf_op jit(solution)/shard_map/ppermute | solution.py:67
  86.1 3.2 %collective-permute-start.12 = (f32[32,128]{1,0:T(8,128)S(1)}, f32[32,128]{1,0:T(8,128)S(1)}, u32[]{:S(2)}, u32[]{:S(2)}) collective-permute-start(f32[32,128]{1,0:T(8,128)S(1)} %row_pass.2.refs_0_), channel_id=1, source_target_pairs={{0,3},{1,2},{2,1},{3,0},{4,7},{5,6},{6,5},{7,4},{8,11},{9,10},{10,... | collective-permute-start | bytes 49160 | tf_op jit(solution)/shard_map/ppermute | solution.py:67
  86.2 3.8 %collective-permute-start.11 = (f32[32,128]{1,0:T(8,128)S(1)}, f32[32,128]{1,0:T(8,128)S(1)}, u32[]{:S(2)}, u32[]{:S(2)}) collective-permute-start(f32[32,128]{1,0:T(8,128)S(1)} %row_pass.2.refs_0_), channel_id=1, source_target_pairs={{0,2},{1,3},{2,0},{3,1},{4,6},{5,7},{6,4},{7,5},{8,10},{9,11},{10,... | collective-permute-start | bytes 49160 | tf_op jit(solution)/shard_map/ppermute | solution.py:67
  87.0 3.0 %collective-permute-start.10 = (f32[32,128]{1,0:T(8,128)S(1)}, f32[32,128]{1,0:T(8,128)S(1)}, u32[]{:S(2)}, u32[]{:S(2)}) collective-permute-start(f32[32,128]{1,0:T(8,128)S(1)} %row_pass.2.refs_0_), channel_id=1, source_target_pairs={{0,1},{1,0},{2,3},{3,2},{4,5},{5,4},{6,7},{7,6},{8,9},{9,8},{10,11... | collective-permute-start | bytes 49160 | tf_op jit(solution)/shard_map/ppermute | solution.py:67
  103.0 3.2 %collective-permute-start.15 = (f32[32,128]{1,0:T(8,128)S(1)}, f32[32,128]{1,0:T(8,128)S(1)}, u32[]{:S(2)}, u32[]{:S(2)}) collective-permute-start(f32[32,128]{1,0:T(8,128)S(1)} %row_pass.3.refs_0_), channel_id=1, source_target_pairs={{0,3},{1,2},{2,1},{3,0},{4,7},{5,6},{6,5},{7,4},{8,11},{9,10},{10,... | collective-permute-start | bytes 49160 | tf_op jit(solution)/shard_map/ppermute | solution.py:67
  103.1 3.8 %collective-permute-start.14 = (f32[32,128]{1,0:T(8,128)S(1)}, f32[32,128]{1,0:T(8,128)S(1)}, u32[]{:S(2)}, u32[]{:S(2)}) collective-permute-start(f32[32,128]{1,0:T(8,128)S(1)} %row_pass.3.refs_0_), channel_id=1, source_target_pairs={{0,2},{1,3},{2,0},{3,1},{4,6},{5,7},{6,4},{7,5},{8,10},{9,11},{10,... | collective-permute-start | bytes 49160 | tf_op jit(solution)/shard_map/ppermute | solution.py:67
  103.9 3.0 %collective-permute-start.13 = (f32[32,128]{1,0:T(8,128)S(1)}, f32[32,128]{1,0:T(8,128)S(1)}, u32[]{:S(2)}, u32[]{:S(2)}) collective-permute-start(f32[32,128]{1,0:T(8,128)S(1)} %row_pass.3.refs_0_), channel_id=1, source_target_pairs={{0,1},{1,0},{2,3},{3,2},{4,5},{5,4},{6,7},{7,6},{8,9},{9,8},{10,11... | collective-permute-start | bytes 49160 | tf_op jit(solution)/shard_map/ppermute | solution.py:67

commit v6 on v5

--- a/solution.py
+++ b/solution.py
@@ -75,7 +75,7 @@
     return lax.all_to_all(copies, axis, 0, 0, tiled=True)
 
 
-def pack_kernel(devices, after_ref, source_ref, target_ref, out_ref):
+def pack_kernel(devices, source_ref, target_ref, out_ref):
     rows = out_ref.shape[0] // devices
     total = jnp.sum(source_ref[...].astype(jnp.float32), axis=(0, 1), keepdims=True)
     target = target_ref[...].astype(jnp.float32)
@@ -85,7 +85,7 @@
         out_ref[d * rows + 1 : d * rows + 1 + target.shape[0], :] = target
 
 
-def near_kernel(near_index_ref, cost_ref, plan_ref, mass_ref, x_ref, term_ref, plan_scr):
+def near_kernel(near_index_ref, cost_ref, plan_ref, mass_ref, totals_ref, x_ref, term_ref, plan_scr):
     g = pl.program_id(0)
     near_count = cost_ref.shape[1]
     width = cost_ref.shape[2]
@@ -327,17 +327,42 @@
     source_count = rows_here * row_devices * width
     target_count = group_blocks * width * col_devices
     f32 = jnp.float32
+    half = row_devices // 2
     arrived = {0: target_cost}
-    late = [mask for mask in range(5, row_devices, 2)]
-    for mask in range(1, row_devices):
-        if mask not in late:
-            arrived[mask] = send(target_cost, "rows", mask)
+    for mask in range(1, half + 1):
+        arrived[mask] = send(target_cost, "rows", mask)
 
     near_t = in_hbm(near_index.T)
     slot_t = in_hbm(coupling_index[:, 0, :].T)
     link_t = in_hbm(jnp.transpose(target_index, (2, 0, 1)))
     mass = in_hbm(source_weights.reshape(rows_here, width))
     small = pltpu.CompilerParams(vmem_limit_bytes=4 * mib)
+
+    pack_rows = 8 * pl.cdiv(1 + target_here, 8)
+    devices = row_devices * col_devices
+    pack = pl.pallas_call(
+        functools.partial(pack_kernel, devices),
+        in_specs=[VMEM, VMEM],
+        out_shape=jax.ShapeDtypeStruct((devices * pack_rows, width), f32),
+        compiler_params=small,
+        name="pack",
+    )(mass, in_hbm(target_weights.reshape(target_here, width)))
+    packs = exchange(pack, ("rows", "cols"))
+
+    direct = list(range(1, half + 1))
+    passed = pl.pallas_call(
+        relay_kernel,
+        in_specs=[ANY] * half,
+        out_specs=[ANY] * half,
+        out_shape=[jax.ShapeDtypeStruct(target_cost.shape, f32)] * half,
+        input_output_aliases={e: e for e in range(half)},
+        compiler_params=small,
+        name="relay",
+    )(*[arrived[mask] for mask in direct])
+    arrived.update(zip(direct, passed))
+    for mask in range(half + 1, row_devices):
+        arrived[mask] = send(arrived[half], "rows", mask - half)
+    cost_parts = [arrived[s] for s in range(row_devices)]
 
     wide = near_count * slots * width
     groups = rows_here // SUB
@@ -349,6 +374,7 @@
             pl.BlockSpec((SUB, near_count, width, width), lambda g: (g, 0, 0, 0)),
             pl.BlockSpec((SUB, 1, slots, width, width), lambda g: (g, 0, 0, 0, 0)),
             whole((rows_here, width)),
+            ANY,
         ],
         out_specs=[VMEM, VMEM],
         out_shape=[
@@ -363,34 +389,7 @@
             transcendentals=0,
         ),
         name="near_product",
-    )(near_t, in_hbm(near_cost), in_hbm(coupling), mass)
-
-    sources = [mask - 1 for mask in late] or [0]
-    passed = pl.pallas_call(
-        relay_kernel,
-        in_specs=[ANY] * (1 + len(sources)),
-        out_specs=[ANY] * len(sources),
-        out_shape=[jax.ShapeDtypeStruct(target_cost.shape, f32)] * len(sources),
-        input_output_aliases={1 + e: e for e in range(len(sources))},
-        compiler_params=small,
-        name="relay",
-    )(in_vmem(term), *[arrived[mask] for mask in sources])
-    for mask, block in zip(sources, passed):
-        arrived[mask] = block
-    for mask in late:
-        arrived[mask] = send(arrived[mask - 1], "rows", 1)
-    cost_parts = [arrived[s] for s in range(row_devices)]
-
-    pack_rows = 8 * pl.cdiv(1 + target_here, 8)
-    devices = row_devices * col_devices
-    pack = pl.pallas_call(
-        functools.partial(pack_kernel, devices),
-        in_specs=[ANY, VMEM, VMEM],
-        out_shape=jax.ShapeDtypeStruct((devices * pack_rows, width), f32),
-        compiler_params=small,
-        name="pack",
-    )(passed[0], mass, in_hbm(target_weights.reshape(target_here, width)))
-    packs = exchange(pack, ("rows", "cols"))
+    )(near_t, in_hbm(near_cost), in_hbm(coupling), mass, packs)
 
     far_bytes = group_blocks * link_count * width * width * 4
     step_rows = SUB

time: 119 us -> 102 us (0.86)
  local copies, waits for them, and re-layouts: 9.08 us -> 0.01 us
  waiting for transfers between devices: 23.2 us -> 17.7 us
  starting transfers between devices: 24.4 us -> 22.8 us
    unnamed x6 -> x2, local copies, waits for them, and re-layouts: 9.08 us -> 0.01 us
    ppermute x16, waiting for transfers between devices: 23.2 us -> 17.7 us  [send(): return lax.ppermute(x, axis, [(d, d ^ mask) for d in range(size)])]
    ppermute x16, starting transfers between devices: 16.7 us -> 15.5 us  [send(): return lax.ppermute(x, axis, [(d, d ^ mask) for d in range(size)])]
  transfers between devices with their start and end apart: 17 -> 17, of which waited for: 11 -> 8; matrix products, arithmetic and copies ran while one was open for 0% -> 0% of each run, Pallas kernels for 8% -> 9%
where the time goes in v6:
time: 102 us
  Pallas kernels  32 us (31%)
  blocking collectives  28.5 us (28%)
  starting transfers between devices  22.8 us (22%)
  waiting for transfers between devices  17.7 us (17%)
    all_to_all x3, blocking collectives, exchange(): return lax.all_to_all(copies, axis, 0, 0, tiled=True)  28.5 us
    ppermute x16, waiting for transfers between devices, send(): return lax.ppermute(x, axis, [(d, d ^ mask) for d in range(size)])  17.7 us
    ppermute x16, starting transfers between devices, send(): return lax.ppermute(x, axis, [(d, d ^ mask) for d in range(size)])  15.5 us
    pallas_call x1, Pallas kernels, per_device(): pl.pallas_call(functools.partial(far_kernel, (row_devices, col_devices, t...  11 us
    pallas_call x1, Pallas kernels, per_device(): pl.pallas_call(near_kernel, grid=(groups,), in_specs=[SMEM, pl.BlockSpec(...  9.14 us
    all_to_all x1, starting transfers between devices, exchange(): return lax.all_to_all(copies, axis, 0, 0, tiled=True)  7.3 us
    pallas_call x3, Pallas kernels, column_step(): pl.pallas_call(functools.partial(column_kernel, col_devices, copies), in_...  5.71 us
    pallas_call x2, Pallas kernels, row_step(): pl.pallas_call(functools.partial(row_kernel, row_devices), in_specs=[SMEM...  4.13 us
  transfers between devices with their start and end apart: 17, of which 8 were waited for; matrix products, arithmetic and copies ran while one was open for 0% of the time, Pallas kernels for 9%

profile of v6, /device:TPU:0, one launch (start us, length us, event | category | flops | bytes accessed | tf_op | source)
XLA Modules:
  0.0 101.7 jit_solution(1675343445433801157)
XLA Ops:
  0.6 1.5 %pack.1 = f32[256,128]{1,0:T(8,128)} custom-call(s32[32,128]{1,0:T(8,128)} %bitcast.25, s32[1,128]{1,0:T(1,128)} %target_ref.1), custom_call_target="tpu_custom_call" | custom-call | tf_op jit(solution)/shard_map/pack/pallas_call | solution.py:343
  2.1 7.3 %all-to-all-start = ((f32[32,8,128]{2,1,0:T(8,128)}), f32[32,8,128]{2,1,0:T(8,128)S(1)}, u32[]{:S(2)}, u32[]{:S(2)}) async-start(f32[32,8,128]{2,1,0:T(8,128)} %bitcast.5), calls=%async_computation | async-start | bytes 262144 | tf_op jit(solution)/shard_map/all_to_all | solution.py:75
  9.4 2.7 %collective-permute-start.2 = (f32[1,1,3,128,128]{4,3,2,1,0:T(8,128)}, f32[1,1,3,128,128]{4,3,2,1,0:T(8,128)S(1)}, u32[]{:S(2)}, u32[]{:S(2)}) collective-permute-start(f32[1,1,3,128,128]{4,3,2,1,0:T(8,128)} %refs_6_.1), channel_id=1, source_target_pairs={{0,12},{4,8},{8,4},{12,0},{16,28},{20,24},{24,20},{28,16},{1,13},{... | collective-permute-start | bytes 589832 | tf_op jit(solution)/shard_map/ppermute | solution.py:67
  12.2 0.6 collective-permute-start.1
  13.0 2.7 %collective-permute-start.3 = (f32[1,1,3,128,128]{4,3,2,1,0:T(8,128)}, f32[1,1,3,128,128]{4,3,2,1,0:T(8,128)S(1)}, u32[]{:S(2)}, u32[]{:S(2)}) collective-permute-start(f32[1,1,3,128,128]{4,3,2,1,0:T(8,128)} %refs_6_.1), channel_id=1, source_target_pairs={{0,16},{4,20},{8,24},{12,28},{16,0},{20,4},{24,8},{28,12},{1,17},{... | collective-permute-start | bytes 589832 | tf_op jit(solution)/shard_map/ppermute | solution.py:67
  15.7 8.5 %collective-permute-done.2.refs_2_ = f32[1,1,3,128,128]{4,3,2,1,0:T(8,128)S(1)} collective-permute-done((f32[1,1,3,128,128]{4,3,2,1,0:T(8,128)}, f32[1,1,3,128,128]{4,3,2,1,0:T(8,128)S(1)}, u32[]{:S(2)}, u32[]{:S(2)}) %collective-permute-start.2) | collective-permute-done | bytes 196640 | tf_op jit(solution)/shard_map/ppermute | solution.py:67
  24.2 3.3 %collective-permute-done.1.refs_1_ = f32[1,1,3,128,128]{4,3,2,1,0:T(8,128)S(1)} collective-permute-done((f32[1,1,3,128,128]{4,3,2,1,0:T(8,128)}, f32[1,1,3,128,128]{4,3,2,1,0:T(8,128)S(1)}, u32[]{:S(2)}, u32[]{:S(2)}) %collective-permute-start.1) | collective-permute-done | bytes 196640 | tf_op jit(solution)/shard_map/ppermute | solution.py:67
  27.5 2.9 %collective-permute-start.6 = (f32[1,1,3,128,128]{4,3,2,1,0:T(8,128)S(1)}, f32[1,1,3,128,128]{4,3,2,1,0:T(8,128)S(1)}, u32[]{:S(2)}, u32[]{:S(2)}) collective-permute-start(f32[1,1,3,128,128]{4,3,2,1,0:T(8,128)S(1)} %get-tuple-element.25.refs_10_), channel_id=1, source_target_pairs={{0,12},{4,8},{8,4},{12,0},{16,28},{20,24},{24,20},{28,16},{1,13},{... | collective-permute-start | bytes 589832 | tf_op jit(solution)/shard_map/ppermute | solution.py:67
  30.4 0.6 collective-permute-start.4
  31.1 9.1 %near_product.1 = (bf16[32,256,768]{2,1,0:T(8,128)(2,1)S(1)}, f32[8,128,4]{2,1,0:T(8,128)S(1)}) custom-call(s32[3,32]{1,0:T(4,128)} %bitcast.31, f32[32,3,128,128]{3,2,1,0:T(8,128)} %cost_ref.1, f32[32,1,2,128,128]{4,3,2,1,0:T(8,128)} %plan_ref.1, s32[32,128]{1,0:T(8,128)} %bitcast.26, f32[256,128]{1,0:T(8,128)S(1)} %bitcast.17), custom_call_target="tpu_custom_call" | custom-call | flops 2415919104 | bytes 10485760 | tf_op jit(solution)/shard_map/near_product/pallas_call | solution.py:369
  40.2 11.0 %far_product.1 = (f32[32,1,2,128,128]{4,3,2,1,0:T(8,128)}, f32[32,2,128,128]{3,2,1,0:T(8,128)S(1)}, f32[32,2,128,128]{3,2,1,0:T(8,128)S(1)}, f32[32,128]{1,0:T(8...) custom-call(s32[3,32]{1,0:T(4,128)} %bitcast.32, s32[2,32]{1,0:T(2,128)} %bitcast.28, ...), custom_call_target="tpu_custom_call" | custom-call | tf_op jit(solution)/shard_map/far_product/pallas_call | solution.py:399
  51.3 1.4 %collective-permute-start.8 = (f32[32,128]{1,0:T(8,128)S(1)}, f32[32,128]{1,0:T(8,128)S(1)}, u32[]{:S(2)}, u32[]{:S(2)}) collective-permute-start(f32[32,128]{1,0:T(8,128)S(1)} %get-tuple-element.32.refs_0_), channel_id=1, source_target_pairs={{0,2},{1,3},{2,0},{3,1},{4,6},{5,7},{6,4},{7,5},{8,10},{9,11},{10,... | collective-permute-start | bytes 49160 | tf_op jit(solution)/shard_map/ppermute | solution.py:67
  52.7 0.4 collective-permute-start.7
  53.1 1.5 %collective-permute-done.9.refs_3_ = f32[32,128]{1,0:T(8,128)S(1)} collective-permute-done((f32[32,128]{1,0:T(8,128)S(1)}, f32[32,128]{1,0:T(8,128)S(1)}, u32[]{:S(2)}, u32[]{:S(2)}) %collective-permute-start.9) | collective-permute-done | bytes 16416 | tf_op jit(solution)/shard_map/ppermute | solution.py:67
  54.5 0.5 collective-permute-done.8.refs_2_
  55.1 1.9 %column_pass.3 = (f32[64,128]{1,0:T(8,128)S(1)}, f32[32,128]{1,0:T(8,128)}) custom-call(f32[32,2,128,128]{3,2,1,0:T(8,128)S(1)} %get-tuple-element.27.work_ref, s32[64,128]{1,0:T(8,128)S(1)} %get-tuple-element.28.select_ref, f32[32,128]{1,0:T(8,128)S(1)} %get-tuple-element.29.log_mass_ref, f32[32,128]{1,0:T(8,128)S(1)} %get-tuple-element.32.refs_0_, ...), custom_call_target="tpu_custom_call" | custom-call | tf_op jit(solution)/shard_map/column_pass/pallas_call | solution.py:444
  57.0 10.6 %all_to_all.44 = f32[8,8,128]{2,1,0:T(8,128)S(1)} all-to-all(f32[8,8,128]{2,1,0:T(8,128)S(1)} %bitcast.21), channel_id=1, replica_groups=mesh['rows'=8,'cols'=4] {'rows'}, dimensions={0} | all-to-all | bytes 65536 | tf_op jit(solution)/shard_map/all_to_all | solution.py:75
  67.5 2.1 %row_pass.2.refs_0_ = f32[32,128]{1,0:T(8,128)S(1)} custom-call(s32[2,32]{1,0:T(2,128)} %bitcast.29, f32[32,2,128,128]{3,2,1,0:T(8,128)S(1)} %get-tuple-element.30.tall_ref, f32[8,128]{1,0:T(8,128)S(1)} %get-tuple-element.31.log_mass_ref, f32[64,128]{1,0:T(8,128)S(1)} %bitcast.20), custom_call_target="tpu_custom_call" | custom-call | tf_op jit(solution)/shard_map/row_pass/pallas_call | solution.py:462
  69.7 1.5 %collective-permute-start.11 = (f32[32,128]{1,0:T(8,128)S(1)}, f32[32,128]{1,0:T(8,128)S(1)}, u32[]{:S(2)}, u32[]{:S(2)}) collective-permute-start(f32[32,128]{1,0:T(8,128)S(1)} %row_pass.2.refs_0_), channel_id=1, source_target_pairs={{0,2},{1,3},{2,0},{3,1},{4,6},{5,7},{6,4},{7,5},{8,10},{9,11},{10,... | collective-permute-start | bytes 49160 | tf_op jit(solution)/shard_map/ppermute | solution.py:67
  71.2 0.4 collective-permute-start.10
  71.5 1.4 %collective-permute-done.12.refs_3_ = f32[32,128]{1,0:T(8,128)S(1)} collective-permute-done((f32[32,128]{1,0:T(8,128)S(1)}, f32[32,128]{1,0:T(8,128)S(1)}, u32[]{:S(2)}, u32[]{:S(2)}) %collective-permute-start.12) | collective-permute-done | bytes 16416 | tf_op jit(solution)/shard_map/ppermute | solution.py:67
  73.0 0.5 collective-permute-done.11.refs_2_
  73.5 1.9 %column_pass.4 = (f32[64,128]{1,0:T(8,128)S(1)}, f32[32,128]{1,0:T(8,128)}) custom-call(f32[32,2,128,128]{3,2,1,0:T(8,128)S(1)} %get-tuple-element.27.work_ref, s32[64,128]{1,0:T(8,128)S(1)} %get-tuple-element.28.select_ref, f32[32,128]{1,0:T(8,128)S(1)} %get-tuple-element.29.log_mass_ref, f32[32,128]{1,0:T(8,128)S(1)} %row_pass.2.refs_0_, ...), custom_call_target="tpu_custom_call" | custom-call | tf_op jit(solution)/shard_map/column_pass/pallas_call | solution.py:444
  75.4 9.0 %all_to_all.45 = f32[8,8,128]{2,1,0:T(8,128)S(1)} all-to-all(f32[8,8,128]{2,1,0:T(8,128)S(1)} %bitcast.22), channel_id=1, replica_groups=mesh['rows'=8,'cols'=4] {'rows'}, dimensions={0} | all-to-all | bytes 65536 | tf_op jit(solution)/shard_map/all_to_all | solution.py:75
  84.5 2.1 %row_pass.3.refs_0_ = f32[32,128]{1,0:T(8,128)S(1)} custom-call(s32[2,32]{1,0:T(2,128)} %bitcast.30, f32[32,2,128,128]{3,2,1,0:T(8,128)S(1)} %get-tuple-element.30.tall_ref, f32[8,128]{1,0:T(8,128)S(1)} %get-tuple-element.31.log_mass_ref, f32[64,128]{1,0:T(8,128)S(1)} %bitcast.19), custom_call_target="tpu_custom_call" | custom-call | tf_op jit(solution)/shard_map/row_pass/pallas_call | solution.py:462
  86.6 1.5 %collective-permute-start.14 = (f32[32,128]{1,0:T(8,128)S(1)}, f32[32,128]{1,0:T(8,128)S(1)}, u32[]{:S(2)}, u32[]{:S(2)}) collective-permute-start(f32[32,128]{1,0:T(8,128)S(1)} %row_pass.3.refs_0_), channel_id=1, source_target_pairs={{0,2},{1,3},{2,0},{3,1},{4,6},{5,7},{6,4},{7,5},{8,10},{9,11},{10,... | collective-permute-start | bytes 49160 | tf_op jit(solution)/shard_map/ppermute | solution.py:67
  88.1 0.4 collective-permute-start.13
  88.4 1.4 %collective-permute-done.15.refs_3_ = f32[32,128]{1,0:T(8,128)S(1)} collective-permute-done((f32[32,128]{1,0:T(8,128)S(1)}, f32[32,128]{1,0:T(8,128)S(1)}, u32[]{:S(2)}, u32[]{:S(2)}) %collective-permute-start.15) | collective-permute-done | bytes 16416 | tf_op jit(solution)/shard_map/ppermute | solution.py:67
  89.9 0.5 collective-permute-done.14.refs_2_
  90.4 1.9 %column_pass.5 = (f32[8,128]{1,0:T(8,128)S(1)}, f32[32,128]{1,0:T(8,128)}) custom-call(f32[32,2,128,128]{3,2,1,0:T(8,128)S(1)} %get-tuple-element.27.work_ref, s32[64,128]{1,0:T(8,128)S(1)} %get-tuple-element.28.select_ref, f32[32,128]{1,0:T(8,128)S(1)} %get-tuple-element.29.log_mass_ref, f32[32,128]{1,0:T(8,128)S(1)} %row_pass.3.refs_0_, ...), custom_call_target="tpu_custom_call" | custom-call | tf_op jit(solution)/shard_map/column_pass/pallas_call | solution.py:444
  92.3 8.8 %all_to_all.46 = f32[8,1,128]{2,1,0:T(1,128)S(1)} all-to-all(f32[8,1,128]{2,1,0:T(1,128)S(1)} %bitcast.24), channel_id=1, replica_groups=mesh['rows'=8,'cols'=4] {'rows'}, dimensions={0} | all-to-all | bytes 8192 | tf_op jit(solution)/shard_map/all_to_all | solution.py:75
  101.1 0.5 last_potential.1
  (17 shorter events, 0.5 us)
Async XLA Ops:
  2.1 28.9 %all-to-all-start = ((f32[32,8,128]{2,1,0:T(8,128)}), f32[32,8,128]{2,1,0:T(8,128)S(1)}, u32[]{:S(2)}, u32[]{:S(2)}) async-start(f32[32,8,128]{2,1,0:T(8,128)} %bitcast.5), calls=%async_computation | async-start | bytes 262144 | tf_op jit(solution)/shard_map/all_to_all | solution.py:75
  9.4 14.8 %collective-permute-start.2 = (f32[1,1,3,128,128]{4,3,2,1,0:T(8,128)}, f32[1,1,3,128,128]{4,3,2,1,0:T(8,128)S(1)}, u32[]{:S(2)}, u32[]{:S(2)}) collective-permute-start(f32[1,1,3,128,128]{4,3,2,1,0:T(8,128)} %refs_6_.1), channel_id=1, source_target_pairs={{0,12},{4,8},{8,4},{12,0},{16,28},{20,24},{24,20},{28,16},{1,13},{... | collective-permute-start | bytes 589832 | tf_op jit(solution)/shard_map/ppermute | solution.py:67
  12.2 15.3 %collective-permute-start.1 = (f32[1,1,3,128,128]{4,3,2,1,0:T(8,128)}, f32[1,1,3,128,128]{4,3,2,1,0:T(8,128)S(1)}, u32[]{:S(2)}, u32[]{:S(2)}) collective-permute-start(f32[1,1,3,128,128]{4,3,2,1,0:T(8,128)} %refs_6_.1), channel_id=1, source_target_pairs={{0,8},{4,12},{8,0},{12,4},{16,24},{20,28},{24,16},{28,20},{1,9},{5... | collective-permute-start | bytes 589832 | tf_op jit(solution)/shard_map/ppermute | solution.py:67
  12.7 14.8 %collective-permute-start = (f32[1,1,3,128,128]{4,3,2,1,0:T(8,128)}, f32[1,1,3,128,128]{4,3,2,1,0:T(8,128)S(1)}, u32[]{:S(2)}, u32[]{:S(2)}) collective-permute-start(f32[1,1,3,128,128]{4,3,2,1,0:T(8,128)} %refs_6_.1), channel_id=1, source_target_pairs={{0,4},{4,0},{8,12},{12,8},{16,20},{20,16},{24,28},{28,24},{1,5},{5... | collective-permute-start | bytes 589832 | tf_op jit(solution)/shard_map/ppermute | solution.py:67
  13.0 14.5 %collective-permute-start.3 = (f32[1,1,3,128,128]{4,3,2,1,0:T(8,128)}, f32[1,1,3,128,128]{4,3,2,1,0:T(8,128)S(1)}, u32[]{:S(2)}, u32[]{:S(2)}) collective-permute-start(f32[1,1,3,128,128]{4,3,2,1,0:T(8,128)} %refs_6_.1), channel_id=1, source_target_pairs={{0,16},{4,20},{8,24},{12,28},{16,0},{20,4},{24,8},{28,12},{1,17},{... | collective-permute-start | bytes 589832 | tf_op jit(solution)/shard_map/ppermute | solution.py:67
  27.5 12.7 %collective-permute-start.6 = (f32[1,1,3,128,128]{4,3,2,1,0:T(8,128)S(1)}, f32[1,1,3,128,128]{4,3,2,1,0:T(8,128)S(1)}, u32[]{:S(2)}, u32[]{:S(2)}) collective-permute-start(f32[1,1,3,128,128]{4,3,2,1,0:T(8,128)S(1)} %get-tuple-element.25.refs_10_), channel_id=1, source_target_pairs={{0,12},{4,8},{8,4},{12,0},{16,28},{20,24},{24,20},{28,16},{1,13},{... | collective-permute-start | bytes 589832 | tf_op jit(solution)/shard_map/ppermute | solution.py:67
  30.4 9.8 %collective-permute-start.5 = (f32[1,1,3,128,128]{4,3,2,1,0:T(8,128)S(1)}, f32[1,1,3,128,128]{4,3,2,1,0:T(8,128)S(1)}, u32[]{:S(2)}, u32[]{:S(2)}) collective-permute-start(f32[1,1,3,128,128]{4,3,2,1,0:T(8,128)S(1)} %get-tuple-element.25.refs_10_), channel_id=1, source_target_pairs={{0,8},{4,12},{8,0},{12,4},{16,24},{20,28},{24,16},{28,20},{1,9},{5... | collective-permute-start | bytes 589832 | tf_op jit(solution)/shard_map/ppermute | solution.py:67
  30.4 9.8 %collective-permute-start.4 = (f32[1,1,3,128,128]{4,3,2,1,0:T(8,128)S(1)}, f32[1,1,3,128,128]{4,3,2,1,0:T(8,128)S(1)}, u32[]{:S(2)}, u32[]{:S(2)}) collective-permute-start(f32[1,1,3,128,128]{4,3,2,1,0:T(8,128)S(1)} %get-tuple-element.25.refs_10_), channel_id=1, source_target_pairs={{0,4},{4,0},{8,12},{12,8},{16,20},{20,16},{24,28},{28,24},{1,5},{5... | collective-permute-start | bytes 589832 | tf_op jit(solution)/shard_map/ppermute | solution.py:67
  31.0 9.2 %copy-start = (f32[1,1,3,128,128]{4,3,2,1,0:T(8,128)S(1)}, f32[1,1,3,128,128]{4,3,2,1,0:T(8,128)}, u32[]{:S(2)}) copy-start(f32[1,1,3,128,128]{4,3,2,1,0:T(8,128)} %refs_6_.1) | copy-start | bytes 589828
  51.2 3.3 %collective-permute-start.9 = (f32[32,128]{1,0:T(8,128)S(1)}, f32[32,128]{1,0:T(8,128)S(1)}, u32[]{:S(2)}, u32[]{:S(2)}) collective-permute-start(f32[32,128]{1,0:T(8,128)S(1)} %get-tuple-element.32.refs_0_), channel_id=1, source_target_pairs={{0,3},{1,2},{2,1},{3,0},{4,7},{5,6},{6,5},{7,4},{8,11},{9,10},{10,... | collective-permute-start | bytes 49160 | tf_op jit(solution)/shard_map/ppermute | solution.py:67
  51.3 3.7 %collective-permute-start.8 = (f32[32,128]{1,0:T(8,128)S(1)}, f32[32,128]{1,0:T(8,128)S(1)}, u32[]{:S(2)}, u32[]{:S(2)}) collective-permute-start(f32[32,128]{1,0:T(8,128)S(1)} %get-tuple-element.32.refs_0_), channel_id=1, source_target_pairs={{0,2},{1,3},{2,0},{3,1},{4,6},{5,7},{6,4},{7,5},{8,10},{9,11},{10,... | collective-permute-start | bytes 49160 | tf_op jit(solution)/shard_map/ppermute | solution.py:67
  52.7 2.4 %collective-permute-start.7 = (f32[32,128]{1,0:T(8,128)S(1)}, f32[32,128]{1,0:T(8,128)S(1)}, u32[]{:S(2)}, u32[]{:S(2)}) collective-permute-start(f32[32,128]{1,0:T(8,128)S(1)} %get-tuple-element.32.refs_0_), channel_id=1, source_target_pairs={{0,1},{1,0},{2,3},{3,2},{4,5},{5,4},{6,7},{7,6},{8,9},{9,8},{10,11... | collective-permute-start | bytes 49160 | tf_op jit(solution)/shard_map/ppermute | solution.py:67
  69.6 3.4 %collective-permute-start.12 = (f32[32,128]{1,0:T(8,128)S(1)}, f32[32,128]{1,0:T(8,128)S(1)}, u32[]{:S(2)}, u32[]{:S(2)}) collective-permute-start(f32[32,128]{1,0:T(8,128)S(1)} %row_pass.2.refs_0_), channel_id=1, source_target_pairs={{0,3},{1,2},{2,1},{3,0},{4,7},{5,6},{6,5},{7,4},{8,11},{9,10},{10,... | collective-permute-start | bytes 49160 | tf_op jit(solution)/shard_map/ppermute | solution.py:67
  69.7 3.8 %collective-permute-start.11 = (f32[32,128]{1,0:T(8,128)S(1)}, f32[32,128]{1,0:T(8,128)S(1)}, u32[]{:S(2)}, u32[]{:S(2)}) collective-permute-start(f32[32,128]{1,0:T(8,128)S(1)} %row_pass.2.refs_0_), channel_id=1, source_target_pairs={{0,2},{1,3},{2,0},{3,1},{4,6},{5,7},{6,4},{7,5},{8,10},{9,11},{10,... | collective-permute-start | bytes 49160 | tf_op jit(solution)/shard_map/ppermute | solution.py:67
  71.2 2.3 %collective-permute-start.10 = (f32[32,128]{1,0:T(8,128)S(1)}, f32[32,128]{1,0:T(8,128)S(1)}, u32[]{:S(2)}, u32[]{:S(2)}) collective-permute-start(f32[32,128]{1,0:T(8,128)S(1)} %row_pass.2.refs_0_), channel_id=1, source_target_pairs={{0,1},{1,0},{2,3},{3,2},{4,5},{5,4},{6,7},{7,6},{8,9},{9,8},{10,11... | collective-permute-start | bytes 49160 | tf_op jit(solution)/shard_map/ppermute | solution.py:67
  86.5 3.4 %collective-permute-start.15 = (f32[32,128]{1,0:T(8,128)S(1)}, f32[32,128]{1,0:T(8,128)S(1)}, u32[]{:S(2)}, u32[]{:S(2)}) collective-permute-start(f32[32,128]{1,0:T(8,128)S(1)} %row_pass.3.refs_0_), channel_id=1, source_target_pairs={{0,3},{1,2},{2,1},{3,0},{4,7},{5,6},{6,5},{7,4},{8,11},{9,10},{10,... | collective-permute-start | bytes 49160 | tf_op jit(solution)/shard_map/ppermute | solution.py:67
  86.6 3.8 %collective-permute-start.14 = (f32[32,128]{1,0:T(8,128)S(1)}, f32[32,128]{1,0:T(8,128)S(1)}, u32[]{:S(2)}, u32[]{:S(2)}) collective-permute-start(f32[32,128]{1,0:T(8,128)S(1)} %row_pass.3.refs_0_), channel_id=1, source_target_pairs={{0,2},{1,3},{2,0},{3,1},{4,6},{5,7},{6,4},{7,5},{8,10},{9,11},{10,... | collective-permute-start | bytes 49160 | tf_op jit(solution)/shard_map/ppermute | solution.py:67
  88.1 2.3 %collective-permute-start.13 = (f32[32,128]{1,0:T(8,128)S(1)}, f32[32,128]{1,0:T(8,128)S(1)}, u32[]{:S(2)}, u32[]{:S(2)}) collective-permute-start(f32[32,128]{1,0:T(8,128)S(1)} %row_pass.3.refs_0_), channel_id=1, source_target_pairs={{0,1},{1,0},{2,3},{3,2},{4,5},{5,4},{6,7},{7,6},{8,9},{9,8},{10,11... | collective-permute-start | bytes 49160 | tf_op jit(solution)/shard_map/ppermute | solution.py:67

commit v7 on v6

--- a/solution.py
+++ b/solution.py
@@ -86,38 +86,39 @@
 
 
 def near_kernel(near_index_ref, cost_ref, plan_ref, mass_ref, totals_ref, x_ref, term_ref, plan_scr):
-    g = pl.program_id(0)
+    rows = cost_ref.shape[0]
+    first = pl.program_id(0) * rows
     near_count = cost_ref.shape[1]
     width = cost_ref.shape[2]
     slots = plan_ref.shape[2]
     wide = slots * width
-    for a in range(SUB):
+    for a in range(rows):
         plan = jnp.concatenate([plan_ref[a, 0, q] for q in range(slots)], axis=1)
         high, low = split(plan)
         plan_scr[a, 0:width, :] = high
         plan_scr[a, width : 2 * width, :] = low
         plan_scr[a, 2 * width : 3 * width, :] = high
     lanes = lax.broadcasted_iota(jnp.int32, (width, SUB), 1)
-    terms = jnp.zeros((width, SUB), jnp.float32)
-    for i in range(SUB):
-        row = g * SUB + i
-        acc = None
-        for k in range(near_count):
-            a = near_index_ref[k, row] & (SUB - 1)
-            cost = cost_ref[i, k]
-            high, low = split(cost)
-            x = jnp.dot(
-                jnp.concatenate([high, high, low], axis=1),
-                plan_scr[a],
-                preferred_element_type=jnp.float32,
-            )
-            x_high, x_low = split(x)
-            x_ref[row, 0:width, k * wide : (k + 1) * wide] = x_high
-            x_ref[row, width : 2 * width, k * wide : (k + 1) * wide] = x_low
-            weighted = cost * cost * mass_ref[pl.ds(g * SUB + a, 1), :].astype(jnp.float32)
-            acc = weighted if acc is None else acc + weighted
-        terms = jnp.where(lanes == i, jnp.sum(acc, axis=1, keepdims=True), terms)
-    term_ref[g] = terms
+    for group in range(rows // SUB):
+        terms = jnp.zeros((width, SUB), jnp.float32)
+        for i in range(group * SUB, (group + 1) * SUB):
+            acc = None
+            for k in range(near_count):
+                a = group * SUB + (near_index_ref[k, first + i] & (SUB - 1))
+                cost = cost_ref[i, k]
+                high, low = split(cost)
+                x = jnp.dot(
+                    jnp.concatenate([high, high, low], axis=1),
+                    plan_scr[a],
+                    preferred_element_type=jnp.float32,
+                )
+                x_high, x_low = split(x)
+                x_ref[first + i, 0:width, k * wide : (k + 1) * wide] = x_high
+                x_ref[first + i, width : 2 * width, k * wide : (k + 1) * wide] = x_low
+                weighted = cost * cost * mass_ref[pl.ds(first + a, 1), :].astype(jnp.float32)
+                acc = weighted if acc is None else acc + weighted
+            terms = jnp.where(lanes == i % SUB, jnp.sum(acc, axis=1, keepdims=True), terms)
+        term_ref[first // SUB + group] = terms
 
 
 def relay_kernel(*refs):
@@ -247,20 +248,16 @@
     potential_scr[...] = scaled
     potential_ref[...] = scaled * from_log2
 
-    def some_rows(g, _):
-        first = pl.multiple_of(g * together, together)
-        tall = potential_scr[pl.ds(first, together), :].T
+    for first in range(0, rows, together):
+        tall = potential_scr[first : first + together, :].T
         for i in range(together):
             for l in range(slots):
                 score = tall[:, i : i + 1] + work_ref[first + i, l]
                 peak = jnp.max(score, axis=0, keepdims=True)
                 total = jnp.sum(jnp.exp2(score - peak), axis=0, keepdims=True)
                 place = (first + i) * slots + l
-                peak_scr[pl.ds(place, 1), :] = peak
-                sum_scr[pl.ds(place, 1), :] = total
-        return 0
-
-    lax.fori_loop(0, rows // together, some_rows, 0)
+                peak_scr[place : place + 1, :] = peak
+                sum_scr[place : place + 1, :] = total
     select = select_ref[...]
     peaks = peak_scr[...]
     sums = sum_scr[...]
@@ -282,19 +279,13 @@
     row_devices, slot_ref, tall_ref, log_mass_ref, parts_ref, out_ref, wide_scr, peak_scr, sum_scr
 ):
     rows, slots, width, _ = tall_ref.shape
-    together = math.gcd(rows, 8)
     potential = (log_mass_ref[...] - log_sum(parts_of(parts_ref, row_devices))).T
     for t in range(wide_scr.shape[0]):
         wide_scr[t] = jnp.broadcast_to(potential[:, t : t + 1], (width, width))
 
-    def some_rows(g, _):
-        for i in range(together):
-            row = g * together + i
-            scores = [wide_scr[slot_ref[l, row]] + tall_ref[row, l] for l in range(slots)]
-            row_pass(scores, row, peak_scr, sum_scr)
-        return 0
-
-    lax.fori_loop(0, rows // together, some_rows, 0)
+    for row in range(rows):
+        scores = [wide_scr[slot_ref[l, row]] + tall_ref[row, l] for l in range(slots)]
+        row_pass(scores, row, peak_scr, sum_scr)
     out_ref[...] = peak_scr[...] + jnp.log2(sum_scr[...])
 
 
@@ -357,6 +348,7 @@
         out_shape=[jax.ShapeDtypeStruct(target_cost.shape, f32)] * half,
         input_output_aliases={e: e for e in range(half)},
         compiler_params=small,
+        cost_estimate=pl.CostEstimate(flops=0, bytes_accessed=256 * mib, transcendentals=0),
         name="relay",
     )(*[arrived[mask] for mask in direct])
     arrived.update(zip(direct, passed))
@@ -366,13 +358,14 @@
 
     wide = near_count * slots * width
     groups = rows_here // SUB
+    step_rows = 2 * SUB if groups % 2 == 0 else SUB
     x, term = pl.pallas_call(
         near_kernel,
-        grid=(groups,),
+        grid=(rows_here // step_rows,),
         in_specs=[
             SMEM,
-            pl.BlockSpec((SUB, near_count, width, width), lambda g: (g, 0, 0, 0)),
-            pl.BlockSpec((SUB, 1, slots, width, width), lambda g: (g, 0, 0, 0, 0)),
+            pl.BlockSpec((step_rows, near_count, width, width), lambda g: (g, 0, 0, 0)),
+            pl.BlockSpec((step_rows, 1, slots, width, width), lambda g: (g, 0, 0, 0, 0)),
             whole((rows_here, width)),
             ANY,
         ],
@@ -381,7 +374,7 @@
             pltpu.VMEM((rows_here, 2 * width, wide), jnp.bfloat16),
             pltpu.VMEM((groups, width, SUB), f32),
         ],
-        scratch_shapes=[pltpu.VMEM((SUB, 3 * width, slots * width), jnp.bfloat16)],
+        scratch_shapes=[pltpu.VMEM((step_rows, 3 * width, slots * width), jnp.bfloat16)],
         compiler_params=pltpu.CompilerParams(vmem_limit_bytes=12 * mib),
         cost_estimate=pl.CostEstimate(
             flops=6 * rows_here * wide * width * width,
@@ -392,7 +385,6 @@
     )(near_t, in_hbm(near_cost), in_hbm(coupling), mass, packs)
 
     far_bytes = group_blocks * link_count * width * width * 4
-    step_rows = SUB
     steps = rows_here // step_rows
     cost_block = pl.BlockSpec((step_rows, 1, slots, width, width), lambda g: (g, 0, 0, 0, 0))
     work_shape = pltpu.VMEM((rows_here, slots, width, width), f32)

time: 102 us -> 98.5 us (0.966)
  Pallas kernels: 32 us -> 26.8 us
  waiting for transfers between devices: 17.7 us -> 19.3 us
    pallas_call x3, Pallas kernels: 5.71 us -> 3.69 us  [column_step(): pl.pallas_call(functools.partial(column_kernel, col_devices, copies), in_...]
    ppermute x16, waiting for transfers between devices: 17.7 us -> 19.3 us  [send(): return lax.ppermute(x, axis, [(d, d ^ mask) for d in range(size)])]
    pallas_call x1, Pallas kernels: 9.14 us -> 7.67 us  [per_device(): pl.pallas_call(near_kernel, grid=(rows_here // step_rows,), in_specs=[SME...]
    pallas_call x1, Pallas kernels: 11 us -> 9.68 us  [per_device(): pl.pallas_call(functools.partial(far_kernel, (row_devices, col_devices, t...]
  transfers between devices with their start and end apart: 17 -> 17, of which waited for: 8 -> 9; matrix products, arithmetic and copies ran while one was open for 0% -> 0% of each run, Pallas kernels for 9% -> 8%
where the time goes in v7:
time: 98.5 us; the launch traced here: 97.9 us
  blocking collectives  28.4 us (29%)
  Pallas kernels  26.8 us (27%)
  starting transfers between devices  22.8 us (23%)
  waiting for transfers between devices  19.3 us (20%)
    all_to_all x3, blocking collectives, exchange(): return lax.all_to_all(copies, axis, 0, 0, tiled=True)  28.4 us
    ppermute x16, waiting for transfers between devices, send(): return lax.ppermute(x, axis, [(d, d ^ mask) for d in range(size)])  19.3 us
    ppermute x16, starting transfers between devices, send(): return lax.ppermute(x, axis, [(d, d ^ mask) for d in range(size)])  15.5 us
    pallas_call x1, Pallas kernels, per_device(): pl.pallas_call(functools.partial(far_kernel, (row_devices, col_devices, t...  9.68 us
    pallas_call x1, Pallas kernels, per_device(): pl.pallas_call(near_kernel, grid=(rows_here // step_rows,), in_specs=[SME...  7.67 us
    all_to_all x1, starting transfers between devices, exchange(): return lax.all_to_all(copies, axis, 0, 0, tiled=True)  7.3 us
    pallas_call x3, Pallas kernels, column_step(): pl.pallas_call(functools.partial(column_kernel, col_devices, copies), in_...  3.69 us
    pallas_call x2, Pallas kernels, row_step(): pl.pallas_call(functools.partial(row_kernel, row_devices), in_specs=[SMEM...  3.69 us
  transfers between devices with their start and end apart: 17, of which 9 were waited for; matrix products, arithmetic and copies ran while one was open for 0% of the time, Pallas kernels for 8%

profile of v7, /device:TPU:0, one launch (start us, length us, event | category | flops | bytes accessed | tf_op | source)
XLA Modules:
  0.0 97.9 jit_solution(11385359522600498729)
XLA Ops:
  0.6 1.5 %pack.1 = f32[256,128]{1,0:T(8,128)} custom-call(s32[32,128]{1,0:T(8,128)} %bitcast.25, s32[1,128]{1,0:T(1,128)} %target_ref.1), custom_call_target="tpu_custom_call" | custom-call | tf_op jit(solution)/shard_map/pack/pallas_call | solution.py:334
  2.1 7.3 %all-to-all-start = ((f32[32,8,128]{2,1,0:T(8,128)}), f32[32,8,128]{2,1,0:T(8,128)S(1)}, u32[]{:S(2)}, u32[]{:S(2)}) async-start(f32[32,8,128]{2,1,0:T(8,128)} %bitcast.5), calls=%async_computation | async-start | bytes 262144 | tf_op jit(solution)/shard_map/all_to_all | solution.py:75
  9.4 2.7 %collective-permute-start.2 = (f32[1,1,3,128,128]{4,3,2,1,0:T(8,128)}, f32[1,1,3,128,128]{4,3,2,1,0:T(8,128)S(1)}, u32[]{:S(2)}, u32[]{:S(2)}) collective-permute-start(f32[1,1,3,128,128]{4,3,2,1,0:T(8,128)} %refs_6_.1), channel_id=1, source_target_pairs={{0,12},{4,8},{8,4},{12,0},{16,28},{20,24},{24,20},{28,16},{1,13},{... | collective-permute-start | bytes 589832 | tf_op jit(solution)/shard_map/ppermute | solution.py:67
  12.2 0.6 collective-permute-start.1
  13.0 2.7 %collective-permute-start.3 = (f32[1,1,3,128,128]{4,3,2,1,0:T(8,128)}, f32[1,1,3,128,128]{4,3,2,1,0:T(8,128)S(1)}, u32[]{:S(2)}, u32[]{:S(2)}) collective-permute-start(f32[1,1,3,128,128]{4,3,2,1,0:T(8,128)} %refs_6_.1), channel_id=1, source_target_pairs={{0,16},{4,20},{8,24},{12,28},{16,0},{20,4},{24,8},{28,12},{1,17},{... | collective-permute-start | bytes 589832 | tf_op jit(solution)/shard_map/ppermute | solution.py:67
  15.7 8.5 %collective-permute-done.2.refs_2_ = f32[1,1,3,128,128]{4,3,2,1,0:T(8,128)S(1)} collective-permute-done((f32[1,1,3,128,128]{4,3,2,1,0:T(8,128)}, f32[1,1,3,128,128]{4,3,2,1,0:T(8,128)S(1)}, u32[]{:S(2)}, u32[]{:S(2)}) %collective-permute-start.2) | collective-permute-done | bytes 196640 | tf_op jit(solution)/shard_map/ppermute | solution.py:67
  24.2 3.3 %collective-permute-done.1.refs_1_ = f32[1,1,3,128,128]{4,3,2,1,0:T(8,128)S(1)} collective-permute-done((f32[1,1,3,128,128]{4,3,2,1,0:T(8,128)}, f32[1,1,3,128,128]{4,3,2,1,0:T(8,128)S(1)}, u32[]{:S(2)}, u32[]{:S(2)}) %collective-permute-start.1) | collective-permute-done | bytes 196640 | tf_op jit(solution)/shard_map/ppermute | solution.py:67
  27.5 2.9 %collective-permute-start.6 = (f32[1,1,3,128,128]{4,3,2,1,0:T(8,128)S(1)}, f32[1,1,3,128,128]{4,3,2,1,0:T(8,128)S(1)}, u32[]{:S(2)}, u32[]{:S(2)}) collective-permute-start(f32[1,1,3,128,128]{4,3,2,1,0:T(8,128)S(1)} %get-tuple-element.25.refs_10_), channel_id=1, source_target_pairs={{0,12},{4,8},{8,4},{12,0},{16,28},{20,24},{24,20},{28,16},{1,13},{... | collective-permute-start | bytes 589832 | tf_op jit(solution)/shard_map/ppermute | solution.py:67
  30.4 0.6 collective-permute-start.4
  31.1 7.7 %near_product.1 = (bf16[32,256,768]{2,1,0:T(8,128)(2,1)S(1)}, f32[8,128,4]{2,1,0:T(8,128)S(1)}) custom-call(s32[3,32]{1,0:T(4,128)} %bitcast.31, f32[32,3,128,128]{3,2,1,0:T(8,128)} %cost_ref.1, f32[32,1,2,128,128]{4,3,2,1,0:T(8,128)} %plan_ref.1, s32[32,128]{1,0:T(8,128)} %bitcast.26, f32[256,128]{1,0:T(8,128)S(1)} %bitcast.17), custom_call_target="tpu_custom_call" | custom-call | flops 2415919104 | bytes 10485760 | tf_op jit(solution)/shard_map/near_product/pallas_call | solution.py:362
  38.8 0.6 collective-permute-done.4.refs_11_
  39.4 9.7 %far_product.1 = (f32[32,1,2,128,128]{4,3,2,1,0:T(8,128)}, f32[32,2,128,128]{3,2,1,0:T(8,128)S(1)}, f32[32,2,128,128]{3,2,1,0:T(8,128)S(1)}, f32[32,128]{1,0:T(8...) custom-call(s32[3,32]{1,0:T(4,128)} %bitcast.32, s32[2,32]{1,0:T(2,128)} %bitcast.28, ...), custom_call_target="tpu_custom_call" | custom-call | tf_op jit(solution)/shard_map/far_product/pallas_call | solution.py:391
  49.0 1.1 %collective-permute-start.9 = (f32[32,128]{1,0:T(8,128)S(1)}, f32[32,128]{1,0:T(8,128)S(1)}, u32[]{:S(2)}, u32[]{:S(2)}) collective-permute-start(f32[32,128]{1,0:T(8,128)S(1)} %get-tuple-element.32.refs_0_), channel_id=1, source_target_pairs={{0,3},{1,2},{2,1},{3,0},{4,7},{5,6},{6,5},{7,4},{8,11},{9,10},{10,... | collective-permute-start | bytes 49160 | tf_op jit(solution)/shard_map/ppermute | solution.py:67
  50.1 0.6 collective-permute-start.8
  50.9 1.3 %collective-permute-done.9.refs_3_ = f32[32,128]{1,0:T(8,128)S(1)} collective-permute-done((f32[32,128]{1,0:T(8,128)S(1)}, f32[32,128]{1,0:T(8,128)S(1)}, u32[]{:S(2)}, u32[]{:S(2)}) %collective-permute-start.9) | collective-permute-done | bytes 16416 | tf_op jit(solution)/shard_map/ppermute | solution.py:67
  52.2 1.6 %collective-permute-done.8.refs_2_ = f32[32,128]{1,0:T(8,128)S(1)} collective-permute-done((f32[32,128]{1,0:T(8,128)S(1)}, f32[32,128]{1,0:T(8,128)S(1)}, u32[]{:S(2)}, u32[]{:S(2)}) %collective-permute-start.8) | collective-permute-done | bytes 16416 | tf_op jit(solution)/shard_map/ppermute | solution.py:67
  53.8 1.2 %column_pass.3 = (f32[64,128]{1,0:T(8,128)S(1)}, f32[32,128]{1,0:T(8,128)}) custom-call(f32[32,2,128,128]{3,2,1,0:T(8,128)S(1)} %get-tuple-element.27.work_ref, s32[64,128]{1,0:T(8,128)S(1)} %get-tuple-element.28.select_ref, f32[32,128]{1,0:T(8,128)S(1)} %get-tuple-element.29.log_mass_ref, f32[32,128]{1,0:T(8,128)S(1)} %get-tuple-element.32.refs_0_, ...), custom_call_target="tpu_custom_call" | custom-call | tf_op jit(solution)/shard_map/column_pass/pallas_call | solution.py:436
  55.1 10.5 %all_to_all.44 = f32[8,8,128]{2,1,0:T(8,128)S(1)} all-to-all(f32[8,8,128]{2,1,0:T(8,128)S(1)} %bitcast.21), channel_id=1, replica_groups=mesh['rows'=8,'cols'=4] {'rows'}, dimensions={0} | all-to-all | bytes 65536 | tf_op jit(solution)/shard_map/all_to_all | solution.py:75
  65.6 1.8 %row_pass.2.refs_0_ = f32[32,128]{1,0:T(8,128)S(1)} custom-call(s32[2,32]{1,0:T(2,128)} %bitcast.29, f32[32,2,128,128]{3,2,1,0:T(8,128)S(1)} %get-tuple-element.30.tall_ref, f32[8,128]{1,0:T(8,128)S(1)} %get-tuple-element.31.log_mass_ref, f32[64,128]{1,0:T(8,128)S(1)} %bitcast.20), custom_call_target="tpu_custom_call" | custom-call | tf_op jit(solution)/shard_map/row_pass/pallas_call | solution.py:454
  67.5 0.7 collective-permute-start.11
  68.2 1.2 %collective-permute-start.10 = (f32[32,128]{1,0:T(8,128)S(1)}, f32[32,128]{1,0:T(8,128)S(1)}, u32[]{:S(2)}, u32[]{:S(2)}) collective-permute-start(f32[32,128]{1,0:T(8,128)S(1)} %row_pass.2.refs_0_), channel_id=1, source_target_pairs={{0,1},{1,0},{2,3},{3,2},{4,5},{5,4},{6,7},{7,6},{8,9},{9,8},{10,11... | collective-permute-start | bytes 49160 | tf_op jit(solution)/shard_map/ppermute | solution.py:67
  69.4 1.3 %collective-permute-done.12.refs_3_ = f32[32,128]{1,0:T(8,128)S(1)} collective-permute-done((f32[32,128]{1,0:T(8,128)S(1)}, f32[32,128]{1,0:T(8,128)S(1)}, u32[]{:S(2)}, u32[]{:S(2)}) %collective-permute-start.12) | collective-permute-done | bytes 16416 | tf_op jit(solution)/shard_map/ppermute | solution.py:67
  70.7 0.7 collective-permute-done.11.refs_2_
  71.3 1.2 %column_pass.4 = (f32[64,128]{1,0:T(8,128)S(1)}, f32[32,128]{1,0:T(8,128)}) custom-call(f32[32,2,128,128]{3,2,1,0:T(8,128)S(1)} %get-tuple-element.27.work_ref, s32[64,128]{1,0:T(8,128)S(1)} %get-tuple-element.28.select_ref, f32[32,128]{1,0:T(8,128)S(1)} %get-tuple-element.29.log_mass_ref, f32[32,128]{1,0:T(8,128)S(1)} %row_pass.2.refs_0_, ...), custom_call_target="tpu_custom_call" | custom-call | tf_op jit(solution)/shard_map/column_pass/pallas_call | solution.py:436
  72.6 9.1 %all_to_all.45 = f32[8,8,128]{2,1,0:T(8,128)S(1)} all-to-all(f32[8,8,128]{2,1,0:T(8,128)S(1)} %bitcast.22), channel_id=1, replica_groups=mesh['rows'=8,'cols'=4] {'rows'}, dimensions={0} | all-to-all | bytes 65536 | tf_op jit(solution)/shard_map/all_to_all | solution.py:75
  81.6 1.8 %row_pass.3.refs_0_ = f32[32,128]{1,0:T(8,128)S(1)} custom-call(s32[2,32]{1,0:T(2,128)} %bitcast.30, f32[32,2,128,128]{3,2,1,0:T(8,128)S(1)} %get-tuple-element.30.tall_ref, f32[8,128]{1,0:T(8,128)S(1)} %get-tuple-element.31.log_mass_ref, f32[64,128]{1,0:T(8,128)S(1)} %bitcast.19), custom_call_target="tpu_custom_call" | custom-call | tf_op jit(solution)/shard_map/row_pass/pallas_call | solution.py:454
  83.5 0.7 collective-permute-start.14
  84.2 1.2 %collective-permute-start.13 = (f32[32,128]{1,0:T(8,128)S(1)}, f32[32,128]{1,0:T(8,128)S(1)}, u32[]{:S(2)}, u32[]{:S(2)}) collective-permute-start(f32[32,128]{1,0:T(8,128)S(1)} %row_pass.3.refs_0_), channel_id=1, source_target_pairs={{0,1},{1,0},{2,3},{3,2},{4,5},{5,4},{6,7},{7,6},{8,9},{9,8},{10,11... | collective-permute-start | bytes 49160 | tf_op jit(solution)/shard_map/ppermute | solution.py:67
  85.4 1.3 %collective-permute-done.15.refs_3_ = f32[32,128]{1,0:T(8,128)S(1)} collective-permute-done((f32[32,128]{1,0:T(8,128)S(1)}, f32[32,128]{1,0:T(8,128)S(1)}, u32[]{:S(2)}, u32[]{:S(2)}) %collective-permute-start.15) | collective-permute-done | bytes 16416 | tf_op jit(solution)/shard_map/ppermute | solution.py:67
  86.7 0.7 collective-permute-done.14.refs_2_
  87.3 1.2 %column_pass.5 = (f32[8,128]{1,0:T(8,128)S(1)}, f32[32,128]{1,0:T(8,128)}) custom-call(f32[32,2,128,128]{3,2,1,0:T(8,128)S(1)} %get-tuple-element.27.work_ref, s32[64,128]{1,0:T(8,128)S(1)} %get-tuple-element.28.select_ref, f32[32,128]{1,0:T(8,128)S(1)} %get-tuple-element.29.log_mass_ref, f32[32,128]{1,0:T(8,128)S(1)} %row_pass.3.refs_0_, ...), custom_call_target="tpu_custom_call" | custom-call | tf_op jit(solution)/shard_map/column_pass/pallas_call | solution.py:436
  88.6 8.8 %all_to_all.46 = f32[8,1,128]{2,1,0:T(1,128)S(1)} all-to-all(f32[8,1,128]{2,1,0:T(1,128)S(1)} %bitcast.24), channel_id=1, replica_groups=mesh['rows'=8,'cols'=4] {'rows'}, dimensions={0} | all-to-all | bytes 8192 | tf_op jit(solution)/shard_map/all_to_all | solution.py:75
  (17 shorter events, 1.2 us)
Async XLA Ops:
  2.1 28.9 %all-to-all-start = ((f32[32,8,128]{2,1,0:T(8,128)}), f32[32,8,128]{2,1,0:T(8,128)S(1)}, u32[]{:S(2)}, u32[]{:S(2)}) async-start(f32[32,8,128]{2,1,0:T(8,128)} %bitcast.5), calls=%async_computation | async-start | bytes 262144 | tf_op jit(solution)/shard_map/all_to_all | solution.py:75
  9.4 14.8 %collective-permute-start.2 = (f32[1,1,3,128,128]{4,3,2,1,0:T(8,128)}, f32[1,1,3,128,128]{4,3,2,1,0:T(8,128)S(1)}, u32[]{:S(2)}, u32[]{:S(2)}) collective-permute-start(f32[1,1,3,128,128]{4,3,2,1,0:T(8,128)} %refs_6_.1), channel_id=1, source_target_pairs={{0,12},{4,8},{8,4},{12,0},{16,28},{20,24},{24,20},{28,16},{1,13},{... | collective-permute-start | bytes 589832 | tf_op jit(solution)/shard_map/ppermute | solution.py:67
  12.2 15.3 %collective-permute-start.1 = (f32[1,1,3,128,128]{4,3,2,1,0:T(8,128)}, f32[1,1,3,128,128]{4,3,2,1,0:T(8,128)S(1)}, u32[]{:S(2)}, u32[]{:S(2)}) collective-permute-start(f32[1,1,3,128,128]{4,3,2,1,0:T(8,128)} %refs_6_.1), channel_id=1, source_target_pairs={{0,8},{4,12},{8,0},{12,4},{16,24},{20,28},{24,16},{28,20},{1,9},{5... | collective-permute-start | bytes 589832 | tf_op jit(solution)/shard_map/ppermute | solution.py:67
  12.7 14.8 %collective-permute-start = (f32[1,1,3,128,128]{4,3,2,1,0:T(8,128)}, f32[1,1,3,128,128]{4,3,2,1,0:T(8,128)S(1)}, u32[]{:S(2)}, u32[]{:S(2)}) collective-permute-start(f32[1,1,3,128,128]{4,3,2,1,0:T(8,128)} %refs_6_.1), channel_id=1, source_target_pairs={{0,4},{4,0},{8,12},{12,8},{16,20},{20,16},{24,28},{28,24},{1,5},{5... | collective-permute-start | bytes 589832 | tf_op jit(solution)/shard_map/ppermute | solution.py:67
  13.0 14.5 %collective-permute-start.3 = (f32[1,1,3,128,128]{4,3,2,1,0:T(8,128)}, f32[1,1,3,128,128]{4,3,2,1,0:T(8,128)S(1)}, u32[]{:S(2)}, u32[]{:S(2)}) collective-permute-start(f32[1,1,3,128,128]{4,3,2,1,0:T(8,128)} %refs_6_.1), channel_id=1, source_target_pairs={{0,16},{4,20},{8,24},{12,28},{16,0},{20,4},{24,8},{28,12},{1,17},{... | collective-permute-start | bytes 589832 | tf_op jit(solution)/shard_map/ppermute | solution.py:67
  27.5 11.2 %collective-permute-start.6 = (f32[1,1,3,128,128]{4,3,2,1,0:T(8,128)S(1)}, f32[1,1,3,128,128]{4,3,2,1,0:T(8,128)S(1)}, u32[]{:S(2)}, u32[]{:S(2)}) collective-permute-start(f32[1,1,3,128,128]{4,3,2,1,0:T(8,128)S(1)} %get-tuple-element.25.refs_10_), channel_id=1, source_target_pairs={{0,12},{4,8},{8,4},{12,0},{16,28},{20,24},{24,20},{28,16},{1,13},{... | collective-permute-start | bytes 589832 | tf_op jit(solution)/shard_map/ppermute | solution.py:67
  30.4 8.3 %collective-permute-start.5 = (f32[1,1,3,128,128]{4,3,2,1,0:T(8,128)S(1)}, f32[1,1,3,128,128]{4,3,2,1,0:T(8,128)S(1)}, u32[]{:S(2)}, u32[]{:S(2)}) collective-permute-start(f32[1,1,3,128,128]{4,3,2,1,0:T(8,128)S(1)} %get-tuple-element.25.refs_10_), channel_id=1, source_target_pairs={{0,8},{4,12},{8,0},{12,4},{16,24},{20,28},{24,16},{28,20},{1,9},{5... | collective-permute-start | bytes 589832 | tf_op jit(solution)/shard_map/ppermute | solution.py:67
  30.4 8.9 %collective-permute-start.4 = (f32[1,1,3,128,128]{4,3,2,1,0:T(8,128)S(1)}, f32[1,1,3,128,128]{4,3,2,1,0:T(8,128)S(1)}, u32[]{:S(2)}, u32[]{:S(2)}) collective-permute-start(f32[1,1,3,128,128]{4,3,2,1,0:T(8,128)S(1)} %get-tuple-element.25.refs_10_), channel_id=1, source_target_pairs={{0,4},{4,0},{8,12},{12,8},{16,20},{20,16},{24,28},{28,24},{1,5},{5... | collective-permute-start | bytes 589832 | tf_op jit(solution)/shard_map/ppermute | solution.py:67
  31.0 8.3 %copy-start = (f32[1,1,3,128,128]{4,3,2,1,0:T(8,128)S(1)}, f32[1,1,3,128,128]{4,3,2,1,0:T(8,128)}, u32[]{:S(2)}) copy-start(f32[1,1,3,128,128]{4,3,2,1,0:T(8,128)} %refs_6_.1) | copy-start | bytes 589828
  49.0 3.2 %collective-permute-start.9 = (f32[32,128]{1,0:T(8,128)S(1)}, f32[32,128]{1,0:T(8,128)S(1)}, u32[]{:S(2)}, u32[]{:S(2)}) collective-permute-start(f32[32,128]{1,0:T(8,128)S(1)} %get-tuple-element.32.refs_0_), channel_id=1, source_target_pairs={{0,3},{1,2},{2,1},{3,0},{4,7},{5,6},{6,5},{7,4},{8,11},{9,10},{10,... | collective-permute-start | bytes 49160 | tf_op jit(solution)/shard_map/ppermute | solution.py:67
  50.1 3.7 %collective-permute-start.8 = (f32[32,128]{1,0:T(8,128)S(1)}, f32[32,128]{1,0:T(8,128)S(1)}, u32[]{:S(2)}, u32[]{:S(2)}) collective-permute-start(f32[32,128]{1,0:T(8,128)S(1)} %get-tuple-element.32.refs_0_), channel_id=1, source_target_pairs={{0,2},{1,3},{2,0},{3,1},{4,6},{5,7},{6,4},{7,5},{8,10},{9,11},{10,... | collective-permute-start | bytes 49160 | tf_op jit(solution)/shard_map/ppermute | solution.py:67
  50.7 3.2 %collective-permute-start.7 = (f32[32,128]{1,0:T(8,128)S(1)}, f32[32,128]{1,0:T(8,128)S(1)}, u32[]{:S(2)}, u32[]{:S(2)}) collective-permute-start(f32[32,128]{1,0:T(8,128)S(1)} %get-tuple-element.32.refs_0_), channel_id=1, source_target_pairs={{0,1},{1,0},{2,3},{3,2},{4,5},{5,4},{6,7},{7,6},{8,9},{9,8},{10,11... | collective-permute-start | bytes 49160 | tf_op jit(solution)/shard_map/ppermute | solution.py:67
  67.4 3.2 %collective-permute-start.12 = (f32[32,128]{1,0:T(8,128)S(1)}, f32[32,128]{1,0:T(8,128)S(1)}, u32[]{:S(2)}, u32[]{:S(2)}) collective-permute-start(f32[32,128]{1,0:T(8,128)S(1)} %row_pass.2.refs_0_), channel_id=1, source_target_pairs={{0,3},{1,2},{2,1},{3,0},{4,7},{5,6},{6,5},{7,4},{8,11},{9,10},{10,... | collective-permute-start | bytes 49160 | tf_op jit(solution)/shard_map/ppermute | solution.py:67
  67.5 3.8 %collective-permute-start.11 = (f32[32,128]{1,0:T(8,128)S(1)}, f32[32,128]{1,0:T(8,128)S(1)}, u32[]{:S(2)}, u32[]{:S(2)}) collective-permute-start(f32[32,128]{1,0:T(8,128)S(1)} %row_pass.2.refs_0_), channel_id=1, source_target_pairs={{0,2},{1,3},{2,0},{3,1},{4,6},{5,7},{6,4},{7,5},{8,10},{9,11},{10,... | collective-permute-start | bytes 49160 | tf_op jit(solution)/shard_map/ppermute | solution.py:67
  68.2 3.1 %collective-permute-start.10 = (f32[32,128]{1,0:T(8,128)S(1)}, f32[32,128]{1,0:T(8,128)S(1)}, u32[]{:S(2)}, u32[]{:S(2)}) collective-permute-start(f32[32,128]{1,0:T(8,128)S(1)} %row_pass.2.refs_0_), channel_id=1, source_target_pairs={{0,1},{1,0},{2,3},{3,2},{4,5},{5,4},{6,7},{7,6},{8,9},{9,8},{10,11... | collective-permute-start | bytes 49160 | tf_op jit(solution)/shard_map/ppermute | solution.py:67
  83.5 3.2 %collective-permute-start.15 = (f32[32,128]{1,0:T(8,128)S(1)}, f32[32,128]{1,0:T(8,128)S(1)}, u32[]{:S(2)}, u32[]{:S(2)}) collective-permute-start(f32[32,128]{1,0:T(8,128)S(1)} %row_pass.3.refs_0_), channel_id=1, source_target_pairs={{0,3},{1,2},{2,1},{3,0},{4,7},{5,6},{6,5},{7,4},{8,11},{9,10},{10,... | collective-permute-start | bytes 49160 | tf_op jit(solution)/shard_map/ppermute | solution.py:67
  83.5 3.8 %collective-permute-start.14 = (f32[32,128]{1,0:T(8,128)S(1)}, f32[32,128]{1,0:T(8,128)S(1)}, u32[]{:S(2)}, u32[]{:S(2)}) collective-permute-start(f32[32,128]{1,0:T(8,128)S(1)} %row_pass.3.refs_0_), channel_id=1, source_target_pairs={{0,2},{1,3},{2,0},{3,1},{4,6},{5,7},{6,4},{7,5},{8,10},{9,11},{10,... | collective-permute-start | bytes 49160 | tf_op jit(solution)/shard_map/ppermute | solution.py:67
  84.2 3.1 %collective-permute-start.13 = (f32[32,128]{1,0:T(8,128)S(1)}, f32[32,128]{1,0:T(8,128)S(1)}, u32[]{:S(2)}, u32[]{:S(2)}) collective-permute-start(f32[32,128]{1,0:T(8,128)S(1)} %row_pass.3.refs_0_), channel_id=1, source_target_pairs={{0,1},{1,0},{2,3},{3,2},{4,5},{5,4},{6,7},{7,6},{8,9},{9,8},{10,11... | collective-permute-start | bytes 49160 | tf_op jit(solution)/shard_map/ppermute | solution.py:67

commit v8 on v7

--- a/solution.py
+++ b/solution.py
@@ -51,17 +51,6 @@
     return peak + jnp.log2(tree([jnp.exp2(p - peak) for p in parts], jnp.add))
 
 
-def parts_of(ref, devices):
-    rows = ref.shape[0] // devices
-    return [ref[d * rows : (d + 1) * rows, :] for d in range(devices)]
-
-
-def put_copies(ref, devices, value):
-    rows = value.shape[0]
-    for d in range(devices):
-        ref[d * rows : (d + 1) * rows, :] = value
-
-
 def send(x, axis, mask):
     size = lax.axis_size(axis)
     return lax.ppermute(x, axis, [(d, d ^ mask) for d in range(size)])
@@ -79,7 +68,6 @@
     rows = out_ref.shape[0] // devices
     total = jnp.sum(source_ref[...].astype(jnp.float32), axis=(0, 1), keepdims=True)
     target = target_ref[...].astype(jnp.float32)
-    out_ref[...] = jnp.zeros_like(out_ref)
     for d in range(devices):
         out_ref[d * rows : d * rows + 1, :] = jnp.broadcast_to(total, (1, out_ref.shape[1]))
         out_ref[d * rows + 1 : d * rows + 1 + target.shape[0], :] = target
@@ -239,7 +227,7 @@
     sum_scr[pl.ds(row, 1), :] = jnp.sum(total, axis=0, keepdims=True)
 
 
-def column_kernel(col_devices, copies, work_ref, select_ref, log_mass_ref, *refs):
+def column_kernel(col_devices, work_ref, select_ref, log_mass_ref, *refs):
     parts = refs[:col_devices]
     out_ref, potential_ref, potential_scr, peak_scr, sum_scr = refs[col_devices:]
     rows, slots, width, _ = work_ref.shape
@@ -261,8 +249,7 @@
     select = select_ref[...]
     peaks = peak_scr[...]
     sums = sum_scr[...]
-    blocks = out_ref.shape[0] // copies
-    for t in range(blocks):
+    for t in range(out_ref.shape[0]):
         chosen = select == t
         peak = jnp.max(jnp.where(chosen, peaks, very_low), axis=0, keepdims=True)
         shifted = jnp.where(chosen, sums * jnp.exp2(jnp.minimum(peaks - peak, 0.0)), 0.0)
@@ -271,15 +258,12 @@
         out_ref[t : t + 1, :] = jnp.where(
             some, peak + jnp.log2(jnp.where(some, total, 1.0)), very_low
         )
-    if copies > 1:
-        put_copies(out_ref, copies, out_ref[0:blocks, :])
-
-
-def row_kernel(
-    row_devices, slot_ref, tall_ref, log_mass_ref, parts_ref, out_ref, wide_scr, peak_scr, sum_scr
-):
+
+
+def row_kernel(slot_ref, tall_ref, log_mass_ref, *refs):
+    parts, (out_ref, wide_scr, peak_scr, sum_scr) = refs[:-4], refs[-4:]
     rows, slots, width, _ = tall_ref.shape
-    potential = (log_mass_ref[...] - log_sum(parts_of(parts_ref, row_devices))).T
+    potential = (log_mass_ref[...] - log_sum([p[...] for p in parts])).T
     for t in range(wide_scr.shape[0]):
         wide_scr[t] = jnp.broadcast_to(potential[:, t : t + 1], (width, width))
 
@@ -289,11 +273,15 @@
     out_ref[...] = peak_scr[...] + jnp.log2(sum_scr[...])
 
 
-def last_kernel(row_devices, row_axis, log_mass_ref, parts_ref, out_ref):
+def join_kernel(first_ref, second_ref, out_ref):
+    out_ref[...] = log_sum([first_ref[...], second_ref[...]])
+
+
+def last_kernel(row_axis, log_mass_ref, *refs):
+    parts, out_ref, scr = refs[:-2], refs[-2], refs[-1]
     here = out_ref.shape[0]
-    start = lax.axis_index(row_axis) * here
-    log_mass = log_mass_ref[pl.ds(start, here), :]
-    out_ref[...] = (log_mass - log_sum(parts_of(parts_ref, row_devices))) * from_log2
+    scr[...] = (log_mass_ref[...] - log_sum([p[...] for p in parts])) * from_log2
+    out_ref[...] = scr[pl.ds(lax.axis_index(row_axis) * here, here), :]
 
 
 def per_device(
@@ -329,7 +317,7 @@
     mass = in_hbm(source_weights.reshape(rows_here, width))
     small = pltpu.CompilerParams(vmem_limit_bytes=4 * mib)
 
-    pack_rows = 8 * pl.cdiv(1 + target_here, 8)
+    pack_rows = 1 + target_here
     devices = row_devices * col_devices
     pack = pl.pallas_call(
         functools.partial(pack_kernel, devices),
@@ -348,7 +336,7 @@
         out_shape=[jax.ShapeDtypeStruct(target_cost.shape, f32)] * half,
         input_output_aliases={e: e for e in range(half)},
         compiler_params=small,
-        cost_estimate=pl.CostEstimate(flops=0, bytes_accessed=256 * mib, transcendentals=0),
+        cost_estimate=pl.CostEstimate(flops=10**11, bytes_accessed=256 * mib, transcendentals=0),
         name="relay",
     )(*[arrived[mask] for mask in direct])
     arrived.update(zip(direct, passed))
@@ -432,13 +420,13 @@
 
     pass_params = pltpu.CompilerParams(vmem_limit_bytes=12 * mib)
 
-    def column_step(row_parts, copies):
+    def column_step(row_parts):
         return pl.pallas_call(
-            functools.partial(column_kernel, col_devices, copies),
+            functools.partial(column_kernel, col_devices),
             in_specs=[VMEM] * (3 + col_devices),
             out_specs=[VMEM, VMEM],
             out_shape=[
-                jax.ShapeDtypeStruct((copies * group_blocks, width), f32),
+                jax.ShapeDtypeStruct((group_blocks, width), f32),
                 jax.ShapeDtypeStruct((rows_here, width), f32),
             ],
             scratch_shapes=[
@@ -450,10 +438,19 @@
             name="column_pass",
         )(in_vmem(work), select, log_source, *row_parts)
 
+    def from_rows(part):
+        part = pl.pallas_call(
+            join_kernel,
+            out_shape=jax.ShapeDtypeStruct(part.shape, f32),
+            compiler_params=small,
+            name="join",
+        )(part, send(part, "rows", 1))
+        return [part] + [send(part, "rows", mask) for mask in range(2, row_devices, 2)]
+
     def row_step(column_parts):
         return pl.pallas_call(
-            functools.partial(row_kernel, row_devices),
-            in_specs=[SMEM, VMEM, VMEM, VMEM],
+            row_kernel,
+            in_specs=[SMEM, VMEM, VMEM] + [VMEM] * len(column_parts),
             out_specs=VMEM,
             out_shape=jax.ShapeDtypeStruct((rows_here, width), f32),
             scratch_shapes=[
@@ -463,22 +460,20 @@
             ],
             compiler_params=pass_params,
             name="row_pass",
-        )(slot_t, in_vmem(tall), log_target, column_parts)
+        )(slot_t, in_vmem(tall), log_target, *column_parts)
 
     for step in range(ITERS):
-        last = step == ITERS - 1
-        column_part, source_potential = column_step(
-            from_all(row_part, "cols"), 1 if last else row_devices
-        )
-        column_parts = exchange(column_part, "rows")
-        if not last:
+        column_part, source_potential = column_step(from_all(row_part, "cols"))
+        column_parts = from_rows(column_part)
+        if step < ITERS - 1:
             row_part = row_step(column_parts)
     own_target = pl.pallas_call(
-        functools.partial(last_kernel, row_devices, "rows"),
+        functools.partial(last_kernel, "rows"),
         out_shape=jax.ShapeDtypeStruct((target_here, width), f32),
+        scratch_shapes=[pltpu.VMEM((group_blocks, width), f32)],
         compiler_params=small,
         name="last_potential",
-    )(log_target, column_parts)
+    )(log_target, *column_parts)
     return (
         cost_blocks,
         source_potential.reshape(rows_here * width),

time: 98.5 us -> 92.1 us (0.935)
  blocking collectives: 28.4 us -> 0 us
  starting transfers between devices: 22.8 us -> 36.7 us
  waiting for transfers between devices: 19.3 us -> 27.5 us
    all_to_all x3 -> x0, blocking collectives: 28.4 us -> none  [exchange(): return lax.all_to_all(copies, axis, 0, 0, tiled=True)]
    ppermute x16 -> x28, starting transfers between devices: 15.5 us -> 32.9 us  [send(): return lax.ppermute(x, axis, [(d, d ^ mask) for d in range(size)])]
    ppermute x16 -> x28, waiting for transfers between devices: 19.3 us -> 27.5 us  [send(): return lax.ppermute(x, axis, [(d, d ^ mask) for d in range(size)])]
    all_to_all x1, starting transfers between devices: 7.3 us -> 3.82 us  [exchange(): return lax.all_to_all(copies, axis, 0, 0, tiled=True)]
    pallas_call x6 -> x9, Pallas kernels: 7.91 us -> 7.92 us  [the longest x2 3.68 us: row_step(): pl.pallas_call(row_kernel, in_specs=[SMEM, VMEM, VMEM] + [VMEM] * len(col...]
  transfers between devices with their start and end apart: 17 -> 29, of which waited for: 9 -> 17; matrix products, arithmetic and copies ran while one was open for 0% -> 0% of each run, Pallas kernels for 8% -> 10%
where the time goes in v8:
time: 92.1 us; the launch traced here: 91.7 us
  starting transfers between devices  36.7 us (40%)
  waiting for transfers between devices  27.5 us (30%)
  Pallas kernels  26.8 us (29%)
    ppermute x28, starting transfers between devices, send(): return lax.ppermute(x, axis, [(d, d ^ mask) for d in range(size)])  32.9 us
    ppermute x28, waiting for transfers between devices, send(): return lax.ppermute(x, axis, [(d, d ^ mask) for d in range(size)])  27.5 us
    pallas_call x1, Pallas kernels, per_device(): pl.pallas_call(functools.partial(far_kernel, (row_devices, col_devices, t...  9.72 us
    pallas_call x1, Pallas kernels, per_device(): pl.pallas_call(near_kernel, grid=(rows_here // step_rows,), in_specs=[SME...  7.67 us
    all_to_all x1, starting transfers between devices, exchange(): return lax.all_to_all(copies, axis, 0, 0, tiled=True)  3.82 us
    pallas_call x2, Pallas kernels, row_step(): pl.pallas_call(row_kernel, in_specs=[SMEM, VMEM, VMEM] + [VMEM] * len(col...  3.68 us
    pallas_call x3, Pallas kernels, column_step(): pl.pallas_call(functools.partial(column_kernel, col_devices), in_specs=[V...  3.67 us
  transfers between devices with their start and end apart: 29, of which 17 were waited for; matrix products, arithmetic and copies ran while one was open for 0% of the time, Pallas kernels for 10%

profile of v8, /device:TPU:0, one launch (start us, length us, event | category | flops | bytes accessed | tf_op | source)
XLA Modules:
  0.0 91.7 jit_solution(3484503759951663822)
XLA Ops:
  0.6 4.0 %collective-permute-start.2 = (f32[1,1,3,128,128]{4,3,2,1,0:T(8,128)}, f32[1,1,3,128,128]{4,3,2,1,0:T(8,128)S(1)}, u32[]{:S(2)}, u32[]{:S(2)}) collective-permute-start(f32[1,1,3,128,128]{4,3,2,1,0:T(8,128)} %refs_6_.1), channel_id=1, source_target_pairs={{0,12},{4,8},{8,4},{12,0},{16,28},{20,24},{24,20},{28,16},{1,13},{... | collective-permute-start | bytes 589832 | tf_op jit(solution)/shard_map/ppermute | solution.py:56
  5.3 2.9 %collective-permute-start.3 = (f32[1,1,3,128,128]{4,3,2,1,0:T(8,128)}, f32[1,1,3,128,128]{4,3,2,1,0:T(8,128)S(1)}, u32[]{:S(2)}, u32[]{:S(2)}) collective-permute-start(f32[1,1,3,128,128]{4,3,2,1,0:T(8,128)} %refs_6_.1), channel_id=1, source_target_pairs={{0,16},{4,20},{8,24},{12,28},{16,0},{20,4},{24,8},{28,12},{1,17},{... | collective-permute-start | bytes 589832 | tf_op jit(solution)/shard_map/ppermute | solution.py:56
  8.2 1.5 %pack.1 = f32[64,128]{1,0:T(8,128)} custom-call(s32[32,128]{1,0:T(8,128)} %bitcast.11, s32[1,128]{1,0:T(1,128)} %target_ref.1), custom_call_target="tpu_custom_call" | custom-call | tf_op jit(solution)/shard_map/pack/pallas_call | solution.py:322
  9.7 3.8 %all-to-all-start = ((f32[32,2,128]{2,1,0:T(2,128)}), f32[32,2,128]{2,1,0:T(2,128)S(1)}, u32[]{:S(2)}, u32[]{:S(2)}) async-start(f32[32,2,128]{2,1,0:T(2,128)} %bitcast.5), calls=%async_computation | async-start | bytes 65536 | tf_op jit(solution)/shard_map/all_to_all | solution.py:64
  13.5 1.3 %collective-permute-done.2.refs_2_ = f32[1,1,3,128,128]{4,3,2,1,0:T(8,128)S(1)} collective-permute-done((f32[1,1,3,128,128]{4,3,2,1,0:T(8,128)}, f32[1,1,3,128,128]{4,3,2,1,0:T(8,128)S(1)}, u32[]{:S(2)}, u32[]{:S(2)}) %collective-permute-start.2) | collective-permute-done | bytes 196640 | tf_op jit(solution)/shard_map/ppermute | solution.py:56
  14.9 3.7 %collective-permute-done.1.refs_1_ = f32[1,1,3,128,128]{4,3,2,1,0:T(8,128)S(1)} collective-permute-done((f32[1,1,3,128,128]{4,3,2,1,0:T(8,128)}, f32[1,1,3,128,128]{4,3,2,1,0:T(8,128)S(1)}, u32[]{:S(2)}, u32[]{:S(2)}) %collective-permute-start.1) | collective-permute-done | bytes 196640 | tf_op jit(solution)/shard_map/ppermute | solution.py:56
  18.6 2.6 %collective-permute-start.6 = (f32[1,1,3,128,128]{4,3,2,1,0:T(8,128)S(1)}, f32[1,1,3,128,128]{4,3,2,1,0:T(8,128)S(1)}, u32[]{:S(2)}, u32[]{:S(2)}) collective-permute-start(f32[1,1,3,128,128]{4,3,2,1,0:T(8,128)S(1)} %get-tuple-element.25.refs_10_), channel_id=1, source_target_pairs={{0,12},{4,8},{8,4},{12,0},{16,28},{20,24},{24,20},{28,16},{1,13},{... | collective-permute-start | bytes 589832 | tf_op jit(solution)/shard_map/ppermute | solution.py:56
  21.3 1.5 %collective-permute-start.4 = (f32[1,1,3,128,128]{4,3,2,1,0:T(8,128)S(1)}, f32[1,1,3,128,128]{4,3,2,1,0:T(8,128)S(1)}, u32[]{:S(2)}, u32[]{:S(2)}) collective-permute-start(f32[1,1,3,128,128]{4,3,2,1,0:T(8,128)S(1)} %get-tuple-element.25.refs_10_), channel_id=1, source_target_pairs={{0,4},{4,0},{8,12},{12,8},{16,20},{20,16},{24,28},{28,24},{1,5},{5... | collective-permute-start | bytes 589832 | tf_op jit(solution)/shard_map/ppermute | solution.py:56
  22.8 7.7 %near_product.1 = (bf16[32,256,768]{2,1,0:T(8,128)(2,1)S(1)}, f32[8,128,4]{2,1,0:T(8,128)S(1)}) custom-call(s32[3,32]{1,0:T(4,128)} %bitcast.17, f32[32,3,128,128]{3,2,1,0:T(8,128)} %cost_ref.1, f32[32,1,2,128,128]{4,3,2,1,0:T(8,128)} %plan_ref.1, s32[32,128]{1,0:T(8,128)} %bitcast.12, f32[64,128]{1,0:T(8,128)S(1)} %bitcast.9), custom_call_target="tpu_custom_call" | custom-call | flops 2415919104 | bytes 10485760 | tf_op jit(solution)/shard_map/near_product/pallas_call | solution.py:350
  30.5 9.7 %far_product.1 = (f32[32,1,2,128,128]{4,3,2,1,0:T(8,128)}, f32[32,2,128,128]{3,2,1,0:T(8,128)S(1)}, f32[32,2,128,128]{3,2,1,0:T(8,128)S(1)}, f32[32,128]{1,0:T(8...) custom-call(s32[3,32]{1,0:T(4,128)} %bitcast.18, s32[2,32]{1,0:T(2,128)} %bitcast.14, ...), custom_call_target="tpu_custom_call" | custom-call | tf_op jit(solution)/shard_map/far_product/pallas_call | solution.py:379
  40.2 1.5 %collective-permute-start.8 = (f32[32,128]{1,0:T(8,128)S(1)}, f32[32,128]{1,0:T(8,128)S(1)}, u32[]{:S(2)}, u32[]{:S(2)}) collective-permute-start(f32[32,128]{1,0:T(8,128)S(1)} %get-tuple-element.32.refs_0_), channel_id=1, source_target_pairs={{0,2},{1,3},{2,0},{3,1},{4,6},{5,7},{6,4},{7,5},{8,10},{9,11},{10,... | collective-permute-start | bytes 49160 | tf_op jit(solution)/shard_map/ppermute | solution.py:56
  42.1 1.4 %collective-permute-done.9.refs_3_ = f32[32,128]{1,0:T(8,128)S(1)} collective-permute-done((f32[32,128]{1,0:T(8,128)S(1)}, f32[32,128]{1,0:T(8,128)S(1)}, u32[]{:S(2)}, u32[]{:S(2)}) %collective-permute-start.9) | collective-permute-done | bytes 16416 | tf_op jit(solution)/shard_map/ppermute | solution.py:56
  44.0 1.2 %column_pass.3 = (f32[8,128]{1,0:T(8,128)S(1)}, f32[32,128]{1,0:T(8,128)}) custom-call(f32[32,2,128,128]{3,2,1,0:T(8,128)S(1)} %get-tuple-element.27.work_ref, s32[64,128]{1,0:T(8,128)S(1)} %get-tuple-element.28.select_ref, f32[32,128]{1,0:T(8,128)S(1)} %get-tuple-element.29.log_mass_ref, f32[32,128]{1,0:T(8,128)S(1)} %get-tuple-element.32.refs_0_, ...), custom_call_target="tpu_custom_call" | custom-call | tf_op jit(solution)/shard_map/column_pass/pallas_call | solution.py:424
  46.1 2.8 %collective-permute-done.10.second_ref = f32[8,128]{1,0:T(8,128)S(1)} collective-permute-done((f32[8,128]{1,0:T(8,128)S(1)}, f32[8,128]{1,0:T(8,128)S(1)}, u32[]{:S(2)}, u32[]{:S(2)}) %collective-permute-start.10) | collective-permute-done | bytes 4128 | tf_op jit(solution)/shard_map/ppermute | solution.py:56
  48.9 3.2 %collective-permute-start.13 = (f32[8,128]{1,0:T(8,128)S(1)}, f32[8,128]{1,0:T(8,128)S(1)}, u32[]{:S(2)}, u32[]{:S(2)}) collective-permute-start(f32[8,128]{1,0:T(8,128)S(1)} %join.3.refs_0_), channel_id=1, source_target_pairs={{0,24},{4,28},{8,16},{12,20},{16,8},{20,12},{24,0},{28,4},{1,25},{... | collective-permute-start | bytes 12296 | tf_op jit(solution)/shard_map/ppermute | solution.py:56
  53.4 1.0 %collective-permute-done.13.refs_3_ = f32[8,128]{1,0:T(8,128)S(1)} collective-permute-done((f32[8,128]{1,0:T(8,128)S(1)}, f32[8,128]{1,0:T(8,128)S(1)}, u32[]{:S(2)}, u32[]{:S(2)}) %collective-permute-start.13) | collective-permute-done | bytes 4128 | tf_op jit(solution)/shard_map/ppermute | solution.py:56
  54.4 2.3 %collective-permute-done.12.refs_2_ = f32[8,128]{1,0:T(8,128)S(1)} collective-permute-done((f32[8,128]{1,0:T(8,128)S(1)}, f32[8,128]{1,0:T(8,128)S(1)}, u32[]{:S(2)}, u32[]{:S(2)}) %collective-permute-start.12) | collective-permute-done | bytes 4128 | tf_op jit(solution)/shard_map/ppermute | solution.py:56
  56.7 1.8 %row_pass.2.refs_0_ = f32[32,128]{1,0:T(8,128)S(1)} custom-call(s32[2,32]{1,0:T(2,128)} %bitcast.15, f32[32,2,128,128]{3,2,1,0:T(8,128)S(1)} %get-tuple-element.30.tall_ref, f32[8,128]{1,0:T(8,128)S(1)} %get-tuple-element.31.log_mass_ref, f32[8,128]{1,0:T(8,128)S(1)} %join.3.refs_0_, f32[8,128]{1,0:T(8,128)S(1)} %collective-permute-done.11.refs_1_, ...), custom_call_target="tpu_custom_call" | custom-call | tf_op jit(solution)/shard_map/row_pass/pallas_call | solution.py:451
  58.6 1.6 %collective-permute-start.15 = (f32[32,128]{1,0:T(8,128)S(1)}, f32[32,128]{1,0:T(8,128)S(1)}, u32[]{:S(2)}, u32[]{:S(2)}) collective-permute-start(f32[32,128]{1,0:T(8,128)S(1)} %row_pass.2.refs_0_), channel_id=1, source_target_pairs={{0,2},{1,3},{2,0},{3,1},{4,6},{5,7},{6,4},{7,5},{8,10},{9,11},{10,... | collective-permute-start | bytes 49160 | tf_op jit(solution)/shard_map/ppermute | solution.py:56
  60.4 1.4 %collective-permute-done.16.refs_3_ = f32[32,128]{1,0:T(8,128)S(1)} collective-permute-done((f32[32,128]{1,0:T(8,128)S(1)}, f32[32,128]{1,0:T(8,128)S(1)}, u32[]{:S(2)}, u32[]{:S(2)}) %collective-permute-start.16) | collective-permute-done | bytes 16416 | tf_op jit(solution)/shard_map/ppermute | solution.py:56
  62.4 1.2 %column_pass.4 = (f32[8,128]{1,0:T(8,128)S(1)}, f32[32,128]{1,0:T(8,128)}) custom-call(f32[32,2,128,128]{3,2,1,0:T(8,128)S(1)} %get-tuple-element.27.work_ref, s32[64,128]{1,0:T(8,128)S(1)} %get-tuple-element.28.select_ref, f32[32,128]{1,0:T(8,128)S(1)} %get-tuple-element.29.log_mass_ref, f32[32,128]{1,0:T(8,128)S(1)} %row_pass.2.refs_0_, ...), custom_call_target="tpu_custom_call" | custom-call | tf_op jit(solution)/shard_map/column_pass/pallas_call | solution.py:424
  64.2 3.1 %collective-permute-done.17.second_ref = f32[8,128]{1,0:T(8,128)S(1)} collective-permute-done((f32[8,128]{1,0:T(8,128)S(1)}, f32[8,128]{1,0:T(8,128)S(1)}, u32[]{:S(2)}, u32[]{:S(2)}) %collective-permute-start.17) | collective-permute-done | bytes 4128 | tf_op jit(solution)/shard_map/ppermute | solution.py:56
  67.3 1.5 %collective-permute-start.20 = (f32[8,128]{1,0:T(8,128)S(1)}, f32[8,128]{1,0:T(8,128)S(1)}, u32[]{:S(2)}, u32[]{:S(2)}) collective-permute-start(f32[8,128]{1,0:T(8,128)S(1)} %join.4.refs_0_), channel_id=1, source_target_pairs={{0,24},{4,28},{8,16},{12,20},{16,8},{20,12},{24,0},{28,4},{1,25},{... | collective-permute-start | bytes 12296 | tf_op jit(solution)/shard_map/ppermute | solution.py:56
  69.5 2.3 %collective-permute-start.18 = (f32[8,128]{1,0:T(8,128)S(1)}, f32[8,128]{1,0:T(8,128)S(1)}, u32[]{:S(2)}, u32[]{:S(2)}) collective-permute-start(f32[8,128]{1,0:T(8,128)S(1)} %join.4.refs_0_), channel_id=1, source_target_pairs={{0,8},{4,12},{8,0},{12,4},{16,24},{20,28},{24,16},{28,20},{1,9},{5... | collective-permute-start | bytes 12296 | tf_op jit(solution)/shard_map/ppermute | solution.py:56
  71.7 1.0 %collective-permute-done.20.refs_3_ = f32[8,128]{1,0:T(8,128)S(1)} collective-permute-done((f32[8,128]{1,0:T(8,128)S(1)}, f32[8,128]{1,0:T(8,128)S(1)}, u32[]{:S(2)}, u32[]{:S(2)}) %collective-permute-start.20) | collective-permute-done | bytes 4128 | tf_op jit(solution)/shard_map/ppermute | solution.py:56
  73.4 1.8 %row_pass.3.refs_0_ = f32[32,128]{1,0:T(8,128)S(1)} custom-call(s32[2,32]{1,0:T(2,128)} %bitcast.16, f32[32,2,128,128]{3,2,1,0:T(8,128)S(1)} %get-tuple-element.30.tall_ref, f32[8,128]{1,0:T(8,128)S(1)} %get-tuple-element.31.log_mass_ref, f32[8,128]{1,0:T(8,128)S(1)} %join.4.refs_0_, f32[8,128]{1,0:T(8,128)S(1)} %collective-permute-done.18.refs_1_, ...), custom_call_target="tpu_custom_call" | custom-call | tf_op jit(solution)/shard_map/row_pass/pallas_call | solution.py:451
  75.3 1.6 %collective-permute-start.22 = (f32[32,128]{1,0:T(8,128)S(1)}, f32[32,128]{1,0:T(8,128)S(1)}, u32[]{:S(2)}, u32[]{:S(2)}) collective-permute-start(f32[32,128]{1,0:T(8,128)S(1)} %row_pass.3.refs_0_), channel_id=1, source_target_pairs={{0,2},{1,3},{2,0},{3,1},{4,6},{5,7},{6,4},{7,5},{8,10},{9,11},{10,... | collective-permute-start | bytes 49160 | tf_op jit(solution)/shard_map/ppermute | solution.py:56
  77.1 1.4 %collective-permute-done.23.refs_3_ = f32[32,128]{1,0:T(8,128)S(1)} collective-permute-done((f32[32,128]{1,0:T(8,128)S(1)}, f32[32,128]{1,0:T(8,128)S(1)}, u32[]{:S(2)}, u32[]{:S(2)}) %collective-permute-start.23) | collective-permute-done | bytes 16416 | tf_op jit(solution)/shard_map/ppermute | solution.py:56
  79.1 1.2 %column_pass.5 = (f32[8,128]{1,0:T(8,128)S(1)}, f32[32,128]{1,0:T(8,128)}) custom-call(f32[32,2,128,128]{3,2,1,0:T(8,128)S(1)} %get-tuple-element.27.work_ref, s32[64,128]{1,0:T(8,128)S(1)} %get-tuple-element.28.select_ref, f32[32,128]{1,0:T(8,128)S(1)} %get-tuple-element.29.log_mass_ref, f32[32,128]{1,0:T(8,128)S(1)} %row_pass.3.refs_0_, ...), custom_call_target="tpu_custom_call" | custom-call | tf_op jit(solution)/shard_map/column_pass/pallas_call | solution.py:424
  80.9 3.1 %collective-permute-done.24.second_ref = f32[8,128]{1,0:T(8,128)S(1)} collective-permute-done((f32[8,128]{1,0:T(8,128)S(1)}, f32[8,128]{1,0:T(8,128)S(1)}, u32[]{:S(2)}, u32[]{:S(2)}) %collective-permute-start.24) | collective-permute-done | bytes 4128 | tf_op jit(solution)/shard_map/ppermute | solution.py:56
  84.0 2.6 %collective-permute-start.27 = (f32[8,128]{1,0:T(8,128)S(1)}, f32[8,128]{1,0:T(8,128)S(1)}, u32[]{:S(2)}, u32[]{:S(2)}) collective-permute-start(f32[8,128]{1,0:T(8,128)S(1)} %join.5.refs_0_), channel_id=1, source_target_pairs={{0,24},{4,28},{8,16},{12,20},{16,8},{20,12},{24,0},{28,4},{1,25},{... | collective-permute-start | bytes 12296 | tf_op jit(solution)/shard_map/ppermute | solution.py:56
  89.5 1.6 %collective-permute-done.26.refs_2_ = f32[8,128]{1,0:T(8,128)S(1)} collective-permute-done((f32[8,128]{1,0:T(8,128)S(1)}, f32[8,128]{1,0:T(8,128)S(1)}, u32[]{:S(2)}, u32[]{:S(2)}) %collective-permute-start.26) | collective-permute-done | bytes 4128 | tf_op jit(solution)/shard_map/ppermute | solution.py:56
  (41 shorter events, 11.3 us)
Async XLA Ops:
  0.6 14.2 %collective-permute-start.2 = (f32[1,1,3,128,128]{4,3,2,1,0:T(8,128)}, f32[1,1,3,128,128]{4,3,2,1,0:T(8,128)S(1)}, u32[]{:S(2)}, u32[]{:S(2)}) collective-permute-start(f32[1,1,3,128,128]{4,3,2,1,0:T(8,128)} %refs_6_.1), channel_id=1, source_target_pairs={{0,12},{4,8},{8,4},{12,0},{16,28},{20,24},{24,20},{28,16},{1,13},{... | collective-permute-start | bytes 589832 | tf_op jit(solution)/shard_map/ppermute | solution.py:56
  4.7 13.9 %collective-permute-start.1 = (f32[1,1,3,128,128]{4,3,2,1,0:T(8,128)}, f32[1,1,3,128,128]{4,3,2,1,0:T(8,128)S(1)}, u32[]{:S(2)}, u32[]{:S(2)}) collective-permute-start(f32[1,1,3,128,128]{4,3,2,1,0:T(8,128)} %refs_6_.1), channel_id=1, source_target_pairs={{0,8},{4,12},{8,0},{12,4},{16,24},{20,28},{24,16},{28,20},{1,9},{5... | collective-permute-start | bytes 589832 | tf_op jit(solution)/shard_map/ppermute | solution.py:56
  5.1 13.5 %collective-permute-start = (f32[1,1,3,128,128]{4,3,2,1,0:T(8,128)}, f32[1,1,3,128,128]{4,3,2,1,0:T(8,128)S(1)}, u32[]{:S(2)}, u32[]{:S(2)}) collective-permute-start(f32[1,1,3,128,128]{4,3,2,1,0:T(8,128)} %refs_6_.1), channel_id=1, source_target_pairs={{0,4},{4,0},{8,12},{12,8},{16,20},{20,16},{24,28},{28,24},{1,5},{5... | collective-permute-start | bytes 589832 | tf_op jit(solution)/shard_map/ppermute | solution.py:56
  5.3 13.3 %collective-permute-start.3 = (f32[1,1,3,128,128]{4,3,2,1,0:T(8,128)}, f32[1,1,3,128,128]{4,3,2,1,0:T(8,128)S(1)}, u32[]{:S(2)}, u32[]{:S(2)}) collective-permute-start(f32[1,1,3,128,128]{4,3,2,1,0:T(8,128)} %refs_6_.1), channel_id=1, source_target_pairs={{0,16},{4,20},{8,24},{12,28},{16,0},{20,4},{24,8},{28,12},{1,17},{... | collective-permute-start | bytes 589832 | tf_op jit(solution)/shard_map/ppermute | solution.py:56
  9.7 13.1 %all-to-all-start = ((f32[32,2,128]{2,1,0:T(2,128)}), f32[32,2,128]{2,1,0:T(2,128)S(1)}, u32[]{:S(2)}, u32[]{:S(2)}) async-start(f32[32,2,128]{2,1,0:T(2,128)} %bitcast.5), calls=%async_computation | async-start | bytes 65536 | tf_op jit(solution)/shard_map/all_to_all | solution.py:64
  18.6 11.9 %collective-permute-start.6 = (f32[1,1,3,128,128]{4,3,2,1,0:T(8,128)S(1)}, f32[1,1,3,128,128]{4,3,2,1,0:T(8,128)S(1)}, u32[]{:S(2)}, u32[]{:S(2)}) collective-permute-start(f32[1,1,3,128,128]{4,3,2,1,0:T(8,128)S(1)} %get-tuple-element.25.refs_10_), channel_id=1, source_target_pairs={{0,12},{4,8},{8,4},{12,0},{16,28},{20,24},{24,20},{28,16},{1,13},{... | collective-permute-start | bytes 589832 | tf_op jit(solution)/shard_map/ppermute | solution.py:56
  21.2 9.3 %collective-permute-start.5 = (f32[1,1,3,128,128]{4,3,2,1,0:T(8,128)S(1)}, f32[1,1,3,128,128]{4,3,2,1,0:T(8,128)S(1)}, u32[]{:S(2)}, u32[]{:S(2)}) collective-permute-start(f32[1,1,3,128,128]{4,3,2,1,0:T(8,128)S(1)} %get-tuple-element.25.refs_10_), channel_id=1, source_target_pairs={{0,8},{4,12},{8,0},{12,4},{16,24},{20,28},{24,16},{28,20},{1,9},{5... | collective-permute-start | bytes 589832 | tf_op jit(solution)/shard_map/ppermute | solution.py:56
  21.3 9.2 %collective-permute-start.4 = (f32[1,1,3,128,128]{4,3,2,1,0:T(8,128)S(1)}, f32[1,1,3,128,128]{4,3,2,1,0:T(8,128)S(1)}, u32[]{:S(2)}, u32[]{:S(2)}) collective-permute-start(f32[1,1,3,128,128]{4,3,2,1,0:T(8,128)S(1)} %get-tuple-element.25.refs_10_), channel_id=1, source_target_pairs={{0,4},{4,0},{8,12},{12,8},{16,20},{20,16},{24,28},{28,24},{1,5},{5... | collective-permute-start | bytes 589832 | tf_op jit(solution)/shard_map/ppermute | solution.py:56
  22.8 7.7 %copy-start = (f32[1,1,3,128,128]{4,3,2,1,0:T(8,128)S(1)}, f32[1,1,3,128,128]{4,3,2,1,0:T(8,128)}, u32[]{:S(2)}) copy-start(f32[1,1,3,128,128]{4,3,2,1,0:T(8,128)} %refs_6_.1) | copy-start | bytes 589828
  40.2 3.3 %collective-permute-start.9 = (f32[32,128]{1,0:T(8,128)S(1)}, f32[32,128]{1,0:T(8,128)S(1)}, u32[]{:S(2)}, u32[]{:S(2)}) collective-permute-start(f32[32,128]{1,0:T(8,128)S(1)} %get-tuple-element.32.refs_0_), channel_id=1, source_target_pairs={{0,3},{1,2},{2,1},{3,0},{4,7},{5,6},{6,5},{7,4},{8,11},{9,10},{10,... | collective-permute-start | bytes 49160 | tf_op jit(solution)/shard_map/ppermute | solution.py:56
  40.2 3.8 %collective-permute-start.8 = (f32[32,128]{1,0:T(8,128)S(1)}, f32[32,128]{1,0:T(8,128)S(1)}, u32[]{:S(2)}, u32[]{:S(2)}) collective-permute-start(f32[32,128]{1,0:T(8,128)S(1)} %get-tuple-element.32.refs_0_), channel_id=1, source_target_pairs={{0,2},{1,3},{2,0},{3,1},{4,6},{5,7},{6,4},{7,5},{8,10},{9,11},{10,... | collective-permute-start | bytes 49160 | tf_op jit(solution)/shard_map/ppermute | solution.py:56
  41.8 2.3 %collective-permute-start.7 = (f32[32,128]{1,0:T(8,128)S(1)}, f32[32,128]{1,0:T(8,128)S(1)}, u32[]{:S(2)}, u32[]{:S(2)}) collective-permute-start(f32[32,128]{1,0:T(8,128)S(1)} %get-tuple-element.32.refs_0_), channel_id=1, source_target_pairs={{0,1},{1,0},{2,3},{3,2},{4,5},{5,4},{6,7},{7,6},{8,9},{9,8},{10,11... | collective-permute-start | bytes 49160 | tf_op jit(solution)/shard_map/ppermute | solution.py:56
  45.2 3.7 %collective-permute-start.10 = (f32[8,128]{1,0:T(8,128)S(1)}, f32[8,128]{1,0:T(8,128)S(1)}, u32[]{:S(2)}, u32[]{:S(2)}) collective-permute-start(f32[8,128]{1,0:T(8,128)S(1)} %get-tuple-element.33.first_ref), channel_id=1, source_target_pairs={{0,4},{4,0},{8,12},{12,8},{16,20},{20,16},{24,28},{28,24},{1,5},{5... | collective-permute-start | bytes 12296 | tf_op jit(solution)/shard_map/ppermute | solution.py:56
  48.9 5.5 %collective-permute-start.13 = (f32[8,128]{1,0:T(8,128)S(1)}, f32[8,128]{1,0:T(8,128)S(1)}, u32[]{:S(2)}, u32[]{:S(2)}) collective-permute-start(f32[8,128]{1,0:T(8,128)S(1)} %join.3.refs_0_), channel_id=1, source_target_pairs={{0,24},{4,28},{8,16},{12,20},{16,8},{20,12},{24,0},{28,4},{1,25},{... | collective-permute-start | bytes 12296 | tf_op jit(solution)/shard_map/ppermute | solution.py:56
  52.1 4.5 %collective-permute-start.12 = (f32[8,128]{1,0:T(8,128)S(1)}, f32[8,128]{1,0:T(8,128)S(1)}, u32[]{:S(2)}, u32[]{:S(2)}) collective-permute-start(f32[8,128]{1,0:T(8,128)S(1)} %join.3.refs_0_), channel_id=1, source_target_pairs={{0,16},{4,20},{8,24},{12,28},{16,0},{20,4},{24,8},{28,12},{1,17},{... | collective-permute-start | bytes 12296 | tf_op jit(solution)/shard_map/ppermute | solution.py:56
  52.5 4.2 %collective-permute-start.11 = (f32[8,128]{1,0:T(8,128)S(1)}, f32[8,128]{1,0:T(8,128)S(1)}, u32[]{:S(2)}, u32[]{:S(2)}) collective-permute-start(f32[8,128]{1,0:T(8,128)S(1)} %join.3.refs_0_), channel_id=1, source_target_pairs={{0,8},{4,12},{8,0},{12,4},{16,24},{20,28},{24,16},{28,20},{1,9},{5... | collective-permute-start | bytes 12296 | tf_op jit(solution)/shard_map/ppermute | solution.py:56
  58.5 3.3 %collective-permute-start.16 = (f32[32,128]{1,0:T(8,128)S(1)}, f32[32,128]{1,0:T(8,128)S(1)}, u32[]{:S(2)}, u32[]{:S(2)}) collective-permute-start(f32[32,128]{1,0:T(8,128)S(1)} %row_pass.2.refs_0_), channel_id=1, source_target_pairs={{0,3},{1,2},{2,1},{3,0},{4,7},{5,6},{6,5},{7,4},{8,11},{9,10},{10,... | collective-permute-start | bytes 49160 | tf_op jit(solution)/shard_map/ppermute | solution.py:56
  58.6 3.8 %collective-permute-start.15 = (f32[32,128]{1,0:T(8,128)S(1)}, f32[32,128]{1,0:T(8,128)S(1)}, u32[]{:S(2)}, u32[]{:S(2)}) collective-permute-start(f32[32,128]{1,0:T(8,128)S(1)} %row_pass.2.refs_0_), channel_id=1, source_target_pairs={{0,2},{1,3},{2,0},{3,1},{4,6},{5,7},{6,4},{7,5},{8,10},{9,11},{10,... | collective-permute-start | bytes 49160 | tf_op jit(solution)/shard_map/ppermute | solution.py:56
  60.2 2.2 %collective-permute-start.14 = (f32[32,128]{1,0:T(8,128)S(1)}, f32[32,128]{1,0:T(8,128)S(1)}, u32[]{:S(2)}, u32[]{:S(2)}) collective-permute-start(f32[32,128]{1,0:T(8,128)S(1)} %row_pass.2.refs_0_), channel_id=1, source_target_pairs={{0,1},{1,0},{2,3},{3,2},{4,5},{5,4},{6,7},{7,6},{8,9},{9,8},{10,11... | collective-permute-start | bytes 49160 | tf_op jit(solution)/shard_map/ppermute | solution.py:56
  63.6 3.7 %collective-permute-start.17 = (f32[8,128]{1,0:T(8,128)S(1)}, f32[8,128]{1,0:T(8,128)S(1)}, u32[]{:S(2)}, u32[]{:S(2)}) collective-permute-start(f32[8,128]{1,0:T(8,128)S(1)} %get-tuple-element.34.first_ref), channel_id=1, source_target_pairs={{0,4},{4,0},{8,12},{12,8},{16,20},{20,16},{24,28},{28,24},{1,5},{5... | collective-permute-start | bytes 12296 | tf_op jit(solution)/shard_map/ppermute | solution.py:56
  67.3 5.5 %collective-permute-start.20 = (f32[8,128]{1,0:T(8,128)S(1)}, f32[8,128]{1,0:T(8,128)S(1)}, u32[]{:S(2)}, u32[]{:S(2)}) collective-permute-start(f32[8,128]{1,0:T(8,128)S(1)} %join.4.refs_0_), channel_id=1, source_target_pairs={{0,24},{4,28},{8,16},{12,20},{16,8},{20,12},{24,0},{28,4},{1,25},{... | collective-permute-start | bytes 12296 | tf_op jit(solution)/shard_map/ppermute | solution.py:56
  68.8 4.5 %collective-permute-start.19 = (f32[8,128]{1,0:T(8,128)S(1)}, f32[8,128]{1,0:T(8,128)S(1)}, u32[]{:S(2)}, u32[]{:S(2)}) collective-permute-start(f32[8,128]{1,0:T(8,128)S(1)} %join.4.refs_0_), channel_id=1, source_target_pairs={{0,16},{4,20},{8,24},{12,28},{16,0},{20,4},{24,8},{28,12},{1,17},{... | collective-permute-start | bytes 12296 | tf_op jit(solution)/shard_map/ppermute | solution.py:56
  69.5 3.9 %collective-permute-start.18 = (f32[8,128]{1,0:T(8,128)S(1)}, f32[8,128]{1,0:T(8,128)S(1)}, u32[]{:S(2)}, u32[]{:S(2)}) collective-permute-start(f32[8,128]{1,0:T(8,128)S(1)} %join.4.refs_0_), channel_id=1, source_target_pairs={{0,8},{4,12},{8,0},{12,4},{16,24},{20,28},{24,16},{28,20},{1,9},{5... | collective-permute-start | bytes 12296 | tf_op jit(solution)/shard_map/ppermute | solution.py:56
  75.2 3.3 %collective-permute-start.23 = (f32[32,128]{1,0:T(8,128)S(1)}, f32[32,128]{1,0:T(8,128)S(1)}, u32[]{:S(2)}, u32[]{:S(2)}) collective-permute-start(f32[32,128]{1,0:T(8,128)S(1)} %row_pass.3.refs_0_), channel_id=1, source_target_pairs={{0,3},{1,2},{2,1},{3,0},{4,7},{5,6},{6,5},{7,4},{8,11},{9,10},{10,... | collective-permute-start | bytes 49160 | tf_op jit(solution)/shard_map/ppermute | solution.py:56
  75.3 3.8 %collective-permute-start.22 = (f32[32,128]{1,0:T(8,128)S(1)}, f32[32,128]{1,0:T(8,128)S(1)}, u32[]{:S(2)}, u32[]{:S(2)}) collective-permute-start(f32[32,128]{1,0:T(8,128)S(1)} %row_pass.3.refs_0_), channel_id=1, source_target_pairs={{0,2},{1,3},{2,0},{3,1},{4,6},{5,7},{6,4},{7,5},{8,10},{9,11},{10,... | collective-permute-start | bytes 49160 | tf_op jit(solution)/shard_map/ppermute | solution.py:56
  76.9 2.2 %collective-permute-start.21 = (f32[32,128]{1,0:T(8,128)S(1)}, f32[32,128]{1,0:T(8,128)S(1)}, u32[]{:S(2)}, u32[]{:S(2)}) collective-permute-start(f32[32,128]{1,0:T(8,128)S(1)} %row_pass.3.refs_0_), channel_id=1, source_target_pairs={{0,1},{1,0},{2,3},{3,2},{4,5},{5,4},{6,7},{7,6},{8,9},{9,8},{10,11... | collective-permute-start | bytes 49160 | tf_op jit(solution)/shard_map/ppermute | solution.py:56
  80.3 3.7 %collective-permute-start.24 = (f32[8,128]{1,0:T(8,128)S(1)}, f32[8,128]{1,0:T(8,128)S(1)}, u32[]{:S(2)}, u32[]{:S(2)}) collective-permute-start(f32[8,128]{1,0:T(8,128)S(1)} %get-tuple-element.36.first_ref), channel_id=1, source_target_pairs={{0,4},{4,0},{8,12},{12,8},{16,20},{20,16},{24,28},{28,24},{1,5},{5... | collective-permute-start | bytes 12296 | tf_op jit(solution)/shard_map/ppermute | solution.py:56
  84.0 5.5 %collective-permute-start.27 = (f32[8,128]{1,0:T(8,128)S(1)}, f32[8,128]{1,0:T(8,128)S(1)}, u32[]{:S(2)}, u32[]{:S(2)}) collective-permute-start(f32[8,128]{1,0:T(8,128)S(1)} %join.5.refs_0_), channel_id=1, source_target_pairs={{0,24},{4,28},{8,16},{12,20},{16,8},{20,12},{24,0},{28,4},{1,25},{... | collective-permute-start | bytes 12296 | tf_op jit(solution)/shard_map/ppermute | solution.py:56
  86.6 4.5 %collective-permute-start.26 = (f32[8,128]{1,0:T(8,128)S(1)}, f32[8,128]{1,0:T(8,128)S(1)}, u32[]{:S(2)}, u32[]{:S(2)}) collective-permute-start(f32[8,128]{1,0:T(8,128)S(1)} %join.5.refs_0_), channel_id=1, source_target_pairs={{0,16},{4,20},{8,24},{12,28},{16,0},{20,4},{24,8},{28,12},{1,17},{... | collective-permute-start | bytes 12296 | tf_op jit(solution)/shard_map/ppermute | solution.py:56
  87.5 3.6 %collective-permute-start.25 = (f32[8,128]{1,0:T(8,128)S(1)}, f32[8,128]{1,0:T(8,128)S(1)}, u32[]{:S(2)}, u32[]{:S(2)}) collective-permute-start(f32[8,128]{1,0:T(8,128)S(1)} %join.5.refs_0_), channel_id=1, source_target_pairs={{0,8},{4,12},{8,0},{12,4},{16,24},{20,28},{24,16},{28,20},{1,9},{5... | collective-permute-start | bytes 12296 | tf_op jit(solution)/shard_map/ppermute | solution.py:56

commit v9 on v7

--- a/solution.py
+++ b/solution.py
@@ -79,46 +79,67 @@
     rows = out_ref.shape[0] // devices
     total = jnp.sum(source_ref[...].astype(jnp.float32), axis=(0, 1), keepdims=True)
     target = target_ref[...].astype(jnp.float32)
-    out_ref[...] = jnp.zeros_like(out_ref)
     for d in range(devices):
         out_ref[d * rows : d * rows + 1, :] = jnp.broadcast_to(total, (1, out_ref.shape[1]))
         out_ref[d * rows + 1 : d * rows + 1 + target.shape[0], :] = target
 
 
-def near_kernel(near_index_ref, cost_ref, plan_ref, mass_ref, totals_ref, x_ref, term_ref, plan_scr):
-    rows = cost_ref.shape[0]
-    first = pl.program_id(0) * rows
-    near_count = cost_ref.shape[1]
-    width = cost_ref.shape[2]
-    slots = plan_ref.shape[2]
+def near_kernel(
+    near_index_ref, cost_hbm, plan_hbm, mass_ref, totals_ref, x_ref, term_ref, cost_scr, plan_in, plan_scr, sems
+):
+    all_rows, near_count, width, _ = cost_hbm.shape
+    slots = plan_hbm.shape[2]
     wide = slots * width
-    for a in range(rows):
-        plan = jnp.concatenate([plan_ref[a, 0, q] for q in range(slots)], axis=1)
-        high, low = split(plan)
-        plan_scr[a, 0:width, :] = high
-        plan_scr[a, width : 2 * width, :] = low
-        plan_scr[a, 2 * width : 3 * width, :] = high
+    groups = all_rows // SUB
+
+    def copies(group):
+        rows = pl.ds(group * SUB, SUB)
+        return (
+            pltpu.make_async_copy(plan_hbm.at[rows], plan_in.at[rows], sems.at[0, group]),
+            pltpu.make_async_copy(cost_hbm.at[rows], cost_scr.at[rows], sems.at[1, group]),
+        )
+
+    for group in range(groups):
+        for copy in copies(group):
+            copy.start()
+
+    together = 2 if groups % 2 == 0 else 1
     lanes = lax.broadcasted_iota(jnp.int32, (width, SUB), 1)
-    for group in range(rows // SUB):
-        terms = jnp.zeros((width, SUB), jnp.float32)
-        for i in range(group * SUB, (group + 1) * SUB):
-            acc = None
-            for k in range(near_count):
-                a = group * SUB + (near_index_ref[k, first + i] & (SUB - 1))
-                cost = cost_ref[i, k]
-                high, low = split(cost)
-                x = jnp.dot(
-                    jnp.concatenate([high, high, low], axis=1),
-                    plan_scr[a],
-                    preferred_element_type=jnp.float32,
-                )
-                x_high, x_low = split(x)
-                x_ref[first + i, 0:width, k * wide : (k + 1) * wide] = x_high
-                x_ref[first + i, width : 2 * width, k * wide : (k + 1) * wide] = x_low
-                weighted = cost * cost * mass_ref[pl.ds(first + a, 1), :].astype(jnp.float32)
-                acc = weighted if acc is None else acc + weighted
-            terms = jnp.where(lanes == i % SUB, jnp.sum(acc, axis=1, keepdims=True), terms)
-        term_ref[first // SUB + group] = terms
+
+    def some_groups(step, _):
+        for here in range(together):
+            for copy in copies(step * together + here):
+                copy.wait()
+        first = step * (together * SUB)
+        for a in range(together * SUB):
+            plan = jnp.concatenate([plan_in[first + a, 0, q] for q in range(slots)], axis=1)
+            high, low = split(plan)
+            plan_scr[a, 0:width, :] = high
+            plan_scr[a, width : 2 * width, :] = low
+            plan_scr[a, 2 * width : 3 * width, :] = high
+        for here in range(together):
+            terms = jnp.zeros((width, SUB), jnp.float32)
+            for i in range(here * SUB, (here + 1) * SUB):
+                acc = None
+                for k in range(near_count):
+                    a = here * SUB + (near_index_ref[k, first + i] & (SUB - 1))
+                    cost = cost_scr[first + i, k]
+                    high, low = split(cost)
+                    x = jnp.dot(
+                        jnp.concatenate([high, high, low], axis=1),
+                        plan_scr[a],
+                        preferred_element_type=jnp.float32,
+                    )
+                    x_high, x_low = split(x)
+                    x_ref[first + i, 0:width, k * wide : (k + 1) * wide] = x_high
+                    x_ref[first + i, width : 2 * width, k * wide : (k + 1) * wide] = x_low
+                    weighted = cost * cost * mass_ref[pl.ds(first + a, 1), :].astype(jnp.float32)
+                    acc = weighted if acc is None else acc + weighted
+                terms = jnp.where(lanes == i % SUB, jnp.sum(acc, axis=1, keepdims=True), terms)
+            term_ref[step * together + here] = terms
+        return 0
+
+    lax.fori_loop(0, groups // together, some_groups, 0)
 
 
 def relay_kernel(*refs):
@@ -329,7 +350,7 @@
     mass = in_hbm(source_weights.reshape(rows_here, width))
     small = pltpu.CompilerParams(vmem_limit_bytes=4 * mib)
 
-    pack_rows = 8 * pl.cdiv(1 + target_here, 8)
+    pack_rows = 1 + target_here
     devices = row_devices * col_devices
     pack = pl.pallas_call(
         functools.partial(pack_kernel, devices),
@@ -348,7 +369,7 @@
         out_shape=[jax.ShapeDtypeStruct(target_cost.shape, f32)] * half,
         input_output_aliases={e: e for e in range(half)},
         compiler_params=small,
-        cost_estimate=pl.CostEstimate(flops=0, bytes_accessed=256 * mib, transcendentals=0),
+        cost_estimate=pl.CostEstimate(flops=10**11, bytes_accessed=256 * mib, transcendentals=0),
         name="relay",
     )(*[arrived[mask] for mask in direct])
     arrived.update(zip(direct, passed))
@@ -361,21 +382,19 @@
     step_rows = 2 * SUB if groups % 2 == 0 else SUB
     x, term = pl.pallas_call(
         near_kernel,
-        grid=(rows_here // step_rows,),
-        in_specs=[
-            SMEM,
-            pl.BlockSpec((step_rows, near_count, width, width), lambda g: (g, 0, 0, 0)),
-            pl.BlockSpec((step_rows, 1, slots, width, width), lambda g: (g, 0, 0, 0, 0)),
-            whole((rows_here, width)),
-            ANY,
-        ],
+        in_specs=[SMEM, ANY, ANY, VMEM, ANY],
         out_specs=[VMEM, VMEM],
         out_shape=[
             pltpu.VMEM((rows_here, 2 * width, wide), jnp.bfloat16),
             pltpu.VMEM((groups, width, SUB), f32),
         ],
-        scratch_shapes=[pltpu.VMEM((step_rows, 3 * width, slots * width), jnp.bfloat16)],
-        compiler_params=pltpu.CompilerParams(vmem_limit_bytes=12 * mib),
+        scratch_shapes=[
+            pltpu.VMEM(near_cost.shape, f32),
+            pltpu.VMEM(coupling.shape, f32),
+            pltpu.VMEM((step_rows, 3 * width, slots * width), jnp.bfloat16),
+            pltpu.SemaphoreType.DMA((2, groups)),
+        ],
+        compiler_params=pltpu.CompilerParams(vmem_limit_bytes=18 * mib),
         cost_estimate=pl.CostEstimate(
             flops=6 * rows_here * wide * width * width,
             bytes_accessed=4 * rows_here * width * (near_count + slots) * width,

time: 98.5 us -> 89.7 us (0.911)
  waiting for transfers between devices: 19.3 us -> 10.9 us
  starting transfers between devices: 22.8 us -> 21.3 us
    ppermute x16, waiting for transfers between devices: 19.3 us -> 10.9 us  [send(): return lax.ppermute(x, axis, [(d, d ^ mask) for d in range(size)])]
    all_to_all x1, starting transfers between devices: 7.3 us -> 3.82 us  [exchange(): return lax.all_to_all(copies, axis, 0, 0, tiled=True)]
    ppermute x16, starting transfers between devices: 15.5 us -> 17.5 us  [send(): return lax.ppermute(x, axis, [(d, d ^ mask) for d in range(size)])]
  transfers between devices with their start and end apart: 17 -> 17, of which waited for: 9 -> 8; matrix products, arithmetic and copies ran while one was open for 0% -> 0% of each run, Pallas kernels for 8% -> 11%
where the time goes in v9:
time: 89.7 us; the launch traced here: 89.2 us
  blocking collectives  28.8 us (32%)
  Pallas kernels  27.4 us (31%)
  starting transfers between devices  21.3 us (24%)
  waiting for transfers between devices  10.9 us (12%)
    all_to_all x3, blocking collectives, exchange(): return lax.all_to_all(copies, axis, 0, 0, tiled=True)  28.8 us
    ppermute x16, starting transfers between devices, send(): return lax.ppermute(x, axis, [(d, d ^ mask) for d in range(size)])  17.5 us
    ppermute x16, waiting for transfers between devices, send(): return lax.ppermute(x, axis, [(d, d ^ mask) for d in range(size)])  10.9 us
    pallas_call x1, Pallas kernels, per_device(): pl.pallas_call(functools.partial(far_kernel, (row_devices, col_devices, t...  9.72 us
    pallas_call x1, Pallas kernels, per_device(): pl.pallas_call(near_kernel, in_specs=[SMEM, ANY, ANY, VMEM, ANY], out_spe...  8.35 us
    all_to_all x1, starting transfers between devices, exchange(): return lax.all_to_all(copies, axis, 0, 0, tiled=True)  3.82 us
    pallas_call x3, Pallas kernels, column_step(): pl.pallas_call(functools.partial(column_kernel, col_devices, copies), in_...  3.69 us
    pallas_call x2, Pallas kernels, row_step(): pl.pallas_call(functools.partial(row_kernel, row_devices), in_specs=[SMEM...  3.69 us
  transfers between devices with their start and end apart: 17, of which 8 were waited for; matrix products, arithmetic and copies ran while one was open for 0% of the time, Pallas kernels for 11%

profile of v9, /device:TPU:0, one launch (start us, length us, event | category | flops | bytes accessed | tf_op | source)
XLA Modules:
  0.0 89.2 jit_solution(573508200415085485)
XLA Ops:
  0.6 4.0 %collective-permute-start.2 = (f32[1,1,3,128,128]{4,3,2,1,0:T(8,128)}, f32[1,1,3,128,128]{4,3,2,1,0:T(8,128)S(1)}, u32[]{:S(2)}, u32[]{:S(2)}) collective-permute-start(f32[1,1,3,128,128]{4,3,2,1,0:T(8,128)} %refs_6_.1), channel_id=1, source_target_pairs={{0,12},{4,8},{8,4},{12,0},{16,28},{20,24},{24,20},{28,16},{1,13},{... | collective-permute-start | bytes 589832 | tf_op jit(solution)/shard_map/ppermute | solution.py:67
  4.7 0.4 collective-permute-start.1
  5.3 2.9 %collective-permute-start.3 = (f32[1,1,3,128,128]{4,3,2,1,0:T(8,128)}, f32[1,1,3,128,128]{4,3,2,1,0:T(8,128)S(1)}, u32[]{:S(2)}, u32[]{:S(2)}) collective-permute-start(f32[1,1,3,128,128]{4,3,2,1,0:T(8,128)} %refs_6_.1), channel_id=1, source_target_pairs={{0,16},{4,20},{8,24},{12,28},{16,0},{20,4},{24,8},{28,12},{1,17},{... | collective-permute-start | bytes 589832 | tf_op jit(solution)/shard_map/ppermute | solution.py:67
  8.2 1.5 %pack.1 = f32[64,128]{1,0:T(8,128)} custom-call(s32[32,128]{1,0:T(8,128)} %bitcast.25, s32[1,128]{1,0:T(1,128)} %target_ref.1), custom_call_target="tpu_custom_call" | custom-call | tf_op jit(solution)/shard_map/pack/pallas_call | solution.py:355
  9.7 3.8 %all-to-all-start = ((f32[32,2,128]{2,1,0:T(2,128)}), f32[32,2,128]{2,1,0:T(2,128)S(1)}, u32[]{:S(2)}, u32[]{:S(2)}) async-start(f32[32,2,128]{2,1,0:T(2,128)} %bitcast.5), calls=%async_computation | async-start | bytes 65536 | tf_op jit(solution)/shard_map/all_to_all | solution.py:75
  13.5 1.3 %collective-permute-done.2.refs_2_ = f32[1,1,3,128,128]{4,3,2,1,0:T(8,128)S(1)} collective-permute-done((f32[1,1,3,128,128]{4,3,2,1,0:T(8,128)}, f32[1,1,3,128,128]{4,3,2,1,0:T(8,128)S(1)}, u32[]{:S(2)}, u32[]{:S(2)}) %collective-permute-start.2) | collective-permute-done | bytes 196640 | tf_op jit(solution)/shard_map/ppermute | solution.py:67
  14.9 3.7 %collective-permute-done.1.refs_1_ = f32[1,1,3,128,128]{4,3,2,1,0:T(8,128)S(1)} collective-permute-done((f32[1,1,3,128,128]{4,3,2,1,0:T(8,128)}, f32[1,1,3,128,128]{4,3,2,1,0:T(8,128)S(1)}, u32[]{:S(2)}, u32[]{:S(2)}) %collective-permute-start.1) | collective-permute-done | bytes 196640 | tf_op jit(solution)/shard_map/ppermute | solution.py:67
  18.6 2.6 %collective-permute-start.6 = (f32[1,1,3,128,128]{4,3,2,1,0:T(8,128)S(1)}, f32[1,1,3,128,128]{4,3,2,1,0:T(8,128)S(1)}, u32[]{:S(2)}, u32[]{:S(2)}) collective-permute-start(f32[1,1,3,128,128]{4,3,2,1,0:T(8,128)S(1)} %get-tuple-element.25.refs_10_), channel_id=1, source_target_pairs={{0,12},{4,8},{8,4},{12,0},{16,28},{20,24},{24,20},{28,16},{1,13},{... | collective-permute-start | bytes 589832 | tf_op jit(solution)/shard_map/ppermute | solution.py:67
  21.3 1.5 %collective-permute-start.4 = (f32[1,1,3,128,128]{4,3,2,1,0:T(8,128)S(1)}, f32[1,1,3,128,128]{4,3,2,1,0:T(8,128)S(1)}, u32[]{:S(2)}, u32[]{:S(2)}) collective-permute-start(f32[1,1,3,128,128]{4,3,2,1,0:T(8,128)S(1)} %get-tuple-element.25.refs_10_), channel_id=1, source_target_pairs={{0,4},{4,0},{8,12},{12,8},{16,20},{20,16},{24,28},{28,24},{1,5},{5... | collective-permute-start | bytes 589832 | tf_op jit(solution)/shard_map/ppermute | solution.py:67
  22.8 8.3 %near_product.1 = (bf16[32,256,768]{2,1,0:T(8,128)(2,1)S(1)}, f32[8,128,4]{2,1,0:T(8,128)S(1)}) custom-call(s32[3,32]{1,0:T(4,128)} %bitcast.31, f32[32,3,128,128]{3,2,1,0:T(8,128)} %cost_hbm.1, f32[32,1,2,128,128]{4,3,2,1,0:T(8,128)} %plan_hbm.1, s32[32,128]{1,0:T(8,128)} %bitcast.26, f32[64,128]{1,0:T(8,128)S(1)} %bitcast.17), custom_call_target="tpu_custom_call" | custom-call | flops 2415919104 | bytes 10485760 | tf_op jit(solution)/shard_map/near_product/pallas_call | solution.py:383
  31.2 9.7 %far_product.1 = (f32[32,1,2,128,128]{4,3,2,1,0:T(8,128)}, f32[32,2,128,128]{3,2,1,0:T(8,128)S(1)}, f32[32,2,128,128]{3,2,1,0:T(8,128)S(1)}, f32[32,128]{1,0:T(8...) custom-call(s32[3,32]{1,0:T(4,128)} %bitcast.32, s32[2,32]{1,0:T(2,128)} %bitcast.28, ...), custom_call_target="tpu_custom_call" | custom-call | tf_op jit(solution)/shard_map/far_product/pallas_call | solution.py:410
  40.9 1.5 %collective-permute-start.8 = (f32[32,128]{1,0:T(8,128)S(1)}, f32[32,128]{1,0:T(8,128)S(1)}, u32[]{:S(2)}, u32[]{:S(2)}) collective-permute-start(f32[32,128]{1,0:T(8,128)S(1)} %get-tuple-element.32.refs_0_), channel_id=1, source_target_pairs={{0,2},{1,3},{2,0},{3,1},{4,6},{5,7},{6,4},{7,5},{8,10},{9,11},{10,... | collective-permute-start | bytes 49160 | tf_op jit(solution)/shard_map/ppermute | solution.py:67
  42.4 0.3 collective-permute-start.7
  42.8 1.4 %collective-permute-done.9.refs_3_ = f32[32,128]{1,0:T(8,128)S(1)} collective-permute-done((f32[32,128]{1,0:T(8,128)S(1)}, f32[32,128]{1,0:T(8,128)S(1)}, u32[]{:S(2)}, u32[]{:S(2)}) %collective-permute-start.9) | collective-permute-done | bytes 16416 | tf_op jit(solution)/shard_map/ppermute | solution.py:67
  44.2 0.5 collective-permute-done.8.refs_2_
  44.7 1.2 %column_pass.3 = (f32[64,128]{1,0:T(8,128)S(1)}, f32[32,128]{1,0:T(8,128)}) custom-call(f32[32,2,128,128]{3,2,1,0:T(8,128)S(1)} %get-tuple-element.27.work_ref, s32[64,128]{1,0:T(8,128)S(1)} %get-tuple-element.28.select_ref, f32[32,128]{1,0:T(8,128)S(1)} %get-tuple-element.29.log_mass_ref, f32[32,128]{1,0:T(8,128)S(1)} %get-tuple-element.32.refs_0_, ...), custom_call_target="tpu_custom_call" | custom-call | tf_op jit(solution)/shard_map/column_pass/pallas_call | solution.py:455
  45.9 10.9 %all_to_all.44 = f32[8,8,128]{2,1,0:T(8,128)S(1)} all-to-all(f32[8,8,128]{2,1,0:T(8,128)S(1)} %bitcast.21), channel_id=1, replica_groups=mesh['rows'=8,'cols'=4] {'rows'}, dimensions={0} | all-to-all | bytes 65536 | tf_op jit(solution)/shard_map/all_to_all | solution.py:75
  56.9 1.8 %row_pass.2.refs_0_ = f32[32,128]{1,0:T(8,128)S(1)} custom-call(s32[2,32]{1,0:T(2,128)} %bitcast.29, f32[32,2,128,128]{3,2,1,0:T(8,128)S(1)} %get-tuple-element.30.tall_ref, f32[8,128]{1,0:T(8,128)S(1)} %get-tuple-element.31.log_mass_ref, f32[64,128]{1,0:T(8,128)S(1)} %bitcast.20), custom_call_target="tpu_custom_call" | custom-call | tf_op jit(solution)/shard_map/row_pass/pallas_call | solution.py:473
  58.8 1.6 %collective-permute-start.11 = (f32[32,128]{1,0:T(8,128)S(1)}, f32[32,128]{1,0:T(8,128)S(1)}, u32[]{:S(2)}, u32[]{:S(2)}) collective-permute-start(f32[32,128]{1,0:T(8,128)S(1)} %row_pass.2.refs_0_), channel_id=1, source_target_pairs={{0,2},{1,3},{2,0},{3,1},{4,6},{5,7},{6,4},{7,5},{8,10},{9,11},{10,... | collective-permute-start | bytes 49160 | tf_op jit(solution)/shard_map/ppermute | solution.py:67
  60.4 0.3 collective-permute-start.10
  60.6 1.4 %collective-permute-done.12.refs_3_ = f32[32,128]{1,0:T(8,128)S(1)} collective-permute-done((f32[32,128]{1,0:T(8,128)S(1)}, f32[32,128]{1,0:T(8,128)S(1)}, u32[]{:S(2)}, u32[]{:S(2)}) %collective-permute-start.12) | collective-permute-done | bytes 16416 | tf_op jit(solution)/shard_map/ppermute | solution.py:67
  62.0 0.6 collective-permute-done.11.refs_2_
  62.6 1.2 %column_pass.4 = (f32[64,128]{1,0:T(8,128)S(1)}, f32[32,128]{1,0:T(8,128)}) custom-call(f32[32,2,128,128]{3,2,1,0:T(8,128)S(1)} %get-tuple-element.27.work_ref, s32[64,128]{1,0:T(8,128)S(1)} %get-tuple-element.28.select_ref, f32[32,128]{1,0:T(8,128)S(1)} %get-tuple-element.29.log_mass_ref, f32[32,128]{1,0:T(8,128)S(1)} %row_pass.2.refs_0_, ...), custom_call_target="tpu_custom_call" | custom-call | tf_op jit(solution)/shard_map/column_pass/pallas_call | solution.py:455
  63.8 9.1 %all_to_all.45 = f32[8,8,128]{2,1,0:T(8,128)S(1)} all-to-all(f32[8,8,128]{2,1,0:T(8,128)S(1)} %bitcast.22), channel_id=1, replica_groups=mesh['rows'=8,'cols'=4] {'rows'}, dimensions={0} | all-to-all | bytes 65536 | tf_op jit(solution)/shard_map/all_to_all | solution.py:75
  72.9 1.8 %row_pass.3.refs_0_ = f32[32,128]{1,0:T(8,128)S(1)} custom-call(s32[2,32]{1,0:T(2,128)} %bitcast.30, f32[32,2,128,128]{3,2,1,0:T(8,128)S(1)} %get-tuple-element.30.tall_ref, f32[8,128]{1,0:T(8,128)S(1)} %get-tuple-element.31.log_mass_ref, f32[64,128]{1,0:T(8,128)S(1)} %bitcast.19), custom_call_target="tpu_custom_call" | custom-call | tf_op jit(solution)/shard_map/row_pass/pallas_call | solution.py:473
  74.8 1.6 %collective-permute-start.14 = (f32[32,128]{1,0:T(8,128)S(1)}, f32[32,128]{1,0:T(8,128)S(1)}, u32[]{:S(2)}, u32[]{:S(2)}) collective-permute-start(f32[32,128]{1,0:T(8,128)S(1)} %row_pass.3.refs_0_), channel_id=1, source_target_pairs={{0,2},{1,3},{2,0},{3,1},{4,6},{5,7},{6,4},{7,5},{8,10},{9,11},{10,... | collective-permute-start | bytes 49160 | tf_op jit(solution)/shard_map/ppermute | solution.py:67
  76.4 0.3 collective-permute-start.13
  76.6 1.4 %collective-permute-done.15.refs_3_ = f32[32,128]{1,0:T(8,128)S(1)} collective-permute-done((f32[32,128]{1,0:T(8,128)S(1)}, f32[32,128]{1,0:T(8,128)S(1)}, u32[]{:S(2)}, u32[]{:S(2)}) %collective-permute-start.15) | collective-permute-done | bytes 16416 | tf_op jit(solution)/shard_map/ppermute | solution.py:67
  78.0 0.6 collective-permute-done.14.refs_2_
  78.6 1.2 %column_pass.5 = (f32[8,128]{1,0:T(8,128)S(1)}, f32[32,128]{1,0:T(8,128)}) custom-call(f32[32,2,128,128]{3,2,1,0:T(8,128)S(1)} %get-tuple-element.27.work_ref, s32[64,128]{1,0:T(8,128)S(1)} %get-tuple-element.28.select_ref, f32[32,128]{1,0:T(8,128)S(1)} %get-tuple-element.29.log_mass_ref, f32[32,128]{1,0:T(8,128)S(1)} %row_pass.3.refs_0_, ...), custom_call_target="tpu_custom_call" | custom-call | tf_op jit(solution)/shard_map/column_pass/pallas_call | solution.py:455
  79.8 8.8 %all_to_all.46 = f32[8,1,128]{2,1,0:T(1,128)S(1)} all-to-all(f32[8,1,128]{2,1,0:T(1,128)S(1)} %bitcast.24), channel_id=1, replica_groups=mesh['rows'=8,'cols'=4] {'rows'}, dimensions={0} | all-to-all | bytes 8192 | tf_op jit(solution)/shard_map/all_to_all | solution.py:75
  88.7 0.5 last_potential.1
  (17 shorter events, 0.5 us)
Async XLA Ops:
  0.6 14.2 %collective-permute-start.2 = (f32[1,1,3,128,128]{4,3,2,1,0:T(8,128)}, f32[1,1,3,128,128]{4,3,2,1,0:T(8,128)S(1)}, u32[]{:S(2)}, u32[]{:S(2)}) collective-permute-start(f32[1,1,3,128,128]{4,3,2,1,0:T(8,128)} %refs_6_.1), channel_id=1, source_target_pairs={{0,12},{4,8},{8,4},{12,0},{16,28},{20,24},{24,20},{28,16},{1,13},{... | collective-permute-start | bytes 589832 | tf_op jit(solution)/shard_map/ppermute | solution.py:67
  4.7 13.9 %collective-permute-start.1 = (f32[1,1,3,128,128]{4,3,2,1,0:T(8,128)}, f32[1,1,3,128,128]{4,3,2,1,0:T(8,128)S(1)}, u32[]{:S(2)}, u32[]{:S(2)}) collective-permute-start(f32[1,1,3,128,128]{4,3,2,1,0:T(8,128)} %refs_6_.1), channel_id=1, source_target_pairs={{0,8},{4,12},{8,0},{12,4},{16,24},{20,28},{24,16},{28,20},{1,9},{5... | collective-permute-start | bytes 589832 | tf_op jit(solution)/shard_map/ppermute | solution.py:67
  5.1 13.5 %collective-permute-start = (f32[1,1,3,128,128]{4,3,2,1,0:T(8,128)}, f32[1,1,3,128,128]{4,3,2,1,0:T(8,128)S(1)}, u32[]{:S(2)}, u32[]{:S(2)}) collective-permute-start(f32[1,1,3,128,128]{4,3,2,1,0:T(8,128)} %refs_6_.1), channel_id=1, source_target_pairs={{0,4},{4,0},{8,12},{12,8},{16,20},{20,16},{24,28},{28,24},{1,5},{5... | collective-permute-start | bytes 589832 | tf_op jit(solution)/shard_map/ppermute | solution.py:67
  5.3 13.3 %collective-permute-start.3 = (f32[1,1,3,128,128]{4,3,2,1,0:T(8,128)}, f32[1,1,3,128,128]{4,3,2,1,0:T(8,128)S(1)}, u32[]{:S(2)}, u32[]{:S(2)}) collective-permute-start(f32[1,1,3,128,128]{4,3,2,1,0:T(8,128)} %refs_6_.1), channel_id=1, source_target_pairs={{0,16},{4,20},{8,24},{12,28},{16,0},{20,4},{24,8},{28,12},{1,17},{... | collective-permute-start | bytes 589832 | tf_op jit(solution)/shard_map/ppermute | solution.py:67
  9.7 13.1 %all-to-all-start = ((f32[32,2,128]{2,1,0:T(2,128)}), f32[32,2,128]{2,1,0:T(2,128)S(1)}, u32[]{:S(2)}, u32[]{:S(2)}) async-start(f32[32,2,128]{2,1,0:T(2,128)} %bitcast.5), calls=%async_computation | async-start | bytes 65536 | tf_op jit(solution)/shard_map/all_to_all | solution.py:75
  18.6 12.6 %collective-permute-start.6 = (f32[1,1,3,128,128]{4,3,2,1,0:T(8,128)S(1)}, f32[1,1,3,128,128]{4,3,2,1,0:T(8,128)S(1)}, u32[]{:S(2)}, u32[]{:S(2)}) collective-permute-start(f32[1,1,3,128,128]{4,3,2,1,0:T(8,128)S(1)} %get-tuple-element.25.refs_10_), channel_id=1, source_target_pairs={{0,12},{4,8},{8,4},{12,0},{16,28},{20,24},{24,20},{28,16},{1,13},{... | collective-permute-start | bytes 589832 | tf_op jit(solution)/shard_map/ppermute | solution.py:67
  21.2 10.0 %collective-permute-start.5 = (f32[1,1,3,128,128]{4,3,2,1,0:T(8,128)S(1)}, f32[1,1,3,128,128]{4,3,2,1,0:T(8,128)S(1)}, u32[]{:S(2)}, u32[]{:S(2)}) collective-permute-start(f32[1,1,3,128,128]{4,3,2,1,0:T(8,128)S(1)} %get-tuple-element.25.refs_10_), channel_id=1, source_target_pairs={{0,8},{4,12},{8,0},{12,4},{16,24},{20,28},{24,16},{28,20},{1,9},{5... | collective-permute-start | bytes 589832 | tf_op jit(solution)/shard_map/ppermute | solution.py:67
  21.3 9.8 %collective-permute-start.4 = (f32[1,1,3,128,128]{4,3,2,1,0:T(8,128)S(1)}, f32[1,1,3,128,128]{4,3,2,1,0:T(8,128)S(1)}, u32[]{:S(2)}, u32[]{:S(2)}) collective-permute-start(f32[1,1,3,128,128]{4,3,2,1,0:T(8,128)S(1)} %get-tuple-element.25.refs_10_), channel_id=1, source_target_pairs={{0,4},{4,0},{8,12},{12,8},{16,20},{20,16},{24,28},{28,24},{1,5},{5... | collective-permute-start | bytes 589832 | tf_op jit(solution)/shard_map/ppermute | solution.py:67
  22.8 8.4 %copy-start = (f32[1,1,3,128,128]{4,3,2,1,0:T(8,128)S(1)}, f32[1,1,3,128,128]{4,3,2,1,0:T(8,128)}, u32[]{:S(2)}) copy-start(f32[1,1,3,128,128]{4,3,2,1,0:T(8,128)} %refs_6_.1) | copy-start | bytes 589828
  40.9 3.3 %collective-permute-start.9 = (f32[32,128]{1,0:T(8,128)S(1)}, f32[32,128]{1,0:T(8,128)S(1)}, u32[]{:S(2)}, u32[]{:S(2)}) collective-permute-start(f32[32,128]{1,0:T(8,128)S(1)} %get-tuple-element.32.refs_0_), channel_id=1, source_target_pairs={{0,3},{1,2},{2,1},{3,0},{4,7},{5,6},{6,5},{7,4},{8,11},{9,10},{10,... | collective-permute-start | bytes 49160 | tf_op jit(solution)/shard_map/ppermute | solution.py:67
  40.9 3.8 %collective-permute-start.8 = (f32[32,128]{1,0:T(8,128)S(1)}, f32[32,128]{1,0:T(8,128)S(1)}, u32[]{:S(2)}, u32[]{:S(2)}) collective-permute-start(f32[32,128]{1,0:T(8,128)S(1)} %get-tuple-element.32.refs_0_), channel_id=1, source_target_pairs={{0,2},{1,3},{2,0},{3,1},{4,6},{5,7},{6,4},{7,5},{8,10},{9,11},{10,... | collective-permute-start | bytes 49160 | tf_op jit(solution)/shard_map/ppermute | solution.py:67
  42.4 2.2 %collective-permute-start.7 = (f32[32,128]{1,0:T(8,128)S(1)}, f32[32,128]{1,0:T(8,128)S(1)}, u32[]{:S(2)}, u32[]{:S(2)}) collective-permute-start(f32[32,128]{1,0:T(8,128)S(1)} %get-tuple-element.32.refs_0_), channel_id=1, source_target_pairs={{0,1},{1,0},{2,3},{3,2},{4,5},{5,4},{6,7},{7,6},{8,9},{9,8},{10,11... | collective-permute-start | bytes 49160 | tf_op jit(solution)/shard_map/ppermute | solution.py:67
  58.7 3.3 %collective-permute-start.12 = (f32[32,128]{1,0:T(8,128)S(1)}, f32[32,128]{1,0:T(8,128)S(1)}, u32[]{:S(2)}, u32[]{:S(2)}) collective-permute-start(f32[32,128]{1,0:T(8,128)S(1)} %row_pass.2.refs_0_), channel_id=1, source_target_pairs={{0,3},{1,2},{2,1},{3,0},{4,7},{5,6},{6,5},{7,4},{8,11},{9,10},{10,... | collective-permute-start | bytes 49160 | tf_op jit(solution)/shard_map/ppermute | solution.py:67
  58.8 3.8 %collective-permute-start.11 = (f32[32,128]{1,0:T(8,128)S(1)}, f32[32,128]{1,0:T(8,128)S(1)}, u32[]{:S(2)}, u32[]{:S(2)}) collective-permute-start(f32[32,128]{1,0:T(8,128)S(1)} %row_pass.2.refs_0_), channel_id=1, source_target_pairs={{0,2},{1,3},{2,0},{3,1},{4,6},{5,7},{6,4},{7,5},{8,10},{9,11},{10,... | collective-permute-start | bytes 49160 | tf_op jit(solution)/shard_map/ppermute | solution.py:67
  60.4 2.2 %collective-permute-start.10 = (f32[32,128]{1,0:T(8,128)S(1)}, f32[32,128]{1,0:T(8,128)S(1)}, u32[]{:S(2)}, u32[]{:S(2)}) collective-permute-start(f32[32,128]{1,0:T(8,128)S(1)} %row_pass.2.refs_0_), channel_id=1, source_target_pairs={{0,1},{1,0},{2,3},{3,2},{4,5},{5,4},{6,7},{7,6},{8,9},{9,8},{10,11... | collective-permute-start | bytes 49160 | tf_op jit(solution)/shard_map/ppermute | solution.py:67
  74.7 3.3 %collective-permute-start.15 = (f32[32,128]{1,0:T(8,128)S(1)}, f32[32,128]{1,0:T(8,128)S(1)}, u32[]{:S(2)}, u32[]{:S(2)}) collective-permute-start(f32[32,128]{1,0:T(8,128)S(1)} %row_pass.3.refs_0_), channel_id=1, source_target_pairs={{0,3},{1,2},{2,1},{3,0},{4,7},{5,6},{6,5},{7,4},{8,11},{9,10},{10,... | collective-permute-start | bytes 49160 | tf_op jit(solution)/shard_map/ppermute | solution.py:67
  74.8 3.8 %collective-permute-start.14 = (f32[32,128]{1,0:T(8,128)S(1)}, f32[32,128]{1,0:T(8,128)S(1)}, u32[]{:S(2)}, u32[]{:S(2)}) collective-permute-start(f32[32,128]{1,0:T(8,128)S(1)} %row_pass.3.refs_0_), channel_id=1, source_target_pairs={{0,2},{1,3},{2,0},{3,1},{4,6},{5,7},{6,4},{7,5},{8,10},{9,11},{10,... | collective-permute-start | bytes 49160 | tf_op jit(solution)/shard_map/ppermute | solution.py:67
  76.4 2.2 %collective-permute-start.13 = (f32[32,128]{1,0:T(8,128)S(1)}, f32[32,128]{1,0:T(8,128)S(1)}, u32[]{:S(2)}, u32[]{:S(2)}) collective-permute-start(f32[32,128]{1,0:T(8,128)S(1)} %row_pass.3.refs_0_), channel_id=1, source_target_pairs={{0,1},{1,0},{2,3},{3,2},{4,5},{5,4},{6,7},{7,6},{8,9},{9,8},{10,11... | collective-permute-start | bytes 49160 | tf_op jit(solution)/shard_map/ppermute | solution.py:67

commit v10 on v7

--- a/solution.py
+++ b/solution.py
@@ -67,8 +67,21 @@
     return lax.ppermute(x, axis, [(d, d ^ mask) for d in range(size)])
 
 
-def from_all(x, axis):
-    return [x] + [send(x, axis, s) for s in range(1, lax.axis_size(axis))]
+def join_kernel(first_ref, second_ref, out_ref):
+    out_ref[...] = log_sum([first_ref[...], second_ref[...]])
+
+
+def last_pair(part, axis):
+    mask = 1
+    while 2 * mask < lax.axis_size(axis):
+        part = pl.pallas_call(
+            join_kernel,
+            out_shape=jax.ShapeDtypeStruct(part.shape, jnp.float32),
+            compiler_params=pltpu.CompilerParams(vmem_limit_bytes=4 * mib),
+            name="join",
+        )(part, send(part, axis, mask))
+        mask *= 2
+    return [part, send(part, axis, mask)]
 
 
 def exchange(copies, axis):
@@ -79,7 +92,6 @@
     rows = out_ref.shape[0] // devices
     total = jnp.sum(source_ref[...].astype(jnp.float32), axis=(0, 1), keepdims=True)
     target = target_ref[...].astype(jnp.float32)
-    out_ref[...] = jnp.zeros_like(out_ref)
     for d in range(devices):
         out_ref[d * rows : d * rows + 1, :] = jnp.broadcast_to(total, (1, out_ref.shape[1]))
         out_ref[d * rows + 1 : d * rows + 1 + target.shape[0], :] = target
@@ -239,9 +251,9 @@
     sum_scr[pl.ds(row, 1), :] = jnp.sum(total, axis=0, keepdims=True)
 
 
-def column_kernel(col_devices, copies, work_ref, select_ref, log_mass_ref, *refs):
-    parts = refs[:col_devices]
-    out_ref, potential_ref, potential_scr, peak_scr, sum_scr = refs[col_devices:]
+def column_kernel(copies, work_ref, select_ref, log_mass_ref, *refs):
+    parts = refs[:-5]
+    out_ref, potential_ref, potential_scr, peak_scr, sum_scr = refs[-5:]
     rows, slots, width, _ = work_ref.shape
     together = math.gcd(rows, 8)
     scaled = log_mass_ref[...] - log_sum([p[...] for p in parts])
@@ -329,7 +341,7 @@
     mass = in_hbm(source_weights.reshape(rows_here, width))
     small = pltpu.CompilerParams(vmem_limit_bytes=4 * mib)
 
-    pack_rows = 8 * pl.cdiv(1 + target_here, 8)
+    pack_rows = 1 + target_here
     devices = row_devices * col_devices
     pack = pl.pallas_call(
         functools.partial(pack_kernel, devices),
@@ -348,7 +360,7 @@
         out_shape=[jax.ShapeDtypeStruct(target_cost.shape, f32)] * half,
         input_output_aliases={e: e for e in range(half)},
         compiler_params=small,
-        cost_estimate=pl.CostEstimate(flops=0, bytes_accessed=256 * mib, transcendentals=0),
+        cost_estimate=pl.CostEstimate(flops=10**11, bytes_accessed=256 * mib, transcendentals=0),
         name="relay",
     )(*[arrived[mask] for mask in direct])
     arrived.update(zip(direct, passed))
@@ -385,8 +397,9 @@
     )(near_t, in_hbm(near_cost), in_hbm(coupling), mass, packs)
 
     far_bytes = group_blocks * link_count * width * width * 4
-    steps = rows_here // step_rows
-    cost_block = pl.BlockSpec((step_rows, 1, slots, width, width), lambda g: (g, 0, 0, 0, 0))
+    far_rows = 2 * step_rows if rows_here % (2 * step_rows) == 0 else step_rows
+    steps = rows_here // far_rows
+    cost_block = pl.BlockSpec((far_rows, 1, slots, width, width), lambda g: (g, 0, 0, 0, 0))
     work_shape = pltpu.VMEM((rows_here, slots, width, width), f32)
     cost_blocks, work, tall, row_part, log_source, log_target, select = pl.pallas_call(
         functools.partial(
@@ -434,8 +447,8 @@
 
     def column_step(row_parts, copies):
         return pl.pallas_call(
-            functools.partial(column_kernel, col_devices, copies),
-            in_specs=[VMEM] * (3 + col_devices),
+            functools.partial(column_kernel, copies),
+            in_specs=[VMEM] * (3 + len(row_parts)),
             out_specs=[VMEM, VMEM],
             out_shape=[
                 jax.ShapeDtypeStruct((copies * group_blocks, width), f32),
@@ -468,7 +481,7 @@
     for step in range(ITERS):
         last = step == ITERS - 1
         column_part, source_potential = column_step(
-            from_all(row_part, "cols"), 1 if last else row_devices
+            last_pair(row_part, "cols"), 1 if last else row_devices
         )
         column_parts = exchange(column_part, "rows")
         if not last:

time: 98.5 us -> 93.6 us (0.950)
  waiting for transfers between devices: 19.3 us -> 15.3 us
  starting transfers between devices: 22.8 us -> 20.5 us
  Pallas kernels: 26.8 us -> 27.9 us
    ppermute x16 -> x13, waiting for transfers between devices: 19.3 us -> 15.3 us  [send(): return lax.ppermute(x, axis, [(d, d ^ mask) for d in range(size)])]
    all_to_all x1, starting transfers between devices: 7.3 us -> 3.82 us  [exchange(): return lax.all_to_all(copies, axis, 0, 0, tiled=True)]
    pallas_call x3 -> x6, Pallas kernels: 3.69 us -> 5.17 us  [the longest x3 5.11 us: column_step(): pl.pallas_call(functools.partial(column_kernel, copies), in_specs=[VMEM]...]
    ppermute x16 -> x13, starting transfers between devices: 15.5 us -> 16.7 us  [send(): return lax.ppermute(x, axis, [(d, d ^ mask) for d in range(size)])]
  transfers between devices with their start and end apart: 17 -> 14, of which waited for: 9 -> 8; matrix products, arithmetic and copies ran while one was open for 0% -> 0% of each run, Pallas kernels for 8% -> 10%
where the time goes in v10:
time: 93.6 us; the launch traced here: 93.2 us
  blocking collectives  28.8 us (31%)
  Pallas kernels  27.9 us (30%)
  starting transfers between devices  20.5 us (22%)
  waiting for transfers between devices  15.3 us (16%)
    all_to_all x3, blocking collectives, exchange(): return lax.all_to_all(copies, axis, 0, 0, tiled=True)  28.8 us
    ppermute x13, starting transfers between devices, send(): return lax.ppermute(x, axis, [(d, d ^ mask) for d in range(size)])  16.7 us
    ppermute x13, waiting for transfers between devices, send(): return lax.ppermute(x, axis, [(d, d ^ mask) for d in range(size)])  15.3 us
    pallas_call x1, Pallas kernels, per_device(): pl.pallas_call(functools.partial(far_kernel, (row_devices, col_devices, t...  9.39 us
    pallas_call x1, Pallas kernels, per_device(): pl.pallas_call(near_kernel, grid=(rows_here // step_rows,), in_specs=[SME...  7.67 us
    pallas_call x3, Pallas kernels, column_step(): pl.pallas_call(functools.partial(column_kernel, copies), in_specs=[VMEM]...  5.11 us
    all_to_all x1, starting transfers between devices, exchange(): return lax.all_to_all(copies, axis, 0, 0, tiled=True)  3.82 us
    pallas_call x2, Pallas kernels, row_step(): pl.pallas_call(functools.partial(row_kernel, row_devices), in_specs=[SMEM...  3.69 us
  transfers between devices with their start and end apart: 14, of which 8 were waited for; matrix products, arithmetic and copies ran while one was open for 0% of the time, Pallas kernels for 10%

profile of v10, /device:TPU:0, one launch (start us, length us, event | category | flops | bytes accessed | tf_op | source)
XLA Modules:
  0.0 93.2 jit_solution(10762723465369960073)
XLA Ops:
  0.6 4.0 %collective-permute-start.2 = (f32[1,1,3,128,128]{4,3,2,1,0:T(8,128)}, f32[1,1,3,128,128]{4,3,2,1,0:T(8,128)S(1)}, u32[]{:S(2)}, u32[]{:S(2)}) collective-permute-start(f32[1,1,3,128,128]{4,3,2,1,0:T(8,128)} %refs_6_.1), channel_id=1, source_target_pairs={{0,12},{4,8},{8,4},{12,0},{16,28},{20,24},{24,20},{28,16},{1,13},{... | collective-permute-start | bytes 589832 | tf_op jit(solution)/shard_map/ppermute | solution.py:67
  4.7 0.4 collective-permute-start.1
  5.1 0.2 collective-permute-start
  5.3 2.9 %collective-permute-start.3 = (f32[1,1,3,128,128]{4,3,2,1,0:T(8,128)}, f32[1,1,3,128,128]{4,3,2,1,0:T(8,128)S(1)}, u32[]{:S(2)}, u32[]{:S(2)}) collective-permute-start(f32[1,1,3,128,128]{4,3,2,1,0:T(8,128)} %refs_6_.1), channel_id=1, source_target_pairs={{0,16},{4,20},{8,24},{12,28},{16,0},{20,4},{24,8},{28,12},{1,17},{... | collective-permute-start | bytes 589832 | tf_op jit(solution)/shard_map/ppermute | solution.py:67
  8.2 1.5 %pack.1 = f32[64,128]{1,0:T(8,128)} custom-call(s32[32,128]{1,0:T(8,128)} %bitcast.25, s32[1,128]{1,0:T(1,128)} %target_ref.1), custom_call_target="tpu_custom_call" | custom-call | tf_op jit(solution)/shard_map/pack/pallas_call | solution.py:346
  9.7 3.8 %all-to-all-start = ((f32[32,2,128]{2,1,0:T(2,128)}), f32[32,2,128]{2,1,0:T(2,128)S(1)}, u32[]{:S(2)}, u32[]{:S(2)}) async-start(f32[32,2,128]{2,1,0:T(2,128)} %bitcast.5), calls=%async_computation | async-start | bytes 65536 | tf_op jit(solution)/shard_map/all_to_all | solution.py:88
  13.5 1.3 %collective-permute-done.2.refs_2_ = f32[1,1,3,128,128]{4,3,2,1,0:T(8,128)S(1)} collective-permute-done((f32[1,1,3,128,128]{4,3,2,1,0:T(8,128)}, f32[1,1,3,128,128]{4,3,2,1,0:T(8,128)S(1)}, u32[]{:S(2)}, u32[]{:S(2)}) %collective-permute-start.2) | collective-permute-done | bytes 196640 | tf_op jit(solution)/shard_map/ppermute | solution.py:67
  14.9 3.7 %collective-permute-done.1.refs_1_ = f32[1,1,3,128,128]{4,3,2,1,0:T(8,128)S(1)} collective-permute-done((f32[1,1,3,128,128]{4,3,2,1,0:T(8,128)}, f32[1,1,3,128,128]{4,3,2,1,0:T(8,128)S(1)}, u32[]{:S(2)}, u32[]{:S(2)}) %collective-permute-start.1) | collective-permute-done | bytes 196640 | tf_op jit(solution)/shard_map/ppermute | solution.py:67
  18.6 2.6 %collective-permute-start.6 = (f32[1,1,3,128,128]{4,3,2,1,0:T(8,128)S(1)}, f32[1,1,3,128,128]{4,3,2,1,0:T(8,128)S(1)}, u32[]{:S(2)}, u32[]{:S(2)}) collective-permute-start(f32[1,1,3,128,128]{4,3,2,1,0:T(8,128)S(1)} %get-tuple-element.25.refs_10_), channel_id=1, source_target_pairs={{0,12},{4,8},{8,4},{12,0},{16,28},{20,24},{24,20},{28,16},{1,13},{... | collective-permute-start | bytes 589832 | tf_op jit(solution)/shard_map/ppermute | solution.py:67
  21.2 0.1 collective-permute-start.5
  21.3 1.5 %collective-permute-start.4 = (f32[1,1,3,128,128]{4,3,2,1,0:T(8,128)S(1)}, f32[1,1,3,128,128]{4,3,2,1,0:T(8,128)S(1)}, u32[]{:S(2)}, u32[]{:S(2)}) collective-permute-start(f32[1,1,3,128,128]{4,3,2,1,0:T(8,128)S(1)} %get-tuple-element.25.refs_10_), channel_id=1, source_target_pairs={{0,4},{4,0},{8,12},{12,8},{16,20},{20,16},{24,28},{28,24},{1,5},{5... | collective-permute-start | bytes 589832 | tf_op jit(solution)/shard_map/ppermute | solution.py:67
  22.8 7.7 %near_product.1 = (bf16[32,256,768]{2,1,0:T(8,128)(2,1)S(1)}, f32[8,128,4]{2,1,0:T(8,128)S(1)}) custom-call(s32[3,32]{1,0:T(4,128)} %bitcast.31, f32[32,3,128,128]{3,2,1,0:T(8,128)} %cost_ref.1, f32[32,1,2,128,128]{4,3,2,1,0:T(8,128)} %plan_ref.1, s32[32,128]{1,0:T(8,128)} %bitcast.26, f32[64,128]{1,0:T(8,128)S(1)} %bitcast.17), custom_call_target="tpu_custom_call" | custom-call | flops 2415919104 | bytes 10485760 | tf_op jit(solution)/shard_map/near_product/pallas_call | solution.py:374
  30.5 9.4 %far_product.1 = (f32[32,1,2,128,128]{4,3,2,1,0:T(8,128)}, f32[32,2,128,128]{3,2,1,0:T(8,128)S(1)}, f32[32,2,128,128]{3,2,1,0:T(8,128)S(1)}, f32[32,128]{1,0:T(8...) custom-call(s32[3,32]{1,0:T(4,128)} %bitcast.32, s32[2,32]{1,0:T(2,128)} %bitcast.28, ...), custom_call_target="tpu_custom_call" | custom-call | tf_op jit(solution)/shard_map/far_product/pallas_call | solution.py:404
  39.9 1.2 %collective-permute-done.7.second_ref = f32[32,128]{1,0:T(8,128)S(1)} collective-permute-done((f32[32,128]{1,0:T(8,128)S(1)}, f32[32,128]{1,0:T(8,128)S(1)}, u32[]{:S(2)}, u32[]{:S(2)}) %collective-permute-start.7) | collective-permute-done | bytes 16416 | tf_op jit(solution)/shard_map/ppermute | solution.py:67
  41.1 1.6 %collective-permute-start.8 = (f32[32,128]{1,0:T(8,128)S(1)}, f32[32,128]{1,0:T(8,128)S(1)}, u32[]{:S(2)}, u32[]{:S(2)}) collective-permute-start(f32[32,128]{1,0:T(8,128)S(1)} %join.3.refs_0_), channel_id=1, source_target_pairs={{0,2},{1,3},{2,0},{3,1},{4,6},{5,7},{6,4},{7,5},{8,10},{9,11},{10,... | collective-permute-start | bytes 49160 | tf_op jit(solution)/shard_map/ppermute | solution.py:67
  42.7 2.2 %collective-permute-done.8.refs_1_ = f32[32,128]{1,0:T(8,128)S(1)} collective-permute-done((f32[32,128]{1,0:T(8,128)S(1)}, f32[32,128]{1,0:T(8,128)S(1)}, u32[]{:S(2)}, u32[]{:S(2)}) %collective-permute-start.8) | collective-permute-done | bytes 16416 | tf_op jit(solution)/shard_map/ppermute | solution.py:67
  44.9 1.7 %column_pass.3 = (f32[64,128]{1,0:T(8,128)S(1)}, f32[32,128]{1,0:T(8,128)}) custom-call(f32[32,2,128,128]{3,2,1,0:T(8,128)S(1)} %get-tuple-element.27.work_ref, s32[64,128]{1,0:T(8,128)S(1)} %get-tuple-element.28.select_ref, f32[32,128]{1,0:T(8,128)S(1)} %get-tuple-element.29.log_mass_ref, f32[32,128]{1,0:T(8,128)S(1)} %join.3.refs_0_, ...), custom_call_target="tpu_custom_call" | custom-call | tf_op jit(solution)/shard_map/column_pass/pallas_call | solution.py:449
  46.6 10.9 %all_to_all.44 = f32[8,8,128]{2,1,0:T(8,128)S(1)} all-to-all(f32[8,8,128]{2,1,0:T(8,128)S(1)} %bitcast.21), channel_id=1, replica_groups=mesh['rows'=8,'cols'=4] {'rows'}, dimensions={0} | all-to-all | bytes 65536 | tf_op jit(solution)/shard_map/all_to_all | solution.py:88
  57.5 1.8 %row_pass.2.first_ref = f32[32,128]{1,0:T(8,128)S(1)} custom-call(s32[2,32]{1,0:T(2,128)} %bitcast.29, f32[32,2,128,128]{3,2,1,0:T(8,128)S(1)} %get-tuple-element.30.tall_ref, f32[8,128]{1,0:T(8,128)S(1)} %get-tuple-element.31.log_mass_ref, f32[64,128]{1,0:T(8,128)S(1)} %bitcast.20), custom_call_target="tpu_custom_call" | custom-call | tf_op jit(solution)/shard_map/row_pass/pallas_call | solution.py:467
  59.4 0.1 collective-permute-start.9
  59.5 1.2 %collective-permute-done.9.second_ref = f32[32,128]{1,0:T(8,128)S(1)} collective-permute-done((f32[32,128]{1,0:T(8,128)S(1)}, f32[32,128]{1,0:T(8,128)S(1)}, u32[]{:S(2)}, u32[]{:S(2)}) %collective-permute-start.9) | collective-permute-done | bytes 16416 | tf_op jit(solution)/shard_map/ppermute | solution.py:67
  60.7 1.6 %collective-permute-start.10 = (f32[32,128]{1,0:T(8,128)S(1)}, f32[32,128]{1,0:T(8,128)S(1)}, u32[]{:S(2)}, u32[]{:S(2)}) collective-permute-start(f32[32,128]{1,0:T(8,128)S(1)} %join.4.refs_0_), channel_id=1, source_target_pairs={{0,2},{1,3},{2,0},{3,1},{4,6},{5,7},{6,4},{7,5},{8,10},{9,11},{10,... | collective-permute-start | bytes 49160 | tf_op jit(solution)/shard_map/ppermute | solution.py:67
  62.3 2.2 %collective-permute-done.10.refs_1_ = f32[32,128]{1,0:T(8,128)S(1)} collective-permute-done((f32[32,128]{1,0:T(8,128)S(1)}, f32[32,128]{1,0:T(8,128)S(1)}, u32[]{:S(2)}, u32[]{:S(2)}) %collective-permute-start.10) | collective-permute-done | bytes 16416 | tf_op jit(solution)/shard_map/ppermute | solution.py:67
  64.5 1.7 %column_pass.4 = (f32[64,128]{1,0:T(8,128)S(1)}, f32[32,128]{1,0:T(8,128)}) custom-call(f32[32,2,128,128]{3,2,1,0:T(8,128)S(1)} %get-tuple-element.27.work_ref, s32[64,128]{1,0:T(8,128)S(1)} %get-tuple-element.28.select_ref, f32[32,128]{1,0:T(8,128)S(1)} %get-tuple-element.29.log_mass_ref, f32[32,128]{1,0:T(8,128)S(1)} %join.4.refs_0_, ...), custom_call_target="tpu_custom_call" | custom-call | tf_op jit(solution)/shard_map/column_pass/pallas_call | solution.py:449
  66.2 9.0 %all_to_all.45 = f32[8,8,128]{2,1,0:T(8,128)S(1)} all-to-all(f32[8,8,128]{2,1,0:T(8,128)S(1)} %bitcast.22), channel_id=1, replica_groups=mesh['rows'=8,'cols'=4] {'rows'}, dimensions={0} | all-to-all | bytes 65536 | tf_op jit(solution)/shard_map/all_to_all | solution.py:88
  75.2 1.8 %row_pass.3.first_ref = f32[32,128]{1,0:T(8,128)S(1)} custom-call(s32[2,32]{1,0:T(2,128)} %bitcast.30, f32[32,2,128,128]{3,2,1,0:T(8,128)S(1)} %get-tuple-element.30.tall_ref, f32[8,128]{1,0:T(8,128)S(1)} %get-tuple-element.31.log_mass_ref, f32[64,128]{1,0:T(8,128)S(1)} %bitcast.19), custom_call_target="tpu_custom_call" | custom-call | tf_op jit(solution)/shard_map/row_pass/pallas_call | solution.py:467
  77.1 1.2 %collective-permute-done.11.second_ref = f32[32,128]{1,0:T(8,128)S(1)} collective-permute-done((f32[32,128]{1,0:T(8,128)S(1)}, f32[32,128]{1,0:T(8,128)S(1)}, u32[]{:S(2)}, u32[]{:S(2)}) %collective-permute-start.11) | collective-permute-done | bytes 16416 | tf_op jit(solution)/shard_map/ppermute | solution.py:67
  78.3 1.6 %collective-permute-start.12 = (f32[32,128]{1,0:T(8,128)S(1)}, f32[32,128]{1,0:T(8,128)S(1)}, u32[]{:S(2)}, u32[]{:S(2)}) collective-permute-start(f32[32,128]{1,0:T(8,128)S(1)} %join.5.refs_0_), channel_id=1, source_target_pairs={{0,2},{1,3},{2,0},{3,1},{4,6},{5,7},{6,4},{7,5},{8,10},{9,11},{10,... | collective-permute-start | bytes 49160 | tf_op jit(solution)/shard_map/ppermute | solution.py:67
  79.9 2.2 %collective-permute-done.12.refs_1_ = f32[32,128]{1,0:T(8,128)S(1)} collective-permute-done((f32[32,128]{1,0:T(8,128)S(1)}, f32[32,128]{1,0:T(8,128)S(1)}, u32[]{:S(2)}, u32[]{:S(2)}) %collective-permute-start.12) | collective-permute-done | bytes 16416 | tf_op jit(solution)/shard_map/ppermute | solution.py:67
  82.1 1.7 %column_pass.5 = (f32[8,128]{1,0:T(8,128)S(1)}, f32[32,128]{1,0:T(8,128)}) custom-call(f32[32,2,128,128]{3,2,1,0:T(8,128)S(1)} %get-tuple-element.27.work_ref, s32[64,128]{1,0:T(8,128)S(1)} %get-tuple-element.28.select_ref, f32[32,128]{1,0:T(8,128)S(1)} %get-tuple-element.29.log_mass_ref, f32[32,128]{1,0:T(8,128)S(1)} %join.5.refs_0_, ...), custom_call_target="tpu_custom_call" | custom-call | tf_op jit(solution)/shard_map/column_pass/pallas_call | solution.py:449
  83.8 8.8 %all_to_all.46 = f32[8,1,128]{2,1,0:T(1,128)S(1)} all-to-all(f32[8,1,128]{2,1,0:T(1,128)S(1)} %bitcast.24), channel_id=1, replica_groups=mesh['rows'=8,'cols'=4] {'rows'}, dimensions={0} | all-to-all | bytes 8192 | tf_op jit(solution)/shard_map/all_to_all | solution.py:88
  92.7 0.5 last_potential.1
  (14 shorter events, 0.1 us)
Async XLA Ops:
  0.6 14.2 %collective-permute-start.2 = (f32[1,1,3,128,128]{4,3,2,1,0:T(8,128)}, f32[1,1,3,128,128]{4,3,2,1,0:T(8,128)S(1)}, u32[]{:S(2)}, u32[]{:S(2)}) collective-permute-start(f32[1,1,3,128,128]{4,3,2,1,0:T(8,128)} %refs_6_.1), channel_id=1, source_target_pairs={{0,12},{4,8},{8,4},{12,0},{16,28},{20,24},{24,20},{28,16},{1,13},{... | collective-permute-start | bytes 589832 | tf_op jit(solution)/shard_map/ppermute | solution.py:67
  4.7 13.9 %collective-permute-start.1 = (f32[1,1,3,128,128]{4,3,2,1,0:T(8,128)}, f32[1,1,3,128,128]{4,3,2,1,0:T(8,128)S(1)}, u32[]{:S(2)}, u32[]{:S(2)}) collective-permute-start(f32[1,1,3,128,128]{4,3,2,1,0:T(8,128)} %refs_6_.1), channel_id=1, source_target_pairs={{0,8},{4,12},{8,0},{12,4},{16,24},{20,28},{24,16},{28,20},{1,9},{5... | collective-permute-start | bytes 589832 | tf_op jit(solution)/shard_map/ppermute | solution.py:67
  5.1 13.5 %collective-permute-start = (f32[1,1,3,128,128]{4,3,2,1,0:T(8,128)}, f32[1,1,3,128,128]{4,3,2,1,0:T(8,128)S(1)}, u32[]{:S(2)}, u32[]{:S(2)}) collective-permute-start(f32[1,1,3,128,128]{4,3,2,1,0:T(8,128)} %refs_6_.1), channel_id=1, source_target_pairs={{0,4},{4,0},{8,12},{12,8},{16,20},{20,16},{24,28},{28,24},{1,5},{5... | collective-permute-start | bytes 589832 | tf_op jit(solution)/shard_map/ppermute | solution.py:67
  5.3 13.3 %collective-permute-start.3 = (f32[1,1,3,128,128]{4,3,2,1,0:T(8,128)}, f32[1,1,3,128,128]{4,3,2,1,0:T(8,128)S(1)}, u32[]{:S(2)}, u32[]{:S(2)}) collective-permute-start(f32[1,1,3,128,128]{4,3,2,1,0:T(8,128)} %refs_6_.1), channel_id=1, source_target_pairs={{0,16},{4,20},{8,24},{12,28},{16,0},{20,4},{24,8},{28,12},{1,17},{... | collective-permute-start | bytes 589832 | tf_op jit(solution)/shard_map/ppermute | solution.py:67
  9.7 13.1 %all-to-all-start = ((f32[32,2,128]{2,1,0:T(2,128)}), f32[32,2,128]{2,1,0:T(2,128)S(1)}, u32[]{:S(2)}, u32[]{:S(2)}) async-start(f32[32,2,128]{2,1,0:T(2,128)} %bitcast.5), calls=%async_computation | async-start | bytes 65536 | tf_op jit(solution)/shard_map/all_to_all | solution.py:88
  18.6 11.9 %collective-permute-start.6 = (f32[1,1,3,128,128]{4,3,2,1,0:T(8,128)S(1)}, f32[1,1,3,128,128]{4,3,2,1,0:T(8,128)S(1)}, u32[]{:S(2)}, u32[]{:S(2)}) collective-permute-start(f32[1,1,3,128,128]{4,3,2,1,0:T(8,128)S(1)} %get-tuple-element.25.refs_10_), channel_id=1, source_target_pairs={{0,12},{4,8},{8,4},{12,0},{16,28},{20,24},{24,20},{28,16},{1,13},{... | collective-permute-start | bytes 589832 | tf_op jit(solution)/shard_map/ppermute | solution.py:67
  21.2 9.3 %collective-permute-start.5 = (f32[1,1,3,128,128]{4,3,2,1,0:T(8,128)S(1)}, f32[1,1,3,128,128]{4,3,2,1,0:T(8,128)S(1)}, u32[]{:S(2)}, u32[]{:S(2)}) collective-permute-start(f32[1,1,3,128,128]{4,3,2,1,0:T(8,128)S(1)} %get-tuple-element.25.refs_10_), channel_id=1, source_target_pairs={{0,8},{4,12},{8,0},{12,4},{16,24},{20,28},{24,16},{28,20},{1,9},{5... | collective-permute-start | bytes 589832 | tf_op jit(solution)/shard_map/ppermute | solution.py:67
  21.3 9.2 %collective-permute-start.4 = (f32[1,1,3,128,128]{4,3,2,1,0:T(8,128)S(1)}, f32[1,1,3,128,128]{4,3,2,1,0:T(8,128)S(1)}, u32[]{:S(2)}, u32[]{:S(2)}) collective-permute-start(f32[1,1,3,128,128]{4,3,2,1,0:T(8,128)S(1)} %get-tuple-element.25.refs_10_), channel_id=1, source_target_pairs={{0,4},{4,0},{8,12},{12,8},{16,20},{20,16},{24,28},{28,24},{1,5},{5... | collective-permute-start | bytes 589832 | tf_op jit(solution)/shard_map/ppermute | solution.py:67
  22.8 7.7 %copy-start = (f32[1,1,3,128,128]{4,3,2,1,0:T(8,128)S(1)}, f32[1,1,3,128,128]{4,3,2,1,0:T(8,128)}, u32[]{:S(2)}) copy-start(f32[1,1,3,128,128]{4,3,2,1,0:T(8,128)} %refs_6_.1) | copy-start | bytes 589828
  39.9 1.2 %collective-permute-start.7 = (f32[32,128]{1,0:T(8,128)S(1)}, f32[32,128]{1,0:T(8,128)S(1)}, u32[]{:S(2)}, u32[]{:S(2)}) collective-permute-start(f32[32,128]{1,0:T(8,128)S(1)} %get-tuple-element.32.first_ref), channel_id=1, source_target_pairs={{0,1},{1,0},{2,3},{3,2},{4,5},{5,4},{6,7},{7,6},{8,9},{9,8},{10,11... | collective-permute-start | bytes 49160 | tf_op jit(solution)/shard_map/ppermute | solution.py:67
  41.1 3.8 %collective-permute-start.8 = (f32[32,128]{1,0:T(8,128)S(1)}, f32[32,128]{1,0:T(8,128)S(1)}, u32[]{:S(2)}, u32[]{:S(2)}) collective-permute-start(f32[32,128]{1,0:T(8,128)S(1)} %join.3.refs_0_), channel_id=1, source_target_pairs={{0,2},{1,3},{2,0},{3,1},{4,6},{5,7},{6,4},{7,5},{8,10},{9,11},{10,... | collective-permute-start | bytes 49160 | tf_op jit(solution)/shard_map/ppermute | solution.py:67
  59.4 1.2 %collective-permute-start.9 = (f32[32,128]{1,0:T(8,128)S(1)}, f32[32,128]{1,0:T(8,128)S(1)}, u32[]{:S(2)}, u32[]{:S(2)}) collective-permute-start(f32[32,128]{1,0:T(8,128)S(1)} %row_pass.2.first_ref), channel_id=1, source_target_pairs={{0,1},{1,0},{2,3},{3,2},{4,5},{5,4},{6,7},{7,6},{8,9},{9,8},{10,11... | collective-permute-start | bytes 49160 | tf_op jit(solution)/shard_map/ppermute | solution.py:67
  60.7 3.8 %collective-permute-start.10 = (f32[32,128]{1,0:T(8,128)S(1)}, f32[32,128]{1,0:T(8,128)S(1)}, u32[]{:S(2)}, u32[]{:S(2)}) collective-permute-start(f32[32,128]{1,0:T(8,128)S(1)} %join.4.refs_0_), channel_id=1, source_target_pairs={{0,2},{1,3},{2,0},{3,1},{4,6},{5,7},{6,4},{7,5},{8,10},{9,11},{10,... | collective-permute-start | bytes 49160 | tf_op jit(solution)/shard_map/ppermute | solution.py:67
  77.1 1.2 %collective-permute-start.11 = (f32[32,128]{1,0:T(8,128)S(1)}, f32[32,128]{1,0:T(8,128)S(1)}, u32[]{:S(2)}, u32[]{:S(2)}) collective-permute-start(f32[32,128]{1,0:T(8,128)S(1)} %row_pass.3.first_ref), channel_id=1, source_target_pairs={{0,1},{1,0},{2,3},{3,2},{4,5},{5,4},{6,7},{7,6},{8,9},{9,8},{10,11... | collective-permute-start | bytes 49160 | tf_op jit(solution)/shard_map/ppermute | solution.py:67
  78.3 3.8 %collective-permute-start.12 = (f32[32,128]{1,0:T(8,128)S(1)}, f32[32,128]{1,0:T(8,128)S(1)}, u32[]{:S(2)}, u32[]{:S(2)}) collective-permute-start(f32[32,128]{1,0:T(8,128)S(1)} %join.5.refs_0_), channel_id=1, source_target_pairs={{0,2},{1,3},{2,0},{3,1},{4,6},{5,7},{6,4},{7,5},{8,10},{9,11},{10,... | collective-permute-start | bytes 49160 | tf_op jit(solution)/shard_map/ppermute | solution.py:67

commit v11 on v10

--- a/solution.py
+++ b/solution.py
@@ -67,21 +67,8 @@
     return lax.ppermute(x, axis, [(d, d ^ mask) for d in range(size)])
 
 
-def join_kernel(first_ref, second_ref, out_ref):
-    out_ref[...] = log_sum([first_ref[...], second_ref[...]])
-
-
-def last_pair(part, axis):
-    mask = 1
-    while 2 * mask < lax.axis_size(axis):
-        part = pl.pallas_call(
-            join_kernel,
-            out_shape=jax.ShapeDtypeStruct(part.shape, jnp.float32),
-            compiler_params=pltpu.CompilerParams(vmem_limit_bytes=4 * mib),
-            name="join",
-        )(part, send(part, axis, mask))
-        mask *= 2
-    return [part, send(part, axis, mask)]
+def from_all(x, axis):
+    return [x] + [send(x, axis, s) for s in range(1, lax.axis_size(axis))]
 
 
 def exchange(copies, axis):
@@ -97,7 +84,9 @@
         out_ref[d * rows + 1 : d * rows + 1 + target.shape[0], :] = target
 
 
-def near_kernel(near_index_ref, cost_ref, plan_ref, mass_ref, totals_ref, x_ref, term_ref, plan_scr):
+def near_kernel(
+    near_index_ref, cost_ref, plan_ref, mass_ref, totals_ref, x_ref, term_ref, plan_scr, cost_scr
+):
     rows = cost_ref.shape[0]
     first = pl.program_id(0) * rows
     near_count = cost_ref.shape[1]
@@ -112,25 +101,38 @@
         plan_scr[a, 2 * width : 3 * width, :] = high
     lanes = lax.broadcasted_iota(jnp.int32, (width, SUB), 1)
     for group in range(rows // SUB):
+        members = range(group * SUB, (group + 1) * SUB)
+        near = [[near_index_ref[k, first + i] & (SUB - 1) for k in range(near_count)] for i in members]
         terms = jnp.zeros((width, SUB), jnp.float32)
-        for i in range(group * SUB, (group + 1) * SUB):
+        for i in members:
             acc = None
             for k in range(near_count):
-                a = group * SUB + (near_index_ref[k, first + i] & (SUB - 1))
                 cost = cost_ref[i, k]
                 high, low = split(cost)
-                x = jnp.dot(
-                    jnp.concatenate([high, high, low], axis=1),
-                    plan_scr[a],
-                    preferred_element_type=jnp.float32,
-                )
-                x_high, x_low = split(x)
-                x_ref[first + i, 0:width, k * wide : (k + 1) * wide] = x_high
-                x_ref[first + i, width : 2 * width, k * wide : (k + 1) * wide] = x_low
-                weighted = cost * cost * mass_ref[pl.ds(first + a, 1), :].astype(jnp.float32)
+                cost_scr[i, k, :, 0:width] = high
+                cost_scr[i, k, :, width : 2 * width] = high
+                cost_scr[i, k, :, 2 * width : 3 * width] = low
+                source = first + group * SUB + near[i % SUB][k]
+                weighted = cost * cost * mass_ref[pl.ds(source, 1), :].astype(jnp.float32)
                 acc = weighted if acc is None else acc + weighted
             terms = jnp.where(lanes == i % SUB, jnp.sum(acc, axis=1, keepdims=True), terms)
         term_ref[first // SUB + group] = terms
+        for a in range(SUB):
+            left = []
+            for i in members:
+                place = near_count - 1
+                for k in range(near_count - 1):
+                    place = jnp.where(near[i % SUB][k] == a, k, place)
+                left.append(cost_scr[i, place])
+            x = jnp.dot(
+                jnp.concatenate(left, axis=0),
+                plan_scr[group * SUB + a],
+                preferred_element_type=jnp.float32,
+            )
+            for i in members:
+                high, low = split(x[(i % SUB) * width : (i % SUB + 1) * width])
+                x_ref[first + i, 0:width, a * wide : (a + 1) * wide] = high
+                x_ref[first + i, width : 2 * width, a * wide : (a + 1) * wide] = low
 
 
 def relay_kernel(*refs):
@@ -212,19 +214,22 @@
         group = row - lax.rem(row, SUB)
         targets = [slot_ref[l, row] for l in range(slots)]
         far_rows = []
+        left = []
         for k in range(near_count):
-            a = group + (near_index_ref[k, row] & (SUB - 1))
+            inside = near_index_ref[k, row] & (SUB - 1)
+            left.append(x_ref[row, :, pl.ds(pl.multiple_of(inside * (slots * width), slots * width), slots * width)])
             for q in range(slots):
-                j = slot_ref[q, a]
+                j = slot_ref[q, group + inside]
                 far_rows.append([table[j * group_blocks + t] for t in targets])
+        left = jnp.concatenate(left, axis=1)
         right_high = jnp.concatenate(
             [jnp.concatenate([far_high[e] for e in r], axis=1) for r in far_rows], axis=0
         )
         right_low = jnp.concatenate(
             [jnp.concatenate([far_low[e] for e in r], axis=1) for r in far_rows], axis=0
         )
-        both = jnp.dot(x_ref[row], right_high, preferred_element_type=jnp.float32)
-        rest = jnp.dot(x_ref[row, 0:width, :], right_low, preferred_element_type=jnp.float32)
+        both = jnp.dot(left, right_high, preferred_element_type=jnp.float32)
+        rest = jnp.dot(left[0:width], right_low, preferred_element_type=jnp.float32)
         product = both[0:width] + (both[width:] + rest)
         tall = term_ref[row // SUB, :, i % SUB : i % SUB + 1] * scale
         scores = []
@@ -383,10 +388,13 @@
         ],
         out_specs=[VMEM, VMEM],
         out_shape=[
-            pltpu.VMEM((rows_here, 2 * width, wide), jnp.bfloat16),
+            pltpu.VMEM((rows_here, 2 * width, SUB * slots * width), jnp.bfloat16),
             pltpu.VMEM((groups, width, SUB), f32),
         ],
-        scratch_shapes=[pltpu.VMEM((step_rows, 3 * width, slots * width), jnp.bfloat16)],
+        scratch_shapes=[
+            pltpu.VMEM((step_rows, 3 * width, slots * width), jnp.bfloat16),
+            pltpu.VMEM((step_rows, near_count, width, 3 * width), jnp.bfloat16),
+        ],
         compiler_params=pltpu.CompilerParams(vmem_limit_bytes=12 * mib),
         cost_estimate=pl.CostEstimate(
             flops=6 * rows_here * wide * width * width,
@@ -481,7 +489,7 @@
     for step in range(ITERS):
         last = step == ITERS - 1
         column_part, source_potential = column_step(
-            last_pair(row_part, "cols"), 1 if last else row_devices
+            from_all(row_part, "cols"), 1 if last else row_devices
         )
         column_parts = exchange(column_part, "rows")
         if not last:

time: 93.6 us -> 89 us (0.951)
  waiting for transfers between devices: 15.3 us -> 10.9 us
  Pallas kernels: 27.9 us -> 26.8 us
    ppermute x13 -> x16, waiting for transfers between devices: 15.3 us -> 10.9 us  [send(): return lax.ppermute(x, axis, [(d, d ^ mask) for d in range(size)])]
    pallas_call x3, Pallas kernels: 5.11 us -> 3.69 us  [column_step(): pl.pallas_call(functools.partial(column_kernel, copies), in_specs=[VMEM]...]
    ppermute x13 -> x16, starting transfers between devices: 16.7 us -> 17.5 us  [send(): return lax.ppermute(x, axis, [(d, d ^ mask) for d in range(size)])]
  transfers between devices with their start and end apart: 14 -> 17, of which waited for: 8 -> 8; matrix products, arithmetic and copies ran while one was open for 0% -> 0% of each run, Pallas kernels for 10% -> 11%
where the time goes in v11:
time: 89 us; the launch traced here: 88.5 us
  blocking collectives  28.8 us (32%)
  Pallas kernels  26.8 us (30%)
  starting transfers between devices  21.3 us (24%)
  waiting for transfers between devices  10.9 us (12%)
    all_to_all x3, blocking collectives, exchange(): return lax.all_to_all(copies, axis, 0, 0, tiled=True)  28.8 us
    ppermute x16, starting transfers between devices, send(): return lax.ppermute(x, axis, [(d, d ^ mask) for d in range(size)])  17.5 us
    ppermute x16, waiting for transfers between devices, send(): return lax.ppermute(x, axis, [(d, d ^ mask) for d in range(size)])  10.9 us
    pallas_call x1, Pallas kernels, per_device(): pl.pallas_call(functools.partial(far_kernel, (row_devices, col_devices, t...  9.11 us
    pallas_call x1, Pallas kernels, per_device(): pl.pallas_call(near_kernel, grid=(rows_here // step_rows,), in_specs=[SME...  8.3 us
    all_to_all x1, starting transfers between devices, exchange(): return lax.all_to_all(copies, axis, 0, 0, tiled=True)  3.82 us
    pallas_call x3, Pallas kernels, column_step(): pl.pallas_call(functools.partial(column_kernel, copies), in_specs=[VMEM]...  3.69 us
    pallas_call x2, Pallas kernels, row_step(): pl.pallas_call(functools.partial(row_kernel, row_devices), in_specs=[SMEM...  3.69 us
  transfers between devices with their start and end apart: 17, of which 8 were waited for; matrix products, arithmetic and copies ran while one was open for 0% of the time, Pallas kernels for 11%

profile of v11, /device:TPU:0, one launch (start us, length us, event | category | flops | bytes accessed | tf_op | source)
XLA Modules:
  0.0 88.5 jit_solution(3290910364602060374)
XLA Ops:
  0.6 4.0 %collective-permute-start.2 = (f32[1,1,3,128,128]{4,3,2,1,0:T(8,128)}, f32[1,1,3,128,128]{4,3,2,1,0:T(8,128)S(1)}, u32[]{:S(2)}, u32[]{:S(2)}) collective-permute-start(f32[1,1,3,128,128]{4,3,2,1,0:T(8,128)} %refs_6_.1), channel_id=1, source_target_pairs={{0,12},{4,8},{8,4},{12,0},{16,28},{20,24},{24,20},{28,16},{1,13},{... | collective-permute-start | bytes 589832 | tf_op jit(solution)/shard_map/ppermute | solution.py:67
  4.7 0.4 collective-permute-start.1
  5.3 2.9 %collective-permute-start.3 = (f32[1,1,3,128,128]{4,3,2,1,0:T(8,128)}, f32[1,1,3,128,128]{4,3,2,1,0:T(8,128)S(1)}, u32[]{:S(2)}, u32[]{:S(2)}) collective-permute-start(f32[1,1,3,128,128]{4,3,2,1,0:T(8,128)} %refs_6_.1), channel_id=1, source_target_pairs={{0,16},{4,20},{8,24},{12,28},{16,0},{20,4},{24,8},{28,12},{1,17},{... | collective-permute-start | bytes 589832 | tf_op jit(solution)/shard_map/ppermute | solution.py:67
  8.2 1.5 %pack.1 = f32[64,128]{1,0:T(8,128)} custom-call(s32[32,128]{1,0:T(8,128)} %bitcast.25, s32[1,128]{1,0:T(1,128)} %target_ref.1), custom_call_target="tpu_custom_call" | custom-call | tf_op jit(solution)/shard_map/pack/pallas_call | solution.py:351
  9.7 3.8 %all-to-all-start = ((f32[32,2,128]{2,1,0:T(2,128)}), f32[32,2,128]{2,1,0:T(2,128)S(1)}, u32[]{:S(2)}, u32[]{:S(2)}) async-start(f32[32,2,128]{2,1,0:T(2,128)} %bitcast.5), calls=%async_computation | async-start | bytes 65536 | tf_op jit(solution)/shard_map/all_to_all | solution.py:75
  13.5 1.3 %collective-permute-done.2.refs_2_ = f32[1,1,3,128,128]{4,3,2,1,0:T(8,128)S(1)} collective-permute-done((f32[1,1,3,128,128]{4,3,2,1,0:T(8,128)}, f32[1,1,3,128,128]{4,3,2,1,0:T(8,128)S(1)}, u32[]{:S(2)}, u32[]{:S(2)}) %collective-permute-start.2) | collective-permute-done | bytes 196640 | tf_op jit(solution)/shard_map/ppermute | solution.py:67
  14.9 3.7 %collective-permute-done.1.refs_1_ = f32[1,1,3,128,128]{4,3,2,1,0:T(8,128)S(1)} collective-permute-done((f32[1,1,3,128,128]{4,3,2,1,0:T(8,128)}, f32[1,1,3,128,128]{4,3,2,1,0:T(8,128)S(1)}, u32[]{:S(2)}, u32[]{:S(2)}) %collective-permute-start.1) | collective-permute-done | bytes 196640 | tf_op jit(solution)/shard_map/ppermute | solution.py:67
  18.6 2.6 %collective-permute-start.6 = (f32[1,1,3,128,128]{4,3,2,1,0:T(8,128)S(1)}, f32[1,1,3,128,128]{4,3,2,1,0:T(8,128)S(1)}, u32[]{:S(2)}, u32[]{:S(2)}) collective-permute-start(f32[1,1,3,128,128]{4,3,2,1,0:T(8,128)S(1)} %get-tuple-element.25.refs_10_), channel_id=1, source_target_pairs={{0,12},{4,8},{8,4},{12,0},{16,28},{20,24},{24,20},{28,16},{1,13},{... | collective-permute-start | bytes 589832 | tf_op jit(solution)/shard_map/ppermute | solution.py:67
  21.3 1.5 %collective-permute-start.4 = (f32[1,1,3,128,128]{4,3,2,1,0:T(8,128)S(1)}, f32[1,1,3,128,128]{4,3,2,1,0:T(8,128)S(1)}, u32[]{:S(2)}, u32[]{:S(2)}) collective-permute-start(f32[1,1,3,128,128]{4,3,2,1,0:T(8,128)S(1)} %get-tuple-element.25.refs_10_), channel_id=1, source_target_pairs={{0,4},{4,0},{8,12},{12,8},{16,20},{20,16},{24,28},{28,24},{1,5},{5... | collective-permute-start | bytes 589832 | tf_op jit(solution)/shard_map/ppermute | solution.py:67
  22.8 8.3 %near_product.1 = (bf16[32,256,1024]{2,1,0:T(8,128)(2,1)S(1)}, f32[8,128,4]{2,1,0:T(8,128)S(1)}) custom-call(s32[3,32]{1,0:T(4,128)} %bitcast.31, f32[32,3,128,128]{3,2,1,0:T(8,128)} %cost_ref.1, f32[32,1,2,128,128]{4,3,2,1,0:T(8,128)} %plan_ref.1, s32[32,128]{1,0:T(8,128)} %bitcast.26, f32[64,128]{1,0:T(8,128)S(1)} %bitcast.17), custom_call_target="tpu_custom_call" | custom-call | flops 2415919104 | bytes 10485760 | tf_op jit(solution)/shard_map/near_product/pallas_call | solution.py:379
  31.1 9.1 %far_product.1 = (f32[32,1,2,128,128]{4,3,2,1,0:T(8,128)}, f32[32,2,128,128]{3,2,1,0:T(8,128)S(1)}, f32[32,2,128,128]{3,2,1,0:T(8,128)S(1)}, f32[32,128]{1,0:T(8...) custom-call(s32[3,32]{1,0:T(4,128)} %bitcast.32, s32[2,32]{1,0:T(2,128)} %bitcast.28, ...), custom_call_target="tpu_custom_call" | custom-call | tf_op jit(solution)/shard_map/far_product/pallas_call | solution.py:412
  40.3 1.5 %collective-permute-start.8 = (f32[32,128]{1,0:T(8,128)S(1)}, f32[32,128]{1,0:T(8,128)S(1)}, u32[]{:S(2)}, u32[]{:S(2)}) collective-permute-start(f32[32,128]{1,0:T(8,128)S(1)} %get-tuple-element.32.refs_0_), channel_id=1, source_target_pairs={{0,2},{1,3},{2,0},{3,1},{4,6},{5,7},{6,4},{7,5},{8,10},{9,11},{10,... | collective-permute-start | bytes 49160 | tf_op jit(solution)/shard_map/ppermute | solution.py:67
  41.8 0.3 collective-permute-start.7
  42.1 1.4 %collective-permute-done.9.refs_3_ = f32[32,128]{1,0:T(8,128)S(1)} collective-permute-done((f32[32,128]{1,0:T(8,128)S(1)}, f32[32,128]{1,0:T(8,128)S(1)}, u32[]{:S(2)}, u32[]{:S(2)}) %collective-permute-start.9) | collective-permute-done | bytes 16416 | tf_op jit(solution)/shard_map/ppermute | solution.py:67
  43.5 0.5 collective-permute-done.8.refs_2_
  44.0 1.2 %column_pass.3 = (f32[64,128]{1,0:T(8,128)S(1)}, f32[32,128]{1,0:T(8,128)}) custom-call(f32[32,2,128,128]{3,2,1,0:T(8,128)S(1)} %get-tuple-element.27.work_ref, s32[64,128]{1,0:T(8,128)S(1)} %get-tuple-element.28.select_ref, f32[32,128]{1,0:T(8,128)S(1)} %get-tuple-element.29.log_mass_ref, f32[32,128]{1,0:T(8,128)S(1)} %get-tuple-element.32.refs_0_, ...), custom_call_target="tpu_custom_call" | custom-call | tf_op jit(solution)/shard_map/column_pass/pallas_call | solution.py:457
  45.3 10.9 %all_to_all.44 = f32[8,8,128]{2,1,0:T(8,128)S(1)} all-to-all(f32[8,8,128]{2,1,0:T(8,128)S(1)} %bitcast.21), channel_id=1, replica_groups=mesh['rows'=8,'cols'=4] {'rows'}, dimensions={0} | all-to-all | bytes 65536 | tf_op jit(solution)/shard_map/all_to_all | solution.py:75
  56.2 1.8 %row_pass.2.refs_0_ = f32[32,128]{1,0:T(8,128)S(1)} custom-call(s32[2,32]{1,0:T(2,128)} %bitcast.29, f32[32,2,128,128]{3,2,1,0:T(8,128)S(1)} %get-tuple-element.30.tall_ref, f32[8,128]{1,0:T(8,128)S(1)} %get-tuple-element.31.log_mass_ref, f32[64,128]{1,0:T(8,128)S(1)} %bitcast.20), custom_call_target="tpu_custom_call" | custom-call | tf_op jit(solution)/shard_map/row_pass/pallas_call | solution.py:475
  58.1 1.6 %collective-permute-start.11 = (f32[32,128]{1,0:T(8,128)S(1)}, f32[32,128]{1,0:T(8,128)S(1)}, u32[]{:S(2)}, u32[]{:S(2)}) collective-permute-start(f32[32,128]{1,0:T(8,128)S(1)} %row_pass.2.refs_0_), channel_id=1, source_target_pairs={{0,2},{1,3},{2,0},{3,1},{4,6},{5,7},{6,4},{7,5},{8,10},{9,11},{10,... | collective-permute-start | bytes 49160 | tf_op jit(solution)/shard_map/ppermute | solution.py:67
  59.7 0.3 collective-permute-start.10
  59.9 1.4 %collective-permute-done.12.refs_3_ = f32[32,128]{1,0:T(8,128)S(1)} collective-permute-done((f32[32,128]{1,0:T(8,128)S(1)}, f32[32,128]{1,0:T(8,128)S(1)}, u32[]{:S(2)}, u32[]{:S(2)}) %collective-permute-start.12) | collective-permute-done | bytes 16416 | tf_op jit(solution)/shard_map/ppermute | solution.py:67
  61.3 0.6 collective-permute-done.11.refs_2_
  61.9 1.2 %column_pass.4 = (f32[64,128]{1,0:T(8,128)S(1)}, f32[32,128]{1,0:T(8,128)}) custom-call(f32[32,2,128,128]{3,2,1,0:T(8,128)S(1)} %get-tuple-element.27.work_ref, s32[64,128]{1,0:T(8,128)S(1)} %get-tuple-element.28.select_ref, f32[32,128]{1,0:T(8,128)S(1)} %get-tuple-element.29.log_mass_ref, f32[32,128]{1,0:T(8,128)S(1)} %row_pass.2.refs_0_, ...), custom_call_target="tpu_custom_call" | custom-call | tf_op jit(solution)/shard_map/column_pass/pallas_call | solution.py:457
  63.1 9.1 %all_to_all.45 = f32[8,8,128]{2,1,0:T(8,128)S(1)} all-to-all(f32[8,8,128]{2,1,0:T(8,128)S(1)} %bitcast.22), channel_id=1, replica_groups=mesh['rows'=8,'cols'=4] {'rows'}, dimensions={0} | all-to-all | bytes 65536 | tf_op jit(solution)/shard_map/all_to_all | solution.py:75
  72.2 1.8 %row_pass.3.refs_0_ = f32[32,128]{1,0:T(8,128)S(1)} custom-call(s32[2,32]{1,0:T(2,128)} %bitcast.30, f32[32,2,128,128]{3,2,1,0:T(8,128)S(1)} %get-tuple-element.30.tall_ref, f32[8,128]{1,0:T(8,128)S(1)} %get-tuple-element.31.log_mass_ref, f32[64,128]{1,0:T(8,128)S(1)} %bitcast.19), custom_call_target="tpu_custom_call" | custom-call | tf_op jit(solution)/shard_map/row_pass/pallas_call | solution.py:475
  74.1 1.6 %collective-permute-start.14 = (f32[32,128]{1,0:T(8,128)S(1)}, f32[32,128]{1,0:T(8,128)S(1)}, u32[]{:S(2)}, u32[]{:S(2)}) collective-permute-start(f32[32,128]{1,0:T(8,128)S(1)} %row_pass.3.refs_0_), channel_id=1, source_target_pairs={{0,2},{1,3},{2,0},{3,1},{4,6},{5,7},{6,4},{7,5},{8,10},{9,11},{10,... | collective-permute-start | bytes 49160 | tf_op jit(solution)/shard_map/ppermute | solution.py:67
  75.7 0.3 collective-permute-start.13
  76.0 1.4 %collective-permute-done.15.refs_3_ = f32[32,128]{1,0:T(8,128)S(1)} collective-permute-done((f32[32,128]{1,0:T(8,128)S(1)}, f32[32,128]{1,0:T(8,128)S(1)}, u32[]{:S(2)}, u32[]{:S(2)}) %collective-permute-start.15) | collective-permute-done | bytes 16416 | tf_op jit(solution)/shard_map/ppermute | solution.py:67
  77.4 0.6 collective-permute-done.14.refs_2_
  77.9 1.2 %column_pass.5 = (f32[8,128]{1,0:T(8,128)S(1)}, f32[32,128]{1,0:T(8,128)}) custom-call(f32[32,2,128,128]{3,2,1,0:T(8,128)S(1)} %get-tuple-element.27.work_ref, s32[64,128]{1,0:T(8,128)S(1)} %get-tuple-element.28.select_ref, f32[32,128]{1,0:T(8,128)S(1)} %get-tuple-element.29.log_mass_ref, f32[32,128]{1,0:T(8,128)S(1)} %row_pass.3.refs_0_, ...), custom_call_target="tpu_custom_call" | custom-call | tf_op jit(solution)/shard_map/column_pass/pallas_call | solution.py:457
  79.2 8.8 %all_to_all.46 = f32[8,1,128]{2,1,0:T(1,128)S(1)} all-to-all(f32[8,1,128]{2,1,0:T(1,128)S(1)} %bitcast.24), channel_id=1, replica_groups=mesh['rows'=8,'cols'=4] {'rows'}, dimensions={0} | all-to-all | bytes 8192 | tf_op jit(solution)/shard_map/all_to_all | solution.py:75
  88.0 0.5 last_potential.1
  (17 shorter events, 0.5 us)
Async XLA Ops:
  0.6 14.2 %collective-permute-start.2 = (f32[1,1,3,128,128]{4,3,2,1,0:T(8,128)}, f32[1,1,3,128,128]{4,3,2,1,0:T(8,128)S(1)}, u32[]{:S(2)}, u32[]{:S(2)}) collective-permute-start(f32[1,1,3,128,128]{4,3,2,1,0:T(8,128)} %refs_6_.1), channel_id=1, source_target_pairs={{0,12},{4,8},{8,4},{12,0},{16,28},{20,24},{24,20},{28,16},{1,13},{... | collective-permute-start | bytes 589832 | tf_op jit(solution)/shard_map/ppermute | solution.py:67
  4.7 13.9 %collective-permute-start.1 = (f32[1,1,3,128,128]{4,3,2,1,0:T(8,128)}, f32[1,1,3,128,128]{4,3,2,1,0:T(8,128)S(1)}, u32[]{:S(2)}, u32[]{:S(2)}) collective-permute-start(f32[1,1,3,128,128]{4,3,2,1,0:T(8,128)} %refs_6_.1), channel_id=1, source_target_pairs={{0,8},{4,12},{8,0},{12,4},{16,24},{20,28},{24,16},{28,20},{1,9},{5... | collective-permute-start | bytes 589832 | tf_op jit(solution)/shard_map/ppermute | solution.py:67
  5.1 13.5 %collective-permute-start = (f32[1,1,3,128,128]{4,3,2,1,0:T(8,128)}, f32[1,1,3,128,128]{4,3,2,1,0:T(8,128)S(1)}, u32[]{:S(2)}, u32[]{:S(2)}) collective-permute-start(f32[1,1,3,128,128]{4,3,2,1,0:T(8,128)} %refs_6_.1), channel_id=1, source_target_pairs={{0,4},{4,0},{8,12},{12,8},{16,20},{20,16},{24,28},{28,24},{1,5},{5... | collective-permute-start | bytes 589832 | tf_op jit(solution)/shard_map/ppermute | solution.py:67
  5.3 13.3 %collective-permute-start.3 = (f32[1,1,3,128,128]{4,3,2,1,0:T(8,128)}, f32[1,1,3,128,128]{4,3,2,1,0:T(8,128)S(1)}, u32[]{:S(2)}, u32[]{:S(2)}) collective-permute-start(f32[1,1,3,128,128]{4,3,2,1,0:T(8,128)} %refs_6_.1), channel_id=1, source_target_pairs={{0,16},{4,20},{8,24},{12,28},{16,0},{20,4},{24,8},{28,12},{1,17},{... | collective-permute-start | bytes 589832 | tf_op jit(solution)/shard_map/ppermute | solution.py:67
  9.7 13.1 %all-to-all-start = ((f32[32,2,128]{2,1,0:T(2,128)}), f32[32,2,128]{2,1,0:T(2,128)S(1)}, u32[]{:S(2)}, u32[]{:S(2)}) async-start(f32[32,2,128]{2,1,0:T(2,128)} %bitcast.5), calls=%async_computation | async-start | bytes 65536 | tf_op jit(solution)/shard_map/all_to_all | solution.py:75
  18.6 12.5 %collective-permute-start.6 = (f32[1,1,3,128,128]{4,3,2,1,0:T(8,128)S(1)}, f32[1,1,3,128,128]{4,3,2,1,0:T(8,128)S(1)}, u32[]{:S(2)}, u32[]{:S(2)}) collective-permute-start(f32[1,1,3,128,128]{4,3,2,1,0:T(8,128)S(1)} %get-tuple-element.25.refs_10_), channel_id=1, source_target_pairs={{0,12},{4,8},{8,4},{12,0},{16,28},{20,24},{24,20},{28,16},{1,13},{... | collective-permute-start | bytes 589832 | tf_op jit(solution)/shard_map/ppermute | solution.py:67
  21.2 9.9 %collective-permute-start.5 = (f32[1,1,3,128,128]{4,3,2,1,0:T(8,128)S(1)}, f32[1,1,3,128,128]{4,3,2,1,0:T(8,128)S(1)}, u32[]{:S(2)}, u32[]{:S(2)}) collective-permute-start(f32[1,1,3,128,128]{4,3,2,1,0:T(8,128)S(1)} %get-tuple-element.25.refs_10_), channel_id=1, source_target_pairs={{0,8},{4,12},{8,0},{12,4},{16,24},{20,28},{24,16},{28,20},{1,9},{5... | collective-permute-start | bytes 589832 | tf_op jit(solution)/shard_map/ppermute | solution.py:67
  21.3 9.8 %collective-permute-start.4 = (f32[1,1,3,128,128]{4,3,2,1,0:T(8,128)S(1)}, f32[1,1,3,128,128]{4,3,2,1,0:T(8,128)S(1)}, u32[]{:S(2)}, u32[]{:S(2)}) collective-permute-start(f32[1,1,3,128,128]{4,3,2,1,0:T(8,128)S(1)} %get-tuple-element.25.refs_10_), channel_id=1, source_target_pairs={{0,4},{4,0},{8,12},{12,8},{16,20},{20,16},{24,28},{28,24},{1,5},{5... | collective-permute-start | bytes 589832 | tf_op jit(solution)/shard_map/ppermute | solution.py:67
  22.8 8.3 %copy-start = (f32[1,1,3,128,128]{4,3,2,1,0:T(8,128)S(1)}, f32[1,1,3,128,128]{4,3,2,1,0:T(8,128)}, u32[]{:S(2)}) copy-start(f32[1,1,3,128,128]{4,3,2,1,0:T(8,128)} %refs_6_.1) | copy-start | bytes 589828
  40.3 3.3 %collective-permute-start.9 = (f32[32,128]{1,0:T(8,128)S(1)}, f32[32,128]{1,0:T(8,128)S(1)}, u32[]{:S(2)}, u32[]{:S(2)}) collective-permute-start(f32[32,128]{1,0:T(8,128)S(1)} %get-tuple-element.32.refs_0_), channel_id=1, source_target_pairs={{0,3},{1,2},{2,1},{3,0},{4,7},{5,6},{6,5},{7,4},{8,11},{9,10},{10,... | collective-permute-start | bytes 49160 | tf_op jit(solution)/shard_map/ppermute | solution.py:67
  40.3 3.8 %collective-permute-start.8 = (f32[32,128]{1,0:T(8,128)S(1)}, f32[32,128]{1,0:T(8,128)S(1)}, u32[]{:S(2)}, u32[]{:S(2)}) collective-permute-start(f32[32,128]{1,0:T(8,128)S(1)} %get-tuple-element.32.refs_0_), channel_id=1, source_target_pairs={{0,2},{1,3},{2,0},{3,1},{4,6},{5,7},{6,4},{7,5},{8,10},{9,11},{10,... | collective-permute-start | bytes 49160 | tf_op jit(solution)/shard_map/ppermute | solution.py:67
  41.8 2.2 %collective-permute-start.7 = (f32[32,128]{1,0:T(8,128)S(1)}, f32[32,128]{1,0:T(8,128)S(1)}, u32[]{:S(2)}, u32[]{:S(2)}) collective-permute-start(f32[32,128]{1,0:T(8,128)S(1)} %get-tuple-element.32.refs_0_), channel_id=1, source_target_pairs={{0,1},{1,0},{2,3},{3,2},{4,5},{5,4},{6,7},{7,6},{8,9},{9,8},{10,11... | collective-permute-start | bytes 49160 | tf_op jit(solution)/shard_map/ppermute | solution.py:67
  58.0 3.3 %collective-permute-start.12 = (f32[32,128]{1,0:T(8,128)S(1)}, f32[32,128]{1,0:T(8,128)S(1)}, u32[]{:S(2)}, u32[]{:S(2)}) collective-permute-start(f32[32,128]{1,0:T(8,128)S(1)} %row_pass.2.refs_0_), channel_id=1, source_target_pairs={{0,3},{1,2},{2,1},{3,0},{4,7},{5,6},{6,5},{7,4},{8,11},{9,10},{10,... | collective-permute-start | bytes 49160 | tf_op jit(solution)/shard_map/ppermute | solution.py:67
  58.1 3.8 %collective-permute-start.11 = (f32[32,128]{1,0:T(8,128)S(1)}, f32[32,128]{1,0:T(8,128)S(1)}, u32[]{:S(2)}, u32[]{:S(2)}) collective-permute-start(f32[32,128]{1,0:T(8,128)S(1)} %row_pass.2.refs_0_), channel_id=1, source_target_pairs={{0,2},{1,3},{2,0},{3,1},{4,6},{5,7},{6,4},{7,5},{8,10},{9,11},{10,... | collective-permute-start | bytes 49160 | tf_op jit(solution)/shard_map/ppermute | solution.py:67
  59.7 2.2 %collective-permute-start.10 = (f32[32,128]{1,0:T(8,128)S(1)}, f32[32,128]{1,0:T(8,128)S(1)}, u32[]{:S(2)}, u32[]{:S(2)}) collective-permute-start(f32[32,128]{1,0:T(8,128)S(1)} %row_pass.2.refs_0_), channel_id=1, source_target_pairs={{0,1},{1,0},{2,3},{3,2},{4,5},{5,4},{6,7},{7,6},{8,9},{9,8},{10,11... | collective-permute-start | bytes 49160 | tf_op jit(solution)/shard_map/ppermute | solution.py:67
  74.0 3.3 %collective-permute-start.15 = (f32[32,128]{1,0:T(8,128)S(1)}, f32[32,128]{1,0:T(8,128)S(1)}, u32[]{:S(2)}, u32[]{:S(2)}) collective-permute-start(f32[32,128]{1,0:T(8,128)S(1)} %row_pass.3.refs_0_), channel_id=1, source_target_pairs={{0,3},{1,2},{2,1},{3,0},{4,7},{5,6},{6,5},{7,4},{8,11},{9,10},{10,... | collective-permute-start | bytes 49160 | tf_op jit(solution)/shard_map/ppermute | solution.py:67
  74.1 3.8 %collective-permute-start.14 = (f32[32,128]{1,0:T(8,128)S(1)}, f32[32,128]{1,0:T(8,128)S(1)}, u32[]{:S(2)}, u32[]{:S(2)}) collective-permute-start(f32[32,128]{1,0:T(8,128)S(1)} %row_pass.3.refs_0_), channel_id=1, source_target_pairs={{0,2},{1,3},{2,0},{3,1},{4,6},{5,7},{6,4},{7,5},{8,10},{9,11},{10,... | collective-permute-start | bytes 49160 | tf_op jit(solution)/shard_map/ppermute | solution.py:67
  75.7 2.2 %collective-permute-start.13 = (f32[32,128]{1,0:T(8,128)S(1)}, f32[32,128]{1,0:T(8,128)S(1)}, u32[]{:S(2)}, u32[]{:S(2)}) collective-permute-start(f32[32,128]{1,0:T(8,128)S(1)} %row_pass.3.refs_0_), channel_id=1, source_target_pairs={{0,1},{1,0},{2,3},{3,2},{4,5},{5,4},{6,7},{7,6},{8,9},{9,8},{10,11... | collective-permute-start | bytes 49160 | tf_op jit(solution)/shard_map/ppermute | solution.py:67

commit v12 on v10

--- a/solution.py
+++ b/solution.py
@@ -67,21 +67,8 @@
     return lax.ppermute(x, axis, [(d, d ^ mask) for d in range(size)])
 
 
-def join_kernel(first_ref, second_ref, out_ref):
-    out_ref[...] = log_sum([first_ref[...], second_ref[...]])
-
-
-def last_pair(part, axis):
-    mask = 1
-    while 2 * mask < lax.axis_size(axis):
-        part = pl.pallas_call(
-            join_kernel,
-            out_shape=jax.ShapeDtypeStruct(part.shape, jnp.float32),
-            compiler_params=pltpu.CompilerParams(vmem_limit_bytes=4 * mib),
-            name="join",
-        )(part, send(part, axis, mask))
-        mask *= 2
-    return [part, send(part, axis, mask)]
+def from_all(x, axis):
+    return [x] + [send(x, axis, s) for s in range(1, lax.axis_size(axis))]
 
 
 def exchange(copies, axis):
@@ -241,14 +228,30 @@
 
     @pl.when(g == pl.num_programs(0) - 1)
     def _():
-        part_ref[...] = peak_scr[...] + jnp.log2(sum_scr[...])
+        part_ref[...] = row_sums(peak_scr, sum_scr)
+
+
+def block_sums(score):
+    pieces = score.reshape(-1, 8, score.shape[-1])
+    peak = jnp.max(pieces, axis=0)
+    return peak, jnp.sum(jnp.exp2(pieces - peak[None]), axis=0)
+
+
+def over_residues(peaks, sums):
+    peak = jnp.max(peaks, axis=1)
+    return peak, jnp.sum(sums * jnp.exp2(peaks - peak[:, None, :]), axis=1)
 
 
 def row_pass(scores, row, peak_scr, sum_scr):
-    peak = jnp.max(functools.reduce(jnp.maximum, scores), axis=0, keepdims=True)
-    total = functools.reduce(jnp.add, [jnp.exp2(s - peak) for s in scores])
-    peak_scr[pl.ds(row, 1), :] = peak
-    sum_scr[pl.ds(row, 1), :] = jnp.sum(total, axis=0, keepdims=True)
+    for l, score in enumerate(scores):
+        peak, total = block_sums(score)
+        peak_scr[row, l * 8 : (l + 1) * 8, :] = peak
+        sum_scr[row, l * 8 : (l + 1) * 8, :] = total
+
+
+def row_sums(peak_scr, sum_scr):
+    peak, total = over_residues(peak_scr[...], sum_scr[...])
+    return peak + jnp.log2(total)
 
 
 def column_kernel(copies, work_ref, select_ref, log_mass_ref, *refs):
@@ -265,14 +268,10 @@
         for i in range(together):
             for l in range(slots):
                 score = tall[:, i : i + 1] + work_ref[first + i, l]
-                peak = jnp.max(score, axis=0, keepdims=True)
-                total = jnp.sum(jnp.exp2(score - peak), axis=0, keepdims=True)
                 place = (first + i) * slots + l
-                peak_scr[place : place + 1, :] = peak
-                sum_scr[place : place + 1, :] = total
+                peak_scr[place], sum_scr[place] = block_sums(score)
     select = select_ref[...]
-    peaks = peak_scr[...]
-    sums = sum_scr[...]
+    peaks, sums = over_residues(peak_scr[...], sum_scr[...])
     blocks = out_ref.shape[0] // copies
     for t in range(blocks):
         chosen = select == t
@@ -298,7 +297,7 @@
     for row in range(rows):
         scores = [wide_scr[slot_ref[l, row]] + tall_ref[row, l] for l in range(slots)]
         row_pass(scores, row, peak_scr, sum_scr)
-    out_ref[...] = peak_scr[...] + jnp.log2(sum_scr[...])
+    out_ref[...] = row_sums(peak_scr, sum_scr)
 
 
 def last_kernel(row_devices, row_axis, log_mass_ref, parts_ref, out_ref):
@@ -436,8 +435,8 @@
             pltpu.SMEM((group_blocks * group_blocks,), jnp.int32),
             pltpu.VMEM((group_blocks, width), f32),
             pltpu.VMEM((1, width), f32),
-            pltpu.VMEM((rows_here, width), f32),
-            pltpu.VMEM((rows_here, width), f32),
+            pltpu.VMEM((rows_here, slots * 8, width), f32),
+            pltpu.VMEM((rows_here, slots * 8, width), f32),
         ],
         compiler_params=pltpu.CompilerParams(vmem_limit_bytes=12 * mib + 2 * far_bytes),
         name="far_product",
@@ -456,8 +455,8 @@
             ],
             scratch_shapes=[
                 pltpu.VMEM((rows_here, width), f32),
-                pltpu.VMEM((rows_here * slots, width), f32),
-                pltpu.VMEM((rows_here * slots, width), f32),
+                pltpu.VMEM((rows_here * slots, 8, width), f32),
+                pltpu.VMEM((rows_here * slots, 8, width), f32),
             ],
             compiler_params=pass_params,
             name="column_pass",
@@ -471,8 +470,8 @@
             out_shape=jax.ShapeDtypeStruct((rows_here, width), f32),
             scratch_shapes=[
                 pltpu.VMEM((group_blocks, width, width), f32),
-                pltpu.VMEM((rows_here, width), f32),
-                pltpu.VMEM((rows_here, width), f32),
+                pltpu.VMEM((rows_here, slots * 8, width), f32),
+                pltpu.VMEM((rows_here, slots * 8, width), f32),
             ],
             compiler_params=pass_params,
             name="row_pass",
@@ -481,7 +480,7 @@
     for step in range(ITERS):
         last = step == ITERS - 1
         column_part, source_potential = column_step(
-            last_pair(row_part, "cols"), 1 if last else row_devices
+            from_all(row_part, "cols"), 1 if last else row_devices
         )
         column_parts = exchange(column_part, "rows")
         if not last:

time: 93.6 us -> 90.3 us (0.965)
  waiting for transfers between devices: 15.3 us -> 10.9 us
    ppermute x13 -> x16, waiting for transfers between devices: 15.3 us -> 10.9 us  [send(): return lax.ppermute(x, axis, [(d, d ^ mask) for d in range(size)])]
    ppermute x13 -> x16, starting transfers between devices: 16.7 us -> 17.5 us  [send(): return lax.ppermute(x, axis, [(d, d ^ mask) for d in range(size)])]
  transfers between devices with their start and end apart: 14 -> 17, of which waited for: 8 -> 8; matrix products, arithmetic and copies ran while one was open for 0% -> 0% of each run, Pallas kernels for 10% -> 10%
where the time goes in v12:
time: 90.3 us; the launch traced here: 89.8 us
  blocking collectives  28.8 us (32%)
  Pallas kernels  28 us (31%)
  starting transfers between devices  21.3 us (24%)
  waiting for transfers between devices  10.9 us (12%)
    all_to_all x3, blocking collectives, exchange(): return lax.all_to_all(copies, axis, 0, 0, tiled=True)  28.8 us
    ppermute x16, starting transfers between devices, send(): return lax.ppermute(x, axis, [(d, d ^ mask) for d in range(size)])  17.5 us
    ppermute x16, waiting for transfers between devices, send(): return lax.ppermute(x, axis, [(d, d ^ mask) for d in range(size)])  10.9 us
    pallas_call x1, Pallas kernels, per_device(): pl.pallas_call(functools.partial(far_kernel, (row_devices, col_devices, t...  9.53 us
    pallas_call x1, Pallas kernels, per_device(): pl.pallas_call(near_kernel, grid=(rows_here // step_rows,), in_specs=[SME...  7.66 us
    pallas_call x3, Pallas kernels, column_step(): pl.pallas_call(functools.partial(column_kernel, copies), in_specs=[VMEM]...  5.22 us
    all_to_all x1, starting transfers between devices, exchange(): return lax.all_to_all(copies, axis, 0, 0, tiled=True)  3.82 us
    pallas_call x2, Pallas kernels, row_step(): pl.pallas_call(functools.partial(row_kernel, row_devices), in_specs=[SMEM...  3.63 us
  transfers between devices with their start and end apart: 17, of which 8 were waited for; matrix products, arithmetic and copies ran while one was open for 0% of the time, Pallas kernels for 10%

profile of v12, /device:TPU:0, one launch (start us, length us, event | category | flops | bytes accessed | tf_op | source)
XLA Modules:
  0.0 89.8 jit_solution(14540934769102339331)
XLA Ops:
  0.6 4.0 %collective-permute-start.2 = (f32[1,1,3,128,128]{4,3,2,1,0:T(8,128)}, f32[1,1,3,128,128]{4,3,2,1,0:T(8,128)S(1)}, u32[]{:S(2)}, u32[]{:S(2)}) collective-permute-start(f32[1,1,3,128,128]{4,3,2,1,0:T(8,128)} %refs_6_.1), channel_id=1, source_target_pairs={{0,12},{4,8},{8,4},{12,0},{16,28},{20,24},{24,20},{28,16},{1,13},{... | collective-permute-start | bytes 589832 | tf_op jit(solution)/shard_map/ppermute | solution.py:67
  4.7 0.4 collective-permute-start.1
  5.3 2.9 %collective-permute-start.3 = (f32[1,1,3,128,128]{4,3,2,1,0:T(8,128)}, f32[1,1,3,128,128]{4,3,2,1,0:T(8,128)S(1)}, u32[]{:S(2)}, u32[]{:S(2)}) collective-permute-start(f32[1,1,3,128,128]{4,3,2,1,0:T(8,128)} %refs_6_.1), channel_id=1, source_target_pairs={{0,16},{4,20},{8,24},{12,28},{16,0},{20,4},{24,8},{28,12},{1,17},{... | collective-permute-start | bytes 589832 | tf_op jit(solution)/shard_map/ppermute | solution.py:67
  8.2 1.5 %pack.1 = f32[64,128]{1,0:T(8,128)} custom-call(s32[32,128]{1,0:T(8,128)} %bitcast.25, s32[1,128]{1,0:T(1,128)} %target_ref.1), custom_call_target="tpu_custom_call" | custom-call | tf_op jit(solution)/shard_map/pack/pallas_call | solution.py:345
  9.7 3.8 %all-to-all-start = ((f32[32,2,128]{2,1,0:T(2,128)}), f32[32,2,128]{2,1,0:T(2,128)S(1)}, u32[]{:S(2)}, u32[]{:S(2)}) async-start(f32[32,2,128]{2,1,0:T(2,128)} %bitcast.5), calls=%async_computation | async-start | bytes 65536 | tf_op jit(solution)/shard_map/all_to_all | solution.py:75
  13.5 1.3 %collective-permute-done.2.refs_2_ = f32[1,1,3,128,128]{4,3,2,1,0:T(8,128)S(1)} collective-permute-done((f32[1,1,3,128,128]{4,3,2,1,0:T(8,128)}, f32[1,1,3,128,128]{4,3,2,1,0:T(8,128)S(1)}, u32[]{:S(2)}, u32[]{:S(2)}) %collective-permute-start.2) | collective-permute-done | bytes 196640 | tf_op jit(solution)/shard_map/ppermute | solution.py:67
  14.9 3.7 %collective-permute-done.1.refs_1_ = f32[1,1,3,128,128]{4,3,2,1,0:T(8,128)S(1)} collective-permute-done((f32[1,1,3,128,128]{4,3,2,1,0:T(8,128)}, f32[1,1,3,128,128]{4,3,2,1,0:T(8,128)S(1)}, u32[]{:S(2)}, u32[]{:S(2)}) %collective-permute-start.1) | collective-permute-done | bytes 196640 | tf_op jit(solution)/shard_map/ppermute | solution.py:67
  18.6 2.6 %collective-permute-start.6 = (f32[1,1,3,128,128]{4,3,2,1,0:T(8,128)S(1)}, f32[1,1,3,128,128]{4,3,2,1,0:T(8,128)S(1)}, u32[]{:S(2)}, u32[]{:S(2)}) collective-permute-start(f32[1,1,3,128,128]{4,3,2,1,0:T(8,128)S(1)} %get-tuple-element.25.refs_10_), channel_id=1, source_target_pairs={{0,12},{4,8},{8,4},{12,0},{16,28},{20,24},{24,20},{28,16},{1,13},{... | collective-permute-start | bytes 589832 | tf_op jit(solution)/shard_map/ppermute | solution.py:67
  21.3 1.5 %collective-permute-start.4 = (f32[1,1,3,128,128]{4,3,2,1,0:T(8,128)S(1)}, f32[1,1,3,128,128]{4,3,2,1,0:T(8,128)S(1)}, u32[]{:S(2)}, u32[]{:S(2)}) collective-permute-start(f32[1,1,3,128,128]{4,3,2,1,0:T(8,128)S(1)} %get-tuple-element.25.refs_10_), channel_id=1, source_target_pairs={{0,4},{4,0},{8,12},{12,8},{16,20},{20,16},{24,28},{28,24},{1,5},{5... | collective-permute-start | bytes 589832 | tf_op jit(solution)/shard_map/ppermute | solution.py:67
  22.8 7.7 %near_product.1 = (bf16[32,256,768]{2,1,0:T(8,128)(2,1)S(1)}, f32[8,128,4]{2,1,0:T(8,128)S(1)}) custom-call(s32[3,32]{1,0:T(4,128)} %bitcast.31, f32[32,3,128,128]{3,2,1,0:T(8,128)} %cost_ref.1, f32[32,1,2,128,128]{4,3,2,1,0:T(8,128)} %plan_ref.1, s32[32,128]{1,0:T(8,128)} %bitcast.26, f32[64,128]{1,0:T(8,128)S(1)} %bitcast.17), custom_call_target="tpu_custom_call" | custom-call | flops 2415919104 | bytes 10485760 | tf_op jit(solution)/shard_map/near_product/pallas_call | solution.py:373
  30.5 9.5 %far_product.1 = (f32[32,1,2,128,128]{4,3,2,1,0:T(8,128)}, f32[32,2,128,128]{3,2,1,0:T(8,128)S(1)}, f32[32,2,128,128]{3,2,1,0:T(8,128)S(1)}, f32[32,128]{1,0:T(8...) custom-call(s32[3,32]{1,0:T(4,128)} %bitcast.32, s32[2,32]{1,0:T(2,128)} %bitcast.28, ...), custom_call_target="tpu_custom_call" | custom-call | tf_op jit(solution)/shard_map/far_product/pallas_call | solution.py:403
  40.0 1.5 %collective-permute-start.8 = (f32[32,128]{1,0:T(8,128)S(1)}, f32[32,128]{1,0:T(8,128)S(1)}, u32[]{:S(2)}, u32[]{:S(2)}) collective-permute-start(f32[32,128]{1,0:T(8,128)S(1)} %get-tuple-element.32.refs_0_), channel_id=1, source_target_pairs={{0,2},{1,3},{2,0},{3,1},{4,6},{5,7},{6,4},{7,5},{8,10},{9,11},{10,... | collective-permute-start | bytes 49160 | tf_op jit(solution)/shard_map/ppermute | solution.py:67
  41.6 0.3 collective-permute-start.7
  41.9 1.4 %collective-permute-done.9.refs_3_ = f32[32,128]{1,0:T(8,128)S(1)} collective-permute-done((f32[32,128]{1,0:T(8,128)S(1)}, f32[32,128]{1,0:T(8,128)S(1)}, u32[]{:S(2)}, u32[]{:S(2)}) %collective-permute-start.9) | collective-permute-done | bytes 16416 | tf_op jit(solution)/shard_map/ppermute | solution.py:67
  43.3 0.5 collective-permute-done.8.refs_2_
  43.8 1.7 %column_pass.3 = (f32[64,128]{1,0:T(8,128)S(1)}, f32[32,128]{1,0:T(8,128)}) custom-call(f32[32,2,128,128]{3,2,1,0:T(8,128)S(1)} %get-tuple-element.27.work_ref, s32[64,128]{1,0:T(8,128)S(1)} %get-tuple-element.28.select_ref, f32[32,128]{1,0:T(8,128)S(1)} %get-tuple-element.29.log_mass_ref, f32[32,128]{1,0:T(8,128)S(1)} %get-tuple-element.32.refs_0_, ...), custom_call_target="tpu_custom_call" | custom-call | tf_op jit(solution)/shard_map/column_pass/pallas_call | solution.py:448
  45.5 10.9 %all_to_all.44 = f32[8,8,128]{2,1,0:T(8,128)S(1)} all-to-all(f32[8,8,128]{2,1,0:T(8,128)S(1)} %bitcast.21), channel_id=1, replica_groups=mesh['rows'=8,'cols'=4] {'rows'}, dimensions={0} | all-to-all | bytes 65536 | tf_op jit(solution)/shard_map/all_to_all | solution.py:75
  56.5 1.8 %row_pass.2.refs_0_ = f32[32,128]{1,0:T(8,128)S(1)} custom-call(s32[2,32]{1,0:T(2,128)} %bitcast.29, f32[32,2,128,128]{3,2,1,0:T(8,128)S(1)} %get-tuple-element.30.tall_ref, f32[8,128]{1,0:T(8,128)S(1)} %get-tuple-element.31.log_mass_ref, f32[64,128]{1,0:T(8,128)S(1)} %bitcast.20), custom_call_target="tpu_custom_call" | custom-call | tf_op jit(solution)/shard_map/row_pass/pallas_call | solution.py:466
  58.4 1.6 %collective-permute-start.11 = (f32[32,128]{1,0:T(8,128)S(1)}, f32[32,128]{1,0:T(8,128)S(1)}, u32[]{:S(2)}, u32[]{:S(2)}) collective-permute-start(f32[32,128]{1,0:T(8,128)S(1)} %row_pass.2.refs_0_), channel_id=1, source_target_pairs={{0,2},{1,3},{2,0},{3,1},{4,6},{5,7},{6,4},{7,5},{8,10},{9,11},{10,... | collective-permute-start | bytes 49160 | tf_op jit(solution)/shard_map/ppermute | solution.py:67
  60.0 0.3 collective-permute-start.10
  60.2 1.4 %collective-permute-done.12.refs_3_ = f32[32,128]{1,0:T(8,128)S(1)} collective-permute-done((f32[32,128]{1,0:T(8,128)S(1)}, f32[32,128]{1,0:T(8,128)S(1)}, u32[]{:S(2)}, u32[]{:S(2)}) %collective-permute-start.12) | collective-permute-done | bytes 16416 | tf_op jit(solution)/shard_map/ppermute | solution.py:67
  61.6 0.6 collective-permute-done.11.refs_2_
  62.2 1.7 %column_pass.4 = (f32[64,128]{1,0:T(8,128)S(1)}, f32[32,128]{1,0:T(8,128)}) custom-call(f32[32,2,128,128]{3,2,1,0:T(8,128)S(1)} %get-tuple-element.27.work_ref, s32[64,128]{1,0:T(8,128)S(1)} %get-tuple-element.28.select_ref, f32[32,128]{1,0:T(8,128)S(1)} %get-tuple-element.29.log_mass_ref, f32[32,128]{1,0:T(8,128)S(1)} %row_pass.2.refs_0_, ...), custom_call_target="tpu_custom_call" | custom-call | tf_op jit(solution)/shard_map/column_pass/pallas_call | solution.py:448
  63.9 9.0 %all_to_all.45 = f32[8,8,128]{2,1,0:T(8,128)S(1)} all-to-all(f32[8,8,128]{2,1,0:T(8,128)S(1)} %bitcast.22), channel_id=1, replica_groups=mesh['rows'=8,'cols'=4] {'rows'}, dimensions={0} | all-to-all | bytes 65536 | tf_op jit(solution)/shard_map/all_to_all | solution.py:75
  73.0 1.8 %row_pass.3.refs_0_ = f32[32,128]{1,0:T(8,128)S(1)} custom-call(s32[2,32]{1,0:T(2,128)} %bitcast.30, f32[32,2,128,128]{3,2,1,0:T(8,128)S(1)} %get-tuple-element.30.tall_ref, f32[8,128]{1,0:T(8,128)S(1)} %get-tuple-element.31.log_mass_ref, f32[64,128]{1,0:T(8,128)S(1)} %bitcast.19), custom_call_target="tpu_custom_call" | custom-call | tf_op jit(solution)/shard_map/row_pass/pallas_call | solution.py:466
  74.9 1.6 %collective-permute-start.14 = (f32[32,128]{1,0:T(8,128)S(1)}, f32[32,128]{1,0:T(8,128)S(1)}, u32[]{:S(2)}, u32[]{:S(2)}) collective-permute-start(f32[32,128]{1,0:T(8,128)S(1)} %row_pass.3.refs_0_), channel_id=1, source_target_pairs={{0,2},{1,3},{2,0},{3,1},{4,6},{5,7},{6,4},{7,5},{8,10},{9,11},{10,... | collective-permute-start | bytes 49160 | tf_op jit(solution)/shard_map/ppermute | solution.py:67
  76.5 0.3 collective-permute-start.13
  76.7 1.4 %collective-permute-done.15.refs_3_ = f32[32,128]{1,0:T(8,128)S(1)} collective-permute-done((f32[32,128]{1,0:T(8,128)S(1)}, f32[32,128]{1,0:T(8,128)S(1)}, u32[]{:S(2)}, u32[]{:S(2)}) %collective-permute-start.15) | collective-permute-done | bytes 16416 | tf_op jit(solution)/shard_map/ppermute | solution.py:67
  78.1 0.6 collective-permute-done.14.refs_2_
  78.7 1.7 %column_pass.5 = (f32[8,128]{1,0:T(8,128)S(1)}, f32[32,128]{1,0:T(8,128)}) custom-call(f32[32,2,128,128]{3,2,1,0:T(8,128)S(1)} %get-tuple-element.27.work_ref, s32[64,128]{1,0:T(8,128)S(1)} %get-tuple-element.28.select_ref, f32[32,128]{1,0:T(8,128)S(1)} %get-tuple-element.29.log_mass_ref, f32[32,128]{1,0:T(8,128)S(1)} %row_pass.3.refs_0_, ...), custom_call_target="tpu_custom_call" | custom-call | tf_op jit(solution)/shard_map/column_pass/pallas_call | solution.py:448
  80.4 8.8 %all_to_all.46 = f32[8,1,128]{2,1,0:T(1,128)S(1)} all-to-all(f32[8,1,128]{2,1,0:T(1,128)S(1)} %bitcast.24), channel_id=1, replica_groups=mesh['rows'=8,'cols'=4] {'rows'}, dimensions={0} | all-to-all | bytes 8192 | tf_op jit(solution)/shard_map/all_to_all | solution.py:75
  89.2 0.5 last_potential.1
  (17 shorter events, 0.5 us)
Async XLA Ops:
  0.6 14.2 %collective-permute-start.2 = (f32[1,1,3,128,128]{4,3,2,1,0:T(8,128)}, f32[1,1,3,128,128]{4,3,2,1,0:T(8,128)S(1)}, u32[]{:S(2)}, u32[]{:S(2)}) collective-permute-start(f32[1,1,3,128,128]{4,3,2,1,0:T(8,128)} %refs_6_.1), channel_id=1, source_target_pairs={{0,12},{4,8},{8,4},{12,0},{16,28},{20,24},{24,20},{28,16},{1,13},{... | collective-permute-start | bytes 589832 | tf_op jit(solution)/shard_map/ppermute | solution.py:67
  4.7 13.9 %collective-permute-start.1 = (f32[1,1,3,128,128]{4,3,2,1,0:T(8,128)}, f32[1,1,3,128,128]{4,3,2,1,0:T(8,128)S(1)}, u32[]{:S(2)}, u32[]{:S(2)}) collective-permute-start(f32[1,1,3,128,128]{4,3,2,1,0:T(8,128)} %refs_6_.1), channel_id=1, source_target_pairs={{0,8},{4,12},{8,0},{12,4},{16,24},{20,28},{24,16},{28,20},{1,9},{5... | collective-permute-start | bytes 589832 | tf_op jit(solution)/shard_map/ppermute | solution.py:67
  5.1 13.5 %collective-permute-start = (f32[1,1,3,128,128]{4,3,2,1,0:T(8,128)}, f32[1,1,3,128,128]{4,3,2,1,0:T(8,128)S(1)}, u32[]{:S(2)}, u32[]{:S(2)}) collective-permute-start(f32[1,1,3,128,128]{4,3,2,1,0:T(8,128)} %refs_6_.1), channel_id=1, source_target_pairs={{0,4},{4,0},{8,12},{12,8},{16,20},{20,16},{24,28},{28,24},{1,5},{5... | collective-permute-start | bytes 589832 | tf_op jit(solution)/shard_map/ppermute | solution.py:67
  5.3 13.3 %collective-permute-start.3 = (f32[1,1,3,128,128]{4,3,2,1,0:T(8,128)}, f32[1,1,3,128,128]{4,3,2,1,0:T(8,128)S(1)}, u32[]{:S(2)}, u32[]{:S(2)}) collective-permute-start(f32[1,1,3,128,128]{4,3,2,1,0:T(8,128)} %refs_6_.1), channel_id=1, source_target_pairs={{0,16},{4,20},{8,24},{12,28},{16,0},{20,4},{24,8},{28,12},{1,17},{... | collective-permute-start | bytes 589832 | tf_op jit(solution)/shard_map/ppermute | solution.py:67
  9.7 13.1 %all-to-all-start = ((f32[32,2,128]{2,1,0:T(2,128)}), f32[32,2,128]{2,1,0:T(2,128)S(1)}, u32[]{:S(2)}, u32[]{:S(2)}) async-start(f32[32,2,128]{2,1,0:T(2,128)} %bitcast.5), calls=%async_computation | async-start | bytes 65536 | tf_op jit(solution)/shard_map/all_to_all | solution.py:75
  18.6 11.9 %collective-permute-start.6 = (f32[1,1,3,128,128]{4,3,2,1,0:T(8,128)S(1)}, f32[1,1,3,128,128]{4,3,2,1,0:T(8,128)S(1)}, u32[]{:S(2)}, u32[]{:S(2)}) collective-permute-start(f32[1,1,3,128,128]{4,3,2,1,0:T(8,128)S(1)} %get-tuple-element.25.refs_10_), channel_id=1, source_target_pairs={{0,12},{4,8},{8,4},{12,0},{16,28},{20,24},{24,20},{28,16},{1,13},{... | collective-permute-start | bytes 589832 | tf_op jit(solution)/shard_map/ppermute | solution.py:67
  21.2 9.3 %collective-permute-start.5 = (f32[1,1,3,128,128]{4,3,2,1,0:T(8,128)S(1)}, f32[1,1,3,128,128]{4,3,2,1,0:T(8,128)S(1)}, u32[]{:S(2)}, u32[]{:S(2)}) collective-permute-start(f32[1,1,3,128,128]{4,3,2,1,0:T(8,128)S(1)} %get-tuple-element.25.refs_10_), channel_id=1, source_target_pairs={{0,8},{4,12},{8,0},{12,4},{16,24},{20,28},{24,16},{28,20},{1,9},{5... | collective-permute-start | bytes 589832 | tf_op jit(solution)/shard_map/ppermute | solution.py:67
  21.3 9.2 %collective-permute-start.4 = (f32[1,1,3,128,128]{4,3,2,1,0:T(8,128)S(1)}, f32[1,1,3,128,128]{4,3,2,1,0:T(8,128)S(1)}, u32[]{:S(2)}, u32[]{:S(2)}) collective-permute-start(f32[1,1,3,128,128]{4,3,2,1,0:T(8,128)S(1)} %get-tuple-element.25.refs_10_), channel_id=1, source_target_pairs={{0,4},{4,0},{8,12},{12,8},{16,20},{20,16},{24,28},{28,24},{1,5},{5... | collective-permute-start | bytes 589832 | tf_op jit(solution)/shard_map/ppermute | solution.py:67
  22.8 7.7 %copy-start = (f32[1,1,3,128,128]{4,3,2,1,0:T(8,128)S(1)}, f32[1,1,3,128,128]{4,3,2,1,0:T(8,128)}, u32[]{:S(2)}) copy-start(f32[1,1,3,128,128]{4,3,2,1,0:T(8,128)} %refs_6_.1) | copy-start | bytes 589828
  40.0 3.3 %collective-permute-start.9 = (f32[32,128]{1,0:T(8,128)S(1)}, f32[32,128]{1,0:T(8,128)S(1)}, u32[]{:S(2)}, u32[]{:S(2)}) collective-permute-start(f32[32,128]{1,0:T(8,128)S(1)} %get-tuple-element.32.refs_0_), channel_id=1, source_target_pairs={{0,3},{1,2},{2,1},{3,0},{4,7},{5,6},{6,5},{7,4},{8,11},{9,10},{10,... | collective-permute-start | bytes 49160 | tf_op jit(solution)/shard_map/ppermute | solution.py:67
  40.0 3.8 %collective-permute-start.8 = (f32[32,128]{1,0:T(8,128)S(1)}, f32[32,128]{1,0:T(8,128)S(1)}, u32[]{:S(2)}, u32[]{:S(2)}) collective-permute-start(f32[32,128]{1,0:T(8,128)S(1)} %get-tuple-element.32.refs_0_), channel_id=1, source_target_pairs={{0,2},{1,3},{2,0},{3,1},{4,6},{5,7},{6,4},{7,5},{8,10},{9,11},{10,... | collective-permute-start | bytes 49160 | tf_op jit(solution)/shard_map/ppermute | solution.py:67
  41.6 2.2 %collective-permute-start.7 = (f32[32,128]{1,0:T(8,128)S(1)}, f32[32,128]{1,0:T(8,128)S(1)}, u32[]{:S(2)}, u32[]{:S(2)}) collective-permute-start(f32[32,128]{1,0:T(8,128)S(1)} %get-tuple-element.32.refs_0_), channel_id=1, source_target_pairs={{0,1},{1,0},{2,3},{3,2},{4,5},{5,4},{6,7},{7,6},{8,9},{9,8},{10,11... | collective-permute-start | bytes 49160 | tf_op jit(solution)/shard_map/ppermute | solution.py:67
  58.3 3.3 %collective-permute-start.12 = (f32[32,128]{1,0:T(8,128)S(1)}, f32[32,128]{1,0:T(8,128)S(1)}, u32[]{:S(2)}, u32[]{:S(2)}) collective-permute-start(f32[32,128]{1,0:T(8,128)S(1)} %row_pass.2.refs_0_), channel_id=1, source_target_pairs={{0,3},{1,2},{2,1},{3,0},{4,7},{5,6},{6,5},{7,4},{8,11},{9,10},{10,... | collective-permute-start | bytes 49160 | tf_op jit(solution)/shard_map/ppermute | solution.py:67
  58.4 3.8 %collective-permute-start.11 = (f32[32,128]{1,0:T(8,128)S(1)}, f32[32,128]{1,0:T(8,128)S(1)}, u32[]{:S(2)}, u32[]{:S(2)}) collective-permute-start(f32[32,128]{1,0:T(8,128)S(1)} %row_pass.2.refs_0_), channel_id=1, source_target_pairs={{0,2},{1,3},{2,0},{3,1},{4,6},{5,7},{6,4},{7,5},{8,10},{9,11},{10,... | collective-permute-start | bytes 49160 | tf_op jit(solution)/shard_map/ppermute | solution.py:67
  60.0 2.2 %collective-permute-start.10 = (f32[32,128]{1,0:T(8,128)S(1)}, f32[32,128]{1,0:T(8,128)S(1)}, u32[]{:S(2)}, u32[]{:S(2)}) collective-permute-start(f32[32,128]{1,0:T(8,128)S(1)} %row_pass.2.refs_0_), channel_id=1, source_target_pairs={{0,1},{1,0},{2,3},{3,2},{4,5},{5,4},{6,7},{7,6},{8,9},{9,8},{10,11... | collective-permute-start | bytes 49160 | tf_op jit(solution)/shard_map/ppermute | solution.py:67
  74.8 3.3 %collective-permute-start.15 = (f32[32,128]{1,0:T(8,128)S(1)}, f32[32,128]{1,0:T(8,128)S(1)}, u32[]{:S(2)}, u32[]{:S(2)}) collective-permute-start(f32[32,128]{1,0:T(8,128)S(1)} %row_pass.3.refs_0_), channel_id=1, source_target_pairs={{0,3},{1,2},{2,1},{3,0},{4,7},{5,6},{6,5},{7,4},{8,11},{9,10},{10,... | collective-permute-start | bytes 49160 | tf_op jit(solution)/shard_map/ppermute | solution.py:67
  74.9 3.8 %collective-permute-start.14 = (f32[32,128]{1,0:T(8,128)S(1)}, f32[32,128]{1,0:T(8,128)S(1)}, u32[]{:S(2)}, u32[]{:S(2)}) collective-permute-start(f32[32,128]{1,0:T(8,128)S(1)} %row_pass.3.refs_0_), channel_id=1, source_target_pairs={{0,2},{1,3},{2,0},{3,1},{4,6},{5,7},{6,4},{7,5},{8,10},{9,11},{10,... | collective-permute-start | bytes 49160 | tf_op jit(solution)/shard_map/ppermute | solution.py:67
  76.5 2.2 %collective-permute-start.13 = (f32[32,128]{1,0:T(8,128)S(1)}, f32[32,128]{1,0:T(8,128)S(1)}, u32[]{:S(2)}, u32[]{:S(2)}) collective-permute-start(f32[32,128]{1,0:T(8,128)S(1)} %row_pass.3.refs_0_), channel_id=1, source_target_pairs={{0,1},{1,0},{2,3},{3,2},{4,5},{5,4},{6,7},{7,6},{8,9},{9,8},{10,11... | collective-permute-start | bytes 49160 | tf_op jit(solution)/shard_map/ppermute | solution.py:67

commit v13 on v10

--- a/solution.py
+++ b/solution.py
@@ -67,21 +67,8 @@
     return lax.ppermute(x, axis, [(d, d ^ mask) for d in range(size)])
 
 
-def join_kernel(first_ref, second_ref, out_ref):
-    out_ref[...] = log_sum([first_ref[...], second_ref[...]])
-
-
-def last_pair(part, axis):
-    mask = 1
-    while 2 * mask < lax.axis_size(axis):
-        part = pl.pallas_call(
-            join_kernel,
-            out_shape=jax.ShapeDtypeStruct(part.shape, jnp.float32),
-            compiler_params=pltpu.CompilerParams(vmem_limit_bytes=4 * mib),
-            name="join",
-        )(part, send(part, axis, mask))
-        mask *= 2
-    return [part, send(part, axis, mask)]
+def from_all(x, axis):
+    return [x] + [send(x, axis, s) for s in range(1, lax.axis_size(axis))]
 
 
 def exchange(copies, axis):
@@ -237,18 +224,27 @@
             turned = scaled.T
             tall_ref[row, l] = turned
             scores.append(turned)
-        row_pass(scores, row, peak_scr, sum_scr)
+        row_pass(scores, row, part_ref.shape[0], peak_scr, sum_scr)
 
     @pl.when(g == pl.num_programs(0) - 1)
     def _():
-        part_ref[...] = peak_scr[...] + jnp.log2(sum_scr[...])
-
-
-def row_pass(scores, row, peak_scr, sum_scr):
-    peak = jnp.max(functools.reduce(jnp.maximum, scores), axis=0, keepdims=True)
-    total = functools.reduce(jnp.add, [jnp.exp2(s - peak) for s in scores])
-    peak_scr[pl.ds(row, 1), :] = peak
-    sum_scr[pl.ds(row, 1), :] = jnp.sum(total, axis=0, keepdims=True)
+        part_ref[...] = row_sums(part_ref.shape[0], peak_scr, sum_scr)
+
+
+def row_pass(scores, row, rows, peak_scr, sum_scr):
+    for l, score in enumerate(scores):
+        peak = jnp.max(score, axis=0, keepdims=True)
+        peak_scr[pl.ds(l * rows + row, 1), :] = peak
+        sum_scr[pl.ds(l * rows + row, 1), :] = jnp.sum(jnp.exp2(score - peak), axis=0, keepdims=True)
+
+
+def row_sums(rows, peak_scr, sum_scr):
+    slots = peak_scr.shape[0] // rows
+    peaks = [peak_scr[l * rows : (l + 1) * rows, :] for l in range(slots)]
+    sums = [sum_scr[l * rows : (l + 1) * rows, :] for l in range(slots)]
+    peak = functools.reduce(jnp.maximum, peaks)
+    total = functools.reduce(jnp.add, [t * jnp.exp2(p - peak) for p, t in zip(peaks, sums)])
+    return peak + jnp.log2(total)
 
 
 def column_kernel(copies, work_ref, select_ref, log_mass_ref, *refs):
@@ -297,8 +293,8 @@
 
     for row in range(rows):
         scores = [wide_scr[slot_ref[l, row]] + tall_ref[row, l] for l in range(slots)]
-        row_pass(scores, row, peak_scr, sum_scr)
-    out_ref[...] = peak_scr[...] + jnp.log2(sum_scr[...])
+        row_pass(scores, row, rows, peak_scr, sum_scr)
+    out_ref[...] = row_sums(rows, peak_scr, sum_scr)
 
 
 def last_kernel(row_devices, row_axis, log_mass_ref, parts_ref, out_ref):
@@ -436,8 +432,8 @@
             pltpu.SMEM((group_blocks * group_blocks,), jnp.int32),
             pltpu.VMEM((group_blocks, width), f32),
             pltpu.VMEM((1, width), f32),
-            pltpu.VMEM((rows_here, width), f32),
-            pltpu.VMEM((rows_here, width), f32),
+            pltpu.VMEM((slots * rows_here, width), f32),
+            pltpu.VMEM((slots * rows_here, width), f32),
         ],
         compiler_params=pltpu.CompilerParams(vmem_limit_bytes=12 * mib + 2 * far_bytes),
         name="far_product",
@@ -471,8 +467,8 @@
             out_shape=jax.ShapeDtypeStruct((rows_here, width), f32),
             scratch_shapes=[
                 pltpu.VMEM((group_blocks, width, width), f32),
-                pltpu.VMEM((rows_here, width), f32),
-                pltpu.VMEM((rows_here, width), f32),
+                pltpu.VMEM((slots * rows_here, width), f32),
+                pltpu.VMEM((slots * rows_here, width), f32),
             ],
             compiler_params=pass_params,
             name="row_pass",
@@ -481,7 +477,7 @@
     for step in range(ITERS):
         last = step == ITERS - 1
         column_part, source_potential = column_step(
-            last_pair(row_part, "cols"), 1 if last else row_devices
+            from_all(row_part, "cols"), 1 if last else row_devices
         )
         column_parts = exchange(column_part, "rows")
         if not last:

time: 93.6 us -> 88.7 us (0.948)
  waiting for transfers between devices: 15.3 us -> 10.9 us
  Pallas kernels: 27.9 us -> 26.4 us
    ppermute x13 -> x16, waiting for transfers between devices: 15.3 us -> 10.9 us  [send(): return lax.ppermute(x, axis, [(d, d ^ mask) for d in range(size)])]
    pallas_call x3, Pallas kernels: 5.11 us -> 3.69 us  [column_step(): pl.pallas_call(functools.partial(column_kernel, copies), in_specs=[VMEM]...]
    ppermute x13 -> x16, starting transfers between devices: 16.7 us -> 17.5 us  [send(): return lax.ppermute(x, axis, [(d, d ^ mask) for d in range(size)])]
  transfers between devices with their start and end apart: 14 -> 17, of which waited for: 8 -> 8; matrix products, arithmetic and copies ran while one was open for 0% -> 0% of each run, Pallas kernels for 10% -> 10%
where the time goes in v13:
time: 88.7 us; the launch traced here: 88.2 us
  blocking collectives  28.8 us (32%)
  Pallas kernels  26.4 us (30%)
  starting transfers between devices  21.3 us (24%)
  waiting for transfers between devices  10.9 us (12%)
    all_to_all x3, blocking collectives, exchange(): return lax.all_to_all(copies, axis, 0, 0, tiled=True)  28.8 us
    ppermute x16, starting transfers between devices, send(): return lax.ppermute(x, axis, [(d, d ^ mask) for d in range(size)])  17.5 us
    ppermute x16, waiting for transfers between devices, send(): return lax.ppermute(x, axis, [(d, d ^ mask) for d in range(size)])  10.9 us
    pallas_call x1, Pallas kernels, per_device(): pl.pallas_call(functools.partial(far_kernel, (row_devices, col_devices, t...  9.4 us
    pallas_call x1, Pallas kernels, per_device(): pl.pallas_call(near_kernel, grid=(rows_here // step_rows,), in_specs=[SME...  7.66 us
    all_to_all x1, starting transfers between devices, exchange(): return lax.all_to_all(copies, axis, 0, 0, tiled=True)  3.82 us
    pallas_call x3, Pallas kernels, column_step(): pl.pallas_call(functools.partial(column_kernel, copies), in_specs=[VMEM]...  3.69 us
    pallas_call x2, Pallas kernels, row_step(): pl.pallas_call(functools.partial(row_kernel, row_devices), in_specs=[SMEM...  3.67 us
  transfers between devices with their start and end apart: 17, of which 8 were waited for; matrix products, arithmetic and copies ran while one was open for 0% of the time, Pallas kernels for 10%

profile of v13, /device:TPU:0, one launch (start us, length us, event | category | flops | bytes accessed | tf_op | source)
XLA Modules:
  0.0 88.2 jit_solution(17143916174679039332)
XLA Ops:
  0.6 4.0 %collective-permute-start.2 = (f32[1,1,3,128,128]{4,3,2,1,0:T(8,128)}, f32[1,1,3,128,128]{4,3,2,1,0:T(8,128)S(1)}, u32[]{:S(2)}, u32[]{:S(2)}) collective-permute-start(f32[1,1,3,128,128]{4,3,2,1,0:T(8,128)} %refs_6_.1), channel_id=1, source_target_pairs={{0,12},{4,8},{8,4},{12,0},{16,28},{20,24},{24,20},{28,16},{1,13},{... | collective-permute-start | bytes 589832 | tf_op jit(solution)/shard_map/ppermute | solution.py:67
  4.7 0.4 collective-permute-start.1
  5.3 2.9 %collective-permute-start.3 = (f32[1,1,3,128,128]{4,3,2,1,0:T(8,128)}, f32[1,1,3,128,128]{4,3,2,1,0:T(8,128)S(1)}, u32[]{:S(2)}, u32[]{:S(2)}) collective-permute-start(f32[1,1,3,128,128]{4,3,2,1,0:T(8,128)} %refs_6_.1), channel_id=1, source_target_pairs={{0,16},{4,20},{8,24},{12,28},{16,0},{20,4},{24,8},{28,12},{1,17},{... | collective-permute-start | bytes 589832 | tf_op jit(solution)/shard_map/ppermute | solution.py:67
  8.2 1.5 %pack.1 = f32[64,128]{1,0:T(8,128)} custom-call(s32[32,128]{1,0:T(8,128)} %bitcast.25, s32[1,128]{1,0:T(1,128)} %target_ref.1), custom_call_target="tpu_custom_call" | custom-call | tf_op jit(solution)/shard_map/pack/pallas_call | solution.py:342
  9.7 3.8 %all-to-all-start = ((f32[32,2,128]{2,1,0:T(2,128)}), f32[32,2,128]{2,1,0:T(2,128)S(1)}, u32[]{:S(2)}, u32[]{:S(2)}) async-start(f32[32,2,128]{2,1,0:T(2,128)} %bitcast.5), calls=%async_computation | async-start | bytes 65536 | tf_op jit(solution)/shard_map/all_to_all | solution.py:75
  13.5 1.3 %collective-permute-done.2.refs_2_ = f32[1,1,3,128,128]{4,3,2,1,0:T(8,128)S(1)} collective-permute-done((f32[1,1,3,128,128]{4,3,2,1,0:T(8,128)}, f32[1,1,3,128,128]{4,3,2,1,0:T(8,128)S(1)}, u32[]{:S(2)}, u32[]{:S(2)}) %collective-permute-start.2) | collective-permute-done | bytes 196640 | tf_op jit(solution)/shard_map/ppermute | solution.py:67
  14.9 3.7 %collective-permute-done.1.refs_1_ = f32[1,1,3,128,128]{4,3,2,1,0:T(8,128)S(1)} collective-permute-done((f32[1,1,3,128,128]{4,3,2,1,0:T(8,128)}, f32[1,1,3,128,128]{4,3,2,1,0:T(8,128)S(1)}, u32[]{:S(2)}, u32[]{:S(2)}) %collective-permute-start.1) | collective-permute-done | bytes 196640 | tf_op jit(solution)/shard_map/ppermute | solution.py:67
  18.6 2.6 %collective-permute-start.6 = (f32[1,1,3,128,128]{4,3,2,1,0:T(8,128)S(1)}, f32[1,1,3,128,128]{4,3,2,1,0:T(8,128)S(1)}, u32[]{:S(2)}, u32[]{:S(2)}) collective-permute-start(f32[1,1,3,128,128]{4,3,2,1,0:T(8,128)S(1)} %get-tuple-element.25.refs_10_), channel_id=1, source_target_pairs={{0,12},{4,8},{8,4},{12,0},{16,28},{20,24},{24,20},{28,16},{1,13},{... | collective-permute-start | bytes 589832 | tf_op jit(solution)/shard_map/ppermute | solution.py:67
  21.3 1.5 %collective-permute-start.4 = (f32[1,1,3,128,128]{4,3,2,1,0:T(8,128)S(1)}, f32[1,1,3,128,128]{4,3,2,1,0:T(8,128)S(1)}, u32[]{:S(2)}, u32[]{:S(2)}) collective-permute-start(f32[1,1,3,128,128]{4,3,2,1,0:T(8,128)S(1)} %get-tuple-element.25.refs_10_), channel_id=1, source_target_pairs={{0,4},{4,0},{8,12},{12,8},{16,20},{20,16},{24,28},{28,24},{1,5},{5... | collective-permute-start | bytes 589832 | tf_op jit(solution)/shard_map/ppermute | solution.py:67
  22.8 7.7 %near_product.1 = (bf16[32,256,768]{2,1,0:T(8,128)(2,1)S(1)}, f32[8,128,4]{2,1,0:T(8,128)S(1)}) custom-call(s32[3,32]{1,0:T(4,128)} %bitcast.31, f32[32,3,128,128]{3,2,1,0:T(8,128)} %cost_ref.1, f32[32,1,2,128,128]{4,3,2,1,0:T(8,128)} %plan_ref.1, s32[32,128]{1,0:T(8,128)} %bitcast.26, f32[64,128]{1,0:T(8,128)S(1)} %bitcast.17), custom_call_target="tpu_custom_call" | custom-call | flops 2415919104 | bytes 10485760 | tf_op jit(solution)/shard_map/near_product/pallas_call | solution.py:370
  30.5 9.4 %far_product.1 = (f32[32,1,2,128,128]{4,3,2,1,0:T(8,128)}, f32[32,2,128,128]{3,2,1,0:T(8,128)S(1)}, f32[32,2,128,128]{3,2,1,0:T(8,128)S(1)}, f32[32,128]{1,0:T(8...) custom-call(s32[3,32]{1,0:T(4,128)} %bitcast.32, s32[2,32]{1,0:T(2,128)} %bitcast.28, ...), custom_call_target="tpu_custom_call" | custom-call | tf_op jit(solution)/shard_map/far_product/pallas_call | solution.py:400
  39.9 1.5 %collective-permute-start.8 = (f32[32,128]{1,0:T(8,128)S(1)}, f32[32,128]{1,0:T(8,128)S(1)}, u32[]{:S(2)}, u32[]{:S(2)}) collective-permute-start(f32[32,128]{1,0:T(8,128)S(1)} %get-tuple-element.32.refs_0_), channel_id=1, source_target_pairs={{0,2},{1,3},{2,0},{3,1},{4,6},{5,7},{6,4},{7,5},{8,10},{9,11},{10,... | collective-permute-start | bytes 49160 | tf_op jit(solution)/shard_map/ppermute | solution.py:67
  41.4 0.3 collective-permute-start.7
  41.8 1.4 %collective-permute-done.9.refs_3_ = f32[32,128]{1,0:T(8,128)S(1)} collective-permute-done((f32[32,128]{1,0:T(8,128)S(1)}, f32[32,128]{1,0:T(8,128)S(1)}, u32[]{:S(2)}, u32[]{:S(2)}) %collective-permute-start.9) | collective-permute-done | bytes 16416 | tf_op jit(solution)/shard_map/ppermute | solution.py:67
  43.2 0.5 collective-permute-done.8.refs_2_
  43.7 1.2 %column_pass.3 = (f32[64,128]{1,0:T(8,128)S(1)}, f32[32,128]{1,0:T(8,128)}) custom-call(f32[32,2,128,128]{3,2,1,0:T(8,128)S(1)} %get-tuple-element.27.work_ref, s32[64,128]{1,0:T(8,128)S(1)} %get-tuple-element.28.select_ref, f32[32,128]{1,0:T(8,128)S(1)} %get-tuple-element.29.log_mass_ref, f32[32,128]{1,0:T(8,128)S(1)} %get-tuple-element.32.refs_0_, ...), custom_call_target="tpu_custom_call" | custom-call | tf_op jit(solution)/shard_map/column_pass/pallas_call | solution.py:445
  44.9 10.9 %all_to_all.44 = f32[8,8,128]{2,1,0:T(8,128)S(1)} all-to-all(f32[8,8,128]{2,1,0:T(8,128)S(1)} %bitcast.21), channel_id=1, replica_groups=mesh['rows'=8,'cols'=4] {'rows'}, dimensions={0} | all-to-all | bytes 65536 | tf_op jit(solution)/shard_map/all_to_all | solution.py:75
  55.8 1.8 %row_pass.2.refs_0_ = f32[32,128]{1,0:T(8,128)S(1)} custom-call(s32[2,32]{1,0:T(2,128)} %bitcast.29, f32[32,2,128,128]{3,2,1,0:T(8,128)S(1)} %get-tuple-element.30.tall_ref, f32[8,128]{1,0:T(8,128)S(1)} %get-tuple-element.31.log_mass_ref, f32[64,128]{1,0:T(8,128)S(1)} %bitcast.20), custom_call_target="tpu_custom_call" | custom-call | tf_op jit(solution)/shard_map/row_pass/pallas_call | solution.py:463
  57.7 1.6 %collective-permute-start.11 = (f32[32,128]{1,0:T(8,128)S(1)}, f32[32,128]{1,0:T(8,128)S(1)}, u32[]{:S(2)}, u32[]{:S(2)}) collective-permute-start(f32[32,128]{1,0:T(8,128)S(1)} %row_pass.2.refs_0_), channel_id=1, source_target_pairs={{0,2},{1,3},{2,0},{3,1},{4,6},{5,7},{6,4},{7,5},{8,10},{9,11},{10,... | collective-permute-start | bytes 49160 | tf_op jit(solution)/shard_map/ppermute | solution.py:67
  59.3 0.3 collective-permute-start.10
  59.6 1.4 %collective-permute-done.12.refs_3_ = f32[32,128]{1,0:T(8,128)S(1)} collective-permute-done((f32[32,128]{1,0:T(8,128)S(1)}, f32[32,128]{1,0:T(8,128)S(1)}, u32[]{:S(2)}, u32[]{:S(2)}) %collective-permute-start.12) | collective-permute-done | bytes 16416 | tf_op jit(solution)/shard_map/ppermute | solution.py:67
  61.0 0.6 collective-permute-done.11.refs_2_
  61.6 1.2 %column_pass.4 = (f32[64,128]{1,0:T(8,128)S(1)}, f32[32,128]{1,0:T(8,128)}) custom-call(f32[32,2,128,128]{3,2,1,0:T(8,128)S(1)} %get-tuple-element.27.work_ref, s32[64,128]{1,0:T(8,128)S(1)} %get-tuple-element.28.select_ref, f32[32,128]{1,0:T(8,128)S(1)} %get-tuple-element.29.log_mass_ref, f32[32,128]{1,0:T(8,128)S(1)} %row_pass.2.refs_0_, ...), custom_call_target="tpu_custom_call" | custom-call | tf_op jit(solution)/shard_map/column_pass/pallas_call | solution.py:445
  62.8 9.1 %all_to_all.45 = f32[8,8,128]{2,1,0:T(8,128)S(1)} all-to-all(f32[8,8,128]{2,1,0:T(8,128)S(1)} %bitcast.22), channel_id=1, replica_groups=mesh['rows'=8,'cols'=4] {'rows'}, dimensions={0} | all-to-all | bytes 65536 | tf_op jit(solution)/shard_map/all_to_all | solution.py:75
  71.9 1.8 %row_pass.3.refs_0_ = f32[32,128]{1,0:T(8,128)S(1)} custom-call(s32[2,32]{1,0:T(2,128)} %bitcast.30, f32[32,2,128,128]{3,2,1,0:T(8,128)S(1)} %get-tuple-element.30.tall_ref, f32[8,128]{1,0:T(8,128)S(1)} %get-tuple-element.31.log_mass_ref, f32[64,128]{1,0:T(8,128)S(1)} %bitcast.19), custom_call_target="tpu_custom_call" | custom-call | tf_op jit(solution)/shard_map/row_pass/pallas_call | solution.py:463
  73.8 1.6 %collective-permute-start.14 = (f32[32,128]{1,0:T(8,128)S(1)}, f32[32,128]{1,0:T(8,128)S(1)}, u32[]{:S(2)}, u32[]{:S(2)}) collective-permute-start(f32[32,128]{1,0:T(8,128)S(1)} %row_pass.3.refs_0_), channel_id=1, source_target_pairs={{0,2},{1,3},{2,0},{3,1},{4,6},{5,7},{6,4},{7,5},{8,10},{9,11},{10,... | collective-permute-start | bytes 49160 | tf_op jit(solution)/shard_map/ppermute | solution.py:67
  75.4 0.3 collective-permute-start.13
  75.6 1.4 %collective-permute-done.15.refs_3_ = f32[32,128]{1,0:T(8,128)S(1)} collective-permute-done((f32[32,128]{1,0:T(8,128)S(1)}, f32[32,128]{1,0:T(8,128)S(1)}, u32[]{:S(2)}, u32[]{:S(2)}) %collective-permute-start.15) | collective-permute-done | bytes 16416 | tf_op jit(solution)/shard_map/ppermute | solution.py:67
  77.0 0.6 collective-permute-done.14.refs_2_
  77.6 1.2 %column_pass.5 = (f32[8,128]{1,0:T(8,128)S(1)}, f32[32,128]{1,0:T(8,128)}) custom-call(f32[32,2,128,128]{3,2,1,0:T(8,128)S(1)} %get-tuple-element.27.work_ref, s32[64,128]{1,0:T(8,128)S(1)} %get-tuple-element.28.select_ref, f32[32,128]{1,0:T(8,128)S(1)} %get-tuple-element.29.log_mass_ref, f32[32,128]{1,0:T(8,128)S(1)} %row_pass.3.refs_0_, ...), custom_call_target="tpu_custom_call" | custom-call | tf_op jit(solution)/shard_map/column_pass/pallas_call | solution.py:445
  78.8 8.8 %all_to_all.46 = f32[8,1,128]{2,1,0:T(1,128)S(1)} all-to-all(f32[8,1,128]{2,1,0:T(1,128)S(1)} %bitcast.24), channel_id=1, replica_groups=mesh['rows'=8,'cols'=4] {'rows'}, dimensions={0} | all-to-all | bytes 8192 | tf_op jit(solution)/shard_map/all_to_all | solution.py:75
  87.6 0.5 last_potential.1
  (17 shorter events, 0.5 us)
Async XLA Ops:
  0.6 14.2 %collective-permute-start.2 = (f32[1,1,3,128,128]{4,3,2,1,0:T(8,128)}, f32[1,1,3,128,128]{4,3,2,1,0:T(8,128)S(1)}, u32[]{:S(2)}, u32[]{:S(2)}) collective-permute-start(f32[1,1,3,128,128]{4,3,2,1,0:T(8,128)} %refs_6_.1), channel_id=1, source_target_pairs={{0,12},{4,8},{8,4},{12,0},{16,28},{20,24},{24,20},{28,16},{1,13},{... | collective-permute-start | bytes 589832 | tf_op jit(solution)/shard_map/ppermute | solution.py:67
  4.7 13.9 %collective-permute-start.1 = (f32[1,1,3,128,128]{4,3,2,1,0:T(8,128)}, f32[1,1,3,128,128]{4,3,2,1,0:T(8,128)S(1)}, u32[]{:S(2)}, u32[]{:S(2)}) collective-permute-start(f32[1,1,3,128,128]{4,3,2,1,0:T(8,128)} %refs_6_.1), channel_id=1, source_target_pairs={{0,8},{4,12},{8,0},{12,4},{16,24},{20,28},{24,16},{28,20},{1,9},{5... | collective-permute-start | bytes 589832 | tf_op jit(solution)/shard_map/ppermute | solution.py:67
  5.1 13.5 %collective-permute-start = (f32[1,1,3,128,128]{4,3,2,1,0:T(8,128)}, f32[1,1,3,128,128]{4,3,2,1,0:T(8,128)S(1)}, u32[]{:S(2)}, u32[]{:S(2)}) collective-permute-start(f32[1,1,3,128,128]{4,3,2,1,0:T(8,128)} %refs_6_.1), channel_id=1, source_target_pairs={{0,4},{4,0},{8,12},{12,8},{16,20},{20,16},{24,28},{28,24},{1,5},{5... | collective-permute-start | bytes 589832 | tf_op jit(solution)/shard_map/ppermute | solution.py:67
  5.3 13.3 %collective-permute-start.3 = (f32[1,1,3,128,128]{4,3,2,1,0:T(8,128)}, f32[1,1,3,128,128]{4,3,2,1,0:T(8,128)S(1)}, u32[]{:S(2)}, u32[]{:S(2)}) collective-permute-start(f32[1,1,3,128,128]{4,3,2,1,0:T(8,128)} %refs_6_.1), channel_id=1, source_target_pairs={{0,16},{4,20},{8,24},{12,28},{16,0},{20,4},{24,8},{28,12},{1,17},{... | collective-permute-start | bytes 589832 | tf_op jit(solution)/shard_map/ppermute | solution.py:67
  9.7 13.1 %all-to-all-start = ((f32[32,2,128]{2,1,0:T(2,128)}), f32[32,2,128]{2,1,0:T(2,128)S(1)}, u32[]{:S(2)}, u32[]{:S(2)}) async-start(f32[32,2,128]{2,1,0:T(2,128)} %bitcast.5), calls=%async_computation | async-start | bytes 65536 | tf_op jit(solution)/shard_map/all_to_all | solution.py:75
  18.6 11.9 %collective-permute-start.6 = (f32[1,1,3,128,128]{4,3,2,1,0:T(8,128)S(1)}, f32[1,1,3,128,128]{4,3,2,1,0:T(8,128)S(1)}, u32[]{:S(2)}, u32[]{:S(2)}) collective-permute-start(f32[1,1,3,128,128]{4,3,2,1,0:T(8,128)S(1)} %get-tuple-element.25.refs_10_), channel_id=1, source_target_pairs={{0,12},{4,8},{8,4},{12,0},{16,28},{20,24},{24,20},{28,16},{1,13},{... | collective-permute-start | bytes 589832 | tf_op jit(solution)/shard_map/ppermute | solution.py:67
  21.2 9.3 %collective-permute-start.5 = (f32[1,1,3,128,128]{4,3,2,1,0:T(8,128)S(1)}, f32[1,1,3,128,128]{4,3,2,1,0:T(8,128)S(1)}, u32[]{:S(2)}, u32[]{:S(2)}) collective-permute-start(f32[1,1,3,128,128]{4,3,2,1,0:T(8,128)S(1)} %get-tuple-element.25.refs_10_), channel_id=1, source_target_pairs={{0,8},{4,12},{8,0},{12,4},{16,24},{20,28},{24,16},{28,20},{1,9},{5... | collective-permute-start | bytes 589832 | tf_op jit(solution)/shard_map/ppermute | solution.py:67
  21.3 9.2 %collective-permute-start.4 = (f32[1,1,3,128,128]{4,3,2,1,0:T(8,128)S(1)}, f32[1,1,3,128,128]{4,3,2,1,0:T(8,128)S(1)}, u32[]{:S(2)}, u32[]{:S(2)}) collective-permute-start(f32[1,1,3,128,128]{4,3,2,1,0:T(8,128)S(1)} %get-tuple-element.25.refs_10_), channel_id=1, source_target_pairs={{0,4},{4,0},{8,12},{12,8},{16,20},{20,16},{24,28},{28,24},{1,5},{5... | collective-permute-start | bytes 589832 | tf_op jit(solution)/shard_map/ppermute | solution.py:67
  22.8 7.7 %copy-start = (f32[1,1,3,128,128]{4,3,2,1,0:T(8,128)S(1)}, f32[1,1,3,128,128]{4,3,2,1,0:T(8,128)}, u32[]{:S(2)}) copy-start(f32[1,1,3,128,128]{4,3,2,1,0:T(8,128)} %refs_6_.1) | copy-start | bytes 589828
  39.9 3.3 %collective-permute-start.9 = (f32[32,128]{1,0:T(8,128)S(1)}, f32[32,128]{1,0:T(8,128)S(1)}, u32[]{:S(2)}, u32[]{:S(2)}) collective-permute-start(f32[32,128]{1,0:T(8,128)S(1)} %get-tuple-element.32.refs_0_), channel_id=1, source_target_pairs={{0,3},{1,2},{2,1},{3,0},{4,7},{5,6},{6,5},{7,4},{8,11},{9,10},{10,... | collective-permute-start | bytes 49160 | tf_op jit(solution)/shard_map/ppermute | solution.py:67
  39.9 3.8 %collective-permute-start.8 = (f32[32,128]{1,0:T(8,128)S(1)}, f32[32,128]{1,0:T(8,128)S(1)}, u32[]{:S(2)}, u32[]{:S(2)}) collective-permute-start(f32[32,128]{1,0:T(8,128)S(1)} %get-tuple-element.32.refs_0_), channel_id=1, source_target_pairs={{0,2},{1,3},{2,0},{3,1},{4,6},{5,7},{6,4},{7,5},{8,10},{9,11},{10,... | collective-permute-start | bytes 49160 | tf_op jit(solution)/shard_map/ppermute | solution.py:67
  41.4 2.3 %collective-permute-start.7 = (f32[32,128]{1,0:T(8,128)S(1)}, f32[32,128]{1,0:T(8,128)S(1)}, u32[]{:S(2)}, u32[]{:S(2)}) collective-permute-start(f32[32,128]{1,0:T(8,128)S(1)} %get-tuple-element.32.refs_0_), channel_id=1, source_target_pairs={{0,1},{1,0},{2,3},{3,2},{4,5},{5,4},{6,7},{7,6},{8,9},{9,8},{10,11... | collective-permute-start | bytes 49160 | tf_op jit(solution)/shard_map/ppermute | solution.py:67
  57.7 3.3 %collective-permute-start.12 = (f32[32,128]{1,0:T(8,128)S(1)}, f32[32,128]{1,0:T(8,128)S(1)}, u32[]{:S(2)}, u32[]{:S(2)}) collective-permute-start(f32[32,128]{1,0:T(8,128)S(1)} %row_pass.2.refs_0_), channel_id=1, source_target_pairs={{0,3},{1,2},{2,1},{3,0},{4,7},{5,6},{6,5},{7,4},{8,11},{9,10},{10,... | collective-permute-start | bytes 49160 | tf_op jit(solution)/shard_map/ppermute | solution.py:67
  57.7 3.8 %collective-permute-start.11 = (f32[32,128]{1,0:T(8,128)S(1)}, f32[32,128]{1,0:T(8,128)S(1)}, u32[]{:S(2)}, u32[]{:S(2)}) collective-permute-start(f32[32,128]{1,0:T(8,128)S(1)} %row_pass.2.refs_0_), channel_id=1, source_target_pairs={{0,2},{1,3},{2,0},{3,1},{4,6},{5,7},{6,4},{7,5},{8,10},{9,11},{10,... | collective-permute-start | bytes 49160 | tf_op jit(solution)/shard_map/ppermute | solution.py:67
  59.3 2.2 %collective-permute-start.10 = (f32[32,128]{1,0:T(8,128)S(1)}, f32[32,128]{1,0:T(8,128)S(1)}, u32[]{:S(2)}, u32[]{:S(2)}) collective-permute-start(f32[32,128]{1,0:T(8,128)S(1)} %row_pass.2.refs_0_), channel_id=1, source_target_pairs={{0,1},{1,0},{2,3},{3,2},{4,5},{5,4},{6,7},{7,6},{8,9},{9,8},{10,11... | collective-permute-start | bytes 49160 | tf_op jit(solution)/shard_map/ppermute | solution.py:67
  73.7 3.3 %collective-permute-start.15 = (f32[32,128]{1,0:T(8,128)S(1)}, f32[32,128]{1,0:T(8,128)S(1)}, u32[]{:S(2)}, u32[]{:S(2)}) collective-permute-start(f32[32,128]{1,0:T(8,128)S(1)} %row_pass.3.refs_0_), channel_id=1, source_target_pairs={{0,3},{1,2},{2,1},{3,0},{4,7},{5,6},{6,5},{7,4},{8,11},{9,10},{10,... | collective-permute-start | bytes 49160 | tf_op jit(solution)/shard_map/ppermute | solution.py:67
  73.8 3.8 %collective-permute-start.14 = (f32[32,128]{1,0:T(8,128)S(1)}, f32[32,128]{1,0:T(8,128)S(1)}, u32[]{:S(2)}, u32[]{:S(2)}) collective-permute-start(f32[32,128]{1,0:T(8,128)S(1)} %row_pass.3.refs_0_), channel_id=1, source_target_pairs={{0,2},{1,3},{2,0},{3,1},{4,6},{5,7},{6,4},{7,5},{8,10},{9,11},{10,... | collective-permute-start | bytes 49160 | tf_op jit(solution)/shard_map/ppermute | solution.py:67
  75.4 2.2 %collective-permute-start.13 = (f32[32,128]{1,0:T(8,128)S(1)}, f32[32,128]{1,0:T(8,128)S(1)}, u32[]{:S(2)}, u32[]{:S(2)}) collective-permute-start(f32[32,128]{1,0:T(8,128)S(1)} %row_pass.3.refs_0_), channel_id=1, source_target_pairs={{0,1},{1,0},{2,3},{3,2},{4,5},{5,4},{6,7},{7,6},{8,9},{9,8},{10,11... | collective-permute-start | bytes 49160 | tf_op jit(solution)/shard_map/ppermute | solution.py:67

commit v14 on v13

--- a/solution.py
+++ b/solution.py
@@ -75,13 +75,17 @@
     return lax.all_to_all(copies, axis, 0, 0, tiled=True)
 
 
-def pack_kernel(devices, source_ref, target_ref, out_ref):
+def pack_kernel(devices, source_ref, target_ref, *refs):
+    small = (len(refs) - 1) // 2
+    out_ref = refs[small]
     rows = out_ref.shape[0] // devices
     total = jnp.sum(source_ref[...].astype(jnp.float32), axis=(0, 1), keepdims=True)
     target = target_ref[...].astype(jnp.float32)
     for d in range(devices):
         out_ref[d * rows : d * rows + 1, :] = jnp.broadcast_to(total, (1, out_ref.shape[1]))
         out_ref[d * rows + 1 : d * rows + 1 + target.shape[0], :] = target
+    for from_ref, to_ref in zip(refs[:small], refs[small + 1 :]):
+        to_ref[...] = from_ref[...]
 
 
 def near_kernel(near_index_ref, cost_ref, plan_ref, mass_ref, totals_ref, x_ref, term_ref, plan_scr):
@@ -248,13 +252,11 @@
 
 
 def column_kernel(copies, work_ref, select_ref, log_mass_ref, *refs):
-    parts = refs[:-5]
-    out_ref, potential_ref, potential_scr, peak_scr, sum_scr = refs[-5:]
+    parts = refs[:-4]
+    out_ref, potential_scr, peak_scr, sum_scr = refs[-4:]
     rows, slots, width, _ = work_ref.shape
     together = math.gcd(rows, 8)
-    scaled = log_mass_ref[...] - log_sum([p[...] for p in parts])
-    potential_scr[...] = scaled
-    potential_ref[...] = scaled * from_log2
+    potential_scr[...] = log_mass_ref[...] - log_sum([p[...] for p in parts])
 
     for first in range(0, rows, together):
         tall = potential_scr[first : first + together, :].T
@@ -297,11 +299,13 @@
     out_ref[...] = row_sums(rows, peak_scr, sum_scr)
 
 
-def last_kernel(row_devices, row_axis, log_mass_ref, parts_ref, out_ref):
-    here = out_ref.shape[0]
+def last_kernel(row_devices, row_axis, log_target_ref, log_source_ref, column_ref, *refs):
+    parts, (source_ref, target_ref) = refs[:-2], refs[-2:]
+    source_ref[...] = (log_source_ref[...] - log_sum([p[...] for p in parts])) * from_log2
+    here = target_ref.shape[0]
     start = lax.axis_index(row_axis) * here
-    log_mass = log_mass_ref[pl.ds(start, here), :]
-    out_ref[...] = (log_mass - log_sum(parts_of(parts_ref, row_devices))) * from_log2
+    log_mass = log_target_ref[pl.ds(start, here), :]
+    target_ref[...] = (log_mass - log_sum(parts_of(column_ref, row_devices))) * from_log2
 
 
 def per_device(
@@ -339,13 +343,16 @@
 
     pack_rows = 1 + target_here
     devices = row_devices * col_devices
-    pack = pl.pallas_call(
+    handed = [near_t, slot_t, link_t, mass]
+    pack, near_t, slot_t, link_t, mass = pl.pallas_call(
         functools.partial(pack_kernel, devices),
-        in_specs=[VMEM, VMEM],
-        out_shape=jax.ShapeDtypeStruct((devices * pack_rows, width), f32),
+        in_specs=[VMEM] * (2 + len(handed)),
+        out_specs=[VMEM] * (1 + len(handed)),
+        out_shape=[jax.ShapeDtypeStruct((devices * pack_rows, width), f32)]
+        + [jax.ShapeDtypeStruct(a.shape, a.dtype) for a in handed],
         compiler_params=small,
         name="pack",
-    )(mass, in_hbm(target_weights.reshape(target_here, width)))
+    )(mass, in_hbm(target_weights.reshape(target_here, width)), *handed)
     packs = exchange(pack, ("rows", "cols"))
 
     direct = list(range(1, half + 1))
@@ -445,11 +452,8 @@
         return pl.pallas_call(
             functools.partial(column_kernel, copies),
             in_specs=[VMEM] * (3 + len(row_parts)),
-            out_specs=[VMEM, VMEM],
-            out_shape=[
-                jax.ShapeDtypeStruct((copies * group_blocks, width), f32),
-                jax.ShapeDtypeStruct((rows_here, width), f32),
-            ],
+            out_specs=VMEM,
+            out_shape=jax.ShapeDtypeStruct((copies * group_blocks, width), f32),
             scratch_shapes=[
                 pltpu.VMEM((rows_here, width), f32),
                 pltpu.VMEM((rows_here * slots, width), f32),
@@ -476,18 +480,19 @@
 
     for step in range(ITERS):
         last = step == ITERS - 1
-        column_part, source_potential = column_step(
-            from_all(row_part, "cols"), 1 if last else row_devices
-        )
-        column_parts = exchange(column_part, "rows")
+        row_parts = from_all(row_part, "cols")
+        column_parts = exchange(column_step(row_parts, 1 if last else row_devices), "rows")
         if not last:
             row_part = row_step(column_parts)
-    own_target = pl.pallas_call(
+    source_potential, own_target = pl.pallas_call(
         functools.partial(last_kernel, row_devices, "rows"),
-        out_shape=jax.ShapeDtypeStruct((target_here, width), f32),
+        out_shape=[
+            jax.ShapeDtypeStruct((rows_here, width), f32),
+            jax.ShapeDtypeStruct((target_here, width), f32),
+        ],
         compiler_params=small,
         name="last_potential",
-    )(log_target, column_parts)
+    )(log_target, log_source, column_parts, *row_parts)
     return (
         cost_blocks,
         source_potential.reshape(rows_here * width),

time: 88.7 us -> 88.6 us (level)
  no operation moved by 1% of the time
where the time goes in v14:
time: 88.6 us; the launch traced here: 88.2 us
  blocking collectives  28.8 us (33%)
  Pallas kernels  26.5 us (30%)
  starting transfers between devices  21.3 us (24%)
  waiting for transfers between devices  10.8 us (12%)
    all_to_all x3, blocking collectives, exchange(): return lax.all_to_all(copies, axis, 0, 0, tiled=True)  28.8 us
    ppermute x16, starting transfers between devices, send(): return lax.ppermute(x, axis, [(d, d ^ mask) for d in range(size)])  17.5 us
    ppermute x16, waiting for transfers between devices, send(): return lax.ppermute(x, axis, [(d, d ^ mask) for d in range(size)])  10.8 us
    pallas_call x1, Pallas kernels, per_device(): pl.pallas_call(functools.partial(far_kernel, (row_devices, col_devices, t...  9 us
    pallas_call x1, Pallas kernels, per_device(): pl.pallas_call(near_kernel, grid=(rows_here // step_rows,), in_specs=[SME...  7.67 us
    pallas_call x3, Pallas kernels, column_step(): pl.pallas_call(functools.partial(column_kernel, copies), in_specs=[VMEM]...  4.01 us
    all_to_all x1, starting transfers between devices, exchange(): return lax.all_to_all(copies, axis, 0, 0, tiled=True)  3.82 us
    pallas_call x2, Pallas kernels, row_step(): pl.pallas_call(functools.partial(row_kernel, row_devices), in_specs=[SMEM...  3.67 us
  transfers between devices with their start and end apart: 17, of which 8 were waited for; matrix products, arithmetic and copies ran while one was open for 0% of the time, Pallas kernels for 10%

profile of v14, /device:TPU:0, one launch (start us, length us, event | category | flops | bytes accessed | tf_op | source)
XLA Modules:
  0.0 88.2 jit_solution(10151271778847040080)
XLA Ops:
  0.6 4.0 %collective-permute-start.2 = (f32[1,1,3,128,128]{4,3,2,1,0:T(8,128)}, f32[1,1,3,128,128]{4,3,2,1,0:T(8,128)S(1)}, u32[]{:S(2)}, u32[]{:S(2)}) collective-permute-start(f32[1,1,3,128,128]{4,3,2,1,0:T(8,128)} %refs_6_.1), channel_id=1, source_target_pairs={{0,12},{4,8},{8,4},{12,0},{16,28},{20,24},{24,20},{28,16},{1,13},{... | collective-permute-start | bytes 589832 | tf_op jit(solution)/shard_map/ppermute | solution.py:67
  4.7 0.4 collective-permute-start.1
  5.3 2.9 %collective-permute-start.3 = (f32[1,1,3,128,128]{4,3,2,1,0:T(8,128)}, f32[1,1,3,128,128]{4,3,2,1,0:T(8,128)S(1)}, u32[]{:S(2)}, u32[]{:S(2)}) collective-permute-start(f32[1,1,3,128,128]{4,3,2,1,0:T(8,128)} %refs_6_.1), channel_id=1, source_target_pairs={{0,16},{4,20},{8,24},{12,28},{16,0},{20,4},{24,8},{28,12},{1,17},{... | collective-permute-start | bytes 589832 | tf_op jit(solution)/shard_map/ppermute | solution.py:67
  8.2 1.5 %pack.1 = (f32[64,128]{1,0:T(8,128)}, s32[3,32]{1,0:T(4,128)S(1)}, s32[2,32]{1,0:T(2,128)S(1)}, s32[3,1,8]{2,1,0:T(1,128)S(1)}, s32[32,128]{1,0:T(8,128)S(1)}) custom-call(s32[32,128]{1,0:T(8,128)} %bitcast.25, s32[1,128]{1,0:T(1,128)} %target_ref.1, s32[3,32]{1,0:T(4,128)} %bitcast.27, s32[2,32]{1,0:T(2,128)} %bitcast.29, s32[3,1,8]{2,1,0:T(1,128)} %bitcast.28, ...), custom_call_target="tpu_custom_call" | custom-call | tf_op jit(solution)/shard_map/pack/pallas_call | solution.py:347
  9.8 3.8 %all-to-all-start = ((f32[32,2,128]{2,1,0:T(2,128)}), f32[32,2,128]{2,1,0:T(2,128)S(1)}, u32[]{:S(2)}, u32[]{:S(2)}) async-start(f32[32,2,128]{2,1,0:T(2,128)} %bitcast.5), calls=%async_computation | async-start | bytes 65536 | tf_op jit(solution)/shard_map/all_to_all | solution.py:75
  13.6 1.3 %collective-permute-done.2.refs_2_ = f32[1,1,3,128,128]{4,3,2,1,0:T(8,128)S(1)} collective-permute-done((f32[1,1,3,128,128]{4,3,2,1,0:T(8,128)}, f32[1,1,3,128,128]{4,3,2,1,0:T(8,128)S(1)}, u32[]{:S(2)}, u32[]{:S(2)}) %collective-permute-start.2) | collective-permute-done | bytes 196640 | tf_op jit(solution)/shard_map/ppermute | solution.py:67
  14.9 3.7 %collective-permute-done.1.refs_1_ = f32[1,1,3,128,128]{4,3,2,1,0:T(8,128)S(1)} collective-permute-done((f32[1,1,3,128,128]{4,3,2,1,0:T(8,128)}, f32[1,1,3,128,128]{4,3,2,1,0:T(8,128)S(1)}, u32[]{:S(2)}, u32[]{:S(2)}) %collective-permute-start.1) | collective-permute-done | bytes 196640 | tf_op jit(solution)/shard_map/ppermute | solution.py:67
  18.6 2.6 %collective-permute-start.6 = (f32[1,1,3,128,128]{4,3,2,1,0:T(8,128)S(1)}, f32[1,1,3,128,128]{4,3,2,1,0:T(8,128)S(1)}, u32[]{:S(2)}, u32[]{:S(2)}) collective-permute-start(f32[1,1,3,128,128]{4,3,2,1,0:T(8,128)S(1)} %get-tuple-element.33.refs_10_), channel_id=1, source_target_pairs={{0,12},{4,8},{8,4},{12,0},{16,28},{20,24},{24,20},{28,16},{1,13},{... | collective-permute-start | bytes 589832 | tf_op jit(solution)/shard_map/ppermute | solution.py:67
  21.3 1.5 %collective-permute-start.4 = (f32[1,1,3,128,128]{4,3,2,1,0:T(8,128)S(1)}, f32[1,1,3,128,128]{4,3,2,1,0:T(8,128)S(1)}, u32[]{:S(2)}, u32[]{:S(2)}) collective-permute-start(f32[1,1,3,128,128]{4,3,2,1,0:T(8,128)S(1)} %get-tuple-element.33.refs_10_), channel_id=1, source_target_pairs={{0,4},{4,0},{8,12},{12,8},{16,20},{20,16},{24,28},{28,24},{1,5},{5... | collective-permute-start | bytes 589832 | tf_op jit(solution)/shard_map/ppermute | solution.py:67
  22.8 7.7 %near_product.1 = (bf16[32,256,768]{2,1,0:T(8,128)(2,1)S(1)}, f32[8,128,4]{2,1,0:T(8,128)S(1)}) custom-call(s32[3,32]{1,0:T(4,128)S(1)} %get-tuple-element.23.near_index_ref.refs_0_, f32[32,3,128,128]{3,2,1,0:T(8,128)} %cost_ref.1, f32[32,1,2,128,128]{4,3,2,1,0:T(8,128)} %plan_ref.1, s32[32,128]{1,0:T(8,128)S(1)} %get-tuple-element.26.mass_ref.refs_5_, ...), custom_call_target="tpu_custom_call" | custom-call | flops 2415919104 | bytes 10485760 | tf_op jit(solution)/shard_map/near_product/pallas_call | solution.py:377
  30.5 9.0 %far_product.1 = (f32[32,1,2,128,128]{4,3,2,1,0:T(8,128)}, f32[32,2,128,128]{3,2,1,0:T(8,128)S(1)}, f32[32,2,128,128]{3,2,1,0:T(8,128)S(1)}, f32[32,128]{1,0:T(8...) custom-call(s32[3,32]{1,0:T(4,128)S(1)} %get-tuple-element.23.near_index_ref.refs_0_, ...), custom_call_target="tpu_custom_call" | custom-call | tf_op jit(solution)/shard_map/far_product/pallas_call | solution.py:407
  39.5 1.5 %collective-permute-start.8 = (f32[32,128]{1,0:T(8,128)S(1)}, f32[32,128]{1,0:T(8,128)S(1)}, u32[]{:S(2)}, u32[]{:S(2)}) collective-permute-start(f32[32,128]{1,0:T(8,128)S(1)} %get-tuple-element.40.refs_0_), channel_id=1, source_target_pairs={{0,2},{1,3},{2,0},{3,1},{4,6},{5,7},{6,4},{7,5},{8,10},{9,11},{10,... | collective-permute-start | bytes 49160 | tf_op jit(solution)/shard_map/ppermute | solution.py:67
  41.0 0.3 collective-permute-start.7
  41.4 1.4 %collective-permute-done.9.refs_3_ = f32[32,128]{1,0:T(8,128)S(1)} collective-permute-done((f32[32,128]{1,0:T(8,128)S(1)}, f32[32,128]{1,0:T(8,128)S(1)}, u32[]{:S(2)}, u32[]{:S(2)}) %collective-permute-start.9) | collective-permute-done | bytes 16416 | tf_op jit(solution)/shard_map/ppermute | solution.py:67
  42.8 0.5 collective-permute-done.8.refs_2_
  43.3 1.3 %column_pass.3 = f32[64,128]{1,0:T(8,128)S(1)} custom-call(f32[32,2,128,128]{3,2,1,0:T(8,128)S(1)} %get-tuple-element.37.work_ref, s32[64,128]{1,0:T(8,128)S(1)} %get-tuple-element.38.select_ref, f32[32,128]{1,0:T(8,128)S(1)} %get-tuple-element.36.log_mass_ref.log_source_ref, f32[32,128]{1,0:T(8,128)S(1)} %get-tuple-element.40.refs_0_, ...), custom_call_target="tpu_custom_call" | custom-call | tf_op jit(solution)/shard_map/column_pass/pallas_call | solution.py:452
  44.6 10.9 %all_to_all.44 = f32[8,8,128]{2,1,0:T(8,128)S(1)} all-to-all(f32[8,8,128]{2,1,0:T(8,128)S(1)} %bitcast.19), channel_id=1, replica_groups=mesh['rows'=8,'cols'=4] {'rows'}, dimensions={0} | all-to-all | bytes 65536 | tf_op jit(solution)/shard_map/all_to_all | solution.py:75
  55.5 1.8 %row_pass.2.refs_0_ = f32[32,128]{1,0:T(8,128)S(1)} custom-call(s32[2,32]{1,0:T(2,128)S(1)} %get-tuple-element.24.refs_1_.slot_ref, f32[32,2,128,128]{3,2,1,0:T(8,128)S(1)} %get-tuple-element.39.tall_ref, f32[8,128]{1,0:T(8,128)S(1)} %get-tuple-element.35.log_mass_ref.log_target_ref, f32[64,128]{1,0:T(8,128)S(1)} %bitcast.22), custom_call_target="tpu_custom_call" | custom-call | tf_op jit(solution)/shard_map/row_pass/pallas_call | solution.py:467
  57.5 1.6 %collective-permute-start.11 = (f32[32,128]{1,0:T(8,128)S(1)}, f32[32,128]{1,0:T(8,128)S(1)}, u32[]{:S(2)}, u32[]{:S(2)}) collective-permute-start(f32[32,128]{1,0:T(8,128)S(1)} %row_pass.2.refs_0_), channel_id=1, source_target_pairs={{0,2},{1,3},{2,0},{3,1},{4,6},{5,7},{6,4},{7,5},{8,10},{9,11},{10,... | collective-permute-start | bytes 49160 | tf_op jit(solution)/shard_map/ppermute | solution.py:67
  59.0 0.3 collective-permute-start.10
  59.3 1.4 %collective-permute-done.12.refs_3_ = f32[32,128]{1,0:T(8,128)S(1)} collective-permute-done((f32[32,128]{1,0:T(8,128)S(1)}, f32[32,128]{1,0:T(8,128)S(1)}, u32[]{:S(2)}, u32[]{:S(2)}) %collective-permute-start.12) | collective-permute-done | bytes 16416 | tf_op jit(solution)/shard_map/ppermute | solution.py:67
  60.7 0.5 collective-permute-done.11.refs_2_
  61.3 1.3 %column_pass.4 = f32[64,128]{1,0:T(8,128)S(1)} custom-call(f32[32,2,128,128]{3,2,1,0:T(8,128)S(1)} %get-tuple-element.37.work_ref, s32[64,128]{1,0:T(8,128)S(1)} %get-tuple-element.38.select_ref, f32[32,128]{1,0:T(8,128)S(1)} %get-tuple-element.36.log_mass_ref.log_source_ref, f32[32,128]{1,0:T(8,128)S(1)} %row_pass.2.refs_0_, ...), custom_call_target="tpu_custom_call" | custom-call | tf_op jit(solution)/shard_map/column_pass/pallas_call | solution.py:452
  62.6 9.1 %all_to_all.45 = f32[8,8,128]{2,1,0:T(8,128)S(1)} all-to-all(f32[8,8,128]{2,1,0:T(8,128)S(1)} %bitcast.20), channel_id=1, replica_groups=mesh['rows'=8,'cols'=4] {'rows'}, dimensions={0} | all-to-all | bytes 65536 | tf_op jit(solution)/shard_map/all_to_all | solution.py:75
  71.7 1.8 %row_pass.3.refs_0_ = f32[32,128]{1,0:T(8,128)S(1)} custom-call(s32[2,32]{1,0:T(2,128)S(1)} %get-tuple-element.24.refs_1_.slot_ref, f32[32,2,128,128]{3,2,1,0:T(8,128)S(1)} %get-tuple-element.39.tall_ref, f32[8,128]{1,0:T(8,128)S(1)} %get-tuple-element.35.log_mass_ref.log_target_ref, f32[64,128]{1,0:T(8,128)S(1)} %bitcast.21), custom_call_target="tpu_custom_call" | custom-call | tf_op jit(solution)/shard_map/row_pass/pallas_call | solution.py:467
  73.6 1.6 %collective-permute-start.14 = (f32[32,128]{1,0:T(8,128)S(1)}, f32[32,128]{1,0:T(8,128)S(1)}, u32[]{:S(2)}, u32[]{:S(2)}) collective-permute-start(f32[32,128]{1,0:T(8,128)S(1)} %row_pass.3.refs_0_), channel_id=1, source_target_pairs={{0,2},{1,3},{2,0},{3,1},{4,6},{5,7},{6,4},{7,5},{8,10},{9,11},{10,... | collective-permute-start | bytes 49160 | tf_op jit(solution)/shard_map/ppermute | solution.py:67
  75.2 0.3 collective-permute-start.13
  75.4 1.4 %collective-permute-done.15.refs_3_ = f32[32,128]{1,0:T(8,128)S(1)} collective-permute-done((f32[32,128]{1,0:T(8,128)S(1)}, f32[32,128]{1,0:T(8,128)S(1)}, u32[]{:S(2)}, u32[]{:S(2)}) %collective-permute-start.15) | collective-permute-done | bytes 16416 | tf_op jit(solution)/shard_map/ppermute | solution.py:67
  76.8 0.5 collective-permute-done.14.refs_2_
  77.4 1.3 %column_pass.5 = f32[8,128]{1,0:T(8,128)S(1)} custom-call(f32[32,2,128,128]{3,2,1,0:T(8,128)S(1)} %get-tuple-element.37.work_ref, s32[64,128]{1,0:T(8,128)S(1)} %get-tuple-element.38.select_ref, f32[32,128]{1,0:T(8,128)S(1)} %get-tuple-element.36.log_mass_ref.log_source_ref, f32[32,128]{1,0:T(8,128)S(1)} %row_pass.3.refs_0_, ...), custom_call_target="tpu_custom_call" | custom-call | tf_op jit(solution)/shard_map/column_pass/pallas_call | solution.py:452
  78.7 8.8 %all_to_all.46 = f32[8,1,128]{2,1,0:T(1,128)S(1)} all-to-all(f32[8,1,128]{2,1,0:T(1,128)S(1)} %bitcast.23), channel_id=1, replica_groups=mesh['rows'=8,'cols'=4] {'rows'}, dimensions={0} | all-to-all | bytes 8192 | tf_op jit(solution)/shard_map/all_to_all | solution.py:75
  87.5 0.6 last_potential.1
  (17 shorter events, 0.5 us)
Async XLA Ops:
  0.6 14.2 %collective-permute-start.2 = (f32[1,1,3,128,128]{4,3,2,1,0:T(8,128)}, f32[1,1,3,128,128]{4,3,2,1,0:T(8,128)S(1)}, u32[]{:S(2)}, u32[]{:S(2)}) collective-permute-start(f32[1,1,3,128,128]{4,3,2,1,0:T(8,128)} %refs_6_.1), channel_id=1, source_target_pairs={{0,12},{4,8},{8,4},{12,0},{16,28},{20,24},{24,20},{28,16},{1,13},{... | collective-permute-start | bytes 589832 | tf_op jit(solution)/shard_map/ppermute | solution.py:67
  4.7 13.9 %collective-permute-start.1 = (f32[1,1,3,128,128]{4,3,2,1,0:T(8,128)}, f32[1,1,3,128,128]{4,3,2,1,0:T(8,128)S(1)}, u32[]{:S(2)}, u32[]{:S(2)}) collective-permute-start(f32[1,1,3,128,128]{4,3,2,1,0:T(8,128)} %refs_6_.1), channel_id=1, source_target_pairs={{0,8},{4,12},{8,0},{12,4},{16,24},{20,28},{24,16},{28,20},{1,9},{5... | collective-permute-start | bytes 589832 | tf_op jit(solution)/shard_map/ppermute | solution.py:67
  5.1 13.4 %collective-permute-start = (f32[1,1,3,128,128]{4,3,2,1,0:T(8,128)}, f32[1,1,3,128,128]{4,3,2,1,0:T(8,128)S(1)}, u32[]{:S(2)}, u32[]{:S(2)}) collective-permute-start(f32[1,1,3,128,128]{4,3,2,1,0:T(8,128)} %refs_6_.1), channel_id=1, source_target_pairs={{0,4},{4,0},{8,12},{12,8},{16,20},{20,16},{24,28},{28,24},{1,5},{5... | collective-permute-start | bytes 589832 | tf_op jit(solution)/shard_map/ppermute | solution.py:67
  5.3 13.2 %collective-permute-start.3 = (f32[1,1,3,128,128]{4,3,2,1,0:T(8,128)}, f32[1,1,3,128,128]{4,3,2,1,0:T(8,128)S(1)}, u32[]{:S(2)}, u32[]{:S(2)}) collective-permute-start(f32[1,1,3,128,128]{4,3,2,1,0:T(8,128)} %refs_6_.1), channel_id=1, source_target_pairs={{0,16},{4,20},{8,24},{12,28},{16,0},{20,4},{24,8},{28,12},{1,17},{... | collective-permute-start | bytes 589832 | tf_op jit(solution)/shard_map/ppermute | solution.py:67
  9.8 13.0 %all-to-all-start = ((f32[32,2,128]{2,1,0:T(2,128)}), f32[32,2,128]{2,1,0:T(2,128)S(1)}, u32[]{:S(2)}, u32[]{:S(2)}) async-start(f32[32,2,128]{2,1,0:T(2,128)} %bitcast.5), calls=%async_computation | async-start | bytes 65536 | tf_op jit(solution)/shard_map/all_to_all | solution.py:75
  18.6 11.9 %collective-permute-start.6 = (f32[1,1,3,128,128]{4,3,2,1,0:T(8,128)S(1)}, f32[1,1,3,128,128]{4,3,2,1,0:T(8,128)S(1)}, u32[]{:S(2)}, u32[]{:S(2)}) collective-permute-start(f32[1,1,3,128,128]{4,3,2,1,0:T(8,128)S(1)} %get-tuple-element.33.refs_10_), channel_id=1, source_target_pairs={{0,12},{4,8},{8,4},{12,0},{16,28},{20,24},{24,20},{28,16},{1,13},{... | collective-permute-start | bytes 589832 | tf_op jit(solution)/shard_map/ppermute | solution.py:67
  21.2 9.3 %collective-permute-start.5 = (f32[1,1,3,128,128]{4,3,2,1,0:T(8,128)S(1)}, f32[1,1,3,128,128]{4,3,2,1,0:T(8,128)S(1)}, u32[]{:S(2)}, u32[]{:S(2)}) collective-permute-start(f32[1,1,3,128,128]{4,3,2,1,0:T(8,128)S(1)} %get-tuple-element.33.refs_10_), channel_id=1, source_target_pairs={{0,8},{4,12},{8,0},{12,4},{16,24},{20,28},{24,16},{28,20},{1,9},{5... | collective-permute-start | bytes 589832 | tf_op jit(solution)/shard_map/ppermute | solution.py:67
  21.3 9.2 %collective-permute-start.4 = (f32[1,1,3,128,128]{4,3,2,1,0:T(8,128)S(1)}, f32[1,1,3,128,128]{4,3,2,1,0:T(8,128)S(1)}, u32[]{:S(2)}, u32[]{:S(2)}) collective-permute-start(f32[1,1,3,128,128]{4,3,2,1,0:T(8,128)S(1)} %get-tuple-element.33.refs_10_), channel_id=1, source_target_pairs={{0,4},{4,0},{8,12},{12,8},{16,20},{20,16},{24,28},{28,24},{1,5},{5... | collective-permute-start | bytes 589832 | tf_op jit(solution)/shard_map/ppermute | solution.py:67
  22.8 7.7 %copy-start = (f32[1,1,3,128,128]{4,3,2,1,0:T(8,128)S(1)}, f32[1,1,3,128,128]{4,3,2,1,0:T(8,128)}, u32[]{:S(2)}) copy-start(f32[1,1,3,128,128]{4,3,2,1,0:T(8,128)} %refs_6_.1) | copy-start | bytes 589828
  39.5 3.3 %collective-permute-start.9 = (f32[32,128]{1,0:T(8,128)S(1)}, f32[32,128]{1,0:T(8,128)S(1)}, u32[]{:S(2)}, u32[]{:S(2)}) collective-permute-start(f32[32,128]{1,0:T(8,128)S(1)} %get-tuple-element.40.refs_0_), channel_id=1, source_target_pairs={{0,3},{1,2},{2,1},{3,0},{4,7},{5,6},{6,5},{7,4},{8,11},{9,10},{10,... | collective-permute-start | bytes 49160 | tf_op jit(solution)/shard_map/ppermute | solution.py:67
  39.5 3.8 %collective-permute-start.8 = (f32[32,128]{1,0:T(8,128)S(1)}, f32[32,128]{1,0:T(8,128)S(1)}, u32[]{:S(2)}, u32[]{:S(2)}) collective-permute-start(f32[32,128]{1,0:T(8,128)S(1)} %get-tuple-element.40.refs_0_), channel_id=1, source_target_pairs={{0,2},{1,3},{2,0},{3,1},{4,6},{5,7},{6,4},{7,5},{8,10},{9,11},{10,... | collective-permute-start | bytes 49160 | tf_op jit(solution)/shard_map/ppermute | solution.py:67
  41.0 2.3 %collective-permute-start.7 = (f32[32,128]{1,0:T(8,128)S(1)}, f32[32,128]{1,0:T(8,128)S(1)}, u32[]{:S(2)}, u32[]{:S(2)}) collective-permute-start(f32[32,128]{1,0:T(8,128)S(1)} %get-tuple-element.40.refs_0_), channel_id=1, source_target_pairs={{0,1},{1,0},{2,3},{3,2},{4,5},{5,4},{6,7},{7,6},{8,9},{9,8},{10,11... | collective-permute-start | bytes 49160 | tf_op jit(solution)/shard_map/ppermute | solution.py:67
  57.4 3.3 %collective-permute-start.12 = (f32[32,128]{1,0:T(8,128)S(1)}, f32[32,128]{1,0:T(8,128)S(1)}, u32[]{:S(2)}, u32[]{:S(2)}) collective-permute-start(f32[32,128]{1,0:T(8,128)S(1)} %row_pass.2.refs_0_), channel_id=1, source_target_pairs={{0,3},{1,2},{2,1},{3,0},{4,7},{5,6},{6,5},{7,4},{8,11},{9,10},{10,... | collective-permute-start | bytes 49160 | tf_op jit(solution)/shard_map/ppermute | solution.py:67
  57.5 3.8 %collective-permute-start.11 = (f32[32,128]{1,0:T(8,128)S(1)}, f32[32,128]{1,0:T(8,128)S(1)}, u32[]{:S(2)}, u32[]{:S(2)}) collective-permute-start(f32[32,128]{1,0:T(8,128)S(1)} %row_pass.2.refs_0_), channel_id=1, source_target_pairs={{0,2},{1,3},{2,0},{3,1},{4,6},{5,7},{6,4},{7,5},{8,10},{9,11},{10,... | collective-permute-start | bytes 49160 | tf_op jit(solution)/shard_map/ppermute | solution.py:67
  59.0 2.2 %collective-permute-start.10 = (f32[32,128]{1,0:T(8,128)S(1)}, f32[32,128]{1,0:T(8,128)S(1)}, u32[]{:S(2)}, u32[]{:S(2)}) collective-permute-start(f32[32,128]{1,0:T(8,128)S(1)} %row_pass.2.refs_0_), channel_id=1, source_target_pairs={{0,1},{1,0},{2,3},{3,2},{4,5},{5,4},{6,7},{7,6},{8,9},{9,8},{10,11... | collective-permute-start | bytes 49160 | tf_op jit(solution)/shard_map/ppermute | solution.py:67
  73.5 3.3 %collective-permute-start.15 = (f32[32,128]{1,0:T(8,128)S(1)}, f32[32,128]{1,0:T(8,128)S(1)}, u32[]{:S(2)}, u32[]{:S(2)}) collective-permute-start(f32[32,128]{1,0:T(8,128)S(1)} %row_pass.3.refs_0_), channel_id=1, source_target_pairs={{0,3},{1,2},{2,1},{3,0},{4,7},{5,6},{6,5},{7,4},{8,11},{9,10},{10,... | collective-permute-start | bytes 49160 | tf_op jit(solution)/shard_map/ppermute | solution.py:67
  73.6 3.8 %collective-permute-start.14 = (f32[32,128]{1,0:T(8,128)S(1)}, f32[32,128]{1,0:T(8,128)S(1)}, u32[]{:S(2)}, u32[]{:S(2)}) collective-permute-start(f32[32,128]{1,0:T(8,128)S(1)} %row_pass.3.refs_0_), channel_id=1, source_target_pairs={{0,2},{1,3},{2,0},{3,1},{4,6},{5,7},{6,4},{7,5},{8,10},{9,11},{10,... | collective-permute-start | bytes 49160 | tf_op jit(solution)/shard_map/ppermute | solution.py:67
  75.2 2.2 %collective-permute-start.13 = (f32[32,128]{1,0:T(8,128)S(1)}, f32[32,128]{1,0:T(8,128)S(1)}, u32[]{:S(2)}, u32[]{:S(2)}) collective-permute-start(f32[32,128]{1,0:T(8,128)S(1)} %row_pass.3.refs_0_), channel_id=1, source_target_pairs={{0,1},{1,0},{2,3},{3,2},{4,5},{5,4},{6,7},{7,6},{8,9},{9,8},{10,11... | collective-permute-start | bytes 49160 | tf_op jit(solution)/shard_map/ppermute | solution.py:67

commit v15 on v13

--- a/solution.py
+++ b/solution.py
@@ -75,13 +75,17 @@
     return lax.all_to_all(copies, axis, 0, 0, tiled=True)
 
 
-def pack_kernel(devices, source_ref, target_ref, out_ref):
+def pack_kernel(devices, source_ref, target_ref, *refs):
+    small = (len(refs) - 1) // 2
+    out_ref = refs[small]
     rows = out_ref.shape[0] // devices
     total = jnp.sum(source_ref[...].astype(jnp.float32), axis=(0, 1), keepdims=True)
     target = target_ref[...].astype(jnp.float32)
     for d in range(devices):
         out_ref[d * rows : d * rows + 1, :] = jnp.broadcast_to(total, (1, out_ref.shape[1]))
         out_ref[d * rows + 1 : d * rows + 1 + target.shape[0], :] = target
+    for from_ref, to_ref in zip(refs[:small], refs[small + 1 :]):
+        to_ref[...] = from_ref[...]
 
 
 def near_kernel(near_index_ref, cost_ref, plan_ref, mass_ref, totals_ref, x_ref, term_ref, plan_scr):
@@ -131,11 +135,12 @@
     pack_ref, out_ref, work_ref, tall_ref, part_ref, log_source_ref, log_target_ref, select_ref = refs[
         6 + row_devices : 14 + row_devices
     ]
-    far_high, far_low, table, column_scr, scale_scr, peak_scr, sum_scr = refs[14 + row_devices :]
+    far_high, far_low, table, column_scr, scale_scr, peak_scr, sum_scr, cost_scr, sems = refs[14 + row_devices :]
     g = pl.program_id(0)
     near_count = near_index_ref.shape[0]
     slots = slot_ref.shape[0]
-    rows = out_ref.shape[0]
+    all_rows = out_ref.shape[0]
+    rows = all_rows // pl.num_programs(0)
     width = out_ref.shape[3]
     zero_block = group_blocks * link_count
 
@@ -191,6 +196,9 @@
                     t = link_ref[m, 0, j]
                     column_scr[pl.ds(t, 1), :] += spread * (1.0 / (link_count * width))
 
+    def out_copy(row):
+        return pltpu.make_async_copy(cost_scr.at[row], out_ref.at[row], sems.at[row])
+
     group_devices = target_count // (group_blocks * width)
     coef = 2.0 * (1.0 / (near_count * width)) * (1.0 / (slots * group_devices * width))
     scale = scale_scr[0:1, 0:1]
@@ -217,18 +225,21 @@
         scores = []
         for l in range(slots):
             cost = tall + column_scr[pl.ds(targets[l], 1), :] - coef * product[:, l * width : (l + 1) * width]
-            out_ref[i, 0, l] = cost
+            cost_scr[row, 0, l] = cost
             select_ref[pl.ds(row * slots + l, 1), :] = jnp.full((1, width), targets[l], jnp.int32)
             scaled = cost * -to_log2
             work_ref[row, l] = scaled
             turned = scaled.T
             tall_ref[row, l] = turned
             scores.append(turned)
+        out_copy(row).start()
         row_pass(scores, row, part_ref.shape[0], peak_scr, sum_scr)
 
     @pl.when(g == pl.num_programs(0) - 1)
     def _():
         part_ref[...] = row_sums(part_ref.shape[0], peak_scr, sum_scr)
+        for row in range(all_rows):
+            out_copy(row).wait()
 
 
 def row_pass(scores, row, rows, peak_scr, sum_scr):
@@ -284,13 +295,16 @@
 
 
 def row_kernel(
-    row_devices, slot_ref, tall_ref, log_mass_ref, parts_ref, out_ref, wide_scr, peak_scr, sum_scr
+    row_devices, slot_any, tall_ref, log_mass_ref, parts_ref, out_ref, wide_scr, peak_scr, sum_scr, slot_ref, sem
 ):
     rows, slots, width, _ = tall_ref.shape
+    slot_copy = pltpu.make_async_copy(slot_any, slot_ref, sem)
+    slot_copy.start()
     potential = (log_mass_ref[...] - log_sum(parts_of(parts_ref, row_devices))).T
     for t in range(wide_scr.shape[0]):
         wide_scr[t] = jnp.broadcast_to(potential[:, t : t + 1], (width, width))
 
+    slot_copy.wait()
     for row in range(rows):
         scores = [wide_scr[slot_ref[l, row]] + tall_ref[row, l] for l in range(slots)]
         row_pass(scores, row, rows, peak_scr, sum_scr)
@@ -339,13 +353,16 @@
 
     pack_rows = 1 + target_here
     devices = row_devices * col_devices
-    pack = pl.pallas_call(
+    handed = [near_t, slot_t, link_t, mass]
+    pack, near_t, slot_t, link_t, mass = pl.pallas_call(
         functools.partial(pack_kernel, devices),
-        in_specs=[VMEM, VMEM],
-        out_shape=jax.ShapeDtypeStruct((devices * pack_rows, width), f32),
+        in_specs=[VMEM] * (2 + len(handed)),
+        out_specs=[VMEM] * (1 + len(handed)),
+        out_shape=[jax.ShapeDtypeStruct((devices * pack_rows, width), f32)]
+        + [jax.ShapeDtypeStruct(a.shape, a.dtype) for a in handed],
         compiler_params=small,
         name="pack",
-    )(mass, in_hbm(target_weights.reshape(target_here, width)))
+    )(mass, in_hbm(target_weights.reshape(target_here, width)), *handed)
     packs = exchange(pack, ("rows", "cols"))
 
     direct = list(range(1, half + 1))
@@ -395,7 +412,6 @@
     far_bytes = group_blocks * link_count * width * width * 4
     far_rows = 2 * step_rows if rows_here % (2 * step_rows) == 0 else step_rows
     steps = rows_here // far_rows
-    cost_block = pl.BlockSpec((far_rows, 1, slots, width, width), lambda g: (g, 0, 0, 0, 0))
     work_shape = pltpu.VMEM((rows_here, slots, width, width), f32)
     cost_blocks, work, tall, row_part, log_source, log_target, select = pl.pallas_call(
         functools.partial(
@@ -409,7 +425,7 @@
         + [VMEM] * row_devices
         + [whole(packs.shape)],
         out_specs=[
-            cost_block,
+            ANY,
             VMEM,
             VMEM,
             whole((rows_here, width)),
@@ -418,7 +434,7 @@
             whole((rows_here * slots, width)),
         ],
         out_shape=[
-            jax.ShapeDtypeStruct(coupling.shape, f32),
+            pltpu.HBM(coupling.shape, f32),
             work_shape,
             work_shape,
             jax.ShapeDtypeStruct((rows_here, width), f32),
@@ -434,6 +450,8 @@
             pltpu.VMEM((1, width), f32),
             pltpu.VMEM((slots * rows_here, width), f32),
             pltpu.VMEM((slots * rows_here, width), f32),
+            pltpu.VMEM(coupling.shape, f32),
+            pltpu.SemaphoreType.DMA((rows_here,)),
         ],
         compiler_params=pltpu.CompilerParams(vmem_limit_bytes=12 * mib + 2 * far_bytes),
         name="far_product",
@@ -462,13 +480,15 @@
     def row_step(column_parts):
         return pl.pallas_call(
             functools.partial(row_kernel, row_devices),
-            in_specs=[SMEM, VMEM, VMEM, VMEM],
+            in_specs=[ANY, VMEM, VMEM, VMEM],
             out_specs=VMEM,
             out_shape=jax.ShapeDtypeStruct((rows_here, width), f32),
             scratch_shapes=[
                 pltpu.VMEM((group_blocks, width, width), f32),
                 pltpu.VMEM((slots * rows_here, width), f32),
                 pltpu.VMEM((slots * rows_here, width), f32),
+                pltpu.SMEM((slots, rows_here), jnp.int32),
+                pltpu.SemaphoreType.DMA,
             ],
             compiler_params=pass_params,
             name="row_pass",

time: 88.7 us -> 87.3 us (0.984)
  Pallas kernels: 26.4 us -> 25.1 us
    pallas_call x1, Pallas kernels: 9.4 us -> 8.5 us  [per_device(): pl.pallas_call(functools.partial(far_kernel, (row_devices, col_devices, t...]
  transfers between devices with their start and end apart: 17 -> 17, of which waited for: 8 -> 8; matrix products, arithmetic and copies ran while one was open for 0% -> 0% of each run, Pallas kernels for 10% -> 11%
where the time goes in v15:
time: 87.3 us; the launch traced here: 86.9 us
  blocking collectives  28.8 us (33%)
  Pallas kernels  25.1 us (29%)
  starting transfers between devices  21.4 us (25%)
  waiting for transfers between devices  10.9 us (12%)
    all_to_all x3, blocking collectives, exchange(): return lax.all_to_all(copies, axis, 0, 0, tiled=True)  28.8 us
    ppermute x16, starting transfers between devices, send(): return lax.ppermute(x, axis, [(d, d ^ mask) for d in range(size)])  17.6 us
    ppermute x16, waiting for transfers between devices, send(): return lax.ppermute(x, axis, [(d, d ^ mask) for d in range(size)])  10.8 us
    pallas_call x1, Pallas kernels, per_device(): pl.pallas_call(functools.partial(far_kernel, (row_devices, col_devices, t...  8.5 us
    pallas_call x1, Pallas kernels, per_device(): pl.pallas_call(near_kernel, grid=(rows_here // step_rows,), in_specs=[SME...  7.67 us
    pallas_call x3, Pallas kernels, column_step(): pl.pallas_call(functools.partial(column_kernel, copies), in_specs=[VMEM]...  3.95 us
    all_to_all x1, starting transfers between devices, exchange(): return lax.all_to_all(copies, axis, 0, 0, tiled=True)  3.82 us
    pallas_call x2, Pallas kernels, row_step(): pl.pallas_call(functools.partial(row_kernel, row_devices), in_specs=[ANY,...  2.89 us
  transfers between devices with their start and end apart: 17, of which 8 were waited for; matrix products, arithmetic and copies ran while one was open for 0% of the time, Pallas kernels for 11%

profile of v15, /device:TPU:0, one launch (start us, length us, event | category | flops | bytes accessed | tf_op | source)
XLA Modules:
  0.0 86.9 jit_solution(11382184327872256990)
XLA Ops:
  0.6 4.0 %collective-permute-start.2 = (f32[1,1,3,128,128]{4,3,2,1,0:T(8,128)}, f32[1,1,3,128,128]{4,3,2,1,0:T(8,128)S(1)}, u32[]{:S(2)}, u32[]{:S(2)}) collective-permute-start(f32[1,1,3,128,128]{4,3,2,1,0:T(8,128)} %refs_6_.1), channel_id=1, source_target_pairs={{0,12},{4,8},{8,4},{12,0},{16,28},{20,24},{24,20},{28,16},{1,13},{... | collective-permute-start | bytes 589832 | tf_op jit(solution)/shard_map/ppermute | solution.py:67
  4.7 0.4 collective-permute-start.1
  5.3 2.9 %collective-permute-start.3 = (f32[1,1,3,128,128]{4,3,2,1,0:T(8,128)}, f32[1,1,3,128,128]{4,3,2,1,0:T(8,128)S(1)}, u32[]{:S(2)}, u32[]{:S(2)}) collective-permute-start(f32[1,1,3,128,128]{4,3,2,1,0:T(8,128)} %refs_6_.1), channel_id=1, source_target_pairs={{0,16},{4,20},{8,24},{12,28},{16,0},{20,4},{24,8},{28,12},{1,17},{... | collective-permute-start | bytes 589832 | tf_op jit(solution)/shard_map/ppermute | solution.py:67
  8.2 1.5 %pack.1 = (f32[64,128]{1,0:T(8,128)}, s32[3,32]{1,0:T(4,128)S(1)}, s32[2,32]{1,0:T(2,128)S(1)}, s32[3,1,8]{2,1,0:T(1,128)S(1)}, s32[32,128]{1,0:T(8,128)S(1)}) custom-call(s32[32,128]{1,0:T(8,128)} %bitcast.25, s32[1,128]{1,0:T(1,128)} %target_ref.1, s32[3,32]{1,0:T(4,128)} %bitcast.27, s32[2,32]{1,0:T(2,128)} %bitcast.29, s32[3,1,8]{2,1,0:T(1,128)} %bitcast.28, ...), custom_call_target="tpu_custom_call" | custom-call | tf_op jit(solution)/shard_map/pack/pallas_call | solution.py:357
  9.8 3.8 %all-to-all-start = ((f32[32,2,128]{2,1,0:T(2,128)}), f32[32,2,128]{2,1,0:T(2,128)S(1)}, u32[]{:S(2)}, u32[]{:S(2)}) async-start(f32[32,2,128]{2,1,0:T(2,128)} %bitcast.5), calls=%async_computation | async-start | bytes 65536 | tf_op jit(solution)/shard_map/all_to_all | solution.py:75
  13.6 1.3 %collective-permute-done.2.refs_2_ = f32[1,1,3,128,128]{4,3,2,1,0:T(8,128)S(1)} collective-permute-done((f32[1,1,3,128,128]{4,3,2,1,0:T(8,128)}, f32[1,1,3,128,128]{4,3,2,1,0:T(8,128)S(1)}, u32[]{:S(2)}, u32[]{:S(2)}) %collective-permute-start.2) | collective-permute-done | bytes 196640 | tf_op jit(solution)/shard_map/ppermute | solution.py:67
  14.9 3.7 %collective-permute-done.1.refs_1_ = f32[1,1,3,128,128]{4,3,2,1,0:T(8,128)S(1)} collective-permute-done((f32[1,1,3,128,128]{4,3,2,1,0:T(8,128)}, f32[1,1,3,128,128]{4,3,2,1,0:T(8,128)S(1)}, u32[]{:S(2)}, u32[]{:S(2)}) %collective-permute-start.1) | collective-permute-done | bytes 196640 | tf_op jit(solution)/shard_map/ppermute | solution.py:67
  18.6 2.6 %collective-permute-start.6 = (f32[1,1,3,128,128]{4,3,2,1,0:T(8,128)S(1)}, f32[1,1,3,128,128]{4,3,2,1,0:T(8,128)S(1)}, u32[]{:S(2)}, u32[]{:S(2)}) collective-permute-start(f32[1,1,3,128,128]{4,3,2,1,0:T(8,128)S(1)} %get-tuple-element.35.refs_10_), channel_id=1, source_target_pairs={{0,12},{4,8},{8,4},{12,0},{16,28},{20,24},{24,20},{28,16},{1,13},{... | collective-permute-start | bytes 589832 | tf_op jit(solution)/shard_map/ppermute | solution.py:67
  21.3 1.5 %collective-permute-start.4 = (f32[1,1,3,128,128]{4,3,2,1,0:T(8,128)S(1)}, f32[1,1,3,128,128]{4,3,2,1,0:T(8,128)S(1)}, u32[]{:S(2)}, u32[]{:S(2)}) collective-permute-start(f32[1,1,3,128,128]{4,3,2,1,0:T(8,128)S(1)} %get-tuple-element.35.refs_10_), channel_id=1, source_target_pairs={{0,4},{4,0},{8,12},{12,8},{16,20},{20,16},{24,28},{28,24},{1,5},{5... | collective-permute-start | bytes 589832 | tf_op jit(solution)/shard_map/ppermute | solution.py:67
  22.8 7.7 %near_product.1 = (bf16[32,256,768]{2,1,0:T(8,128)(2,1)S(1)}, f32[8,128,4]{2,1,0:T(8,128)S(1)}) custom-call(s32[3,32]{1,0:T(4,128)S(1)} %get-tuple-element.25.near_index_ref.refs_0_, f32[32,3,128,128]{3,2,1,0:T(8,128)} %cost_ref.1, f32[32,1,2,128,128]{4,3,2,1,0:T(8,128)} %plan_ref.1, s32[32,128]{1,0:T(8,128)S(1)} %get-tuple-element.28.mass_ref.refs_5_, ...), custom_call_target="tpu_custom_call" | custom-call | flops 2415919104 | bytes 10485760 | tf_op jit(solution)/shard_map/near_product/pallas_call | solution.py:387
  30.5 8.5 %far_product.1 = (f32[32,1,2,128,128]{4,3,2,1,0:T(8,128)}, f32[32,2,128,128]{3,2,1,0:T(8,128)S(1)}, f32[32,2,128,128]{3,2,1,0:T(8,128)S(1)}, f32[32,128]{1,0:T(8...) custom-call(s32[3,32]{1,0:T(4,128)S(1)} %get-tuple-element.25.near_index_ref.refs_0_, ...), custom_call_target="tpu_custom_call" | custom-call | tf_op jit(solution)/shard_map/far_product/pallas_call | solution.py:416
  39.1 1.5 %collective-permute-start.8 = (f32[32,128]{1,0:T(8,128)S(1)}, f32[32,128]{1,0:T(8,128)S(1)}, u32[]{:S(2)}, u32[]{:S(2)}) collective-permute-start(f32[32,128]{1,0:T(8,128)S(1)} %get-tuple-element.42.refs_0_), channel_id=1, source_target_pairs={{0,2},{1,3},{2,0},{3,1},{4,6},{5,7},{6,4},{7,5},{8,10},{9,11},{10,... | collective-permute-start | bytes 49160 | tf_op jit(solution)/shard_map/ppermute | solution.py:67
  40.7 0.3 collective-permute-start.7
  41.0 1.4 %collective-permute-done.9.refs_3_ = f32[32,128]{1,0:T(8,128)S(1)} collective-permute-done((f32[32,128]{1,0:T(8,128)S(1)}, f32[32,128]{1,0:T(8,128)S(1)}, u32[]{:S(2)}, u32[]{:S(2)}) %collective-permute-start.9) | collective-permute-done | bytes 16416 | tf_op jit(solution)/shard_map/ppermute | solution.py:67
  42.4 0.5 collective-permute-done.8.refs_2_
  42.9 1.3 %column_pass.3 = (f32[64,128]{1,0:T(8,128)S(1)}, f32[32,128]{1,0:T(8,128)}) custom-call(f32[32,2,128,128]{3,2,1,0:T(8,128)S(1)} %get-tuple-element.37.work_ref, s32[64,128]{1,0:T(8,128)S(1)} %get-tuple-element.38.select_ref, f32[32,128]{1,0:T(8,128)S(1)} %get-tuple-element.39.log_mass_ref, f32[32,128]{1,0:T(8,128)S(1)} %get-tuple-element.42.refs_0_, ...), custom_call_target="tpu_custom_call" | custom-call | tf_op jit(solution)/shard_map/column_pass/pallas_call | solution.py:463
  44.2 10.9 %all_to_all.44 = f32[8,8,128]{2,1,0:T(8,128)S(1)} all-to-all(f32[8,8,128]{2,1,0:T(8,128)S(1)} %bitcast.21), channel_id=1, replica_groups=mesh['rows'=8,'cols'=4] {'rows'}, dimensions={0} | all-to-all | bytes 65536 | tf_op jit(solution)/shard_map/all_to_all | solution.py:75
  55.2 1.4 %row_pass.2.refs_0_ = f32[32,128]{1,0:T(8,128)S(1)} custom-call(s32[2,32]{1,0:T(2,128)S(1)} %get-tuple-element.26.refs_1_.slot_any, f32[32,2,128,128]{3,2,1,0:T(8,128)S(1)} %get-tuple-element.40.tall_ref, f32[8,128]{1,0:T(8,128)S(1)} %get-tuple-element.41.log_mass_ref, f32[64,128]{1,0:T(8,128)S(1)} %bitcast.20), custom_call_target="tpu_custom_call" | custom-call | tf_op jit(solution)/shard_map/row_pass/pallas_call | solution.py:481
  56.7 1.6 %collective-permute-start.11 = (f32[32,128]{1,0:T(8,128)S(1)}, f32[32,128]{1,0:T(8,128)S(1)}, u32[]{:S(2)}, u32[]{:S(2)}) collective-permute-start(f32[32,128]{1,0:T(8,128)S(1)} %row_pass.2.refs_0_), channel_id=1, source_target_pairs={{0,2},{1,3},{2,0},{3,1},{4,6},{5,7},{6,4},{7,5},{8,10},{9,11},{10,... | collective-permute-start | bytes 49160 | tf_op jit(solution)/shard_map/ppermute | solution.py:67
  58.3 0.3 collective-permute-start.10
  58.5 1.4 %collective-permute-done.12.refs_3_ = f32[32,128]{1,0:T(8,128)S(1)} collective-permute-done((f32[32,128]{1,0:T(8,128)S(1)}, f32[32,128]{1,0:T(8,128)S(1)}, u32[]{:S(2)}, u32[]{:S(2)}) %collective-permute-start.12) | collective-permute-done | bytes 16416 | tf_op jit(solution)/shard_map/ppermute | solution.py:67
  59.9 0.5 collective-permute-done.11.refs_2_
  60.5 1.3 %column_pass.4 = (f32[64,128]{1,0:T(8,128)S(1)}, f32[32,128]{1,0:T(8,128)}) custom-call(f32[32,2,128,128]{3,2,1,0:T(8,128)S(1)} %get-tuple-element.37.work_ref, s32[64,128]{1,0:T(8,128)S(1)} %get-tuple-element.38.select_ref, f32[32,128]{1,0:T(8,128)S(1)} %get-tuple-element.39.log_mass_ref, f32[32,128]{1,0:T(8,128)S(1)} %row_pass.2.refs_0_, ...), custom_call_target="tpu_custom_call" | custom-call | tf_op jit(solution)/shard_map/column_pass/pallas_call | solution.py:463
  61.8 9.1 %all_to_all.45 = f32[8,8,128]{2,1,0:T(8,128)S(1)} all-to-all(f32[8,8,128]{2,1,0:T(8,128)S(1)} %bitcast.22), channel_id=1, replica_groups=mesh['rows'=8,'cols'=4] {'rows'}, dimensions={0} | all-to-all | bytes 65536 | tf_op jit(solution)/shard_map/all_to_all | solution.py:75
  70.9 1.4 %row_pass.3.refs_0_ = f32[32,128]{1,0:T(8,128)S(1)} custom-call(s32[2,32]{1,0:T(2,128)S(1)} %get-tuple-element.26.refs_1_.slot_any, f32[32,2,128,128]{3,2,1,0:T(8,128)S(1)} %get-tuple-element.40.tall_ref, f32[8,128]{1,0:T(8,128)S(1)} %get-tuple-element.41.log_mass_ref, f32[64,128]{1,0:T(8,128)S(1)} %bitcast.19), custom_call_target="tpu_custom_call" | custom-call | tf_op jit(solution)/shard_map/row_pass/pallas_call | solution.py:481
  72.4 1.6 %collective-permute-start.14 = (f32[32,128]{1,0:T(8,128)S(1)}, f32[32,128]{1,0:T(8,128)S(1)}, u32[]{:S(2)}, u32[]{:S(2)}) collective-permute-start(f32[32,128]{1,0:T(8,128)S(1)} %row_pass.3.refs_0_), channel_id=1, source_target_pairs={{0,2},{1,3},{2,0},{3,1},{4,6},{5,7},{6,4},{7,5},{8,10},{9,11},{10,... | collective-permute-start | bytes 49160 | tf_op jit(solution)/shard_map/ppermute | solution.py:67
  74.0 0.3 collective-permute-start.13
  74.2 1.4 %collective-permute-done.15.refs_3_ = f32[32,128]{1,0:T(8,128)S(1)} collective-permute-done((f32[32,128]{1,0:T(8,128)S(1)}, f32[32,128]{1,0:T(8,128)S(1)}, u32[]{:S(2)}, u32[]{:S(2)}) %collective-permute-start.15) | collective-permute-done | bytes 16416 | tf_op jit(solution)/shard_map/ppermute | solution.py:67
  75.7 0.5 collective-permute-done.14.refs_2_
  76.2 1.3 %column_pass.5 = (f32[8,128]{1,0:T(8,128)S(1)}, f32[32,128]{1,0:T(8,128)}) custom-call(f32[32,2,128,128]{3,2,1,0:T(8,128)S(1)} %get-tuple-element.37.work_ref, s32[64,128]{1,0:T(8,128)S(1)} %get-tuple-element.38.select_ref, f32[32,128]{1,0:T(8,128)S(1)} %get-tuple-element.39.log_mass_ref, f32[32,128]{1,0:T(8,128)S(1)} %row_pass.3.refs_0_, ...), custom_call_target="tpu_custom_call" | custom-call | tf_op jit(solution)/shard_map/column_pass/pallas_call | solution.py:463
  77.5 8.8 %all_to_all.46 = f32[8,1,128]{2,1,0:T(1,128)S(1)} all-to-all(f32[8,1,128]{2,1,0:T(1,128)S(1)} %bitcast.24), channel_id=1, replica_groups=mesh['rows'=8,'cols'=4] {'rows'}, dimensions={0} | all-to-all | bytes 8192 | tf_op jit(solution)/shard_map/all_to_all | solution.py:75
  86.4 0.5 last_potential.1
  (17 shorter events, 0.6 us)
Async XLA Ops:
  0.6 14.2 %collective-permute-start.2 = (f32[1,1,3,128,128]{4,3,2,1,0:T(8,128)}, f32[1,1,3,128,128]{4,3,2,1,0:T(8,128)S(1)}, u32[]{:S(2)}, u32[]{:S(2)}) collective-permute-start(f32[1,1,3,128,128]{4,3,2,1,0:T(8,128)} %refs_6_.1), channel_id=1, source_target_pairs={{0,12},{4,8},{8,4},{12,0},{16,28},{20,24},{24,20},{28,16},{1,13},{... | collective-permute-start | bytes 589832 | tf_op jit(solution)/shard_map/ppermute | solution.py:67
  4.7 13.9 %collective-permute-start.1 = (f32[1,1,3,128,128]{4,3,2,1,0:T(8,128)}, f32[1,1,3,128,128]{4,3,2,1,0:T(8,128)S(1)}, u32[]{:S(2)}, u32[]{:S(2)}) collective-permute-start(f32[1,1,3,128,128]{4,3,2,1,0:T(8,128)} %refs_6_.1), channel_id=1, source_target_pairs={{0,8},{4,12},{8,0},{12,4},{16,24},{20,28},{24,16},{28,20},{1,9},{5... | collective-permute-start | bytes 589832 | tf_op jit(solution)/shard_map/ppermute | solution.py:67
  5.1 13.4 %collective-permute-start = (f32[1,1,3,128,128]{4,3,2,1,0:T(8,128)}, f32[1,1,3,128,128]{4,3,2,1,0:T(8,128)S(1)}, u32[]{:S(2)}, u32[]{:S(2)}) collective-permute-start(f32[1,1,3,128,128]{4,3,2,1,0:T(8,128)} %refs_6_.1), channel_id=1, source_target_pairs={{0,4},{4,0},{8,12},{12,8},{16,20},{20,16},{24,28},{28,24},{1,5},{5... | collective-permute-start | bytes 589832 | tf_op jit(solution)/shard_map/ppermute | solution.py:67
  5.3 13.2 %collective-permute-start.3 = (f32[1,1,3,128,128]{4,3,2,1,0:T(8,128)}, f32[1,1,3,128,128]{4,3,2,1,0:T(8,128)S(1)}, u32[]{:S(2)}, u32[]{:S(2)}) collective-permute-start(f32[1,1,3,128,128]{4,3,2,1,0:T(8,128)} %refs_6_.1), channel_id=1, source_target_pairs={{0,16},{4,20},{8,24},{12,28},{16,0},{20,4},{24,8},{28,12},{1,17},{... | collective-permute-start | bytes 589832 | tf_op jit(solution)/shard_map/ppermute | solution.py:67
  9.8 13.0 %all-to-all-start = ((f32[32,2,128]{2,1,0:T(2,128)}), f32[32,2,128]{2,1,0:T(2,128)S(1)}, u32[]{:S(2)}, u32[]{:S(2)}) async-start(f32[32,2,128]{2,1,0:T(2,128)} %bitcast.5), calls=%async_computation | async-start | bytes 65536 | tf_op jit(solution)/shard_map/all_to_all | solution.py:75
  18.6 11.9 %collective-permute-start.6 = (f32[1,1,3,128,128]{4,3,2,1,0:T(8,128)S(1)}, f32[1,1,3,128,128]{4,3,2,1,0:T(8,128)S(1)}, u32[]{:S(2)}, u32[]{:S(2)}) collective-permute-start(f32[1,1,3,128,128]{4,3,2,1,0:T(8,128)S(1)} %get-tuple-element.35.refs_10_), channel_id=1, source_target_pairs={{0,12},{4,8},{8,4},{12,0},{16,28},{20,24},{24,20},{28,16},{1,13},{... | collective-permute-start | bytes 589832 | tf_op jit(solution)/shard_map/ppermute | solution.py:67
  21.2 9.3 %collective-permute-start.5 = (f32[1,1,3,128,128]{4,3,2,1,0:T(8,128)S(1)}, f32[1,1,3,128,128]{4,3,2,1,0:T(8,128)S(1)}, u32[]{:S(2)}, u32[]{:S(2)}) collective-permute-start(f32[1,1,3,128,128]{4,3,2,1,0:T(8,128)S(1)} %get-tuple-element.35.refs_10_), channel_id=1, source_target_pairs={{0,8},{4,12},{8,0},{12,4},{16,24},{20,28},{24,16},{28,20},{1,9},{5... | collective-permute-start | bytes 589832 | tf_op jit(solution)/shard_map/ppermute | solution.py:67
  21.3 9.2 %collective-permute-start.4 = (f32[1,1,3,128,128]{4,3,2,1,0:T(8,128)S(1)}, f32[1,1,3,128,128]{4,3,2,1,0:T(8,128)S(1)}, u32[]{:S(2)}, u32[]{:S(2)}) collective-permute-start(f32[1,1,3,128,128]{4,3,2,1,0:T(8,128)S(1)} %get-tuple-element.35.refs_10_), channel_id=1, source_target_pairs={{0,4},{4,0},{8,12},{12,8},{16,20},{20,16},{24,28},{28,24},{1,5},{5... | collective-permute-start | bytes 589832 | tf_op jit(solution)/shard_map/ppermute | solution.py:67
  22.8 7.7 %copy-start = (f32[1,1,3,128,128]{4,3,2,1,0:T(8,128)S(1)}, f32[1,1,3,128,128]{4,3,2,1,0:T(8,128)}, u32[]{:S(2)}) copy-start(f32[1,1,3,128,128]{4,3,2,1,0:T(8,128)} %refs_6_.1) | copy-start | bytes 589828
  39.0 3.4 %collective-permute-start.9 = (f32[32,128]{1,0:T(8,128)S(1)}, f32[32,128]{1,0:T(8,128)S(1)}, u32[]{:S(2)}, u32[]{:S(2)}) collective-permute-start(f32[32,128]{1,0:T(8,128)S(1)} %get-tuple-element.42.refs_0_), channel_id=1, source_target_pairs={{0,3},{1,2},{2,1},{3,0},{4,7},{5,6},{6,5},{7,4},{8,11},{9,10},{10,... | collective-permute-start | bytes 49160 | tf_op jit(solution)/shard_map/ppermute | solution.py:67
  39.1 3.8 %collective-permute-start.8 = (f32[32,128]{1,0:T(8,128)S(1)}, f32[32,128]{1,0:T(8,128)S(1)}, u32[]{:S(2)}, u32[]{:S(2)}) collective-permute-start(f32[32,128]{1,0:T(8,128)S(1)} %get-tuple-element.42.refs_0_), channel_id=1, source_target_pairs={{0,2},{1,3},{2,0},{3,1},{4,6},{5,7},{6,4},{7,5},{8,10},{9,11},{10,... | collective-permute-start | bytes 49160 | tf_op jit(solution)/shard_map/ppermute | solution.py:67
  40.7 2.3 %collective-permute-start.7 = (f32[32,128]{1,0:T(8,128)S(1)}, f32[32,128]{1,0:T(8,128)S(1)}, u32[]{:S(2)}, u32[]{:S(2)}) collective-permute-start(f32[32,128]{1,0:T(8,128)S(1)} %get-tuple-element.42.refs_0_), channel_id=1, source_target_pairs={{0,1},{1,0},{2,3},{3,2},{4,5},{5,4},{6,7},{7,6},{8,9},{9,8},{10,11... | collective-permute-start | bytes 49160 | tf_op jit(solution)/shard_map/ppermute | solution.py:67
  56.6 3.3 %collective-permute-start.12 = (f32[32,128]{1,0:T(8,128)S(1)}, f32[32,128]{1,0:T(8,128)S(1)}, u32[]{:S(2)}, u32[]{:S(2)}) collective-permute-start(f32[32,128]{1,0:T(8,128)S(1)} %row_pass.2.refs_0_), channel_id=1, source_target_pairs={{0,3},{1,2},{2,1},{3,0},{4,7},{5,6},{6,5},{7,4},{8,11},{9,10},{10,... | collective-permute-start | bytes 49160 | tf_op jit(solution)/shard_map/ppermute | solution.py:67
  56.7 3.8 %collective-permute-start.11 = (f32[32,128]{1,0:T(8,128)S(1)}, f32[32,128]{1,0:T(8,128)S(1)}, u32[]{:S(2)}, u32[]{:S(2)}) collective-permute-start(f32[32,128]{1,0:T(8,128)S(1)} %row_pass.2.refs_0_), channel_id=1, source_target_pairs={{0,2},{1,3},{2,0},{3,1},{4,6},{5,7},{6,4},{7,5},{8,10},{9,11},{10,... | collective-permute-start | bytes 49160 | tf_op jit(solution)/shard_map/ppermute | solution.py:67
  58.3 2.2 %collective-permute-start.10 = (f32[32,128]{1,0:T(8,128)S(1)}, f32[32,128]{1,0:T(8,128)S(1)}, u32[]{:S(2)}, u32[]{:S(2)}) collective-permute-start(f32[32,128]{1,0:T(8,128)S(1)} %row_pass.2.refs_0_), channel_id=1, source_target_pairs={{0,1},{1,0},{2,3},{3,2},{4,5},{5,4},{6,7},{7,6},{8,9},{9,8},{10,11... | collective-permute-start | bytes 49160 | tf_op jit(solution)/shard_map/ppermute | solution.py:67
  72.3 3.3 %collective-permute-start.15 = (f32[32,128]{1,0:T(8,128)S(1)}, f32[32,128]{1,0:T(8,128)S(1)}, u32[]{:S(2)}, u32[]{:S(2)}) collective-permute-start(f32[32,128]{1,0:T(8,128)S(1)} %row_pass.3.refs_0_), channel_id=1, source_target_pairs={{0,3},{1,2},{2,1},{3,0},{4,7},{5,6},{6,5},{7,4},{8,11},{9,10},{10,... | collective-permute-start | bytes 49160 | tf_op jit(solution)/shard_map/ppermute | solution.py:67
  72.4 3.8 %collective-permute-start.14 = (f32[32,128]{1,0:T(8,128)S(1)}, f32[32,128]{1,0:T(8,128)S(1)}, u32[]{:S(2)}, u32[]{:S(2)}) collective-permute-start(f32[32,128]{1,0:T(8,128)S(1)} %row_pass.3.refs_0_), channel_id=1, source_target_pairs={{0,2},{1,3},{2,0},{3,1},{4,6},{5,7},{6,4},{7,5},{8,10},{9,11},{10,... | collective-permute-start | bytes 49160 | tf_op jit(solution)/shard_map/ppermute | solution.py:67
  74.0 2.2 %collective-permute-start.13 = (f32[32,128]{1,0:T(8,128)S(1)}, f32[32,128]{1,0:T(8,128)S(1)}, u32[]{:S(2)}, u32[]{:S(2)}) collective-permute-start(f32[32,128]{1,0:T(8,128)S(1)} %row_pass.3.refs_0_), channel_id=1, source_target_pairs={{0,1},{1,0},{2,3},{3,2},{4,5},{5,4},{6,7},{7,6},{8,9},{9,8},{10,11... | collective-permute-start | bytes 49160 | tf_op jit(solution)/shard_map/ppermute | solution.py:67

commit v16 on v15

--- a/solution.py
+++ b/solution.py
@@ -88,7 +88,11 @@
         to_ref[...] = from_ref[...]
 
 
-def near_kernel(near_index_ref, cost_ref, plan_ref, mass_ref, totals_ref, x_ref, term_ref, plan_scr):
+def near_kernel(
+    near_any, cost_ref, plan_ref, mass_ref, totals_ref, x_ref, term_ref, plan_scr, near_index_ref, sem
+):
+    index_copy = pltpu.make_async_copy(near_any, near_index_ref, sem)
+    pl.when(pl.program_id(0) == 0)(index_copy.start)
     rows = cost_ref.shape[0]
     first = pl.program_id(0) * rows
     near_count = cost_ref.shape[1]
@@ -101,6 +105,7 @@
         plan_scr[a, 0:width, :] = high
         plan_scr[a, width : 2 * width, :] = low
         plan_scr[a, 2 * width : 3 * width, :] = high
+    pl.when(pl.program_id(0) == 0)(index_copy.wait)
     lanes = lax.broadcasted_iota(jnp.int32, (width, SUB), 1)
     for group in range(rows // SUB):
         terms = jnp.zeros((width, SUB), jnp.float32)
@@ -130,12 +135,13 @@
 
 def far_kernel(counts, row_axis, col_axis, *refs):
     row_devices, col_devices, target_here, source_count, target_count, group_blocks, link_count = counts
-    near_index_ref, slot_ref, link_ref, x_ref, term_ref, mass_ref = refs[:6]
+    tables, (x_ref, term_ref, mass_ref) = refs[:3], refs[3:6]
     cost_parts = refs[6 : 6 + row_devices]
     pack_ref, out_ref, work_ref, tall_ref, part_ref, log_source_ref, log_target_ref, select_ref = refs[
         6 + row_devices : 14 + row_devices
     ]
-    far_high, far_low, table, column_scr, scale_scr, peak_scr, sum_scr, cost_scr, sems = refs[14 + row_devices :]
+    far_high, far_low, table, column_scr, scale_scr, peak_scr, sum_scr, cost_scr, sems = refs[14 + row_devices : -4]
+    near_index_ref, slot_ref, link_ref, table_sems = refs[-4:]
     g = pl.program_id(0)
     near_count = near_index_ref.shape[0]
     slots = slot_ref.shape[0]
@@ -146,6 +152,12 @@
 
     @pl.when(g == 0)
     def _():
+        table_copies = [
+            pltpu.make_async_copy(table_any, table_ref, table_sems.at[e])
+            for e, (table_any, table_ref) in enumerate(zip(tables, (near_index_ref, slot_ref, link_ref)))
+        ]
+        for copy in table_copies:
+            copy.start()
         me = lax.axis_index(row_axis)
         col = lax.axis_index(col_axis)
         far_high[zero_block] = jnp.zeros((width, width), jnp.bfloat16)
@@ -157,12 +169,6 @@
 
         lax.fori_loop(0, group_blocks * group_blocks, clear, 0)
 
-        def mark(j, _):
-            for m in range(link_count):
-                table[j * group_blocks + link_ref[m, 0, j]] = j * link_count + m
-            return 0
-
-        lax.fori_loop(0, group_blocks, mark, 0)
         pack_rows = pack_ref.shape[0] // (row_devices * col_devices)
         total_source = functools.reduce(
             jnp.add,
@@ -180,6 +186,15 @@
         log_source_ref[...] = jnp.log2(source_count * mass_ref[...].astype(jnp.float32) / total_source)
         scale_scr[...] = source_count / (total_source * (near_count * width))
         column_scr[...] = jnp.zeros_like(column_scr)
+        for copy in table_copies:
+            copy.wait()
+
+        def mark(j, _):
+            for m in range(link_count):
+                table[j * group_blocks + link_ref[m, 0, j]] = j * link_count + m
+            return 0
+
+        lax.fori_loop(0, group_blocks, mark, 0)
         for s in range(row_devices):
             for h in range(target_here):
                 j = (me ^ s) * target_here + h
@@ -388,7 +403,7 @@
         near_kernel,
         grid=(rows_here // step_rows,),
         in_specs=[
-            SMEM,
+            ANY,
             pl.BlockSpec((step_rows, near_count, width, width), lambda g: (g, 0, 0, 0)),
             pl.BlockSpec((step_rows, 1, slots, width, width), lambda g: (g, 0, 0, 0, 0)),
             whole((rows_here, width)),
@@ -399,7 +414,11 @@
             pltpu.VMEM((rows_here, 2 * width, wide), jnp.bfloat16),
             pltpu.VMEM((groups, width, SUB), f32),
         ],
-        scratch_shapes=[pltpu.VMEM((step_rows, 3 * width, slots * width), jnp.bfloat16)],
+        scratch_shapes=[
+            pltpu.VMEM((step_rows, 3 * width, slots * width), jnp.bfloat16),
+            pltpu.SMEM(near_t.shape, jnp.int32),
+            pltpu.SemaphoreType.DMA,
+        ],
         compiler_params=pltpu.CompilerParams(vmem_limit_bytes=12 * mib),
         cost_estimate=pl.CostEstimate(
             flops=6 * rows_here * wide * width * width,
@@ -421,7 +440,7 @@
             "cols",
         ),
         grid=(steps,),
-        in_specs=[SMEM, SMEM, SMEM, VMEM, VMEM, whole((rows_here, width))]
+        in_specs=[ANY, ANY, ANY, VMEM, VMEM, whole((rows_here, width))]
         + [VMEM] * row_devices
         + [whole(packs.shape)],
         out_specs=[
@@ -452,6 +471,10 @@
             pltpu.VMEM((slots * rows_here, width), f32),
             pltpu.VMEM(coupling.shape, f32),
             pltpu.SemaphoreType.DMA((rows_here,)),
+            pltpu.SMEM(near_t.shape, jnp.int32),
+            pltpu.SMEM(slot_t.shape, jnp.int32),
+            pltpu.SMEM(link_t.shape, jnp.int32),
+            pltpu.SemaphoreType.DMA((3,)),
         ],
         compiler_params=pltpu.CompilerParams(vmem_limit_bytes=12 * mib + 2 * far_bytes),
         name="far_product",

time: 87.3 us -> 86.8 us (level)
  no operation moved by 1% of the time
where the time goes in v16:
time: 86.8 us; the launch traced here: 86.4 us
  blocking collectives  28.8 us (33%)
  Pallas kernels  24.6 us (28%)
  starting transfers between devices  21.4 us (25%)
  waiting for transfers between devices  10.9 us (13%)
    all_to_all x3, blocking collectives, exchange(): return lax.all_to_all(copies, axis, 0, 0, tiled=True)  28.8 us
    ppermute x16, starting transfers between devices, send(): return lax.ppermute(x, axis, [(d, d ^ mask) for d in range(size)])  17.6 us
    ppermute x16, waiting for transfers between devices, send(): return lax.ppermute(x, axis, [(d, d ^ mask) for d in range(size)])  10.8 us
    pallas_call x1, Pallas kernels, per_device(): pl.pallas_call(functools.partial(far_kernel, (row_devices, col_devices, t...  8 us
    pallas_call x1, Pallas kernels, per_device(): pl.pallas_call(near_kernel, grid=(rows_here // step_rows,), in_specs=[ANY...  7.69 us
    pallas_call x3, Pallas kernels, column_step(): pl.pallas_call(functools.partial(column_kernel, copies), in_specs=[VMEM]...  3.95 us
    all_to_all x1, starting transfers between devices, exchange(): return lax.all_to_all(copies, axis, 0, 0, tiled=True)  3.82 us
    pallas_call x2, Pallas kernels, row_step(): pl.pallas_call(functools.partial(row_kernel, row_devices), in_specs=[ANY,...  2.89 us
  transfers between devices with their start and end apart: 17, of which 8 were waited for; matrix products, arithmetic and copies ran while one was open for 0% of the time, Pallas kernels for 11%

profile of v16, /device:TPU:0, one launch (start us, length us, event | category | flops | bytes accessed | tf_op | source)
XLA Modules:
  0.0 86.4 jit_solution(598849910628272517)
XLA Ops:
  0.6 4.0 %collective-permute-start.2 = (f32[1,1,3,128,128]{4,3,2,1,0:T(8,128)}, f32[1,1,3,128,128]{4,3,2,1,0:T(8,128)S(1)}, u32[]{:S(2)}, u32[]{:S(2)}) collective-permute-start(f32[1,1,3,128,128]{4,3,2,1,0:T(8,128)} %refs_6_.1), channel_id=1, source_target_pairs={{0,12},{4,8},{8,4},{12,0},{16,28},{20,24},{24,20},{28,16},{1,13},{... | collective-permute-start | bytes 589832 | tf_op jit(solution)/shard_map/ppermute | solution.py:67
  4.7 0.4 collective-permute-start.1
  5.3 2.9 %collective-permute-start.3 = (f32[1,1,3,128,128]{4,3,2,1,0:T(8,128)}, f32[1,1,3,128,128]{4,3,2,1,0:T(8,128)S(1)}, u32[]{:S(2)}, u32[]{:S(2)}) collective-permute-start(f32[1,1,3,128,128]{4,3,2,1,0:T(8,128)} %refs_6_.1), channel_id=1, source_target_pairs={{0,16},{4,20},{8,24},{12,28},{16,0},{20,4},{24,8},{28,12},{1,17},{... | collective-permute-start | bytes 589832 | tf_op jit(solution)/shard_map/ppermute | solution.py:67
  8.2 1.5 %pack.1 = (f32[64,128]{1,0:T(8,128)}, s32[3,32]{1,0:T(4,128)S(1)}, s32[2,32]{1,0:T(2,128)S(1)}, s32[3,1,8]{2,1,0:T(1,128)S(1)}, s32[32,128]{1,0:T(8,128)S(1)}) custom-call(s32[32,128]{1,0:T(8,128)} %bitcast.25, s32[1,128]{1,0:T(1,128)} %target_ref.1, s32[3,32]{1,0:T(4,128)} %bitcast.27, s32[2,32]{1,0:T(2,128)} %bitcast.29, s32[3,1,8]{2,1,0:T(1,128)} %bitcast.28, ...), custom_call_target="tpu_custom_call" | custom-call | tf_op jit(solution)/shard_map/pack/pallas_call | solution.py:372
  9.8 3.8 %all-to-all-start = ((f32[32,2,128]{2,1,0:T(2,128)}), f32[32,2,128]{2,1,0:T(2,128)S(1)}, u32[]{:S(2)}, u32[]{:S(2)}) async-start(f32[32,2,128]{2,1,0:T(2,128)} %bitcast.5), calls=%async_computation | async-start | bytes 65536 | tf_op jit(solution)/shard_map/all_to_all | solution.py:75
  13.6 1.3 %collective-permute-done.2.refs_2_ = f32[1,1,3,128,128]{4,3,2,1,0:T(8,128)S(1)} collective-permute-done((f32[1,1,3,128,128]{4,3,2,1,0:T(8,128)}, f32[1,1,3,128,128]{4,3,2,1,0:T(8,128)S(1)}, u32[]{:S(2)}, u32[]{:S(2)}) %collective-permute-start.2) | collective-permute-done | bytes 196640 | tf_op jit(solution)/shard_map/ppermute | solution.py:67
  14.9 3.7 %collective-permute-done.1.refs_1_ = f32[1,1,3,128,128]{4,3,2,1,0:T(8,128)S(1)} collective-permute-done((f32[1,1,3,128,128]{4,3,2,1,0:T(8,128)}, f32[1,1,3,128,128]{4,3,2,1,0:T(8,128)S(1)}, u32[]{:S(2)}, u32[]{:S(2)}) %collective-permute-start.1) | collective-permute-done | bytes 196640 | tf_op jit(solution)/shard_map/ppermute | solution.py:67
  18.6 2.6 %collective-permute-start.6 = (f32[1,1,3,128,128]{4,3,2,1,0:T(8,128)S(1)}, f32[1,1,3,128,128]{4,3,2,1,0:T(8,128)S(1)}, u32[]{:S(2)}, u32[]{:S(2)}) collective-permute-start(f32[1,1,3,128,128]{4,3,2,1,0:T(8,128)S(1)} %get-tuple-element.35.refs_10_), channel_id=1, source_target_pairs={{0,12},{4,8},{8,4},{12,0},{16,28},{20,24},{24,20},{28,16},{1,13},{... | collective-permute-start | bytes 589832 | tf_op jit(solution)/shard_map/ppermute | solution.py:67
  21.3 1.5 %collective-permute-start.4 = (f32[1,1,3,128,128]{4,3,2,1,0:T(8,128)S(1)}, f32[1,1,3,128,128]{4,3,2,1,0:T(8,128)S(1)}, u32[]{:S(2)}, u32[]{:S(2)}) collective-permute-start(f32[1,1,3,128,128]{4,3,2,1,0:T(8,128)S(1)} %get-tuple-element.35.refs_10_), channel_id=1, source_target_pairs={{0,4},{4,0},{8,12},{12,8},{16,20},{20,16},{24,28},{28,24},{1,5},{5... | collective-permute-start | bytes 589832 | tf_op jit(solution)/shard_map/ppermute | solution.py:67
  22.8 7.7 %near_product.1 = (bf16[32,256,768]{2,1,0:T(8,128)(2,1)S(1)}, f32[8,128,4]{2,1,0:T(8,128)S(1)}) custom-call(s32[3,32]{1,0:T(4,128)S(1)} %get-tuple-element.25.near_any.refs_0_, f32[32,3,128,128]{3,2,1,0:T(8,128)} %cost_ref.1, f32[32,1,2,128,128]{4,3,2,1,0:T(8,128)} %plan_ref.1, s32[32,128]{1,0:T(8,128)S(1)} %get-tuple-element.28.mass_ref.refs_5_, ...), custom_call_target="tpu_custom_call" | custom-call | flops 2415919104 | bytes 10485760 | tf_op jit(solution)/shard_map/near_product/pallas_call | solution.py:402
  30.5 8.0 %far_product.1 = (f32[32,1,2,128,128]{4,3,2,1,0:T(8,128)}, f32[32,2,128,128]{3,2,1,0:T(8,128)S(1)}, f32[32,2,128,128]{3,2,1,0:T(8,128)S(1)}, f32[32,128]{1,0:T(8...) custom-call(s32[3,32]{1,0:T(4,128)S(1)} %get-tuple-element.25.near_any.refs_0_, ...), custom_call_target="tpu_custom_call" | custom-call | tf_op jit(solution)/shard_map/far_product/pallas_call | solution.py:435
  38.6 1.5 %collective-permute-start.8 = (f32[32,128]{1,0:T(8,128)S(1)}, f32[32,128]{1,0:T(8,128)S(1)}, u32[]{:S(2)}, u32[]{:S(2)}) collective-permute-start(f32[32,128]{1,0:T(8,128)S(1)} %get-tuple-element.42.refs_0_), channel_id=1, source_target_pairs={{0,2},{1,3},{2,0},{3,1},{4,6},{5,7},{6,4},{7,5},{8,10},{9,11},{10,... | collective-permute-start | bytes 49160 | tf_op jit(solution)/shard_map/ppermute | solution.py:67
  40.2 0.3 collective-permute-start.7
  40.5 1.4 %collective-permute-done.9.refs_3_ = f32[32,128]{1,0:T(8,128)S(1)} collective-permute-done((f32[32,128]{1,0:T(8,128)S(1)}, f32[32,128]{1,0:T(8,128)S(1)}, u32[]{:S(2)}, u32[]{:S(2)}) %collective-permute-start.9) | collective-permute-done | bytes 16416 | tf_op jit(solution)/shard_map/ppermute | solution.py:67
  41.9 0.5 collective-permute-done.8.refs_2_
  42.4 1.3 %column_pass.3 = (f32[64,128]{1,0:T(8,128)S(1)}, f32[32,128]{1,0:T(8,128)}) custom-call(f32[32,2,128,128]{3,2,1,0:T(8,128)S(1)} %get-tuple-element.37.work_ref, s32[64,128]{1,0:T(8,128)S(1)} %get-tuple-element.38.select_ref, f32[32,128]{1,0:T(8,128)S(1)} %get-tuple-element.39.log_mass_ref, f32[32,128]{1,0:T(8,128)S(1)} %get-tuple-element.42.refs_0_, ...), custom_call_target="tpu_custom_call" | custom-call | tf_op jit(solution)/shard_map/column_pass/pallas_call | solution.py:486
  43.8 10.9 %all_to_all.44 = f32[8,8,128]{2,1,0:T(8,128)S(1)} all-to-all(f32[8,8,128]{2,1,0:T(8,128)S(1)} %bitcast.21), channel_id=1, replica_groups=mesh['rows'=8,'cols'=4] {'rows'}, dimensions={0} | all-to-all | bytes 65536 | tf_op jit(solution)/shard_map/all_to_all | solution.py:75
  54.7 1.4 %row_pass.2.refs_0_ = f32[32,128]{1,0:T(8,128)S(1)} custom-call(s32[2,32]{1,0:T(2,128)S(1)} %get-tuple-element.26.refs_1_.slot_any, f32[32,2,128,128]{3,2,1,0:T(8,128)S(1)} %get-tuple-element.40.tall_ref, f32[8,128]{1,0:T(8,128)S(1)} %get-tuple-element.41.log_mass_ref, f32[64,128]{1,0:T(8,128)S(1)} %bitcast.20), custom_call_target="tpu_custom_call" | custom-call | tf_op jit(solution)/shard_map/row_pass/pallas_call | solution.py:504
  56.2 1.6 %collective-permute-start.11 = (f32[32,128]{1,0:T(8,128)S(1)}, f32[32,128]{1,0:T(8,128)S(1)}, u32[]{:S(2)}, u32[]{:S(2)}) collective-permute-start(f32[32,128]{1,0:T(8,128)S(1)} %row_pass.2.refs_0_), channel_id=1, source_target_pairs={{0,2},{1,3},{2,0},{3,1},{4,6},{5,7},{6,4},{7,5},{8,10},{9,11},{10,... | collective-permute-start | bytes 49160 | tf_op jit(solution)/shard_map/ppermute | solution.py:67
  57.8 0.3 collective-permute-start.10
  58.1 1.4 %collective-permute-done.12.refs_3_ = f32[32,128]{1,0:T(8,128)S(1)} collective-permute-done((f32[32,128]{1,0:T(8,128)S(1)}, f32[32,128]{1,0:T(8,128)S(1)}, u32[]{:S(2)}, u32[]{:S(2)}) %collective-permute-start.12) | collective-permute-done | bytes 16416 | tf_op jit(solution)/shard_map/ppermute | solution.py:67
  59.5 0.5 collective-permute-done.11.refs_2_
  60.0 1.3 %column_pass.4 = (f32[64,128]{1,0:T(8,128)S(1)}, f32[32,128]{1,0:T(8,128)}) custom-call(f32[32,2,128,128]{3,2,1,0:T(8,128)S(1)} %get-tuple-element.37.work_ref, s32[64,128]{1,0:T(8,128)S(1)} %get-tuple-element.38.select_ref, f32[32,128]{1,0:T(8,128)S(1)} %get-tuple-element.39.log_mass_ref, f32[32,128]{1,0:T(8,128)S(1)} %row_pass.2.refs_0_, ...), custom_call_target="tpu_custom_call" | custom-call | tf_op jit(solution)/shard_map/column_pass/pallas_call | solution.py:486
  61.3 9.1 %all_to_all.45 = f32[8,8,128]{2,1,0:T(8,128)S(1)} all-to-all(f32[8,8,128]{2,1,0:T(8,128)S(1)} %bitcast.22), channel_id=1, replica_groups=mesh['rows'=8,'cols'=4] {'rows'}, dimensions={0} | all-to-all | bytes 65536 | tf_op jit(solution)/shard_map/all_to_all | solution.py:75
  70.4 1.4 %row_pass.3.refs_0_ = f32[32,128]{1,0:T(8,128)S(1)} custom-call(s32[2,32]{1,0:T(2,128)S(1)} %get-tuple-element.26.refs_1_.slot_any, f32[32,2,128,128]{3,2,1,0:T(8,128)S(1)} %get-tuple-element.40.tall_ref, f32[8,128]{1,0:T(8,128)S(1)} %get-tuple-element.41.log_mass_ref, f32[64,128]{1,0:T(8,128)S(1)} %bitcast.19), custom_call_target="tpu_custom_call" | custom-call | tf_op jit(solution)/shard_map/row_pass/pallas_call | solution.py:504
  71.9 1.6 %collective-permute-start.14 = (f32[32,128]{1,0:T(8,128)S(1)}, f32[32,128]{1,0:T(8,128)S(1)}, u32[]{:S(2)}, u32[]{:S(2)}) collective-permute-start(f32[32,128]{1,0:T(8,128)S(1)} %row_pass.3.refs_0_), channel_id=1, source_target_pairs={{0,2},{1,3},{2,0},{3,1},{4,6},{5,7},{6,4},{7,5},{8,10},{9,11},{10,... | collective-permute-start | bytes 49160 | tf_op jit(solution)/shard_map/ppermute | solution.py:67
  73.5 0.3 collective-permute-start.13
  73.8 1.4 %collective-permute-done.15.refs_3_ = f32[32,128]{1,0:T(8,128)S(1)} collective-permute-done((f32[32,128]{1,0:T(8,128)S(1)}, f32[32,128]{1,0:T(8,128)S(1)}, u32[]{:S(2)}, u32[]{:S(2)}) %collective-permute-start.15) | collective-permute-done | bytes 16416 | tf_op jit(solution)/shard_map/ppermute | solution.py:67
  75.2 0.5 collective-permute-done.14.refs_2_
  75.7 1.3 %column_pass.5 = (f32[8,128]{1,0:T(8,128)S(1)}, f32[32,128]{1,0:T(8,128)}) custom-call(f32[32,2,128,128]{3,2,1,0:T(8,128)S(1)} %get-tuple-element.37.work_ref, s32[64,128]{1,0:T(8,128)S(1)} %get-tuple-element.38.select_ref, f32[32,128]{1,0:T(8,128)S(1)} %get-tuple-element.39.log_mass_ref, f32[32,128]{1,0:T(8,128)S(1)} %row_pass.3.refs_0_, ...), custom_call_target="tpu_custom_call" | custom-call | tf_op jit(solution)/shard_map/column_pass/pallas_call | solution.py:486
  77.1 8.8 %all_to_all.46 = f32[8,1,128]{2,1,0:T(1,128)S(1)} all-to-all(f32[8,1,128]{2,1,0:T(1,128)S(1)} %bitcast.24), channel_id=1, replica_groups=mesh['rows'=8,'cols'=4] {'rows'}, dimensions={0} | all-to-all | bytes 8192 | tf_op jit(solution)/shard_map/all_to_all | solution.py:75
  85.9 0.5 last_potential.1
  (17 shorter events, 0.6 us)
Async XLA Ops:
  0.6 14.2 %collective-permute-start.2 = (f32[1,1,3,128,128]{4,3,2,1,0:T(8,128)}, f32[1,1,3,128,128]{4,3,2,1,0:T(8,128)S(1)}, u32[]{:S(2)}, u32[]{:S(2)}) collective-permute-start(f32[1,1,3,128,128]{4,3,2,1,0:T(8,128)} %refs_6_.1), channel_id=1, source_target_pairs={{0,12},{4,8},{8,4},{12,0},{16,28},{20,24},{24,20},{28,16},{1,13},{... | collective-permute-start | bytes 589832 | tf_op jit(solution)/shard_map/ppermute | solution.py:67
  4.7 13.9 %collective-permute-start.1 = (f32[1,1,3,128,128]{4,3,2,1,0:T(8,128)}, f32[1,1,3,128,128]{4,3,2,1,0:T(8,128)S(1)}, u32[]{:S(2)}, u32[]{:S(2)}) collective-permute-start(f32[1,1,3,128,128]{4,3,2,1,0:T(8,128)} %refs_6_.1), channel_id=1, source_target_pairs={{0,8},{4,12},{8,0},{12,4},{16,24},{20,28},{24,16},{28,20},{1,9},{5... | collective-permute-start | bytes 589832 | tf_op jit(solution)/shard_map/ppermute | solution.py:67
  5.1 13.4 %collective-permute-start = (f32[1,1,3,128,128]{4,3,2,1,0:T(8,128)}, f32[1,1,3,128,128]{4,3,2,1,0:T(8,128)S(1)}, u32[]{:S(2)}, u32[]{:S(2)}) collective-permute-start(f32[1,1,3,128,128]{4,3,2,1,0:T(8,128)} %refs_6_.1), channel_id=1, source_target_pairs={{0,4},{4,0},{8,12},{12,8},{16,20},{20,16},{24,28},{28,24},{1,5},{5... | collective-permute-start | bytes 589832 | tf_op jit(solution)/shard_map/ppermute | solution.py:67
  5.3 13.2 %collective-permute-start.3 = (f32[1,1,3,128,128]{4,3,2,1,0:T(8,128)}, f32[1,1,3,128,128]{4,3,2,1,0:T(8,128)S(1)}, u32[]{:S(2)}, u32[]{:S(2)}) collective-permute-start(f32[1,1,3,128,128]{4,3,2,1,0:T(8,128)} %refs_6_.1), channel_id=1, source_target_pairs={{0,16},{4,20},{8,24},{12,28},{16,0},{20,4},{24,8},{28,12},{1,17},{... | collective-permute-start | bytes 589832 | tf_op jit(solution)/shard_map/ppermute | solution.py:67
  9.8 13.0 %all-to-all-start = ((f32[32,2,128]{2,1,0:T(2,128)}), f32[32,2,128]{2,1,0:T(2,128)S(1)}, u32[]{:S(2)}, u32[]{:S(2)}) async-start(f32[32,2,128]{2,1,0:T(2,128)} %bitcast.5), calls=%async_computation | async-start | bytes 65536 | tf_op jit(solution)/shard_map/all_to_all | solution.py:75
  18.6 11.9 %collective-permute-start.6 = (f32[1,1,3,128,128]{4,3,2,1,0:T(8,128)S(1)}, f32[1,1,3,128,128]{4,3,2,1,0:T(8,128)S(1)}, u32[]{:S(2)}, u32[]{:S(2)}) collective-permute-start(f32[1,1,3,128,128]{4,3,2,1,0:T(8,128)S(1)} %get-tuple-element.35.refs_10_), channel_id=1, source_target_pairs={{0,12},{4,8},{8,4},{12,0},{16,28},{20,24},{24,20},{28,16},{1,13},{... | collective-permute-start | bytes 589832 | tf_op jit(solution)/shard_map/ppermute | solution.py:67
  21.2 9.3 %collective-permute-start.5 = (f32[1,1,3,128,128]{4,3,2,1,0:T(8,128)S(1)}, f32[1,1,3,128,128]{4,3,2,1,0:T(8,128)S(1)}, u32[]{:S(2)}, u32[]{:S(2)}) collective-permute-start(f32[1,1,3,128,128]{4,3,2,1,0:T(8,128)S(1)} %get-tuple-element.35.refs_10_), channel_id=1, source_target_pairs={{0,8},{4,12},{8,0},{12,4},{16,24},{20,28},{24,16},{28,20},{1,9},{5... | collective-permute-start | bytes 589832 | tf_op jit(solution)/shard_map/ppermute | solution.py:67
  21.3 9.2 %collective-permute-start.4 = (f32[1,1,3,128,128]{4,3,2,1,0:T(8,128)S(1)}, f32[1,1,3,128,128]{4,3,2,1,0:T(8,128)S(1)}, u32[]{:S(2)}, u32[]{:S(2)}) collective-permute-start(f32[1,1,3,128,128]{4,3,2,1,0:T(8,128)S(1)} %get-tuple-element.35.refs_10_), channel_id=1, source_target_pairs={{0,4},{4,0},{8,12},{12,8},{16,20},{20,16},{24,28},{28,24},{1,5},{5... | collective-permute-start | bytes 589832 | tf_op jit(solution)/shard_map/ppermute | solution.py:67
  22.8 7.7 %copy-start = (f32[1,1,3,128,128]{4,3,2,1,0:T(8,128)S(1)}, f32[1,1,3,128,128]{4,3,2,1,0:T(8,128)}, u32[]{:S(2)}) copy-start(f32[1,1,3,128,128]{4,3,2,1,0:T(8,128)} %refs_6_.1) | copy-start | bytes 589828
  38.6 3.4 %collective-permute-start.9 = (f32[32,128]{1,0:T(8,128)S(1)}, f32[32,128]{1,0:T(8,128)S(1)}, u32[]{:S(2)}, u32[]{:S(2)}) collective-permute-start(f32[32,128]{1,0:T(8,128)S(1)} %get-tuple-element.42.refs_0_), channel_id=1, source_target_pairs={{0,3},{1,2},{2,1},{3,0},{4,7},{5,6},{6,5},{7,4},{8,11},{9,10},{10,... | collective-permute-start | bytes 49160 | tf_op jit(solution)/shard_map/ppermute | solution.py:67
  38.6 3.8 %collective-permute-start.8 = (f32[32,128]{1,0:T(8,128)S(1)}, f32[32,128]{1,0:T(8,128)S(1)}, u32[]{:S(2)}, u32[]{:S(2)}) collective-permute-start(f32[32,128]{1,0:T(8,128)S(1)} %get-tuple-element.42.refs_0_), channel_id=1, source_target_pairs={{0,2},{1,3},{2,0},{3,1},{4,6},{5,7},{6,4},{7,5},{8,10},{9,11},{10,... | collective-permute-start | bytes 49160 | tf_op jit(solution)/shard_map/ppermute | solution.py:67
  40.2 2.3 %collective-permute-start.7 = (f32[32,128]{1,0:T(8,128)S(1)}, f32[32,128]{1,0:T(8,128)S(1)}, u32[]{:S(2)}, u32[]{:S(2)}) collective-permute-start(f32[32,128]{1,0:T(8,128)S(1)} %get-tuple-element.42.refs_0_), channel_id=1, source_target_pairs={{0,1},{1,0},{2,3},{3,2},{4,5},{5,4},{6,7},{7,6},{8,9},{9,8},{10,11... | collective-permute-start | bytes 49160 | tf_op jit(solution)/shard_map/ppermute | solution.py:67
  56.1 3.3 %collective-permute-start.12 = (f32[32,128]{1,0:T(8,128)S(1)}, f32[32,128]{1,0:T(8,128)S(1)}, u32[]{:S(2)}, u32[]{:S(2)}) collective-permute-start(f32[32,128]{1,0:T(8,128)S(1)} %row_pass.2.refs_0_), channel_id=1, source_target_pairs={{0,3},{1,2},{2,1},{3,0},{4,7},{5,6},{6,5},{7,4},{8,11},{9,10},{10,... | collective-permute-start | bytes 49160 | tf_op jit(solution)/shard_map/ppermute | solution.py:67
  56.2 3.8 %collective-permute-start.11 = (f32[32,128]{1,0:T(8,128)S(1)}, f32[32,128]{1,0:T(8,128)S(1)}, u32[]{:S(2)}, u32[]{:S(2)}) collective-permute-start(f32[32,128]{1,0:T(8,128)S(1)} %row_pass.2.refs_0_), channel_id=1, source_target_pairs={{0,2},{1,3},{2,0},{3,1},{4,6},{5,7},{6,4},{7,5},{8,10},{9,11},{10,... | collective-permute-start | bytes 49160 | tf_op jit(solution)/shard_map/ppermute | solution.py:67
  57.8 2.2 %collective-permute-start.10 = (f32[32,128]{1,0:T(8,128)S(1)}, f32[32,128]{1,0:T(8,128)S(1)}, u32[]{:S(2)}, u32[]{:S(2)}) collective-permute-start(f32[32,128]{1,0:T(8,128)S(1)} %row_pass.2.refs_0_), channel_id=1, source_target_pairs={{0,1},{1,0},{2,3},{3,2},{4,5},{5,4},{6,7},{7,6},{8,9},{9,8},{10,11... | collective-permute-start | bytes 49160 | tf_op jit(solution)/shard_map/ppermute | solution.py:67
  71.8 3.3 %collective-permute-start.15 = (f32[32,128]{1,0:T(8,128)S(1)}, f32[32,128]{1,0:T(8,128)S(1)}, u32[]{:S(2)}, u32[]{:S(2)}) collective-permute-start(f32[32,128]{1,0:T(8,128)S(1)} %row_pass.3.refs_0_), channel_id=1, source_target_pairs={{0,3},{1,2},{2,1},{3,0},{4,7},{5,6},{6,5},{7,4},{8,11},{9,10},{10,... | collective-permute-start | bytes 49160 | tf_op jit(solution)/shard_map/ppermute | solution.py:67
  71.9 3.8 %collective-permute-start.14 = (f32[32,128]{1,0:T(8,128)S(1)}, f32[32,128]{1,0:T(8,128)S(1)}, u32[]{:S(2)}, u32[]{:S(2)}) collective-permute-start(f32[32,128]{1,0:T(8,128)S(1)} %row_pass.3.refs_0_), channel_id=1, source_target_pairs={{0,2},{1,3},{2,0},{3,1},{4,6},{5,7},{6,4},{7,5},{8,10},{9,11},{10,... | collective-permute-start | bytes 49160 | tf_op jit(solution)/shard_map/ppermute | solution.py:67
  73.5 2.2 %collective-permute-start.13 = (f32[32,128]{1,0:T(8,128)S(1)}, f32[32,128]{1,0:T(8,128)S(1)}, u32[]{:S(2)}, u32[]{:S(2)}) collective-permute-start(f32[32,128]{1,0:T(8,128)S(1)} %row_pass.3.refs_0_), channel_id=1, source_target_pairs={{0,1},{1,0},{2,3},{3,2},{4,5},{5,4},{6,7},{7,6},{8,9},{9,8},{10,11... | collective-permute-start | bytes 49160 | tf_op jit(solution)/shard_map/ppermute | solution.py:67

commit v17 on v16

--- a/solution.py
+++ b/solution.py
@@ -429,7 +429,7 @@
     )(near_t, in_hbm(near_cost), in_hbm(coupling), mass, packs)
 
     far_bytes = group_blocks * link_count * width * width * 4
-    far_rows = 2 * step_rows if rows_here % (2 * step_rows) == 0 else step_rows
+    far_rows = rows_here
     steps = rows_here // far_rows
     work_shape = pltpu.VMEM((rows_here, slots, width, width), f32)
     cost_blocks, work, tall, row_part, log_source, log_target, select = pl.pallas_call(

time: 86.8 us -> 86.5 us (level)
  no operation moved by 1% of the time
where the time goes in v17:
time: 86.5 us; the launch traced here: 86.1 us
  blocking collectives  29 us (34%)
  Pallas kernels  24.2 us (28%)
  starting transfers between devices  21.4 us (25%)
  waiting for transfers between devices  10.9 us (13%)
    all_to_all x3, blocking collectives, exchange(): return lax.all_to_all(copies, axis, 0, 0, tiled=True)  29 us
    ppermute x16, starting transfers between devices, send(): return lax.ppermute(x, axis, [(d, d ^ mask) for d in range(size)])  17.6 us
    ppermute x16, waiting for transfers between devices, send(): return lax.ppermute(x, axis, [(d, d ^ mask) for d in range(size)])  10.8 us
    pallas_call x1, Pallas kernels, per_device(): pl.pallas_call(near_kernel, grid=(rows_here // step_rows,), in_specs=[ANY...  7.69 us
    pallas_call x1, Pallas kernels, per_device(): pl.pallas_call(functools.partial(far_kernel, (row_devices, col_devices, t...  7.55 us
    pallas_call x3, Pallas kernels, column_step(): pl.pallas_call(functools.partial(column_kernel, copies), in_specs=[VMEM]...  3.95 us
    all_to_all x1, starting transfers between devices, exchange(): return lax.all_to_all(copies, axis, 0, 0, tiled=True)  3.82 us
    pallas_call x2, Pallas kernels, row_step(): pl.pallas_call(functools.partial(row_kernel, row_devices), in_specs=[ANY,...  2.89 us
  transfers between devices with their start and end apart: 17, of which 8 were waited for; matrix products, arithmetic and copies ran while one was open for 0% of the time, Pallas kernels for 11%

profile of v17, /device:TPU:0, one launch (start us, length us, event | category | flops | bytes accessed | tf_op | source)
XLA Modules:
  0.0 86.1 jit_solution(8380217333660499753)
XLA Ops:
  0.6 4.0 %collective-permute-start.2 = (f32[1,1,3,128,128]{4,3,2,1,0:T(8,128)}, f32[1,1,3,128,128]{4,3,2,1,0:T(8,128)S(1)}, u32[]{:S(2)}, u32[]{:S(2)}) collective-permute-start(f32[1,1,3,128,128]{4,3,2,1,0:T(8,128)} %refs_6_.1), channel_id=1, source_target_pairs={{0,12},{4,8},{8,4},{12,0},{16,28},{20,24},{24,20},{28,16},{1,13},{... | collective-permute-start | bytes 589832 | tf_op jit(solution)/shard_map/ppermute | solution.py:67
  4.7 0.4 collective-permute-start.1
  5.3 2.9 %collective-permute-start.3 = (f32[1,1,3,128,128]{4,3,2,1,0:T(8,128)}, f32[1,1,3,128,128]{4,3,2,1,0:T(8,128)S(1)}, u32[]{:S(2)}, u32[]{:S(2)}) collective-permute-start(f32[1,1,3,128,128]{4,3,2,1,0:T(8,128)} %refs_6_.1), channel_id=1, source_target_pairs={{0,16},{4,20},{8,24},{12,28},{16,0},{20,4},{24,8},{28,12},{1,17},{... | collective-permute-start | bytes 589832 | tf_op jit(solution)/shard_map/ppermute | solution.py:67
  8.2 1.5 %pack.1 = (f32[64,128]{1,0:T(8,128)}, s32[3,32]{1,0:T(4,128)S(1)}, s32[2,32]{1,0:T(2,128)S(1)}, s32[3,1,8]{2,1,0:T(1,128)S(1)}, s32[32,128]{1,0:T(8,128)S(1)}) custom-call(s32[32,128]{1,0:T(8,128)} %bitcast.25, s32[1,128]{1,0:T(1,128)} %target_ref.1, s32[3,32]{1,0:T(4,128)} %bitcast.27, s32[2,32]{1,0:T(2,128)} %bitcast.29, s32[3,1,8]{2,1,0:T(1,128)} %bitcast.28, ...), custom_call_target="tpu_custom_call" | custom-call | tf_op jit(solution)/shard_map/pack/pallas_call | solution.py:372
  9.8 3.8 %all-to-all-start = ((f32[32,2,128]{2,1,0:T(2,128)}), f32[32,2,128]{2,1,0:T(2,128)S(1)}, u32[]{:S(2)}, u32[]{:S(2)}) async-start(f32[32,2,128]{2,1,0:T(2,128)} %bitcast.5), calls=%async_computation | async-start | bytes 65536 | tf_op jit(solution)/shard_map/all_to_all | solution.py:75
  13.6 1.3 %collective-permute-done.2.refs_2_ = f32[1,1,3,128,128]{4,3,2,1,0:T(8,128)S(1)} collective-permute-done((f32[1,1,3,128,128]{4,3,2,1,0:T(8,128)}, f32[1,1,3,128,128]{4,3,2,1,0:T(8,128)S(1)}, u32[]{:S(2)}, u32[]{:S(2)}) %collective-permute-start.2) | collective-permute-done | bytes 196640 | tf_op jit(solution)/shard_map/ppermute | solution.py:67
  14.9 3.7 %collective-permute-done.1.refs_1_ = f32[1,1,3,128,128]{4,3,2,1,0:T(8,128)S(1)} collective-permute-done((f32[1,1,3,128,128]{4,3,2,1,0:T(8,128)}, f32[1,1,3,128,128]{4,3,2,1,0:T(8,128)S(1)}, u32[]{:S(2)}, u32[]{:S(2)}) %collective-permute-start.1) | collective-permute-done | bytes 196640 | tf_op jit(solution)/shard_map/ppermute | solution.py:67
  18.6 2.6 %collective-permute-start.6 = (f32[1,1,3,128,128]{4,3,2,1,0:T(8,128)S(1)}, f32[1,1,3,128,128]{4,3,2,1,0:T(8,128)S(1)}, u32[]{:S(2)}, u32[]{:S(2)}) collective-permute-start(f32[1,1,3,128,128]{4,3,2,1,0:T(8,128)S(1)} %get-tuple-element.35.refs_10_), channel_id=1, source_target_pairs={{0,12},{4,8},{8,4},{12,0},{16,28},{20,24},{24,20},{28,16},{1,13},{... | collective-permute-start | bytes 589832 | tf_op jit(solution)/shard_map/ppermute | solution.py:67
  21.3 1.5 %collective-permute-start.4 = (f32[1,1,3,128,128]{4,3,2,1,0:T(8,128)S(1)}, f32[1,1,3,128,128]{4,3,2,1,0:T(8,128)S(1)}, u32[]{:S(2)}, u32[]{:S(2)}) collective-permute-start(f32[1,1,3,128,128]{4,3,2,1,0:T(8,128)S(1)} %get-tuple-element.35.refs_10_), channel_id=1, source_target_pairs={{0,4},{4,0},{8,12},{12,8},{16,20},{20,16},{24,28},{28,24},{1,5},{5... | collective-permute-start | bytes 589832 | tf_op jit(solution)/shard_map/ppermute | solution.py:67
  22.8 7.7 %near_product.1 = (bf16[32,256,768]{2,1,0:T(8,128)(2,1)S(1)}, f32[8,128,4]{2,1,0:T(8,128)S(1)}) custom-call(s32[3,32]{1,0:T(4,128)S(1)} %get-tuple-element.25.near_any.refs_0_, f32[32,3,128,128]{3,2,1,0:T(8,128)} %cost_ref.1, f32[32,1,2,128,128]{4,3,2,1,0:T(8,128)} %plan_ref.1, s32[32,128]{1,0:T(8,128)S(1)} %get-tuple-element.28.mass_ref.refs_5_, ...), custom_call_target="tpu_custom_call" | custom-call | flops 2415919104 | bytes 10485760 | tf_op jit(solution)/shard_map/near_product/pallas_call | solution.py:402
  30.5 7.5 %far_product.1 = (f32[32,1,2,128,128]{4,3,2,1,0:T(8,128)}, f32[32,2,128,128]{3,2,1,0:T(8,128)S(1)}, f32[32,2,128,128]{3,2,1,0:T(8,128)S(1)}, f32[32,128]{1,0:T(8...) custom-call(s32[3,32]{1,0:T(4,128)S(1)} %get-tuple-element.25.near_any.refs_0_, ...), custom_call_target="tpu_custom_call" | custom-call | tf_op jit(solution)/shard_map/far_product/pallas_call | solution.py:435
  38.2 1.5 %collective-permute-start.8 = (f32[32,128]{1,0:T(8,128)S(1)}, f32[32,128]{1,0:T(8,128)S(1)}, u32[]{:S(2)}, u32[]{:S(2)}) collective-permute-start(f32[32,128]{1,0:T(8,128)S(1)} %get-tuple-element.42.refs_0_), channel_id=1, source_target_pairs={{0,2},{1,3},{2,0},{3,1},{4,6},{5,7},{6,4},{7,5},{8,10},{9,11},{10,... | collective-permute-start | bytes 49160 | tf_op jit(solution)/shard_map/ppermute | solution.py:67
  39.7 0.3 collective-permute-start.7
  40.0 1.4 %collective-permute-done.9.refs_3_ = f32[32,128]{1,0:T(8,128)S(1)} collective-permute-done((f32[32,128]{1,0:T(8,128)S(1)}, f32[32,128]{1,0:T(8,128)S(1)}, u32[]{:S(2)}, u32[]{:S(2)}) %collective-permute-start.9) | collective-permute-done | bytes 16416 | tf_op jit(solution)/shard_map/ppermute | solution.py:67
  41.5 0.5 collective-permute-done.8.refs_2_
  42.0 1.3 %column_pass.3 = (f32[64,128]{1,0:T(8,128)S(1)}, f32[32,128]{1,0:T(8,128)}) custom-call(f32[32,2,128,128]{3,2,1,0:T(8,128)S(1)} %get-tuple-element.37.work_ref, s32[64,128]{1,0:T(8,128)S(1)} %get-tuple-element.38.select_ref, f32[32,128]{1,0:T(8,128)S(1)} %get-tuple-element.39.log_mass_ref, f32[32,128]{1,0:T(8,128)S(1)} %get-tuple-element.42.refs_0_, ...), custom_call_target="tpu_custom_call" | custom-call | tf_op jit(solution)/shard_map/column_pass/pallas_call | solution.py:486
  43.3 10.9 %all_to_all.44 = f32[8,8,128]{2,1,0:T(8,128)S(1)} all-to-all(f32[8,8,128]{2,1,0:T(8,128)S(1)} %bitcast.21), channel_id=1, replica_groups=mesh['rows'=8,'cols'=4] {'rows'}, dimensions={0} | all-to-all | bytes 65536 | tf_op jit(solution)/shard_map/all_to_all | solution.py:75
  54.2 1.4 %row_pass.2.refs_0_ = f32[32,128]{1,0:T(8,128)S(1)} custom-call(s32[2,32]{1,0:T(2,128)S(1)} %get-tuple-element.26.refs_1_.slot_any, f32[32,2,128,128]{3,2,1,0:T(8,128)S(1)} %get-tuple-element.40.tall_ref, f32[8,128]{1,0:T(8,128)S(1)} %get-tuple-element.41.log_mass_ref, f32[64,128]{1,0:T(8,128)S(1)} %bitcast.20), custom_call_target="tpu_custom_call" | custom-call | tf_op jit(solution)/shard_map/row_pass/pallas_call | solution.py:504
  55.7 1.6 %collective-permute-start.11 = (f32[32,128]{1,0:T(8,128)S(1)}, f32[32,128]{1,0:T(8,128)S(1)}, u32[]{:S(2)}, u32[]{:S(2)}) collective-permute-start(f32[32,128]{1,0:T(8,128)S(1)} %row_pass.2.refs_0_), channel_id=1, source_target_pairs={{0,2},{1,3},{2,0},{3,1},{4,6},{5,7},{6,4},{7,5},{8,10},{9,11},{10,... | collective-permute-start | bytes 49160 | tf_op jit(solution)/shard_map/ppermute | solution.py:67
  57.3 0.3 collective-permute-start.10
  57.6 1.4 %collective-permute-done.12.refs_3_ = f32[32,128]{1,0:T(8,128)S(1)} collective-permute-done((f32[32,128]{1,0:T(8,128)S(1)}, f32[32,128]{1,0:T(8,128)S(1)}, u32[]{:S(2)}, u32[]{:S(2)}) %collective-permute-start.12) | collective-permute-done | bytes 16416 | tf_op jit(solution)/shard_map/ppermute | solution.py:67
  59.0 0.5 collective-permute-done.11.refs_2_
  59.6 1.3 %column_pass.4 = (f32[64,128]{1,0:T(8,128)S(1)}, f32[32,128]{1,0:T(8,128)}) custom-call(f32[32,2,128,128]{3,2,1,0:T(8,128)S(1)} %get-tuple-element.37.work_ref, s32[64,128]{1,0:T(8,128)S(1)} %get-tuple-element.38.select_ref, f32[32,128]{1,0:T(8,128)S(1)} %get-tuple-element.39.log_mass_ref, f32[32,128]{1,0:T(8,128)S(1)} %row_pass.2.refs_0_, ...), custom_call_target="tpu_custom_call" | custom-call | tf_op jit(solution)/shard_map/column_pass/pallas_call | solution.py:486
  60.9 9.2 %all_to_all.45 = f32[8,8,128]{2,1,0:T(8,128)S(1)} all-to-all(f32[8,8,128]{2,1,0:T(8,128)S(1)} %bitcast.22), channel_id=1, replica_groups=mesh['rows'=8,'cols'=4] {'rows'}, dimensions={0} | all-to-all | bytes 65536 | tf_op jit(solution)/shard_map/all_to_all | solution.py:75
  70.1 1.4 %row_pass.3.refs_0_ = f32[32,128]{1,0:T(8,128)S(1)} custom-call(s32[2,32]{1,0:T(2,128)S(1)} %get-tuple-element.26.refs_1_.slot_any, f32[32,2,128,128]{3,2,1,0:T(8,128)S(1)} %get-tuple-element.40.tall_ref, f32[8,128]{1,0:T(8,128)S(1)} %get-tuple-element.41.log_mass_ref, f32[64,128]{1,0:T(8,128)S(1)} %bitcast.19), custom_call_target="tpu_custom_call" | custom-call | tf_op jit(solution)/shard_map/row_pass/pallas_call | solution.py:504
  71.6 1.6 %collective-permute-start.14 = (f32[32,128]{1,0:T(8,128)S(1)}, f32[32,128]{1,0:T(8,128)S(1)}, u32[]{:S(2)}, u32[]{:S(2)}) collective-permute-start(f32[32,128]{1,0:T(8,128)S(1)} %row_pass.3.refs_0_), channel_id=1, source_target_pairs={{0,2},{1,3},{2,0},{3,1},{4,6},{5,7},{6,4},{7,5},{8,10},{9,11},{10,... | collective-permute-start | bytes 49160 | tf_op jit(solution)/shard_map/ppermute | solution.py:67
  73.2 0.3 collective-permute-start.13
  73.5 1.4 %collective-permute-done.15.refs_3_ = f32[32,128]{1,0:T(8,128)S(1)} collective-permute-done((f32[32,128]{1,0:T(8,128)S(1)}, f32[32,128]{1,0:T(8,128)S(1)}, u32[]{:S(2)}, u32[]{:S(2)}) %collective-permute-start.15) | collective-permute-done | bytes 16416 | tf_op jit(solution)/shard_map/ppermute | solution.py:67
  74.9 0.5 collective-permute-done.14.refs_2_
  75.5 1.3 %column_pass.5 = (f32[8,128]{1,0:T(8,128)S(1)}, f32[32,128]{1,0:T(8,128)}) custom-call(f32[32,2,128,128]{3,2,1,0:T(8,128)S(1)} %get-tuple-element.37.work_ref, s32[64,128]{1,0:T(8,128)S(1)} %get-tuple-element.38.select_ref, f32[32,128]{1,0:T(8,128)S(1)} %get-tuple-element.39.log_mass_ref, f32[32,128]{1,0:T(8,128)S(1)} %row_pass.3.refs_0_, ...), custom_call_target="tpu_custom_call" | custom-call | tf_op jit(solution)/shard_map/column_pass/pallas_call | solution.py:486
  76.8 8.8 %all_to_all.46 = f32[8,1,128]{2,1,0:T(1,128)S(1)} all-to-all(f32[8,1,128]{2,1,0:T(1,128)S(1)} %bitcast.24), channel_id=1, replica_groups=mesh['rows'=8,'cols'=4] {'rows'}, dimensions={0} | all-to-all | bytes 8192 | tf_op jit(solution)/shard_map/all_to_all | solution.py:75
  85.6 0.5 last_potential.1
  (17 shorter events, 0.6 us)
Async XLA Ops:
  0.6 14.2 %collective-permute-start.2 = (f32[1,1,3,128,128]{4,3,2,1,0:T(8,128)}, f32[1,1,3,128,128]{4,3,2,1,0:T(8,128)S(1)}, u32[]{:S(2)}, u32[]{:S(2)}) collective-permute-start(f32[1,1,3,128,128]{4,3,2,1,0:T(8,128)} %refs_6_.1), channel_id=1, source_target_pairs={{0,12},{4,8},{8,4},{12,0},{16,28},{20,24},{24,20},{28,16},{1,13},{... | collective-permute-start | bytes 589832 | tf_op jit(solution)/shard_map/ppermute | solution.py:67
  4.7 13.9 %collective-permute-start.1 = (f32[1,1,3,128,128]{4,3,2,1,0:T(8,128)}, f32[1,1,3,128,128]{4,3,2,1,0:T(8,128)S(1)}, u32[]{:S(2)}, u32[]{:S(2)}) collective-permute-start(f32[1,1,3,128,128]{4,3,2,1,0:T(8,128)} %refs_6_.1), channel_id=1, source_target_pairs={{0,8},{4,12},{8,0},{12,4},{16,24},{20,28},{24,16},{28,20},{1,9},{5... | collective-permute-start | bytes 589832 | tf_op jit(solution)/shard_map/ppermute | solution.py:67
  5.1 13.4 %collective-permute-start = (f32[1,1,3,128,128]{4,3,2,1,0:T(8,128)}, f32[1,1,3,128,128]{4,3,2,1,0:T(8,128)S(1)}, u32[]{:S(2)}, u32[]{:S(2)}) collective-permute-start(f32[1,1,3,128,128]{4,3,2,1,0:T(8,128)} %refs_6_.1), channel_id=1, source_target_pairs={{0,4},{4,0},{8,12},{12,8},{16,20},{20,16},{24,28},{28,24},{1,5},{5... | collective-permute-start | bytes 589832 | tf_op jit(solution)/shard_map/ppermute | solution.py:67
  5.3 13.2 %collective-permute-start.3 = (f32[1,1,3,128,128]{4,3,2,1,0:T(8,128)}, f32[1,1,3,128,128]{4,3,2,1,0:T(8,128)S(1)}, u32[]{:S(2)}, u32[]{:S(2)}) collective-permute-start(f32[1,1,3,128,128]{4,3,2,1,0:T(8,128)} %refs_6_.1), channel_id=1, source_target_pairs={{0,16},{4,20},{8,24},{12,28},{16,0},{20,4},{24,8},{28,12},{1,17},{... | collective-permute-start | bytes 589832 | tf_op jit(solution)/shard_map/ppermute | solution.py:67
  9.8 13.0 %all-to-all-start = ((f32[32,2,128]{2,1,0:T(2,128)}), f32[32,2,128]{2,1,0:T(2,128)S(1)}, u32[]{:S(2)}, u32[]{:S(2)}) async-start(f32[32,2,128]{2,1,0:T(2,128)} %bitcast.5), calls=%async_computation | async-start | bytes 65536 | tf_op jit(solution)/shard_map/all_to_all | solution.py:75
  18.6 11.9 %collective-permute-start.6 = (f32[1,1,3,128,128]{4,3,2,1,0:T(8,128)S(1)}, f32[1,1,3,128,128]{4,3,2,1,0:T(8,128)S(1)}, u32[]{:S(2)}, u32[]{:S(2)}) collective-permute-start(f32[1,1,3,128,128]{4,3,2,1,0:T(8,128)S(1)} %get-tuple-element.35.refs_10_), channel_id=1, source_target_pairs={{0,12},{4,8},{8,4},{12,0},{16,28},{20,24},{24,20},{28,16},{1,13},{... | collective-permute-start | bytes 589832 | tf_op jit(solution)/shard_map/ppermute | solution.py:67
  21.2 9.3 %collective-permute-start.5 = (f32[1,1,3,128,128]{4,3,2,1,0:T(8,128)S(1)}, f32[1,1,3,128,128]{4,3,2,1,0:T(8,128)S(1)}, u32[]{:S(2)}, u32[]{:S(2)}) collective-permute-start(f32[1,1,3,128,128]{4,3,2,1,0:T(8,128)S(1)} %get-tuple-element.35.refs_10_), channel_id=1, source_target_pairs={{0,8},{4,12},{8,0},{12,4},{16,24},{20,28},{24,16},{28,20},{1,9},{5... | collective-permute-start | bytes 589832 | tf_op jit(solution)/shard_map/ppermute | solution.py:67
  21.3 9.2 %collective-permute-start.4 = (f32[1,1,3,128,128]{4,3,2,1,0:T(8,128)S(1)}, f32[1,1,3,128,128]{4,3,2,1,0:T(8,128)S(1)}, u32[]{:S(2)}, u32[]{:S(2)}) collective-permute-start(f32[1,1,3,128,128]{4,3,2,1,0:T(8,128)S(1)} %get-tuple-element.35.refs_10_), channel_id=1, source_target_pairs={{0,4},{4,0},{8,12},{12,8},{16,20},{20,16},{24,28},{28,24},{1,5},{5... | collective-permute-start | bytes 589832 | tf_op jit(solution)/shard_map/ppermute | solution.py:67
  22.8 7.7 %copy-start = (f32[1,1,3,128,128]{4,3,2,1,0:T(8,128)S(1)}, f32[1,1,3,128,128]{4,3,2,1,0:T(8,128)}, u32[]{:S(2)}) copy-start(f32[1,1,3,128,128]{4,3,2,1,0:T(8,128)} %refs_6_.1) | copy-start | bytes 589828
  38.1 3.4 %collective-permute-start.9 = (f32[32,128]{1,0:T(8,128)S(1)}, f32[32,128]{1,0:T(8,128)S(1)}, u32[]{:S(2)}, u32[]{:S(2)}) collective-permute-start(f32[32,128]{1,0:T(8,128)S(1)} %get-tuple-element.42.refs_0_), channel_id=1, source_target_pairs={{0,3},{1,2},{2,1},{3,0},{4,7},{5,6},{6,5},{7,4},{8,11},{9,10},{10,... | collective-permute-start | bytes 49160 | tf_op jit(solution)/shard_map/ppermute | solution.py:67
  38.2 3.8 %collective-permute-start.8 = (f32[32,128]{1,0:T(8,128)S(1)}, f32[32,128]{1,0:T(8,128)S(1)}, u32[]{:S(2)}, u32[]{:S(2)}) collective-permute-start(f32[32,128]{1,0:T(8,128)S(1)} %get-tuple-element.42.refs_0_), channel_id=1, source_target_pairs={{0,2},{1,3},{2,0},{3,1},{4,6},{5,7},{6,4},{7,5},{8,10},{9,11},{10,... | collective-permute-start | bytes 49160 | tf_op jit(solution)/shard_map/ppermute | solution.py:67
  39.7 2.3 %collective-permute-start.7 = (f32[32,128]{1,0:T(8,128)S(1)}, f32[32,128]{1,0:T(8,128)S(1)}, u32[]{:S(2)}, u32[]{:S(2)}) collective-permute-start(f32[32,128]{1,0:T(8,128)S(1)} %get-tuple-element.42.refs_0_), channel_id=1, source_target_pairs={{0,1},{1,0},{2,3},{3,2},{4,5},{5,4},{6,7},{7,6},{8,9},{9,8},{10,11... | collective-permute-start | bytes 49160 | tf_op jit(solution)/shard_map/ppermute | solution.py:67
  55.7 3.3 %collective-permute-start.12 = (f32[32,128]{1,0:T(8,128)S(1)}, f32[32,128]{1,0:T(8,128)S(1)}, u32[]{:S(2)}, u32[]{:S(2)}) collective-permute-start(f32[32,128]{1,0:T(8,128)S(1)} %row_pass.2.refs_0_), channel_id=1, source_target_pairs={{0,3},{1,2},{2,1},{3,0},{4,7},{5,6},{6,5},{7,4},{8,11},{9,10},{10,... | collective-permute-start | bytes 49160 | tf_op jit(solution)/shard_map/ppermute | solution.py:67
  55.7 3.8 %collective-permute-start.11 = (f32[32,128]{1,0:T(8,128)S(1)}, f32[32,128]{1,0:T(8,128)S(1)}, u32[]{:S(2)}, u32[]{:S(2)}) collective-permute-start(f32[32,128]{1,0:T(8,128)S(1)} %row_pass.2.refs_0_), channel_id=1, source_target_pairs={{0,2},{1,3},{2,0},{3,1},{4,6},{5,7},{6,4},{7,5},{8,10},{9,11},{10,... | collective-permute-start | bytes 49160 | tf_op jit(solution)/shard_map/ppermute | solution.py:67
  57.3 2.2 %collective-permute-start.10 = (f32[32,128]{1,0:T(8,128)S(1)}, f32[32,128]{1,0:T(8,128)S(1)}, u32[]{:S(2)}, u32[]{:S(2)}) collective-permute-start(f32[32,128]{1,0:T(8,128)S(1)} %row_pass.2.refs_0_), channel_id=1, source_target_pairs={{0,1},{1,0},{2,3},{3,2},{4,5},{5,4},{6,7},{7,6},{8,9},{9,8},{10,11... | collective-permute-start | bytes 49160 | tf_op jit(solution)/shard_map/ppermute | solution.py:67
  71.6 3.3 %collective-permute-start.15 = (f32[32,128]{1,0:T(8,128)S(1)}, f32[32,128]{1,0:T(8,128)S(1)}, u32[]{:S(2)}, u32[]{:S(2)}) collective-permute-start(f32[32,128]{1,0:T(8,128)S(1)} %row_pass.3.refs_0_), channel_id=1, source_target_pairs={{0,3},{1,2},{2,1},{3,0},{4,7},{5,6},{6,5},{7,4},{8,11},{9,10},{10,... | collective-permute-start | bytes 49160 | tf_op jit(solution)/shard_map/ppermute | solution.py:67
  71.6 3.8 %collective-permute-start.14 = (f32[32,128]{1,0:T(8,128)S(1)}, f32[32,128]{1,0:T(8,128)S(1)}, u32[]{:S(2)}, u32[]{:S(2)}) collective-permute-start(f32[32,128]{1,0:T(8,128)S(1)} %row_pass.3.refs_0_), channel_id=1, source_target_pairs={{0,2},{1,3},{2,0},{3,1},{4,6},{5,7},{6,4},{7,5},{8,10},{9,11},{10,... | collective-permute-start | bytes 49160 | tf_op jit(solution)/shard_map/ppermute | solution.py:67
  73.2 2.2 %collective-permute-start.13 = (f32[32,128]{1,0:T(8,128)S(1)}, f32[32,128]{1,0:T(8,128)S(1)}, u32[]{:S(2)}, u32[]{:S(2)}) collective-permute-start(f32[32,128]{1,0:T(8,128)S(1)} %row_pass.3.refs_0_), channel_id=1, source_target_pairs={{0,1},{1,0},{2,3},{3,2},{4,5},{5,4},{6,7},{7,6},{8,9},{9,8},{10,11... | collective-permute-start | bytes 49160 | tf_op jit(solution)/shard_map/ppermute | solution.py:67
